TPU v7x, 32 devices: a whole 2x2x4 slice. The times are simulated.
32 devices in a mesh: seq: 8 (over z, y), wshard: 4 (over x, core).
Axes of the slice: x: 2, y: 2, z: 4, core: 2. Of those that a mesh axis runs over, the one named last changes fastest.
Arguments:
- hidden_in: bfloat16 [4, 8192, 768], P('wshard', 'seq'), may hold values from -6 to 6
- cotangent: bfloat16 [4, 8192, 768], P('wshard', 'seq'), may hold values from -6 to 6
- block_seq: int32 [4, 8], P('wshard'), may hold values from 0 to 31, as said below
- block_place: int32 [4, 8], P('wshard'), may hold values from 0 to 3, as said below
- attn_in: bfloat16 [768, 2304], P('wshard'), may hold values from -0.21875 to 0.21875
- attn_out: bfloat16 [768, 768], P('wshard'), may hold values from -1.25 to 1.25
- ffn_in: bfloat16 [768, 2304], P('wshard'), may hold values from -0.21875 to 0.21875
- ffn_out: bfloat16 [1152, 768], P('wshard'), may hold values from -0.1875 to 0.1875
- norm_attn: bfloat16 [768], P('wshard'), may hold values from 0.5 to 1.5
- norm_ffn: bfloat16 [768], P('wshard'), may hold values from 0.5 to 1.5
- first_attn_in: float32 [768, 2304], P('wshard'), may hold values from -128 to 128
- first_attn_out: float32 [768, 768], P('wshard'), may hold values from -24 to 24
- first_ffn_in: float32 [768, 2304], P('wshard'), may hold values from -64 to 64
- first_ffn_out: float32 [1152, 768], P('wshard'), may hold values from -80 to 80
- first_norm_attn: float32 [768], P('wshard'), may hold values from -160 to 160
- first_norm_ffn: float32 [768], P('wshard'), may hold values from -112 to 112
- second_attn_in: float32 [768, 2304], P('wshard'), may hold values from 163.84 to 1310.72
- second_attn_out: float32 [768, 768], P('wshard'), may hold values from 13.1072 to 98.304
- second_ffn_in: float32 [768, 2304], P('wshard'), may hold values from 65.536 to 327.68
- second_ffn_out: float32 [1152, 768], P('wshard'), may hold values from 98.304 to 557.056
- second_norm_attn: float32 [768], P('wshard'), may hold values from 327.68 to 1966.08
- second_norm_ffn: float32 [768], P('wshard'), may hold values from 163.84 to 983.04
Outputs:
- block_out: bfloat16 [4, 8192, 768], P('wshard', 'seq')
- grad_in: bfloat16 [4, 8192, 768], P('wshard', 'seq')
- grad_attn_in: float32 [768, 2304], P('wshard')
- grad_attn_out: float32 [768, 768], P('wshard')
- grad_ffn_in: float32 [768, 2304], P('wshard')
- grad_ffn_out: float32 [1152, 768], P('wshard')
- grad_norm_attn: float32 [768], P('wshard')
- grad_norm_ffn: float32 [768], P('wshard')
- new_first_attn_in: float32 [768, 2304], P('wshard')
- new_first_attn_out: float32 [768, 768], P('wshard')
- new_first_ffn_in: float32 [768, 2304], P('wshard')
- new_first_ffn_out: float32 [1152, 768], P('wshard')
- new_first_norm_attn: float32 [768], P('wshard')
- new_first_norm_ffn: float32 [768], P('wshard')
- new_second_attn_in: float32 [768, 2304], P('wshard')
- new_second_attn_out: float32 [768, 768], P('wshard')
- new_second_ffn_in: float32 [768, 2304], P('wshard')
- new_second_ffn_out: float32 [1152, 768], P('wshard')
- new_second_norm_attn: float32 [768], P('wshard')
- new_second_norm_ffn: float32 [768], P('wshard')
- step_attn_in: float32 [768, 2304], P('wshard')
- step_attn_out: float32 [768, 768], P('wshard')
- step_ffn_in: float32 [768, 2304], P('wshard')
- step_ffn_out: float32 [1152, 768], P('wshard')
- step_norm_attn: float32 [768], P('wshard')
- step_norm_ffn: float32 [768], P('wshard')
Inputs may be any that keep to these rules, and one draw needn't show every extreme that they name: `block_seq`: blocks of one sequence are consecutive within a stream and share one id; ids of different sequences differ, also across streams; a sequence has 4, 2 or 1 blocks, fewer only where a stream begins or ends; in every stream block 4 is the third block of a sequence of 4 blocks. `block_place`: counts 0, 1, 2 upward along the blocks of each sequence.
All inputs are finite; a program needn't handle non-finite values.
Results may differ from a plain program's by a relative error of at most 0.025.
Values may be sent and summed in bfloat16 or wider, within the bound.
No kernel may reach another device: no remote copies, remote signals or barrier semaphores. Data moves between devices by JAX's collectives and lax.ppermute only.
A program may use at most 256 MiB of HBM per device.

v0:
```python
import jax
import jax.numpy as jnp
from jax import lax
from jax.sharding import PartitionSpec as P

D = 768
FF = 1152
HEADS = 12
HD = 64
HALF = 64
STEP = 10
QBLK = 512


NORM_EPS = 1e-05
BETA_ONE = 0.9
BETA_TWO = 0.98
LEARN_RATE = 0.05
WEIGHT_DECAY = 0.01
ADAM_EPS = 1e-06
NEG_FILL = -1e30
THETA = 10000.0


def with_halo(shard, sides, width):
    for axis, dim in sides:
        count, length = (lax.axis_size(axis), shard.shape[dim])
        up = [(i, (i + 1) % count) for i in range(count - 1)]
        down = [(j, i) for i, j in up]
        last = lax.slice_in_dim(shard, length - width, length, axis=dim)
        first = lax.slice_in_dim(shard, 0, width, axis=dim)
        before = lax.ppermute(last, axis, up)
        after = lax.ppermute(first, axis, down)
        shard = jnp.concatenate([before, shard, after], axis=dim)
    return shard


def layer_norm(inputs, scales):
    row_mean = jnp.mean(inputs, axis=-1, keepdims=True)
    centered = inputs - row_mean
    variance = jnp.mean(centered * centered, axis=-1, keepdims=True)
    return centered * lax.rsqrt(variance + NORM_EPS) * scales


def rotary(inputs, positions, turning):
    half_dim = HD // 2
    frequency = THETA ** (-2.0 * jnp.arange(half_dim).astype(jnp.float32) / HD)
    angles = positions.astype(jnp.float32)[:, None] * frequency[None, :]
    cosine = jnp.cos(angles)[:, None, :]
    sine_part = turning * jnp.sin(angles)[:, None, :]
    first_half = inputs[..., :half_dim]
    second_half = inputs[..., half_dim:]
    return jnp.concatenate(
        [
            first_half * cosine - second_half * sine_part,
            second_half * cosine + first_half * sine_part,
        ],
        axis=-1,
    )


def gated_unit(gate_up):
    return jax.nn.gelu(gate_up[:, :FF], approximate=False) * gate_up[:, FF:]


def rows_contract(left, right):
    return lax.dot_general(
        left, right, (((0,), (0,)), ((), ())), preferred_element_type=jnp.float32
    )


def cols_contract(left, right):
    return lax.dot_general(
        left, right, (((1,), (1,)), ((), ())), preferred_element_type=jnp.float32
    )


def window_mask(valid_win):
    query_count = valid_win.shape[0] - 2 * HALF
    offsets = jnp.arange(query_count + 2 * HALF)[None, :] - jnp.arange(query_count)[:, None]
    return (offsets >= 0) & (offsets <= 2 * HALF) & valid_win[None, :]


def block_scores(query_blk, window, allowed):
    key_win = window[:, :D].reshape(window.shape[0], HEADS, HD)
    scores = jnp.einsum(
        "qhd,khd->hqk", query_blk, key_win, preferred_element_type=jnp.float32
    ) * HD ** (-0.5)
    return jnp.where(allowed[None], scores, NEG_FILL)


def forward_pass(x_rows, full_weights, own_place, valid_ext, rim_fn):
    attn_w, out_w, ffn_w, down_w, norm_one, norm_two = full_weights
    row_count = x_rows.shape[0]
    win_rows = QBLK + 2 * HALF
    inputs = x_rows.astype(jnp.float32)
    normed = layer_norm(inputs, norm_one.astype(jnp.float32)).astype(jnp.bfloat16)
    qkv_rows = jnp.dot(normed, attn_w, preferred_element_type=jnp.float32)
    positions = own_place * row_count + jnp.arange(row_count, dtype=jnp.int32)
    queries = rotary(qkv_rows[:, :D].reshape(row_count, HEADS, HD), positions, 1.0).astype(
        jnp.bfloat16
    )
    key_rows = rotary(qkv_rows[:, D : 2 * D].reshape(row_count, HEADS, HD), positions, 1.0).astype(
        jnp.bfloat16
    )
    value_rows = qkv_rows[:, 2 * D :].astype(jnp.bfloat16)
    own_pairs = jnp.concatenate([key_rows.reshape(row_count, D), value_rows], axis=1)
    key_value = rim_fn(own_pairs)
    mixed_parts = []
    log_totals = []
    for blk_start in range(0, row_count, QBLK):
        window = key_value[blk_start : blk_start + win_rows]
        allowed = window_mask(valid_ext[blk_start : blk_start + win_rows])
        scores = block_scores(queries[blk_start : blk_start + QBLK], window, allowed)
        row_max = jnp.max(scores, axis=-1, keepdims=True)
        exp_scores = jnp.exp(scores - row_max)
        row_total = jnp.sum(exp_scores, axis=-1, keepdims=True)
        soft_probs = (exp_scores / row_total).astype(jnp.bfloat16)
        log_totals.append(row_max + jnp.log(row_total))
        value_win = window[:, D:].reshape(win_rows, HEADS, HD)
        mixed_parts.append(
            jnp.einsum("hqk,khd->qhd", soft_probs, value_win, preferred_element_type=jnp.float32)
        )
    mixed_rows = jnp.concatenate(mixed_parts, axis=0).reshape(row_count, D).astype(jnp.bfloat16)
    middle = inputs + jnp.dot(mixed_rows, out_w, preferred_element_type=jnp.float32)
    normed_two = layer_norm(middle, norm_two.astype(jnp.float32)).astype(jnp.bfloat16)
    gate_up = jnp.dot(normed_two, ffn_w, preferred_element_type=jnp.float32)
    activated = gated_unit(gate_up).astype(jnp.bfloat16)
    block_out = (middle + jnp.dot(activated, down_w, preferred_element_type=jnp.float32)).astype(
        jnp.bfloat16
    )
    kept_state = (
        inputs,
        normed,
        queries,
        key_value,
        log_totals,
        mixed_rows,
        middle,
        normed_two,
        gate_up,
        activated,
        positions,
    )
    return (kept_state, block_out)


def backward_pass(kept_state, full_weights, cot_rows, valid_ext):
    (
        inputs,
        normed,
        queries,
        key_value,
        log_totals,
        mixed_rows,
        middle,
        normed_two,
        gate_up,
        activated,
        positions,
    ) = kept_state
    attn_w, out_w, ffn_w, down_w, norm_one, norm_two = full_weights
    row_count = inputs.shape[0]
    win_rows = QBLK + 2 * HALF
    grad_down = rows_contract(activated, cot_rows)
    grad_act = cols_contract(cot_rows, down_w)
    gated_pull = jax.vjp(gated_unit, gate_up)[1]
    grad_gate_up = gated_pull(grad_act)[0].astype(jnp.bfloat16)
    grad_ffn = rows_contract(normed_two, grad_gate_up)
    grad_normed_two = cols_contract(grad_gate_up, ffn_w)
    norm_pull_two = jax.vjp(layer_norm, middle, norm_two.astype(jnp.float32))[1]
    grad_middle_norm, grad_norm_two = norm_pull_two(grad_normed_two)
    grad_middle = cot_rows.astype(jnp.float32) + grad_middle_norm
    grad_branch = grad_middle.astype(jnp.bfloat16)
    grad_out = rows_contract(mixed_rows, grad_branch)
    grad_mixed = (
        cols_contract(grad_branch, out_w).astype(jnp.bfloat16).reshape(row_count, HEADS, HD)
    )
    grad_query_parts = []
    grad_window = jnp.zeros((row_count + 2 * HALF, 2 * D), jnp.float32)
    for block_number, blk_start in enumerate(range(0, row_count, QBLK)):
        window = key_value[blk_start : blk_start + win_rows]
        allowed = window_mask(valid_ext[blk_start : blk_start + win_rows])
        query_blk = queries[blk_start : blk_start + QBLK]
        grad_blk = grad_mixed[blk_start : blk_start + QBLK]
        scores = block_scores(query_blk, window, allowed)
        soft_probs = jnp.exp(scores - log_totals[block_number])
        key_win = window[:, :D].reshape(win_rows, HEADS, HD)
        value_win = window[:, D:].reshape(win_rows, HEADS, HD)
        grad_probs = jnp.einsum(
            "qhd,khd->hqk", grad_blk, value_win, preferred_element_type=jnp.float32
        )
        row_delta = jnp.sum(soft_probs * grad_probs, axis=-1, keepdims=True)
        grad_scores = (soft_probs * (grad_probs - row_delta)).astype(jnp.bfloat16)
        grad_query_parts.append(
            jnp.einsum("hqk,khd->qhd", grad_scores, key_win, preferred_element_type=jnp.float32)
            * HD ** (-0.5)
        )
        grad_keys = jnp.einsum(
            "hqk,qhd->khd", grad_scores, query_blk, preferred_element_type=jnp.float32
        ) * HD ** (-0.5)
        grad_values = jnp.einsum(
            "hqk,qhd->khd",
            soft_probs.astype(jnp.bfloat16),
            grad_blk,
            preferred_element_type=jnp.float32,
        )
        grad_window = grad_window.at[blk_start : blk_start + win_rows].add(
            jnp.concatenate(
                [grad_keys.reshape(win_rows, D), grad_values.reshape(win_rows, D)], axis=1
            )
        )
    grad_queries = jnp.concatenate(grad_query_parts, axis=0)
    return (grad_down, grad_ffn, grad_out, grad_norm_two, grad_middle, grad_queries, grad_window)


def adam_update(weight, grad, first_old, second, decay_rate):
    new_first = BETA_ONE * first_old + (1.0 - BETA_ONE) * grad
    new_second = BETA_TWO * second + (1.0 - BETA_TWO) * grad * grad
    first_hat = new_first / (1.0 - BETA_ONE**STEP)
    second_hat = new_second / (1.0 - BETA_TWO**STEP)
    change = -LEARN_RATE * (first_hat / (jnp.sqrt(second_hat) + ADAM_EPS) + decay_rate * weight)
    return (new_first, new_second, change)


def shards(
    hidden_in,
    cotangent,
    block_seq,
    block_place,
    attn_in,
    attn_out,
    ffn_in,
    ffn_out,
    norm_attn,
    norm_ffn,
    first_attn_in,
    first_attn_out,
    first_ffn_in,
    first_ffn_out,
    first_norm_attn,
    first_norm_ffn,
    second_attn_in,
    second_attn_out,
    second_ffn_in,
    second_ffn_out,
    second_norm_attn,
    second_norm_ffn,
):
    full_weights = (
        lax.all_gather(attn_in, "wshard", axis=0, tiled=True),
        lax.all_gather(attn_out, "wshard", axis=0, tiled=True),
        lax.all_gather(ffn_in, "wshard", axis=0, tiled=True),
        lax.all_gather(ffn_out, "wshard", axis=0, tiled=True),
        lax.all_gather(norm_attn, "wshard", axis=0, tiled=True),
        lax.all_gather(norm_ffn, "wshard", axis=0, tiled=True),
    )
    seq_count = lax.axis_size("seq")
    seq_index = lax.axis_index("seq")
    stream_ids = block_seq[0]
    own_id = lax.dynamic_index_in_dim(stream_ids, seq_index, keepdims=False)
    left_id = jnp.where(
        seq_index > 0,
        lax.dynamic_index_in_dim(stream_ids, jnp.maximum(seq_index - 1, 0), keepdims=False),
        -1,
    )
    right_id = jnp.where(
        seq_index < seq_count - 1,
        lax.dynamic_index_in_dim(
            stream_ids, jnp.minimum(seq_index + 1, seq_count - 1), keepdims=False
        ),
        -1,
    )
    own_place = lax.dynamic_index_in_dim(block_place[0], seq_index, keepdims=False)
    x_rows = hidden_in[0]
    row_count = x_rows.shape[0]
    valid_ext = jnp.concatenate(
        [
            jnp.full((HALF,), left_id == own_id),
            jnp.ones((row_count,), jnp.bool_),
            jnp.full((HALF,), right_id == own_id),
        ]
    )

    def send_rims(own_pairs):
        return with_halo(own_pairs, (("seq", 0),), HALF)

    kept_state, block_out = forward_pass(x_rows, full_weights, own_place, valid_ext, send_rims)
    kept_inputs, kept_pairs = lax.optimization_barrier((x_rows, kept_state[3]))
    kept_state = forward_pass(
        kept_inputs, full_weights, own_place, valid_ext, lambda own_pairs: kept_pairs
    )[0]
    grad_down, grad_ffn, grad_out, grad_norm_two, grad_middle, grad_queries, grad_window = (
        backward_pass(kept_state, full_weights, cotangent[0], valid_ext)
    )
    rim_send = jnp.concatenate([grad_window[:HALF], grad_window[row_count + HALF :]], axis=0)
    rim_back = with_halo(rim_send.astype(jnp.bfloat16), (("seq", 0),), HALF).astype(rim_send.dtype)
    grad_pairs = grad_window[HALF : HALF + row_count]
    grad_pairs = grad_pairs.at[:HALF].add(rim_back[:HALF])
    grad_pairs = grad_pairs.at[row_count - HALF :].add(rim_back[3 * HALF :])
    inputs = kept_state[0]
    normed = kept_state[1]
    positions = kept_state[10]
    grad_qkv = jnp.concatenate(
        [
            rotary(grad_queries, positions, -1.0).reshape(row_count, D),
            rotary(grad_pairs[:, :D].reshape(row_count, HEADS, HD), positions, -1.0).reshape(
                row_count, D
            ),
            grad_pairs[:, D:],
        ],
        axis=1,
    ).astype(jnp.bfloat16)
    grad_attn = rows_contract(normed, grad_qkv)
    grad_normed = cols_contract(grad_qkv, full_weights[0])
    norm_pull_one = jax.vjp(layer_norm, inputs, full_weights[4].astype(jnp.float32))[1]
    grad_inputs_norm, grad_norm_one = norm_pull_one(grad_normed)
    grad_in = (grad_middle + grad_inputs_norm).astype(jnp.bfloat16)[None]
    local_grads = (grad_attn, grad_out, grad_ffn, grad_down, grad_norm_one, grad_norm_two)
    summed = (
        lax.psum(local_grads[0].astype(jnp.bfloat16), "seq").astype(jnp.float32),
        lax.psum(local_grads[1].astype(jnp.bfloat16), "seq").astype(jnp.float32),
        lax.psum(local_grads[2].astype(jnp.bfloat16), "seq").astype(jnp.float32),
        lax.psum(local_grads[3].astype(jnp.bfloat16), "seq").astype(jnp.float32),
        lax.psum(local_grads[4].astype(jnp.bfloat16), "seq").astype(jnp.float32),
        lax.psum(local_grads[5].astype(jnp.bfloat16), "seq").astype(jnp.float32),
    )
    shard_grads = (
        lax.psum_scatter(
            summed[0].astype(jnp.bfloat16), "wshard", scatter_dimension=0, tiled=True
        ).astype(jnp.float32),
        lax.psum_scatter(
            summed[1].astype(jnp.bfloat16), "wshard", scatter_dimension=0, tiled=True
        ).astype(jnp.float32),
        lax.psum_scatter(
            summed[2].astype(jnp.bfloat16), "wshard", scatter_dimension=0, tiled=True
        ).astype(jnp.float32),
        lax.psum_scatter(
            summed[3].astype(jnp.bfloat16), "wshard", scatter_dimension=0, tiled=True
        ).astype(jnp.float32),
        lax.psum_scatter(
            summed[4].astype(jnp.bfloat16), "wshard", scatter_dimension=0, tiled=True
        ).astype(jnp.float32),
        lax.psum_scatter(
            summed[5].astype(jnp.bfloat16), "wshard", scatter_dimension=0, tiled=True
        ).astype(jnp.float32),
    )
    own_weights = (attn_in, attn_out, ffn_in, ffn_out, norm_attn, norm_ffn)
    firsts = (
        first_attn_in,
        first_attn_out,
        first_ffn_in,
        first_ffn_out,
        first_norm_attn,
        first_norm_ffn,
    )
    seconds = (
        second_attn_in,
        second_attn_out,
        second_ffn_in,
        second_ffn_out,
        second_norm_attn,
        second_norm_ffn,
    )
    decays = (WEIGHT_DECAY, WEIGHT_DECAY, WEIGHT_DECAY, WEIGHT_DECAY, 0.0, 0.0)
    updates = [
        adam_update(weight.astype(jnp.float32), grad, first_old, second, decay_rate)
        for weight, grad, first_old, second, decay_rate in zip(
            own_weights, shard_grads, firsts, seconds, decays
        )
    ]
    new_firsts = tuple((update_set[0] for update_set in updates))
    new_seconds = tuple((update_set[1] for update_set in updates))
    changes = tuple((update_set[2] for update_set in updates))
    return (block_out[None], grad_in) + tuple(shard_grads) + new_firsts + new_seconds + changes


def solution(mesh):
    in_specs = (
        P("wshard", "seq", None),
        P("wshard", "seq", None),
        P("wshard", None),
        P("wshard", None),
        P("wshard", None),
        P("wshard", None),
        P("wshard", None),
        P("wshard", None),
        P("wshard"),
        P("wshard"),
        P("wshard", None),
        P("wshard", None),
        P("wshard", None),
        P("wshard", None),
        P("wshard"),
        P("wshard"),
        P("wshard", None),
        P("wshard", None),
        P("wshard", None),
        P("wshard", None),
        P("wshard"),
        P("wshard"),
    )
    out_specs = (
        P("wshard", "seq", None),
        P("wshard", "seq", None),
        P("wshard", None),
        P("wshard", None),
        P("wshard", None),
        P("wshard", None),
        P("wshard"),
        P("wshard"),
        P("wshard", None),
        P("wshard", None),
        P("wshard", None),
        P("wshard", None),
        P("wshard"),
        P("wshard"),
        P("wshard", None),
        P("wshard", None),
        P("wshard", None),
        P("wshard", None),
        P("wshard"),
        P("wshard"),
        P("wshard", None),
        P("wshard", None),
        P("wshard", None),
        P("wshard", None),
        P("wshard"),
        P("wshard"),
    )
    return jax.shard_map(shards, mesh=mesh, in_specs=in_specs, out_specs=out_specs, check_vma=False)
```

profile of v0, /device:TPU:0, one launch (start us, length us, event | category | flops | bytes accessed | tf_op | source)
XLA Modules:
  0.0 545.7 jit_solution(10793984770611910041)
XLA Ops:
  17.8 8.6 %all-reduce.12 = (bf16[768]{0:T(1024)(128)(2,1)S(1)}, bf16[768]{0:T(1024)(128)(2,1)S(1)}) all-reduce(bf16[768]{0:T(1024)(128)(2,1)S(1)} %dynamic-update-slice.12, bf16[768]{0:T(1024)(128)(2,1)S(1)} %dynamic-update-slice.13), channel_id=1, replica_groups=mesh['seq'=8,'wshard'=4] {'wshard'}, use_global_device_ids=true, to_apply=%add.5 | all-reduce | flops 1536 | bytes 6144
  34.2 9.0 %all-gather.5.cloned.1.call-done = bf16[768,2304]{1,0:T(8,128)(2,1)} async-done(((bf16[192,2304]{1,0:T(8,128)(2,1)}), bf16[768,2304]{1,0:T(8,128)(2,1)}) %all-gather.5.cloned.1.call-update) | async-done | bytes 3538960 | tf_op jit(solution)/shard_map/all_gather | solution.py:251
  43.2 6.2 %fusion.72 = f32[1024,2304]{1,0:T(8,128)S(1)} fusion(bf16[768,2304]{1,0:T(8,128)(2,1)} %all-gather.5.cloned.1.call-done, f32[768]{0:T(1024)S(1)} %convert_element_type.186, f32[1024]{0:T(1024)S(1)} %add_rsqrt_fusion.1, f32[1024]{0:T(1024)S(1)} %broadcast_multiply_fusion.4, bf16[1,1024,768]{1,2,0:T(8,128)(2,1)S(1)} %copy.88), kind=kOutput, calls=%fused_computation.143 | convolution fusion | flops 3627810816 | bytes 14560256 | tf_op jit(solution)/shard_map/dot_general | solution.py:98
  49.6 3.2 fusion.177
  52.8 3.6 copy.89
  56.4 2.4 subtract_convert_fusion.4
  60.1 2.6 copy.90
  64.4 3.4 collective-permute-start
  70.1 3.8 copy.92
  73.9 2.7 collective-permute-done.1
  76.6 4.1 pad_maximum_fusion.1
  83.7 2.2 copy.100
  85.9 2.2 copy.102
  90.8 3.0 fusion.99
  96.1 3.3 fusion.189
  99.4 3.4 fusion.3
  102.8 2.7 copy-done
  105.5 5.5 %fusion.98 = bf16[512,12,64]{0,2,1:T(8,128)(2,1)S(1)} fusion(bf16[640,12,64]{0,2,1:T(8,128)(2,1)S(1)} %bitcast.140, f32[12,512,640]{2,1,0:T(8,128)S(1)} %get-tuple-element.245, f32[12,512]{1,0:T(8,128)S(1)} %fusion.3, f32[12,512]{1,0:T(8,128)S(1)} %get-tuple-element.244), kind=kOutput, calls=%fused_computation.190 | convolution fusion | flops 515506176 | bytes 17547264 | tf_op jit(solution)/shard_map/hqk,khd->qhd/dot_general | solution.py:122
  111.1 3.3 fusion.190
  114.3 3.4 fusion.2
  119.9 5.1 fusion.97
  126.3 3.3 fusion.191
  131.8 10.6 %fusion.168 = f32[1024,2304]{1,0:T(8,128)} fusion(bf16[768,2304]{1,0:T(8,128)(2,1)} %all-gather.9.cloned.1.call-done, f32[1024,768]{0,1:T(8,128)} %copy-done.14, f32[1024]{0:T(1024)S(1)} %fusion.113, f32[1024]{0:T(1024)S(1)} %broadcast_multiply_fusion.1, f32[768]{0:T(1024)S(1)} %convert_element_type.194), kind=kOutput, calls=%fused_computation.302 | convolution fusion | flops 3627024384 | bytes 16133120 | tf_op jit(solution)/shard_map/dot_general | solution.py:127
  142.4 15.0 %fusion.84 = (f32[1024,1152]{1,0:T(8,128)}, f32[1024,1152]{1,0:T(8,128)S(1)}, f32[1024,1152]{1,0:T(8,128)S(1)}) fusion(f32[1024,2304]{1,0:T(8,128)} %fusion.168, bf16[1152,768]{1,0:T(8,128)(2,1)} %all-gather.11.cloned.1.call-done, bf16[1,1024,768]{2,1,0:T(8,128)(2,1)S(1)} %copy-done.43), kind=kOutput, calls=%fused_computation.176 | convolution fusion | flops 1888616448 | bytes 22216704 | tf_op jit(solution)/shard_map/dot_general | solution.py:73
  161.6 7.9 %multiply_reduce_fusion.2 = (bf16[768]{0:T(1024)(128)(2,1)}, f32[1024]{0:T(1024)S(1)}, f32[1024,768]{0,1:T(8,128)S(1)}) fusion(f32[1024,768]{0,1:T(8,128)S(1)} %copy-done.15, f32[1024]{0:T(1024)S(1)} %fusion.113, f32[1024]{0:T(1024)S(1)} %broadcast_multiply_fusion.1, f32[768]{0:T(1024)S(1)} %convert_element_type.194, ...), kind=kOutput, calls=%fused_computation.117 | convolution fusion | flops 3634100480 | bytes 19284480 | tf_op jit(solution)/shard_map/dot_general | solution.py:73
  172.8 2.5 convolution_convert_fusion.4
  175.3 2.7 convolution_convert_fusion.3
  178.2 14.0 %multiply_reduce_fusion.1 = (f32[12,512]{1,0:T(8,128)S(1)}, f32[12,512,640]{2,1,0:T(8,128)}) fusion(f32[12,512,640]{2,1,0:T(8,128)} %copy-done.1, f32[12,512]{1,0:T(8,128)S(1)} %log_add_fusion.1, bf16[512,12,64]{0,2,1:T(8,128)(2,1)S(1)} %bitcast.136, bf16[640,12,64]{0,2,1:T(8,128)(2,1)} %bitcast.141), kind=kOutput, calls=%fused_computation.6 | convolution fusion | flops 515106816 | bytes 33275904 | tf_op jit(solution)/shard_map/qhd,khd->hqk/dot_general | solution.py:190
  194.2 7.7 %multiply_convert_fusion.1 = bf16[12,512,640]{2,1,0:T(8,128)(2,1)S(1)} fusion(f32[12,512,640]{2,1,0:T(8,128)} %get-tuple-element.253, f32[12,512,640]{2,1,0:T(8,128)S(1)} %bitcast.112, f32[12,512]{1,0:T(8,128)S(1)} %get-tuple-element.252, f32[12,512]{1,0:T(8,128)S(1)} %log_add_fusion.1), kind=kLoop, calls=%fused_computation.5 | loop fusion | flops 15728640 | bytes 39370752 | tf_op jit(solution)/shard_map/convert_element_type | solution.py:194
  202.0 2.7 convolution_multiply_fusion.1
  205.8 8.5 %convolution_convert_fusion.2 = bf16[1152,768]{1,0:T(8,128)(2,1)} fusion(f32[1024,2304]{1,0:T(8,128)} %fusion.168, bf16[1,1024,768]{2,1,0:T(8,128)(2,1)S(1)} %copy-done.44, f32[1024,1152]{1,0:T(8,128)} %copy-done.28), kind=kOutput, calls=%fused_computation.105 | convolution fusion | flops 1817542656 | bytes 17498112 | tf_op jit(solution)/shard_map/dot_general | solution.py:67
  214.4 14.3 %multiply_reduce_fusion = (f32[12,512]{1,0:T(8,128)S(1)}, f32[12,512,640]{2,1,0:T(8,128)}) fusion(f32[12,512,640]{2,1,0:T(8,128)} %copy-done, f32[12,512]{1,0:T(8,128)S(1)} %log_add_fusion, bf16[512,12,64]{0,2,1:T(8,128)(2,1)S(1)} %bitcast.134, bf16[640,12,64]{0,2,1:T(8,128)(2,1)} %bitcast.139), kind=kOutput, calls=%fused_computation.3 | convolution fusion | flops 515106816 | bytes 33275904 | tf_op jit(solution)/shard_map/qhd,khd->hqk/dot_general | solution.py:190
  230.6 7.8 %multiply_convert_fusion = bf16[12,512,640]{2,1,0:T(8,128)(2,1)S(1)} fusion(f32[12,512,640]{2,1,0:T(8,128)} %get-tuple-element.255, f32[12,512,640]{2,1,0:T(8,128)S(1)} %bitcast.110, f32[12,512]{1,0:T(8,128)S(1)} %get-tuple-element.254, f32[12,512]{1,0:T(8,128)S(1)} %log_add_fusion), kind=kLoop, calls=%fused_computation.2 | loop fusion | flops 15728640 | bytes 39370752 | tf_op jit(solution)/shard_map/convert_element_type | solution.py:194
  238.4 2.9 convolution_multiply_fusion
  241.3 3.7 multiply_bitcast_fusion
  244.9 8.1 %fusion.14 = f32[12,64,640]{2,1,0:T(8,128)} fusion(bf16[512,12,64]{0,2,1:T(8,128)(2,1)S(1)} %bitcast.137, f32[12,512,640]{2,1,0:T(8,128)} %copy-done.1, f32[12,512]{1,0:T(8,128)S(1)} %log_add_fusion.1), kind=kOutput, calls=%fused_computation.30 | convolution fusion | flops 511180800 | bytes 18505728 | tf_op jit(solution)/shard_map/hqk,qhd->khd/dot_general | solution.py:202
  253.1 4.1 fusion.12
  257.2 9.5 %convolution_convert_fusion = bf16[768,2304]{1,0:T(8,128)(2,1)} fusion(f32[1024,1152]{1,0:T(8,128)} %copy-done.27, f32[1024,1152]{1,0:T(8,128)} %get-tuple-element.198, f32[1024,768]{0,1:T(8,128)S(1)} %copy-done.16, f32[1024]{0:T(1024)S(1)} %fusion.113, f32[1024]{0:T(1024)S(1)} %broadcast_multiply_fusion.1, f32[768]{0:T(1024)S(1)} %convert_element_type.194), kind=kOutput, calls=%fused_computation.47 | convolution fusion | flops 3633512448 | bytes 16133120 | tf_op jit(solution)/shard_map/dot_general | solution.py:67
  271.0 2.8 constant_dynamic-update-slice_fusion
  273.9 3.2 pad_maximum_fusion.13
  285.2 6.2 %collective-permute-start.2 = (bf16[64,1536]{0,1:T(8,128)(2,1)S(1)}, bf16[64,1536]{0,1:T(8,128)(2,1)}, u32[]{:S(2)}, u32[]{:S(2)}) collective-permute-start(bf16[64,1536]{0,1:T(8,128)(2,1)S(1)} %slice.431), channel_id=1, source_target_pairs={{0,4},{4,8},{8,12},{12,16},{16,20},{20,24},{24,28},{1,5},{5,9},{9,... | collective-permute-start | bytes 589832 | tf_op jit(solution)/shard_map/ppermute | solution.py:32
  291.4 10.2 %fusion.182 = (f32[12,512]{1,0:T(8,128)S(1)}, f32[12,512,640]{2,1,0:T(8,128)}) fusion(bf16[640,12,64]{0,2,1:T(8,128)(2,1)S(1)} %bitcast.154, pred[512,640]{1,0:T(8,128)(4,1)S(1)} %copy-done.49, bf16[1024,12,32]{0,2,1:T(8,128)(2,1)} %get-tuple-element.228, bf16[1024,12,32]{0,2,1:T(8,128)(2,1)} %get-tuple-element.229), kind=kOutput, calls=%fused_computation.309 | convolution fusion | flops 520618624 | bytes 18636800 | tf_op jit(solution)/shard_map/sub | solution.py:116
  301.6 10.7 %fusion.183 = (f32[12,512]{1,0:T(8,128)S(1)}, f32[12,512,640]{2,1,0:T(8,128)}) fusion(bf16[640,12,64]{0,2,1:T(8,128)(2,1)} %bitcast.153, pred[512,640]{1,0:T(8,128)(4,1)} %fusion.106, bf16[1024,12,32]{0,2,1:T(8,128)(2,1)} %get-tuple-element.229, bf16[1024,12,32]{0,2,1:T(8,128)(2,1)} %get-tuple-element.228), kind=kOutput, calls=%fused_computation.310 | convolution fusion | flops 520618624 | bytes 18636800 | tf_op jit(solution)/shard_map/sub | solution.py:116
  312.2 8.1 %fusion.95 = bf16[512,12,64]{0,2,1:T(8,128)(2,1)} fusion(bf16[640,12,64]{0,2,1:T(8,128)(2,1)} %bitcast.152, f32[12,512,640]{2,1,0:T(8,128)} %get-tuple-element.241, f32[12,512]{1,0:T(8,128)S(1)} %get-tuple-element.240), kind=kOutput, calls=%fused_computation.187 | convolution fusion | flops 511574016 | bytes 17522688 | tf_op jit(solution)/shard_map/hqk,khd->qhd/dot_general | solution.py:122
  320.3 6.9 %multiply_bitcast_fusion.1 = f32[512,12,64]{0,2,1:T(8,128)} fusion(bf16[640,12,64]{0,2,1:T(8,128)(2,1)S(1)} %bitcast.129, bf16[12,512,640]{2,1,0:T(8,128)(2,1)} %copy-done.2), kind=kOutput, calls=%fused_computation.162 | convolution fusion | flops 503709696 | bytes 10420224 | tf_op jit(solution)/shard_map/hqk,khd->qhd/dot_general | solution.py:196
  327.2 4.3 slice.320
  336.9 4.8 scatter-add.16
  343.3 5.0 scatter-add.19
  350.5 2.4 slice.327
  356.5 8.6 %convolution_convert_fusion.1 = bf16[768,2304]{1,0:T(8,128)(2,1)} fusion(bf16[1024,768]{0,1:T(8,128)(2,1)S(1)} %slice.428, bf16[1024,768]{0,1:T(8,128)(2,1)S(1)} %bitcast.146, bf16[1024,768]{0,1:T(8,128)(2,1)S(1)} %bitcast.144, bf16[1024,768]{0,1:T(8,128)(2,1)S(1)} %bitcast.117, f32[1024]{0:T(1024)S(1)} %copy-done.71, f32[1024]{0:T(1024)S(1)} %copy-done.67, ...), kind=kOutput, calls=%fused_computation.48 | convolution fusion | flops 3643736064 | bytes 9841664 | tf_op jit(solution)/shard_map/dot_general | solution.py:67
  365.1 7.3 %fusion.96 = bf16[512,12,64]{0,2,1:T(8,128)(2,1)S(1)} fusion(bf16[640,12,64]{0,2,1:T(8,128)(2,1)} %bitcast.151, f32[12,512,640]{2,1,0:T(8,128)} %get-tuple-element.239, f32[12,512]{1,0:T(8,128)S(1)} %get-tuple-element.238), kind=kOutput, calls=%fused_computation.188 | convolution fusion | flops 511574016 | bytes 17522688 | tf_op jit(solution)/shard_map/hqk,khd->qhd/dot_general | solution.py:122
  376.3 4.1 fusion.69
  380.4 14.1 %fusion.85 = bf16[1,1024,768]{1,2,0:T(8,128)(2,1)} fusion(f32[1024,768]{0,1:T(8,128)S(1)} %get-tuple-element.243, bf16[1152,768]{1,0:T(8,128)(2,1)S(1)} %copy-done.84, f32[1024,2304]{1,0:T(8,128)S(1)} %fusion.69), kind=kOutput, calls=%fused_computation.177 | convolution fusion | flops 1891368960 | bytes 15925248 | tf_op jit(solution)/shard_map/dot_general | solution.py:129
  394.6 2.7 copy.103
  397.4 8.9 %reduce-scatter.5.cloned.1.call-done = bf16[192,2304]{1,0:T(8,128)(2,1)} async-done(((bf16[768,2304]{1,0:T(8,128)(2,1)}), bf16[192,2304]{1,0:T(8,128)(2,1)}) %reduce-scatter.5.cloned.1.call-update) | async-done | bytes 884752 | tf_op jit(solution)/shard_map/reduce_scatter | solution.py:329
  406.3 6.8 %fusion.60 = (f32[1024]{0:T(1024)S(1)}, f32[1024,768]{0,1:T(8,128)S(1)}) fusion(bf16[1024,768]{0,1:T(8,128)(2,1)S(1)} %bitcast.118, f32[1024]{0:T(1024)S(1)} %copy-done.67, f32[768]{0:T(1024)S(1)} %copy-done.69, bf16[768,2304]{1,0:T(8,128)(2,1)} %all-gather.5.cloned.1.call-done, bf16[1024,768]{0,1:T(8,128)(2,1)S(1)} %slice.428, ...), kind=kOutput, calls=%fused_computation.112 | convolution fusion | flops 3641965568 | bytes 12987392 | tf_op jit(solution)/shard_map/dot_general | solution.py:73
  416.1 6.1 %all-reduce.11 = (bf16[768]{0:T(1024)(128)(2,1)S(1)}, bf16[768]{0:T(1024)(128)(2,1)S(1)}) all-reduce(bf16[768]{0:T(1024)(128)(2,1)S(1)} %get-tuple-element.158, bf16[768]{0:T(1024)(128)(2,1)S(1)} %copy-done.76), channel_id=6, replica_groups=mesh['seq'=8,'wshard'=4] {'wshard'}, use_global_device_ids=true, to_apply=%region_32.33.clone | all-reduce | flops 1536 | bytes 6144
  422.3 5.5 %fusion.70 = bf16[1,1024,768]{1,2,0:T(8,128)(2,1)} fusion(f32[1024,768]{0,1:T(8,128)} %copy-done.6, bf16[1,1024,768]{1,2,0:T(8,128)(2,1)S(1)} %copy-done.11, f32[1024]{0:T(1024)S(1)} %negate_multiply_fusion.2, f32[1024]{0:T(1024)S(1)} %copy-done.75, f32[1024]{0:T(1024)S(1)} %multiply_multiply_fusion.14, f32[1024]{0:T(1024)S(1)} %copy-done.67, ...), kind=kLoop, calls=%fused_computation.141 | loop fusion | flops 10223616 | bytes 11033600 | tf_op jit(solution)/shard_map/broadcast_in_dim | solution.py:318
  427.9 2.7 copy.104
  430.6 22.1 %all-reduce.9 = (bf16[192]{0:T(256)(128)(2,1)S(1)}, bf16[192]{0:T(256)(128)(2,1)S(1)}) all-reduce(bf16[192]{0:T(256)(128)(2,1)S(1)} %dynamic-slice.38, bf16[192]{0:T(256)(128)(2,1)S(1)} %dynamic-slice.40), channel_id=1, replica_groups=mesh['seq'=8,'wshard'=4] {'seq'}, use_global_device_ids=true, to_apply=%region_31.32 | all-reduce | flops 384 | bytes 1536 | tf_op jit(solution)/shard_map/psum | solution.py:325
  453.9 70.3 %all-reduce.15.cloned.1.call-done = (bf16[192,2304]{1,0:T(8,128)(2,1)}, bf16[192,768]{1,0:T(8,128)(2,1)}, bf16[192,2304]{1,0:T(8,128)(2,1)}, bf16[288,768]{1,0:T(8,128)(2,1)}) async-done(((bf16[192,2304]{1,0:T(8,128)(2,1)}, bf16[192,768]{1,0:T(8,128)(2,1)}, bf16[192,2304]{1,0:T(8,128)(2,1)}, bf16[288,768]{1,0:T(8,128)(2,1)}), (bf16[192,2304]{1,0:T(8,128)(2,1)}, bf16[192,768]{1,0:T(8,128)(2,1)}, ...) | async-done | bytes 2506768 | tf_op jit(solution)/shard_map/psum | solution.py:321
  524.2 2.7 add_multiply_fusion.3
  530.7 3.9 add_multiply_fusion.1
  535.7 3.3 add_multiply_fusion
  (296 shorter events, 84.0 us)
Async XLA Ops:
  7.2 20.8 %copy-start.41 = (bf16[1,1024,768]{2,1,0:T(8,128)(2,1)S(1)}, bf16[1,1024,768]{2,1,0:T(8,128)(2,1)}, u32[]{:S(2)}) copy-start(bf16[1,1024,768]{2,1,0:T(8,128)(2,1)} %param.30) | copy-start | bytes 4718596
  7.2 36.0 %all-gather.5.cloned.1.call-start = ((), (), s32[]{:S(2)}) async-start(), calls=%async_computation.4 | async-start | bytes 4423680 | tf_op jit(solution)/shard_map/all_gather | solution.py:251
  7.9 118.4 %all-gather.7.cloned.1.call-start = ((), (), s32[]{:S(2)}) async-start(), calls=%async_computation.5 | async-start | bytes 1474560 | tf_op jit(solution)/shard_map/all_gather | solution.py:252
  8.7 123.1 %all-gather.9.cloned.1.call-start = ((), (), s32[]{:S(2)}) async-start(), calls=%async_computation.6 | async-start | bytes 4423680 | tf_op jit(solution)/shard_map/all_gather | solution.py:253
  9.4 132.9 %all-gather.11.cloned.1.call-start = ((), (), s32[]{:S(2)}) async-start(), calls=%async_computation.7 | async-start | bytes 2211840 | tf_op jit(solution)/shard_map/all_gather | solution.py:254
  10.0 387.3 %reduce-scatter.7.cloned.1.call-start = ((), (), s32[]{:S(2)}) async-start(), calls=%async_computation.9 | async-start | bytes 1474560 | tf_op jit(solution)/shard_map/reduce_scatter | solution.py:332
  26.3 64.4 %copy-start.68 = (f32[768]{0:T(1024)}, f32[768]{0:T(1024)S(1)}, u32[]{:S(2)}) copy-start(f32[768]{0:T(1024)S(1)} %convert_element_type.186) | copy-start | bytes 9220
  28.8 97.6 %copy-start.3 = (bf16[1,1024,768]{1,2,0:T(8,128)(2,1)}, bf16[1,1024,768]{1,2,0:T(8,128)(2,1)S(1)}, u32[]{:S(2)}) copy-start(bf16[1,1024,768]{1,2,0:T(8,128)(2,1)S(1)} %copy.88) | copy-start | bytes 4718596
  34.2 22.2 %copy-start.33 = (f32[1024,32]{0,1:T(8,128)}, f32[1024,32]{0,1:T(8,128)S(1)}, u32[]{:S(2)}) copy-start(f32[1024,32]{0,1:T(8,128)S(1)} %get-tuple-element.232) | copy-start | bytes 393220
  34.2 22.2 %copy-start.51 = (f32[1024,32]{0,1:T(8,128)}, f32[1024,32]{0,1:T(8,128)S(1)}, u32[]{:S(2)}) copy-start(f32[1024,32]{0,1:T(8,128)S(1)} %get-tuple-element.231) | copy-start | bytes 393220
  49.6 27.0 %copy-start.7 = (bf16[1024,768]{1,0:T(8,128)(2,1)}, bf16[1024,768]{1,0:T(8,128)(2,1)S(1)}, u32[]{:S(2)}) copy-start(bf16[1024,768]{1,0:T(8,128)(2,1)S(1)} %slice.429) | copy-start | bytes 4718596
  64.4 9.6 %collective-permute-start = (bf16[64,1536]{1,0:T(8,128)(2,1)}, bf16[64,1536]{1,0:T(8,128)(2,1)S(1)}, u32[]{:S(2)}, u32[]{:S(2)}) collective-permute-start(bf16[64,1536]{1,0:T(8,128)(2,1)} %get-tuple-element.222), channel_id=1, source_target_pairs={{0,4},{4,8},{8,12},{12,16},{16,20},{20,24},{24,28},{1,5},{5,9},{9,... | collective-permute-start | bytes 589832 | tf_op jit(solution)/shard_map/ppermute | solution.py:32
  67.7 8.9 %collective-permute-start.1 = (bf16[64,1536]{1,0:T(8,128)(2,1)}, bf16[64,1536]{1,0:T(8,128)(2,1)S(1)}, u32[]{:S(2)}, u32[]{:S(2)}) collective-permute-start(bf16[64,1536]{1,0:T(8,128)(2,1)} %get-tuple-element.223), channel_id=1, source_target_pairs={{4,0},{8,4},{12,8},{16,12},{20,16},{24,20},{28,24},{5,1},{9,5},{13... | collective-permute-start | bytes 589832 | tf_op jit(solution)/shard_map/ppermute | solution.py:33
  73.9 6.8 %copy-start.58 = (bf16[64,1536]{1,0:T(8,128)(2,1)}, bf16[64,1536]{1,0:T(8,128)(2,1)S(1)}, u32[]{:S(2)}) copy-start(bf16[64,1536]{1,0:T(8,128)(2,1)S(1)} %collective-permute-done) | copy-start | bytes 589828
  76.6 4.1 copy-start.60
  81.0 9.8 %copy-start.66 = (f32[1024]{0:T(1024)}, f32[1024]{0:T(1024)S(1)}, u32[]{:S(2)}) copy-start(f32[1024]{0:T(1024)S(1)} %broadcast_multiply_fusion.2) | copy-start | bytes 12292
  82.1 8.7 %copy-start.70 = (f32[1024]{0:T(1024)}, f32[1024]{0:T(1024)S(1)}, u32[]{:S(2)}) copy-start(f32[1024]{0:T(1024)S(1)} %fusion.112) | copy-start | bytes 12292
  99.4 6.1 %copy-start = (f32[12,512,640]{2,1,0:T(8,128)}, f32[12,512,640]{2,1,0:T(8,128)S(1)}, u32[]{:S(2)}) copy-start(f32[12,512,640]{2,1,0:T(8,128)S(1)} %get-tuple-element.245) | copy-start | bytes 47185924
  99.4 6.1 %copy-start.29 = (bf16[640,768]{0,1:T(8,128)(2,1)S(1)}, bf16[640,768]{0,1:T(8,128)(2,1)}, u32[]{:S(2)}) copy-start(bf16[640,768]{0,1:T(8,128)(2,1)} %copy.101) | copy-start | bytes 2949124
  105.5 5.5 %copy-start.20 = (bf16[640,768]{0,1:T(8,128)(2,1)S(1)}, bf16[640,768]{0,1:T(8,128)(2,1)}, u32[]{:S(2)}) copy-start(bf16[640,768]{0,1:T(8,128)(2,1)} %copy.100) | copy-start | bytes 2949124
  105.5 5.5 %copy-start.50 = (pred[512,640]{1,0:T(8,128)(4,1)S(1)}, pred[512,640]{1,0:T(8,128)(4,1)}, u32[]{:S(2)}) copy-start(pred[512,640]{1,0:T(8,128)(4,1)} %fusion.106) | copy-start | bytes 983044
  114.3 5.6 %copy-start.1 = (f32[12,512,640]{2,1,0:T(8,128)}, f32[12,512,640]{2,1,0:T(8,128)S(1)}, u32[]{:S(2)}) copy-start(f32[12,512,640]{2,1,0:T(8,128)S(1)} %get-tuple-element.247) | copy-start | bytes 47185924
  114.3 5.6 %copy-start.30 = (bf16[640,768]{0,1:T(8,128)(2,1)S(1)}, bf16[640,768]{0,1:T(8,128)(2,1)}, u32[]{:S(2)}) copy-start(bf16[640,768]{0,1:T(8,128)(2,1)} %copy.98) | copy-start | bytes 2949124
  131.7 10.6 %copy-start.43 = (bf16[1,1024,768]{2,1,0:T(8,128)(2,1)S(1)}, bf16[1,1024,768]{2,1,0:T(8,128)(2,1)}, u32[]{:S(2)}) copy-start(bf16[1,1024,768]{2,1,0:T(8,128)(2,1)} %param.31) | copy-start | bytes 4718596
  142.4 15.0 %copy-start.19 = (f32[1024,2304]{1,0:T(8,128)S(1)}, f32[1024,2304]{1,0:T(8,128)}, u32[]{:S(2)}) copy-start(f32[1024,2304]{1,0:T(8,128)} %fusion.168) | copy-start | bytes 28311556
  157.4 4.2 copy-start.15
  159.8 9.7 %copy-start.27 = (f32[1024,1152]{1,0:T(8,128)}, f32[1024,1152]{1,0:T(8,128)S(1)}, u32[]{:S(2)}) copy-start(f32[1024,1152]{1,0:T(8,128)S(1)} %multiply_add_fusion) | copy-start | bytes 14155780
  178.1 219.2 %reduce-scatter.11.cloned.1.call-start = ((), (), s32[]{:S(2)}) async-start(), calls=%async_computation.11 | async-start | bytes 2211840 | tf_op jit(solution)/shard_map/reduce_scatter | solution.py:338
  178.1 14.1 %slice-start.4 = ((s8[15728640]{0:T(1024)(128)(4,1)}), s8[4194304]{0:T(1024)(128)(4,1)S(1)}, s32[]{:S(2)}) async-start(s8[15728640]{0:T(1024)(128)(4,1)} %bitcast.111), calls=%async_computation.17 | async-start | bytes 8388608
  178.1 14.1 %slice-start.5 = ((s8[15728640]{0:T(1024)(128)(4,1)}), s8[4194304]{0:T(1024)(128)(4,1)S(1)}, s32[]{:S(2)}) async-start(s8[15728640]{0:T(1024)(128)(4,1)} %bitcast.111), calls=%async_computation.18 | async-start | bytes 8388608
  178.2 15.1 %slice-start.6 = ((s8[15728640]{0:T(1024)(128)(4,1)}), s8[4194304]{0:T(1024)(128)(4,1)S(1)}, s32[]{:S(2)}) async-start(s8[15728640]{0:T(1024)(128)(4,1)} %bitcast.111), calls=%async_computation.19 | async-start | bytes 8388608
  178.2 16.0 %slice-start.7 = ((s8[15728640]{0:T(1024)(128)(4,1)}), s8[3145728]{0:T(1024)(128)(4,1)S(1)}, s32[]{:S(2)}) async-start(s8[15728640]{0:T(1024)(128)(4,1)} %bitcast.111), calls=%async_computation.20 | async-start | bytes 6291456
  214.3 183.1 %reduce-scatter.9.cloned.1.call-start = ((), (), s32[]{:S(2)}) async-start(), calls=%async_computation.10 | async-start | bytes 4423680 | tf_op jit(solution)/shard_map/reduce_scatter | solution.py:335
  214.3 14.4 %slice-start = ((s8[15728640]{0:T(1024)(128)(4,1)}), s8[4194304]{0:T(1024)(128)(4,1)S(1)}, s32[]{:S(2)}) async-start(s8[15728640]{0:T(1024)(128)(4,1)} %bitcast.109), calls=%async_computation.13 | async-start | bytes 8388608
  214.4 14.4 %slice-start.1 = ((s8[15728640]{0:T(1024)(128)(4,1)}), s8[4194304]{0:T(1024)(128)(4,1)S(1)}, s32[]{:S(2)}) async-start(s8[15728640]{0:T(1024)(128)(4,1)} %bitcast.109), calls=%async_computation.14 | async-start | bytes 8388608
  214.4 15.1 %slice-start.2 = ((s8[15728640]{0:T(1024)(128)(4,1)}), s8[4194304]{0:T(1024)(128)(4,1)S(1)}, s32[]{:S(2)}) async-start(s8[15728640]{0:T(1024)(128)(4,1)} %bitcast.109), calls=%async_computation.15 | async-start | bytes 8388608
  214.4 16.2 %slice-start.3 = ((s8[15728640]{0:T(1024)(128)(4,1)}), s8[3145728]{0:T(1024)(128)(4,1)S(1)}, s32[]{:S(2)}) async-start(s8[15728640]{0:T(1024)(128)(4,1)} %bitcast.109), calls=%async_computation.16 | async-start | bytes 6291456
  253.1 4.1 copy-start.16
  266.8 139.5 %reduce-scatter.5.cloned.1.call-start = ((), (), s32[]{:S(2)}) async-start(), calls=%async_computation.8 | async-start | bytes 4423680 | tf_op jit(solution)/shard_map/reduce_scatter | solution.py:329
  278.9 12.5 %copy-start.49 = (pred[512,640]{1,0:T(8,128)(4,1)S(1)}, pred[512,640]{1,0:T(8,128)(4,1)}, u32[]{:S(2)}) copy-start(pred[512,640]{1,0:T(8,128)(4,1)} %fusion.105) | copy-start | bytes 983044
  283.9 49.9 %collective-permute-start.3 = (bf16[64,1536]{0,1:T(8,128)(2,1)}, bf16[64,1536]{0,1:T(8,128)(2,1)}, u32[]{:S(2)}, u32[]{:S(2)}) collective-permute-start(bf16[64,1536]{0,1:T(8,128)(2,1)} %slice.430), channel_id=1, source_target_pairs={{4,0},{8,4},{12,8},{16,12},{20,16},{24,20},{28,24},{5,1},{9,5},{13... | collective-permute-start | bytes 589832 | tf_op jit(solution)/shard_map/ppermute | solution.py:33
  285.2 48.6 %collective-permute-start.2 = (bf16[64,1536]{0,1:T(8,128)(2,1)S(1)}, bf16[64,1536]{0,1:T(8,128)(2,1)}, u32[]{:S(2)}, u32[]{:S(2)}) collective-permute-start(bf16[64,1536]{0,1:T(8,128)(2,1)S(1)} %slice.431), channel_id=1, source_target_pairs={{0,4},{4,8},{8,12},{12,16},{16,20},{20,24},{24,28},{1,5},{5,9},{9,... | collective-permute-start | bytes 589832 | tf_op jit(solution)/shard_map/ppermute | solution.py:32
  301.6 25.7 %slice-start.8 = ((s8[7077888]{0:T(1024)(128)(4,1)}), s8[2883584]{0:T(1024)(128)(4,1)S(1)}, s32[]{:S(2)}) async-start(s8[7077888]{0:T(1024)(128)(4,1)} %bitcast.121), calls=%async_computation.21 | async-start | bytes 5767168
  312.2 8.1 %copy-start.21 = (bf16[640,768]{0,1:T(8,128)(2,1)S(1)}, bf16[640,768]{0,1:T(8,128)(2,1)}, u32[]{:S(2)}) copy-start(bf16[640,768]{0,1:T(8,128)(2,1)} %copy.100) | copy-start | bytes 2949124
  312.2 15.0 %slice-start.9 = ((s8[7077888]{0:T(1024)(128)(4,1)}), s8[4194304]{0:T(1024)(128)(4,1)S(1)}, s32[]{:S(2)}) async-start(s8[7077888]{0:T(1024)(128)(4,1)} %bitcast.121), calls=%async_computation.22 | async-start | bytes 8388608
  365.1 159.1 %all-reduce.15.cloned.1.call-start = ((), (), s32[]{:S(2)}) async-start(), calls=%async_computation.12 | async-start | bytes 5013504 | tf_op jit(solution)/shard_map/psum | solution.py:321
  365.1 7.3 %copy-start.62 = (bf16[512,12,64]{0,2,1:T(8,128)(2,1)S(1)}, bf16[512,12,64]{0,2,1:T(8,128)(2,1)}, u32[]{:S(2)}) copy-start(bf16[512,12,64]{0,2,1:T(8,128)(2,1)} %fusion.95) | copy-start | bytes 2359300
  376.3 4.1 copy-start.84
  406.3 6.9 %copy-start.73 = (f32[1024]{0:T(1024)S(1)}, f32[1024]{0:T(1024)}, u32[]{:S(2)}) copy-start(f32[1024]{0:T(1024)} %copy-done.72) | copy-start | bytes 12292
  413.1 9.2 %copy-start.11 = (bf16[1,1024,768]{1,2,0:T(8,128)(2,1)S(1)}, bf16[1,1024,768]{1,2,0:T(8,128)(2,1)}, u32[]{:S(2)}) copy-start(bf16[1,1024,768]{1,2,0:T(8,128)(2,1)} %copy.97) | copy-start | bytes 4718596
  413.1 9.2 %copy-start.75 = (f32[1024]{0:T(1024)S(1)}, f32[1024]{0:T(1024)}, u32[]{:S(2)}) copy-start(f32[1024]{0:T(1024)} %copy-done.74) | copy-start | bytes 12292
  427.8 25.0 %copy-start.77 = (f32[192]{0:T(256)S(1)}, f32[192]{0:T(256)}, u32[]{:S(2)}) copy-start(f32[192]{0:T(256)} %param.50) | copy-start | bytes 2308
  427.8 25.0 %copy-start.78 = (f32[192]{0:T(256)S(1)}, f32[192]{0:T(256)}, u32[]{:S(2)}) copy-start(f32[192]{0:T(256)} %param.44) | copy-start | bytes 2308
  427.8 25.0 %copy-start.81 = (bf16[192]{0:T(256)(128)(2,1)S(1)}, bf16[192]{0:T(256)(128)(2,1)}, u32[]{:S(2)}) copy-start(bf16[192]{0:T(256)(128)(2,1)} %param.38) | copy-start | bytes 1156
  427.8 25.6 %copy-start.79 = (f32[192]{0:T(256)S(1)}, f32[192]{0:T(256)}, u32[]{:S(2)}) copy-start(f32[192]{0:T(256)} %param.51) | copy-start | bytes 2308
  427.8 25.6 %copy-start.80 = (f32[192]{0:T(256)S(1)}, f32[192]{0:T(256)}, u32[]{:S(2)}) copy-start(f32[192]{0:T(256)} %param.45) | copy-start | bytes 2308
  427.8 25.5 %copy-start.82 = (bf16[192]{0:T(256)(128)(2,1)S(1)}, bf16[192]{0:T(256)(128)(2,1)}, u32[]{:S(2)}) copy-start(bf16[192]{0:T(256)(128)(2,1)} %param.39) | copy-start | bytes 1156
  427.8 96.4 %copy-start.53 = (bf16[192,768]{1,0:T(8,128)(2,1)S(1)}, bf16[192,768]{1,0:T(8,128)(2,1)}, u32[]{:S(2)}) copy-start(bf16[192,768]{1,0:T(8,128)(2,1)} %param.35) | copy-start | bytes 884740
  427.8 96.4 %copy-start.63 = (f32[192,768]{1,0:T(8,128)S(1)}, f32[192,768]{1,0:T(8,128)}, u32[]{:S(2)}) copy-start(f32[192,768]{1,0:T(8,128)} %param.47) | copy-start | bytes 1769476
  427.8 99.1 %copy-start.36 = (bf16[288,768]{1,0:T(8,128)(2,1)S(1)}, bf16[288,768]{1,0:T(8,128)(2,1)}, u32[]{:S(2)}) copy-start(bf16[288,768]{1,0:T(8,128)(2,1)} %param.37) | copy-start | bytes 1327108
  427.8 99.1 %copy-start.56 = (f32[288,768]{1,0:T(8,128)S(1)}, f32[288,768]{1,0:T(8,128)}, u32[]{:S(2)}) copy-start(f32[288,768]{1,0:T(8,128)} %param.49) | copy-start | bytes 2654212
  427.9 99.1 %copy-start.57 = (f32[288,768]{1,0:T(8,128)S(1)}, f32[288,768]{1,0:T(8,128)}, u32[]{:S(2)}) copy-start(f32[288,768]{1,0:T(8,128)} %param.43) | copy-start | bytes 2654212
  530.7 4.6 copy-start.40
  530.7 5.0 copy-start.54
  (45 other events, 112.4 us)
Sparse Core Ops, SparseCore 0:
  9.6 33.5 all-gather.4
  44.8 17.4 all-gather.6
  63.9 30.7 all-gather.8
  96.1 20.7 all-gather.10
  178.2 26.9 reduce-scatter.6
  214.4 30.5 reduce-scatter.10
  266.9 41.5 reduce-scatter.8
  365.2 40.9 reduce-scatter.4
  410.2 113.9 all-reduce.14
where the time goes:
time: 554 us; the launch traced here: 546 us
  matrix products  214 us (39%)
  waiting for transfers between devices  93.6 us (17%)
  local copies, waits for them, and re-layouts  88.7 us (16%)
  other arithmetic  80.5 us (15%)
  blocking collectives  36.8 us (7%)
  between operations  19.1 us (3%)
  starting transfers between devices  12.7 us (2%)
    psum x1, waiting for transfers between devices, shards(): lax.psum(local_grads[0].astype(jnp.bfloat16), 'seq').astype(jnp.float32)  70.3 us
    unnamed x203, local copies, waits for them, and re-layouts  39.2 us
    dot_general x4, matrix products, cols_contract(): lax.dot_general(left, right, (((1,), (1,)), ((), ())), preferred_element_...  32.4 us
    dot_general x4, matrix products, rows_contract(): lax.dot_general(left, right, (((0,), (0,)), ((), ())), preferred_element_...  29.1 us
    dot_general x2, matrix products, backward_pass(): jnp.einsum('qhd,khd->hqk', grad_blk, value_win, preferred_element_type=jn...  28.4 us
    dot_general x4, matrix products, forward_pass(): jnp.einsum('hqk,khd->qhd', soft_probs, value_win, preferred_element_type=...  26 us
    psum x1, blocking collectives, shards(): lax.psum(local_grads[4].astype(jnp.bfloat16), 'seq').astype(jnp.float32)  22.1 us
    sub x2, matrix products, forward_pass(): exp_scores = jnp.exp(scores - row_max)  20.8 us
  transfers between devices with their start and end apart: 13, of which 4 were waited for; matrix products, arithmetic and copies ran while one was open for 57% of the time, Pallas kernels for 0%

commit v1 on v0

v1 whole, which is shorter than its diff:
```python
import jax
import jax.numpy as jnp
from jax import lax
from jax.experimental import pallas as pl
from jax.experimental.pallas import tpu as pltpu
from jax.sharding import PartitionSpec as P

D = 768
FF = 1152
HEADS = 12
HD = 64
HALF = 64
STEP = 10
PAIR = 2 * HD
QB = 128
TILE = 256
CHUNK = 384

NORM_EPS = 1e-05
BETA_ONE = 0.9
BETA_TWO = 0.98
LEARN_RATE = 0.05
WEIGHT_DECAY = 0.01
ADAM_EPS = 1e-06
NEG_FILL = -1e30
THETA = 10000.0
BF = jnp.bfloat16
F32 = jnp.float32
VMEM_BYTES = 56 * 1024 * 1024


def dot(left, right):
    return lax.dot_general(left, right, (((1,), (0,)), ((), ())), preferred_element_type=F32)


def dot_bt(left, right):
    return lax.dot_general(left, right, (((1,), (1,)), ((), ())), preferred_element_type=F32)


def dot_at(left, right):
    return lax.dot_general(left, right, (((0,), (0,)), ((), ())), preferred_element_type=F32)


def full(shape):
    return pl.BlockSpec(shape, lambda i: (0,) * len(shape))


def rows(tile, width):
    return pl.BlockSpec((tile, width), lambda i: (i, 0))


def params():
    return pltpu.CompilerParams(
        dimension_semantics=("arbitrary",), vmem_limit_bytes=VMEM_BYTES
    )


def cost(flops, nbytes, trans=0):
    return pl.CostEstimate(flops=int(flops), bytes_accessed=int(nbytes), transcendentals=int(trans))


def normalize(x):
    mean = jnp.mean(x, axis=-1, keepdims=True)
    centered = x - mean
    var = jnp.mean(centered * centered, axis=-1, keepdims=True)
    r = lax.rsqrt(var + NORM_EPS)
    return centered * r, r


def turn(u, cos, sin_left, sin_right):
    return u * cos + pltpu.roll(u, PAIR - HD // 2, 1) * sin_left + pltpu.roll(u, HD // 2, 1) * sin_right


def qkv_body(x_ref, gain_ref, w_ref, cos_ref, sl_ref, sr_ref, normed_ref, q_ref, k_ref, v_ref):
    n, _ = normalize(x_ref[...].astype(F32))
    normed = (n * gain_ref[...]).astype(BF)
    normed_ref[...] = normed
    cos, sl, sr = cos_ref[...], sl_ref[...], sr_ref[...]
    for part, ref, scale in ((0, q_ref, HD**-0.5), (1, k_ref, 1.0)):
        u = dot(normed, w_ref[:, part * D : (part + 1) * D])
        for p in range(D // PAIR):
            t = turn(u[:, p * PAIR : (p + 1) * PAIR], cos, sl, sr)
            ref[:, p * PAIR : (p + 1) * PAIR] = (t * scale).astype(BF)
    v_ref[...] = dot(normed, w_ref[:, 2 * D :]).astype(BF)


def qkv_call(x_ext, gain, w, cos, sl, sr):
    ext = x_ext.shape[0]
    t = ext // 3
    out = jax.ShapeDtypeStruct((ext, D), BF)
    return pl.pallas_call(
        qkv_body,
        grid=(3,),
        in_specs=[rows(t, D), full((1, D)), full((D, 3 * D)), rows(t, PAIR), rows(t, PAIR), rows(t, PAIR)],
        out_specs=[rows(t, D)] * 4,
        out_shape=[out] * 4,
        compiler_params=params(),
        cost_estimate=cost(2 * ext * D * 3 * D, ext * D * 10 + D * D * 6),
        name="qkv",
    )(x_ext, gain, w, cos, sl, sr)


def two_heads(u):
    lane = lax.broadcasted_iota(jnp.int32, u.shape, 1)
    zero = jnp.zeros_like(u)
    return jnp.concatenate([jnp.where(lane < HD, u, zero), jnp.where(lane >= HD, u, zero)], axis=0)


def one_row(u):
    n = u.shape[0] // 2
    lane = lax.broadcasted_iota(jnp.int32, (n, PAIR), 1)
    return jnp.where(lane < HD, u[:n], u[n:])


def band(key_axis, b, last, side_ref):
    shape = (2 * QB, QB + 2 * HALF) if key_axis == 1 else (QB + 2 * HALF, 2 * QB)
    key = lax.broadcasted_iota(jnp.int32, shape, key_axis)
    query = lax.broadcasted_iota(jnp.int32, shape, 1 - key_axis) & (QB - 1)
    off = key - query
    low = jnp.where((b > 0) | (side_ref[0] > 0), 0, HALF)
    high = jnp.where((b < last) | (side_ref[1] > 0), QB + 2 * HALF, QB + HALF)
    return (off >= 0) & (off <= 2 * HALF) & (key >= low) & (key < high)


def attend_body(side_ref, q_ref, k_ref, v_ref, x_ref, w_ref, gain_ref, mixed_ref, middle_ref, n2_ref):
    i = pl.program_id(0)
    last = pl.num_programs(0) * (TILE // QB) - 1
    for s in range(TILE // QB):
        b = i * (TILE // QB) + s
        start = pl.multiple_of(b * QB, QB)
        ok = band(1, b, last, side_ref)
        for p in range(D // PAIR):
            cols = slice(p * PAIR, (p + 1) * PAIR)
            q2 = two_heads(q_ref[pl.ds(start + HALF, QB), cols])
            scores = dot_bt(q2, k_ref[pl.ds(start, QB + 2 * HALF), cols])
            scores = jnp.where(ok, scores, NEG_FILL)
            e = jnp.exp(scores - jnp.max(scores, axis=1, keepdims=True))
            probs = (e * (1.0 / jnp.sum(e, axis=1, keepdims=True))).astype(BF)
            o = dot(probs, v_ref[pl.ds(start, QB + 2 * HALF), cols])
            mixed_ref[s * QB : (s + 1) * QB, cols] = one_row(o).astype(BF)
    middle = x_ref[...].astype(F32) + dot(mixed_ref[...], w_ref[...])
    middle_ref[...] = middle
    n, _ = normalize(middle)
    n2_ref[...] = (n * gain_ref[...]).astype(BF)


def attend_call(side, q, k, v, x, w, gain):
    n = x.shape[0]
    ext = q.shape[0]
    return pl.pallas_call(
        attend_body,
        grid=(n // TILE,),
        in_specs=[
            pl.BlockSpec(memory_space=pltpu.SMEM),
            full((ext, D)), full((ext, D)), full((ext, D)), rows(TILE, D), full((D, D)), full((1, D)),
        ],
        out_specs=[rows(TILE, D)] * 3,
        out_shape=[
            jax.ShapeDtypeStruct((n, D), BF), jax.ShapeDtypeStruct((n, D), F32), jax.ShapeDtypeStruct((n, D), BF),
        ],
        compiler_params=params(),
        cost_estimate=cost(2 * n * D * (D + 16 * QB), n * D * 16),
        name="attend",
    )(side, q, k, v, x, w, gain)


def ffn_body(first, *refs):
    if first:
        n2_ref, cot_ref, wg_ref, wu_ref, wd_ref, out_ref, gn_ref, gg_ref, gu_ref, gd_ref, ag, au, ad = refs
    else:
        n2_ref, cot_ref, wg_ref, wu_ref, wd_ref, pout_ref, pgn_ref, out_ref, gn_ref, gg_ref, gu_ref, gd_ref, ag, au, ad = refs
    i = pl.program_id(0)
    n2 = n2_ref[...]
    cot = cot_ref[...]
    gate = dot(n2, wg_ref[...])
    up = dot(n2, wu_ref[...])
    ga = dot_bt(cot, wd_ref[...])
    phi = 0.5 + 0.5 * lax.erf(gate * (2.0**-0.5))
    gelu = gate * phi
    act = (gelu * up).astype(BF)
    slope = phi + gate * (jnp.exp(-0.5 * gate * gate) * 0.3989422804014327)
    dgate = (ga * up * slope).astype(BF)
    dup = (ga * gelu).astype(BF)
    out = dot(act, wd_ref[...])
    gn = dot_bt(dgate, wg_ref[...]) + dot_bt(dup, wu_ref[...])
    if first:
        out_ref[...] = out
        gn_ref[...] = gn
    else:
        out_ref[...] = pout_ref[...] + out
        gn_ref[...] = pgn_ref[...] + gn

    @pl.when(i == 0)
    def _():
        ag[...] = jnp.zeros_like(ag)
        au[...] = jnp.zeros_like(au)
        ad[...] = jnp.zeros_like(ad)

    ag[...] += dot_at(n2, dgate)
    au[...] += dot_at(n2, dup)
    ad[...] += dot_at(act, cot)

    @pl.when(i == pl.num_programs(0) - 1)
    def _():
        gg_ref[...] = ag[...].astype(BF)
        gu_ref[...] = au[...].astype(BF)
        gd_ref[...] = ad[...].astype(BF)


def ffn_call(c, n2, cot, w_in, w_down, before):
    import functools

    n = n2.shape[0]
    up_at = FF // CHUNK
    first = before is None
    in_specs = [
        rows(TILE, D), rows(TILE, D),
        pl.BlockSpec((D, CHUNK), lambda i: (0, c)),
        pl.BlockSpec((D, CHUNK), lambda i: (0, up_at + c)),
        pl.BlockSpec((CHUNK, D), lambda i: (c, 0)),
    ]
    args = [n2, cot, w_in, w_in, w_down]
    if not first:
        in_specs += [rows(TILE, D)] * 2
        args += list(before)
    part = jax.ShapeDtypeStruct((n, D), F32)
    return pl.pallas_call(
        functools.partial(ffn_body, first),
        grid=(n // TILE,),
        in_specs=in_specs,
        out_specs=[rows(TILE, D), rows(TILE, D), full((D, CHUNK)), full((D, CHUNK)), full((CHUNK, D))],
        out_shape=[
            part, part,
            jax.ShapeDtypeStruct((D, CHUNK), BF), jax.ShapeDtypeStruct((D, CHUNK), BF), jax.ShapeDtypeStruct((CHUNK, D), BF),
        ],
        scratch_shapes=[pltpu.VMEM((D, CHUNK), F32), pltpu.VMEM((D, CHUNK), F32), pltpu.VMEM((CHUNK, D), F32)],
        compiler_params=params(),
        cost_estimate=cost(2 * n * D * CHUNK * 9, n * D * 20),
        name="ffn",
    )(*args)


def norm_back(grad, n, r, gain):
    e = grad * gain
    return r * (e - jnp.mean(e, axis=-1, keepdims=True) - n * jnp.mean(e * n, axis=-1, keepdims=True))


def middle_body(mid_ref, gn_ref, ffn_ref, cot_ref, mixed_ref, w_ref, gain_ref,
                out_ref, gmid_ref, gmix_ref, gw_ref, gg_ref, acc):
    i = pl.program_id(0)
    middle = mid_ref[...]
    gn = gn_ref[...]
    out_ref[...] = (middle + ffn_ref[...]).astype(BF)
    n, r = normalize(middle)

    @pl.when(i == 0)
    def _():
        gg_ref[...] = jnp.zeros_like(gg_ref)
        acc[...] = jnp.zeros_like(acc)

    gg_ref[...] += jnp.sum(gn * n, axis=0, keepdims=True)
    gmid = cot_ref[...].astype(F32) + norm_back(gn, n, r, gain_ref[...])
    gmid_ref[...] = gmid
    branch = gmid.astype(BF)
    gmix_ref[...] = dot_bt(branch, w_ref[...]).astype(BF)
    acc[...] += dot_at(mixed_ref[...], branch)

    @pl.when(i == pl.num_programs(0) - 1)
    def _():
        gw_ref[...] = acc[...].astype(BF)


def middle_call(middle, gn, ffn, cot, mixed, w, gain):
    n = middle.shape[0]
    return pl.pallas_call(
        middle_body,
        grid=(n // TILE,),
        in_specs=[rows(TILE, D)] * 5 + [full((D, D)), full((1, D))],
        out_specs=[rows(TILE, D)] * 3 + [full((D, D)), full((1, D))],
        out_shape=[
            jax.ShapeDtypeStruct((n, D), BF), jax.ShapeDtypeStruct((n, D), F32), jax.ShapeDtypeStruct((n, D), BF),
            jax.ShapeDtypeStruct((D, D), BF), jax.ShapeDtypeStruct((1, D), F32),
        ],
        scratch_shapes=[pltpu.VMEM((D, D), F32)],
        compiler_params=params(),
        cost_estimate=cost(4 * n * D * D, n * D * 24),
        name="middle",
    )(middle, gn, ffn, cot, mixed, w, gain)


def attend_back_body(side_ref, q_ref, k_ref, v_ref, g_ref, cos_ref, sl_ref, sr_ref,
                     dq_ref, dk_ref, dv_ref, ak, av):
    b = pl.program_id(0)
    last = pl.num_programs(0) - 1
    start = pl.multiple_of(b * QB, QB)
    win = pl.ds(start, QB + 2 * HALF)
    here = pl.ds(start + HALF, QB)

    @pl.when(b == 0)
    def _():
        ak[...] = jnp.zeros_like(ak)
        av[...] = jnp.zeros_like(av)

    ok = band(0, b, last, side_ref)
    cos, sl, sr = cos_ref[here, :], sl_ref[here, :], sr_ref[here, :]
    for p in range(D // PAIR):
        cols = slice(p * PAIR, (p + 1) * PAIR)
        q2 = two_heads(q_ref[here, cols])
        g2 = two_heads(g_ref[:, cols])
        kw = k_ref[win, cols]
        scores = jnp.where(ok, dot_bt(kw, q2), NEG_FILL)
        e = jnp.exp(scores - jnp.max(scores, axis=0, keepdims=True))
        probs = e * (1.0 / jnp.sum(e, axis=0, keepdims=True))
        dp = dot_bt(v_ref[win, cols], g2)
        ds = (probs * (dp - jnp.sum(probs * dp, axis=0, keepdims=True))).astype(BF)
        ak[win, cols] += dot(ds, q2)
        av[win, cols] += dot(probs.astype(BF), g2)
        dq = one_row(dot_at(ds, kw)) * HD**-0.5
        dq_ref[:, cols] = turn(dq, cos, -sl, -sr).astype(BF)

    @pl.when(b == last)
    def _():
        cos, sl, sr = cos_ref[...], -sl_ref[...], -sr_ref[...]
        for p in range(D // PAIR):
            cols = slice(p * PAIR, (p + 1) * PAIR)
            dk_ref[:, cols] = turn(ak[:, cols], cos, sl, sr).astype(BF)
        dv_ref[...] = av[...].astype(BF)


def attend_back_call(side, q, k, v, g, cos, sl, sr):
    n = g.shape[0]
    ext = q.shape[0]
    return pl.pallas_call(
        attend_back_body,
        grid=(n // QB,),
        in_specs=[
            pl.BlockSpec(memory_space=pltpu.SMEM),
            full((ext, D)), full((ext, D)), full((ext, D)), rows(QB, D),
            full((ext, PAIR)), full((ext, PAIR)), full((ext, PAIR)),
        ],
        out_specs=[rows(QB, D), full((ext, D)), full((ext, D))],
        out_shape=[
            jax.ShapeDtypeStruct((n, D), BF), jax.ShapeDtypeStruct((ext, D), BF), jax.ShapeDtypeStruct((ext, D), BF),
        ],
        scratch_shapes=[pltpu.VMEM((ext, D), F32), pltpu.VMEM((ext, D), F32)],
        compiler_params=params(),
        cost_estimate=cost(2 * n * D * 40 * QB, n * D * 16),
        name="attend_back",
    )(side, q, k, v, g, cos, sl, sr)


def qkv_back_body(x_ref, normed_ref, dq_ref, dk_ref, dv_ref, rim_ref, gmid_ref, w_ref, gain_ref,
                  gin_ref, gw_ref, gg_ref, acc):
    i = pl.program_id(0)
    last = pl.num_programs(0) - 1
    start = pl.multiple_of(i * TILE, TILE)
    here = pl.ds(start + HALF, TILE)

    @pl.when(i == 0)
    def _():
        gg_ref[...] = jnp.zeros_like(gg_ref)
        acc[...] = jnp.zeros_like(acc)
        for at, ref in ((0, dk_ref), (D, dv_ref)):
            ref[HALF : 2 * HALF, :] += rim_ref[:HALF, at : at + D]

    @pl.when(i == last)
    def _():
        end = dk_ref.shape[0] - HALF
        for at, ref in ((0, dk_ref), (D, dv_ref)):
            ref[end - HALF : end, :] += rim_ref[HALF:, at : at + D]

    normed = normed_ref[here, :]
    total = jnp.zeros((TILE, D), F32)
    for part, d in enumerate((dq_ref[...], dk_ref[here, :], dv_ref[here, :])):
        cols = slice(part * D, (part + 1) * D)
        total += dot_bt(d, w_ref[:, cols])
        acc[:, cols] += dot_at(normed, d)
    n, r = normalize(x_ref[here, :].astype(F32))
    gg_ref[...] += jnp.sum(total * n, axis=0, keepdims=True)
    gin_ref[...] = (gmid_ref[...] + norm_back(total, n, r, gain_ref[...])).astype(BF)

    @pl.when(i == last)
    def _():
        gw_ref[...] = acc[...].astype(BF)


def qkv_back_call(x_ext, normed, dq, dk, dv, rim, gmid, w, gain):
    n = gmid.shape[0]
    ext = x_ext.shape[0]
    return pl.pallas_call(
        qkv_back_body,
        grid=(n // TILE,),
        in_specs=[
            full((ext, D)), full((ext, D)), rows(TILE, D), full((ext, D)), full((ext, D)), full((2 * HALF, 2 * D)),
            rows(TILE, D), full((D, 3 * D)), full((1, D)),
        ],
        out_specs=[rows(TILE, D), full((D, 3 * D)), full((1, D))],
        out_shape=[
            jax.ShapeDtypeStruct((n, D), BF), jax.ShapeDtypeStruct((D, 3 * D), BF), jax.ShapeDtypeStruct((1, D), F32),
        ],
        scratch_shapes=[pltpu.VMEM((D, 3 * D), F32)],
        compiler_params=params(),
        cost_estimate=cost(4 * n * D * 3 * D, n * D * 24),
        name="qkv_back",
    )(x_ext, normed, dq, dk, dv, rim, gmid, w, gain)


def adam_update(weight, grad, first_old, second, decay_rate):
    new_first = BETA_ONE * first_old + (1.0 - BETA_ONE) * grad
    new_second = BETA_TWO * second + (1.0 - BETA_TWO) * grad * grad
    first_hat = new_first / (1.0 - BETA_ONE**STEP)
    second_hat = new_second / (1.0 - BETA_TWO**STEP)
    change = -LEARN_RATE * (first_hat / (jnp.sqrt(second_hat) + ADAM_EPS) + decay_rate * weight)
    return (new_first, new_second, change)


def neighbours(count):
    up = [(i, i + 1) for i in range(count - 1)]
    return up, [(j, i) for i, j in up]


def local_part(x_ext, cot, side, place, weights, swap_rims):
    attn_w, out_w, ffn_w, down_w, gain_one, gain_two = weights
    ext = x_ext.shape[0]
    n = ext - 2 * HALF
    pos = place * n - HALF + jnp.arange(ext, dtype=jnp.int32)
    lane = jnp.arange(PAIR)
    freq = THETA ** (-2.0 * (lane % (HD // 2)).astype(F32) / HD)
    angle = pos.astype(F32)[:, None] * freq[None, :]
    cos = jnp.cos(angle)
    sin = jnp.sin(angle)
    low = (lane % HD < HD // 2)[None, :]
    sl = jnp.where(low, -sin, 0.0)
    sr = jnp.where(low, 0.0, sin)
    g1 = gain_one.astype(F32).reshape(1, D)
    g2 = gain_two.astype(F32).reshape(1, D)
    x = x_ext[HALF : HALF + n]
    normed, q, k, v = qkv_call(x_ext, g1, attn_w, cos, sl, sr)
    mixed, middle, n2 = attend_call(side, q, k, v, x, out_w, g2)
    acc = None
    gates, ups, downs = [], [], []
    for c in range(FF // CHUNK):
        ffn, gn, gg, gu, gd = ffn_call(c, n2, cot, ffn_w, down_w, acc)
        acc = (ffn, gn)
        gates.append(gg)
        ups.append(gu)
        downs.append(gd)
    block_out, gmid, gmix, g_out, gg_two = middle_call(middle, gn, ffn, cot, mixed, out_w, g2)
    dq, dk, dv = attend_back_call(side, q, k, v, gmix, cos, sl, sr)
    rim = swap_rims(dk, dv)
    grad_in, g_attn, gg_one = qkv_back_call(x_ext, normed, dq, dk, dv, rim, gmid, attn_w, g1)
    g_ffn = jnp.concatenate(gates + ups, axis=1)
    g_down = jnp.concatenate(downs, axis=0)
    return block_out, grad_in, (g_attn, g_out, g_ffn, g_down, gg_one.reshape(D), gg_two.reshape(D))


def shards(*args):
    hidden_in, cotangent, block_seq, block_place = args[:4]
    own_weights = args[4:10]
    firsts = args[10:16]
    seconds = args[16:22]
    weights = tuple(lax.all_gather(w, "wshard", axis=0, tiled=True) for w in own_weights)
    count = lax.axis_size("seq")
    at = lax.axis_index("seq")
    ids = block_seq[0]

    def pick(i):
        return lax.dynamic_index_in_dim(ids, i, keepdims=False)

    own = pick(at)
    left = (at > 0) & (pick(jnp.maximum(at - 1, 0)) == own)
    right = (at < count - 1) & (pick(jnp.minimum(at + 1, count - 1)) == own)
    side = jnp.stack([left, right]).astype(jnp.int32)
    place = lax.dynamic_index_in_dim(block_place[0], at, keepdims=False)
    x = hidden_in[0]
    n = x.shape[0]
    up, down = neighbours(count)
    x_ext = jnp.concatenate(
        [lax.ppermute(x[n - HALF :], "seq", up), x, lax.ppermute(x[:HALF], "seq", down)], axis=0
    )

    def swap_rims(dk, dv):
        first = jnp.concatenate([dk[:HALF], dv[:HALF]], axis=1)
        last = jnp.concatenate([dk[n + HALF :], dv[n + HALF :]], axis=1)
        return jnp.concatenate([lax.ppermute(last, "seq", up), lax.ppermute(first, "seq", down)], axis=0)

    block_out, grad_in, grads = local_part(x_ext, cotangent[0], side, place, weights, swap_rims)
    shard_grads = []
    for g in grads:
        s = lax.psum_scatter(g.astype(BF), "wshard", scatter_dimension=0, tiled=True)
        shard_grads.append(lax.psum(s, "seq").astype(F32))
    decays = (WEIGHT_DECAY, WEIGHT_DECAY, WEIGHT_DECAY, WEIGHT_DECAY, 0.0, 0.0)
    updates = [
        adam_update(w.astype(F32), g, m, v, c)
        for w, g, m, v, c in zip(own_weights, shard_grads, firsts, seconds, decays)
    ]
    return (
        (block_out[None], grad_in[None]) + tuple(shard_grads)
        + tuple(u[0] for u in updates) + tuple(u[1] for u in updates) + tuple(u[2] for u in updates)
    )


def solution(mesh):
    big = P("wshard", "seq", None)
    mat = P("wshard", None)
    vec = P("wshard")
    group = (mat, mat, mat, mat, vec, vec)
    in_specs = (big, big, mat, mat) + group * 3
    out_specs = (big, big) + group * 4
    return jax.shard_map(shards, mesh=mesh, in_specs=in_specs, out_specs=out_specs, check_vma=False)
```

time: 554 us -> 454 us (0.82); the launches traced: 546 us -> 453 us
  matrix products: 214 us -> 0 us
  waiting for transfers between devices: 93.6 us -> 233 us
  Pallas kernels: 0 us -> 120 us
  local copies, waits for them, and re-layouts: 88.7 us -> 13 us
  other arithmetic: 80.5 us -> 21.1 us
    dot_general x28 -> x0, matrix products: 191 us -> none  [the longest x4 32.4 us: cols_contract(): lax.dot_general(left, right, (((1,), (1,)), ((), ())), preferred_element_...]
    pallas_call x0 -> x8, Pallas kernels: none -> 120 us  [the longest x3 41 us: ffn_call(): pl.pallas_call(functools.partial(ffn_body, first), grid=(n // TILE,), in_...]
    reduce_scatter x4, waiting for transfers between devices: 8.93 us -> 77.4 us  [shards(): lax.psum_scatter(g.astype(BF), 'wshard', scatter_dimension=0, tiled=True)]
    all_gather x4, waiting for transfers between devices: 9.03 us -> 57.7 us  [shards(): lax.all_gather(w, 'wshard', axis=0, tiled=True)]
    slice x21 -> x3, local copies, waits for them, and re-layouts: 37.1 us -> 1.96 us  [the longest x2 1.94 us: swap_rims(): last = jnp.concatenate([dk[n + HALF:], dv[n + HALF:]], axis=1)]
    unnamed x203 -> x80, local copies, waits for them, and re-layouts: 39.2 us -> 9.79 us
    sub x2 -> x0, matrix products: 20.8 us -> none  [forward_pass(): exp_scores = jnp.exp(scores - row_max)]
    convert_element_type x7 -> x4, other arithmetic: 18.5 us -> 0.64 us  [the longest x1 0.58 us: shards(): side = jnp.stack([left, right]).astype(jnp.int32)]
  transfers between devices with their start and end apart: 13 -> 13, of which waited for: 4 -> 9; matrix products, arithmetic and copies ran while one was open for 57% -> 4% of each run, Pallas kernels for 0% -> 15%
where the time goes in v1:
time: 454 us; the launch traced here: 453 us
  waiting for transfers between devices  233 us (51%)
  Pallas kernels  120 us (26%)
  blocking collectives  35.1 us (8%)
  other arithmetic  21.1 us (5%)
  between operations  19 us (4%)
  local copies, waits for them, and re-layouts  13 us (3%)
  starting transfers between devices  12.4 us (3%)
    psum x1, waiting for transfers between devices, shards(): shard_grads.append(lax.psum(s, 'seq').astype(F32))  87.6 us
    reduce_scatter x4, waiting for transfers between devices, shards(): lax.psum_scatter(g.astype(BF), 'wshard', scatter_dimension=0, tiled=True)  77.4 us
    all_gather x4, waiting for transfers between devices, shards(): lax.all_gather(w, 'wshard', axis=0, tiled=True)  57.7 us
    pallas_call x3, Pallas kernels, ffn_call(): pl.pallas_call(functools.partial(ffn_body, first), grid=(n // TILE,), in_...  41 us
    pallas_call x1, Pallas kernels, attend_back_call(): pl.pallas_call(attend_back_body, grid=(n // QB,), in_specs=[pl.BlockSpec(...  27.6 us
    psum x1, blocking collectives, shards(): shard_grads.append(lax.psum(s, 'seq').astype(F32))  22.6 us
    pallas_call x1, Pallas kernels, qkv_back_call(): pl.pallas_call(qkv_back_body, grid=(n // TILE,), in_specs=[full((ext, D))...  16.4 us
    pallas_call x1, Pallas kernels, attend_call(): pl.pallas_call(attend_body, grid=(n // TILE,), in_specs=[pl.BlockSpec(mem...  14.7 us
  transfers between devices with their start and end apart: 13, of which 9 were waited for; matrix products, arithmetic and copies ran while one was open for 4% of the time, Pallas kernels for 15%

profile of v1, /device:TPU:0, one launch (start us, length us, event | category | flops | bytes accessed | tf_op | source)
XLA Modules:
  0.0 453.5 jit_solution(14013321252879381511)
XLA Ops:
  7.3 0.7 all-gather.5.cloned.1.call-update
  8.0 0.7 all-gather.7.cloned.1.call-update
  8.8 0.7 all-gather.11.cloned.1.call-update
  9.5 0.5 all-gather.9.cloned.1.call-update
  10.1 4.9 %collective-permute-start = (bf16[64,768]{1,0:T(8,128)(2,1)S(1)}, bf16[64,768]{1,0:T(8,128)(2,1)S(1)}, u32[]{:S(2)}, u32[]{:S(2)}) collective-permute-start(bf16[64,768]{1,0:T(8,128)(2,1)S(1)} %get-tuple-element.130), channel_id=1, source_target_pairs={{0,4},{4,8},{8,12},{12,16},{16,20},{20,24},{24,28},{1,5},{5,9},{9,... | collective-permute-start | bytes 294920 | tf_op jit(solution)/shard_map/ppermute | solution.py:479
  15.0 1.3 collective-permute-start.1
  16.4 0.6 constant_dynamic-slice_fusion.3
  19.6 0.6 fusion.21
  20.9 0.2 dynamic-update-slice
  21.1 0.2 dynamic-update-slice.1
  21.3 6.8 %all-reduce.7 = (bf16[768]{0:T(1024)(128)(2,1)S(1)}, bf16[768]{0:T(1024)(128)(2,1)S(1)}) all-reduce(bf16[768]{0:T(1024)(128)(2,1)S(1)} %dynamic-update-slice, bf16[768]{0:T(1024)(128)(2,1)S(1)} %dynamic-update-slice.1), channel_id=1, replica_groups=mesh['seq'=8,'wshard'=4] {'wshard'}, use_global_device_ids=true, to_apply=%add | all-reduce | flops 1536 | bytes 6144
  28.1 0.6 reshape.114.gain_ref
  28.7 0.6 reshape.116.gain_ref
  30.0 3.4 fusion.3
  33.4 0.6 add_convert_fusion.1.side_ref
  34.0 1.3 pad_maximum_fusion.x_ref
  35.3 8.0 %all-gather.5.cloned.1.call-done.w_ref = bf16[768,2304]{1,0:T(8,128)(2,1)} async-done(((bf16[192,2304]{1,0:T(8,128)(2,1)}), bf16[768,2304]{1,0:T(8,128)(2,1)}) %all-gather.5.cloned.1.call-update) | async-done | bytes 3538960 | tf_op jit(solution)/shard_map/all_gather | solution.py:462
  43.3 9.1 %qkv.1 = (bf16[1152,768]{1,0:T(8,128)(2,1)}, bf16[1152,768]{1,0:T(8,128)(2,1)}, bf16[1152,768]{1,0:T(8,128)(2,1)}, bf16[1152,768]{1,0:T(8,128)(2,1)}) custom-call(bf16[1152,768]{1,0:T(8,128)(2,1)} %pad_maximum_fusion.x_ref, f32[1,768]{1,0:T(1,128)} %reshape.114.gain_ref, bf16[768,2304]{1,0:T(8,128)(2,1)} %all-gather.5.cloned.1.call-done.w_ref, ...), custom_call_target="tpu_custom_call" | custom-call | flops 4076863488 | bytes 12386304 | tf_op jit(solution)/shard_map/qkv/pallas_call | solution.py:91
  52.4 9.9 %all-gather.7.cloned.1.call-done.w_ref = bf16[768,768]{1,0:T(8,128)(2,1)} async-done(((bf16[192,768]{1,0:T(8,128)(2,1)}), bf16[768,768]{1,0:T(8,128)(2,1)}) %all-gather.7.cloned.1.call-update) | async-done | bytes 1179664 | tf_op jit(solution)/shard_map/all_gather | solution.py:462
  62.4 14.7 %attend.1 = (bf16[1024,768]{1,0:T(8,128)(2,1)}, f32[1024,768]{1,0:T(8,128)}, bf16[1024,768]{1,0:T(8,128)(2,1)}) custom-call(s32[2]{0:T(128)} %add_convert_fusion.1.side_ref, bf16[1152,768]{1,0:T(8,128)(2,1)} %get-tuple-element.59.q_ref, bf16[1152,768]{1,0:T(8,128)(2,1)} %get-tuple-element.60.k_ref, bf16[1152,768]{1,0:T(8,128)(2,1)} %get-tuple-element.61.v_ref, ...), custom_call_target="tpu_custom_call" | custom-call | flops 4429185024 | bytes 12582912 | tf_op jit(solution)/shard_map/attend/pallas_call | solution.py:150
  77.1 7.6 %all-gather.11.cloned.1.call-done.refs_4_ = bf16[1152,768]{1,0:T(8,128)(2,1)} async-done(((bf16[288,768]{1,0:T(8,128)(2,1)}), bf16[1152,768]{1,0:T(8,128)(2,1)}) %all-gather.11.cloned.1.call-update) | async-done | bytes 1769488 | tf_op jit(solution)/shard_map/all_gather | solution.py:462
  84.7 32.2 %all-gather.9.cloned.1.call-done.refs_2_.refs_3_ = bf16[768,2304]{1,0:T(8,128)(2,1)} async-done(((bf16[192,2304]{1,0:T(8,128)(2,1)}), bf16[768,2304]{1,0:T(8,128)(2,1)}) %all-gather.9.cloned.1.call-update) | async-done | bytes 3538960 | tf_op jit(solution)/shard_map/all_gather | solution.py:462
  116.9 13.1 %ffn.3 = (f32[1024,768]{1,0:T(8,128)}, f32[1024,768]{1,0:T(8,128)}, bf16[768,384]{1,0:T(8,128)(2,1)}, bf16[768,384]{1,0:T(8,128)(2,1)}, bf16[384,768]{1,0:T(8,128)(2,1)}) custom-call(bf16[1024,768]{1,0:T(8,128)(2,1)} %get-tuple-element.63.refs_0_, bf16[1024,768]{1,0:T(8,128)(2,1)} %bitcast.17, ...), custom_call_target="tpu_custom_call" | custom-call | flops 5435817984 | bytes 15728640 | tf_op jit(solution)/shard_map/ffn/pallas_call | solution.py:227
  130.1 13.8 %ffn.4 = (f32[1024,768]{1,0:T(8,128)}, f32[1024,768]{1,0:T(8,128)}, bf16[768,384]{1,0:T(8,128)(2,1)}, bf16[768,384]{1,0:T(8,128)(2,1)}, bf16[384,768]{1,0:T(8,128)(2,1)}) custom-call(bf16[1024,768]{1,0:T(8,128)(2,1)} %get-tuple-element.63.refs_0_, bf16[1024,768]{1,0:T(8,128)(2,1)} %bitcast.18, ...), custom_call_target="tpu_custom_call" | custom-call | flops 5435817984 | bytes 15728640 | tf_op jit(solution)/shard_map/ffn/pallas_call | solution.py:227
  143.9 14.0 %ffn.5 = (f32[1024,768]{1,0:T(8,128)}, f32[1024,768]{1,0:T(8,128)}, bf16[768,384]{1,0:T(8,128)(2,1)}, bf16[768,384]{1,0:T(8,128)(2,1)}, bf16[384,768]{1,0:T(8,128)(2,1)}) custom-call(bf16[1024,768]{1,0:T(8,128)(2,1)} %get-tuple-element.63.refs_0_, bf16[1024,768]{1,0:T(8,128)(2,1)} %bitcast.19, ...), custom_call_target="tpu_custom_call" | custom-call | flops 5435817984 | bytes 15728640 | tf_op jit(solution)/shard_map/ffn/pallas_call | solution.py:227
  157.9 11.4 %middle.1 = (bf16[1024,768]{1,0:T(8,128)(2,1)}, f32[1024,768]{1,0:T(8,128)}, bf16[1024,768]{1,0:T(8,128)(2,1)}, bf16[768,768]{1,0:T(8,128)(2,1)}, f32[1,768]{1,0:T(1,128)}) custom-call(f32[1024,768]{1,0:T(8,128)} %get-tuple-element.62.mid_ref, f32[1024,768]{1,0:T(8,128)} %get-tuple-element.68.gn_ref, f32[1024,768]{1,0:T(8,128)} %get-tuple-element.69.ffn_ref, ...), custom_call_target="tpu_custom_call" | custom-call | flops 2415919104 | bytes 18874368 | tf_op jit(solution)/shard_map/middle/pallas_call | solution.py:275
  169.4 0.0 reduce-scatter.11.cloned.1.call-start
  169.5 1.3 pad_maximum_fusion.1
  170.8 0.0 reduce-scatter.9.cloned.1.call-start
  170.9 1.2 constant_dynamic-update-slice_fusion.5
  172.1 1.2 constant_dynamic-update-slice_fusion.4
  173.3 1.2 constant_dynamic-update-slice_fusion.3
  174.5 0.1 constant_dynamic-update-slice_fusion.2
  174.7 0.1 constant_dynamic-update-slice_fusion.1
  174.8 0.1 constant_dynamic-update-slice_fusion
  174.9 1.8 copy-done
  176.7 27.6 %attend_back.1 = (bf16[1024,768]{1,0:T(8,128)(2,1)}, bf16[1152,768]{1,0:T(8,128)(2,1)}, bf16[1152,768]{1,0:T(8,128)(2,1)}) custom-call(s32[2]{0:T(128)} %add_convert_fusion.1.side_ref, bf16[1152,768]{1,0:T(8,128)(2,1)} %get-tuple-element.59.q_ref, bf16[1152,768]{1,0:T(8,128)(2,1)} %get-tuple-element.60.k_ref, bf16[1152,768]{1,0:T(8,128)(2,1)} %get-tuple-element.61.v_ref, ...), custom_call_target="tpu_custom_call" | custom-call | flops 8053063680 | bytes 12582912 | tf_op jit(solution)/shard_map/attend_back/pallas_call | solution.py:333
  204.3 1.0 fusion.19
  205.3 1.0 fusion.20
  206.3 1.3 collective-permute-start.3
  207.6 4.6 %collective-permute-start.2 = (bf16[64,1536]{1,0:T(8,128)(2,1)S(1)}, bf16[64,1536]{1,0:T(8,128)(2,1)S(1)}, u32[]{:S(2)}, u32[]{:S(2)}) collective-permute-start(bf16[64,1536]{1,0:T(8,128)(2,1)S(1)} %pad_maximum_fusion.3), channel_id=1, source_target_pairs={{0,4},{4,8},{8,12},{12,16},{16,20},{20,24},{24,28},{1,5},{5,9},{9,... | collective-permute-start | bytes 589832 | tf_op jit(solution)/shard_map/ppermute | solution.py:485
  212.2 3.1 collective-permute-done.3
  215.2 4.2 collective-permute-done.2
  219.4 0.8 pad_maximum_fusion.2.rim_ref
  220.2 16.4 %qkv_back.1 = (bf16[1024,768]{1,0:T(8,128)(2,1)}, bf16[768,2304]{1,0:T(8,128)(2,1)}, f32[1,768]{1,0:T(1,128)}) custom-call(bf16[1152,768]{1,0:T(8,128)(2,1)} %pad_maximum_fusion.x_ref, bf16[1152,768]{1,0:T(8,128)(2,1)} %get-tuple-element.72.normed_ref, bf16[1024,768]{1,0:T(8,128)(2,1)} %get-tuple-element.74.dq_ref, ...), custom_call_target="tpu_custom_call" | custom-call | flops 7247757312 | bytes 18874368 | tf_op jit(solution)/shard_map/qkv_back/pallas_call | solution.py:390
  236.7 0.0 all-reduce.10.cloned.1.call-start
  236.8 34.1 %reduce-scatter.9.cloned.1.call-done = bf16[192,2304]{1,0:T(8,128)(2,1)} async-done(((bf16[768,2304]{1,0:T(8,128)(2,1)}), bf16[192,2304]{1,0:T(8,128)(2,1)}) %reduce-scatter.9.cloned.1.call-update) | async-done | bytes 884752 | tf_op jit(solution)/shard_map/reduce_scatter | solution.py:490
  271.0 43.2 %reduce-scatter.5.cloned.1.call-done = bf16[192,2304]{1,0:T(8,128)(2,1)} async-done(((bf16[768,2304]{1,0:T(8,128)(2,1)}), bf16[192,2304]{1,0:T(8,128)(2,1)}) %reduce-scatter.5.cloned.1.call-update) | async-done | bytes 884752 | tf_op jit(solution)/shard_map/reduce_scatter | solution.py:490
  314.9 5.8 %all-reduce.6 = (bf16[768]{0:T(1024)(128)(2,1)S(1)}, bf16[768]{0:T(1024)(128)(2,1)S(1)}) all-reduce(bf16[768]{0:T(1024)(128)(2,1)S(1)} %convert_reduce_fusion.1, bf16[768]{0:T(1024)(128)(2,1)S(1)} %convert_reduce_fusion), channel_id=6, replica_groups=mesh['seq'=8,'wshard'=4] {'wshard'}, use_global_device_ids=true, to_apply=%region_8.9.clone | all-reduce | flops 1536 | bytes 6144
  320.7 0.1 dynamic-slice.7
  320.7 0.1 dynamic-slice.9
  320.8 22.6 %all-reduce.4 = (bf16[192]{0:T(256)(128)(2,1)S(1)}, bf16[192]{0:T(256)(128)(2,1)S(1)}) all-reduce(bf16[192]{0:T(256)(128)(2,1)S(1)} %dynamic-slice.7, bf16[192]{0:T(256)(128)(2,1)S(1)} %dynamic-slice.9), channel_id=1, replica_groups=mesh['seq'=8,'wshard'=4] {'seq'}, use_global_device_ids=true, to_apply=%region_9.10 | all-reduce | flops 384 | bytes 1536 | tf_op jit(solution)/shard_map/psum | solution.py:491
  343.4 0.6 add_multiply_fusion.5
  344.0 0.6 add_multiply_fusion.4
  344.6 87.6 %all-reduce.10.cloned.1.call-done = (bf16[192,2304]{1,0:T(8,128)(2,1)}, bf16[192,768]{1,0:T(8,128)(2,1)}, bf16[192,2304]{1,0:T(8,128)(2,1)}, bf16[288,768]{1,0:T(8,128)(2,1)}) async-done(((bf16[192,2304]{1,0:T(8,128)(2,1)}, bf16[192,768]{1,0:T(8,128)(2,1)}, bf16[192,2304]{1,0:T(8,128)(2,1)}, bf16[288,768]{1,0:T(8,128)(2,1)}), (bf16[192,2304]{1,0:T(8,128)(2,1)}, bf16[192,768]{1,0:T(8,128)(2,1)}, ...) | async-done | bytes 2506768 | tf_op jit(solution)/shard_map/psum | solution.py:491
  432.2 2.6 add_multiply_fusion.3
  434.9 2.0 add_multiply_fusion.2
  436.9 1.0 copy-done.5
  437.9 0.5 copy-done.6
  438.4 0.2 copy-done.11
  438.7 3.9 add_multiply_fusion.1
  442.6 0.7 copy-done.8
  443.3 0.4 copy-done.10
  443.7 3.3 add_multiply_fusion
  (87 shorter events, 0.6 us)
Async XLA Ops:
  7.2 12.4 %copy-start.26 = (u32[32]{0:T(128)S(1)}, u32[32]{0:T(128)}, u32[]{:S(2)}) copy-start(u32[32]{0:T(128)} %constant.136) | copy-start | bytes 388
  7.2 2.9 copy-start.3
  7.2 9.1 %copy-start.33 = (s32[1,8]{1,0:T(1,128)S(1)}, s32[1,8]{1,0:T(1,128)}, u32[]{:S(2)}) copy-start(s32[1,8]{1,0:T(1,128)} %param.25) | copy-start | bytes 100
  7.2 9.1 %copy-start.23 = (s32[1,8]{1,0:T(1,128)S(1)}, s32[1,8]{1,0:T(1,128)}, u32[]{:S(2)}) copy-start(s32[1,8]{1,0:T(1,128)} %param.24) | copy-start | bytes 100
  7.2 13.6 %copy-start.31 = (bf16[192]{0:T(256)(128)(2,1)S(1)}, bf16[192]{0:T(256)(128)(2,1)}, u32[]{:S(2)}) copy-start(bf16[192]{0:T(256)(128)(2,1)} %param.30) | copy-start | bytes 1156
  7.3 13.8 %copy-start.32 = (bf16[192]{0:T(256)(128)(2,1)S(1)}, bf16[192]{0:T(256)(128)(2,1)}, u32[]{:S(2)}) copy-start(bf16[192]{0:T(256)(128)(2,1)} %param.31) | copy-start | bytes 1156
  7.3 36.0 %all-gather.5.cloned.1.call-start = ((), (), s32[]{:S(2)}) async-start(), calls=%async_computation.4 | async-start | bytes 4423680 | tf_op jit(solution)/shard_map/all_gather | solution.py:462
  8.0 54.4 %all-gather.7.cloned.1.call-start = ((), (), s32[]{:S(2)}) async-start(), calls=%async_computation.5 | async-start | bytes 1474560 | tf_op jit(solution)/shard_map/all_gather | solution.py:462
  8.8 76.0 %all-gather.11.cloned.1.call-start = ((), (), s32[]{:S(2)}) async-start(), calls=%async_computation.7 | async-start | bytes 2211840 | tf_op jit(solution)/shard_map/all_gather | solution.py:462
  9.5 107.4 %all-gather.9.cloned.1.call-start = ((), (), s32[]{:S(2)}) async-start(), calls=%async_computation.6 | async-start | bytes 4423680 | tf_op jit(solution)/shard_map/all_gather | solution.py:462
  10.1 226.7 %reduce-scatter.7.cloned.1.call-start = ((), (), s32[]{:S(2)}) async-start(), calls=%async_computation.9 | async-start | bytes 1474560 | tf_op jit(solution)/shard_map/reduce_scatter | solution.py:490
  10.1 23.8 %collective-permute-start = (bf16[64,768]{1,0:T(8,128)(2,1)S(1)}, bf16[64,768]{1,0:T(8,128)(2,1)S(1)}, u32[]{:S(2)}, u32[]{:S(2)}) collective-permute-start(bf16[64,768]{1,0:T(8,128)(2,1)S(1)} %get-tuple-element.130), channel_id=1, source_target_pairs={{0,4},{4,8},{8,12},{12,16},{16,20},{20,24},{24,28},{1,5},{5,9},{9,... | collective-permute-start | bytes 294920 | tf_op jit(solution)/shard_map/ppermute | solution.py:479
  15.0 19.0 %collective-permute-start.1 = (bf16[64,768]{1,0:T(8,128)(2,1)S(1)}, bf16[64,768]{1,0:T(8,128)(2,1)S(1)}, u32[]{:S(2)}, u32[]{:S(2)}) collective-permute-start(bf16[64,768]{1,0:T(8,128)(2,1)S(1)} %get-tuple-element.131), channel_id=1, source_target_pairs={{4,0},{8,4},{12,8},{16,12},{20,16},{24,20},{28,24},{5,1},{9,5},{13... | collective-permute-start | bytes 294920 | tf_op jit(solution)/shard_map/ppermute | solution.py:479
  157.9 11.5 %copy-start.14 = (bf16[384,768]{1,0:T(8,128)(2,1)S(1)}, bf16[384,768]{1,0:T(8,128)(2,1)}, u32[]{:S(2)}) copy-start(bf16[384,768]{1,0:T(8,128)(2,1)} %get-tuple-element.87) | copy-start | bytes 1769476
  157.9 11.5 %copy-start.15 = (bf16[384,768]{1,0:T(8,128)(2,1)S(1)}, bf16[384,768]{1,0:T(8,128)(2,1)}, u32[]{:S(2)}) copy-start(bf16[384,768]{1,0:T(8,128)(2,1)} %get-tuple-element.88) | copy-start | bytes 1769476
  157.9 11.5 %copy-start.16 = (bf16[384,768]{1,0:T(8,128)(2,1)S(1)}, bf16[384,768]{1,0:T(8,128)(2,1)}, u32[]{:S(2)}) copy-start(bf16[384,768]{1,0:T(8,128)(2,1)} %get-tuple-element.89) | copy-start | bytes 1769476
  169.4 67.4 %reduce-scatter.11.cloned.1.call-start = ((), (), s32[]{:S(2)}) async-start(), calls=%async_computation.11 | async-start | bytes 2211840 | tf_op jit(solution)/shard_map/reduce_scatter | solution.py:490
  170.8 100.1 %reduce-scatter.9.cloned.1.call-start = ((), (), s32[]{:S(2)}) async-start(), calls=%async_computation.10 | async-start | bytes 4423680 | tf_op jit(solution)/shard_map/reduce_scatter | solution.py:490
  170.9 3.7 copy-start.17
  172.1 2.6 copy-start.18
  173.3 1.5 copy-start.19
  174.9 1.8 copy-start
  176.7 137.5 %reduce-scatter.5.cloned.1.call-start = ((), (), s32[]{:S(2)}) async-start(), calls=%async_computation.8 | async-start | bytes 4423680 | tf_op jit(solution)/shard_map/reduce_scatter | solution.py:490
  206.3 9.0 %collective-permute-start.3 = (bf16[64,1536]{1,0:T(8,128)(2,1)S(1)}, bf16[64,1536]{1,0:T(8,128)(2,1)S(1)}, u32[]{:S(2)}, u32[]{:S(2)}) collective-permute-start(bf16[64,1536]{1,0:T(8,128)(2,1)S(1)} %pad_maximum_fusion.4), channel_id=1, source_target_pairs={{4,0},{8,4},{12,8},{16,12},{20,16},{24,20},{28,24},{5,1},{9,5},{13... | collective-permute-start | bytes 589832 | tf_op jit(solution)/shard_map/ppermute | solution.py:485
  207.6 11.8 %collective-permute-start.2 = (bf16[64,1536]{1,0:T(8,128)(2,1)S(1)}, bf16[64,1536]{1,0:T(8,128)(2,1)S(1)}, u32[]{:S(2)}, u32[]{:S(2)}) collective-permute-start(bf16[64,1536]{1,0:T(8,128)(2,1)S(1)} %pad_maximum_fusion.3), channel_id=1, source_target_pairs={{0,4},{4,8},{8,12},{12,16},{16,20},{20,24},{24,28},{1,5},{5,9},{9,... | collective-permute-start | bytes 589832 | tf_op jit(solution)/shard_map/ppermute | solution.py:485
  236.6 78.2 %copy-start.24 = (f32[1,768]{1,0:T(1,128)S(1)}, f32[1,768]{1,0:T(1,128)}, u32[]{:S(2)}) copy-start(f32[1,768]{1,0:T(1,128)} %get-tuple-element.91) | copy-start | bytes 9220
  236.6 78.2 %copy-start.25 = (f32[1,768]{1,0:T(1,128)S(1)}, f32[1,768]{1,0:T(1,128)}, u32[]{:S(2)}) copy-start(f32[1,768]{1,0:T(1,128)} %get-tuple-element.90) | copy-start | bytes 9220
  236.6 106.7 %copy-start.27 = (f32[192]{0:T(256)S(1)}, f32[192]{0:T(256)}, u32[]{:S(2)}) copy-start(f32[192]{0:T(256)} %param.42) | copy-start | bytes 2308
  236.7 106.7 %copy-start.28 = (f32[192]{0:T(256)S(1)}, f32[192]{0:T(256)}, u32[]{:S(2)}) copy-start(f32[192]{0:T(256)} %param.36) | copy-start | bytes 2308
  236.7 107.3 %copy-start.29 = (f32[192]{0:T(256)S(1)}, f32[192]{0:T(256)}, u32[]{:S(2)}) copy-start(f32[192]{0:T(256)} %param.43) | copy-start | bytes 2308
  236.7 107.3 %copy-start.30 = (f32[192]{0:T(256)S(1)}, f32[192]{0:T(256)}, u32[]{:S(2)}) copy-start(f32[192]{0:T(256)} %param.37) | copy-start | bytes 2308
  236.7 195.5 %copy-start.9 = (bf16[192,768]{1,0:T(8,128)(2,1)S(1)}, bf16[192,768]{1,0:T(8,128)(2,1)}, u32[]{:S(2)}) copy-start(bf16[192,768]{1,0:T(8,128)(2,1)} %param.27) | copy-start | bytes 884740
  236.7 195.5 %copy-start.20 = (f32[192,768]{1,0:T(8,128)S(1)}, f32[192,768]{1,0:T(8,128)}, u32[]{:S(2)}) copy-start(f32[192,768]{1,0:T(8,128)} %param.39) | copy-start | bytes 1769476
  236.7 195.4 %copy-start.21 = (f32[192,768]{1,0:T(8,128)S(1)}, f32[192,768]{1,0:T(8,128)}, u32[]{:S(2)}) copy-start(f32[192,768]{1,0:T(8,128)} %param.33) | copy-start | bytes 1769476
  236.7 195.4 %all-reduce.10.cloned.1.call-start = ((), (), s32[]{:S(2)}) async-start(), calls=%async_computation.12 | async-start | bytes 5013504 | tf_op jit(solution)/shard_map/psum | solution.py:491
  432.2 2.7 copy-start.4
  432.2 2.7 copy-start.12
  432.2 2.7 copy-start.13
  432.2 2.7 copy-start.22
  434.9 2.0 copy-start.1
  434.9 3.0 copy-start.5
  434.9 3.5 copy-start.6
  434.9 3.7 copy-start.11
  438.6 3.9 copy-start.2
  438.6 3.9 copy-start.7
  438.7 4.6 %copy-start.8 = (f32[192,2304]{1,0:T(8,128)S(1)}, f32[192,2304]{1,0:T(8,128)}, u32[]{:S(2)}) copy-start(f32[192,2304]{1,0:T(8,128)} %param.34) | copy-start | bytes 5308420
  438.7 5.0 %copy-start.10 = (bf16[192,2304]{1,0:T(8,128)(2,1)S(1)}, bf16[192,2304]{1,0:T(8,128)(2,1)}, u32[]{:S(2)}) copy-start(bf16[192,2304]{1,0:T(8,128)(2,1)} %get-tuple-element.96) | copy-start | bytes 2654212
Sparse Core Ops, SparseCore 0:
  9.7 33.5 all-gather.4
  44.8 17.4 all-gather.6
  63.9 20.7 all-gather.10
  86.1 30.7 all-gather.8
  169.5 25.7 reduce-scatter.6
  198.5 29.3 reduce-scatter.10
  230.5 40.4 reduce-scatter.8
  273.7 40.4 reduce-scatter.4
  318.1 114.0 all-reduce.9

commit v2 on v1

v2 whole, which is shorter than its diff:
```python
import functools

import jax
import jax.numpy as jnp
from jax import lax
from jax.experimental import pallas as pl
from jax.experimental.pallas import tpu as pltpu
from jax.sharding import PartitionSpec as P

D = 768
FF = 1152
HEADS = 12
HD = 64
HALF = 64
STEP = 10
PAIR = 2 * HD
QB = 128
TILE = 256
WIDE = 384
QUAD = 4 * HD

NORM_EPS = 1e-05
BETA_ONE = 0.9
BETA_TWO = 0.98
LEARN_RATE = 0.05
WEIGHT_DECAY = 0.01
ADAM_EPS = 1e-06
NEG_FILL = -1e30
THETA = 10000.0
BF = jnp.bfloat16
F32 = jnp.float32


def dot(left, right):
    return lax.dot_general(left, right, (((1,), (0,)), ((), ())), preferred_element_type=F32)


def dot_bt(left, right):
    return lax.dot_general(left, right, (((1,), (1,)), ((), ())), preferred_element_type=F32)


def dot_at(left, right):
    return lax.dot_general(left, right, (((0,), (0,)), ((), ())), preferred_element_type=F32)


def call(body, args, in_specs, out_specs, out_shape, megabytes, deps=(), aliases=None, **kw):
    first = len(args)
    n_out = len(out_shape)

    def wrapped(*refs):
        refs = refs[:first] + refs[first + len(deps) :]
        token = refs[first + n_out]
        token[...] = jnp.zeros_like(token)
        body(*refs[: first + n_out], *refs[first + n_out + 1 :])

    return pl.pallas_call(
        wrapped,
        in_specs=list(in_specs) + [pl.BlockSpec(memory_space=pl.ANY)] * len(deps),
        out_specs=list(out_specs) + [full((8, 128))],
        out_shape=list(out_shape) + [jax.ShapeDtypeStruct((8, 128), F32)],
        input_output_aliases=aliases or {},
        compiler_params=pltpu.CompilerParams(
            dimension_semantics=("arbitrary",), vmem_limit_bytes=megabytes * 1024 * 1024
        ),
        **kw,
    )(*args, *deps)


def full(shape):
    return pl.BlockSpec(shape, lambda i: (0,) * len(shape))


def rows(tile, width):
    return pl.BlockSpec((tile, width), lambda i: (i, 0))


def cost(microseconds):
    return pl.CostEstimate(flops=int(microseconds * 1.1e9), bytes_accessed=0, transcendentals=0)


def normalize(x):
    mean = jnp.mean(x, axis=-1, keepdims=True)
    centered = x - mean
    var = jnp.mean(centered * centered, axis=-1, keepdims=True)
    r = lax.rsqrt(var + NORM_EPS)
    return centered * r, r


def turn(u, cos, sin_left, sin_right):
    return u * cos + pltpu.roll(u, PAIR - HD // 2, 1) * sin_left + pltpu.roll(u, HD // 2, 1) * sin_right


def lay(w, parts, out_ref, first=0):
    r = out_ref.shape[0] // 4
    for i, ref in enumerate(parts):
        out_ref[pl.ds(pl.multiple_of((w ^ i) * r, 32), r), :] = ref[first : first + r, :]


def deal(w, acc, cols, keep_ref, send_ref, at):
    r = acc.shape[0] // 4
    c = w & 1
    for x in range(2):
        keep_ref[x, at : at + r, :] = acc[pl.ds(pl.multiple_of((2 * x + c) * r, 32), r), cols].astype(BF)
        send_ref[x, at : at + r, :] = acc[pl.ds(pl.multiple_of((2 * x + 1 - c) * r, 32), r), cols].astype(BF)


def smem():
    return pl.BlockSpec(memory_space=pltpu.SMEM)


def piece(n_rows):
    return jax.ShapeDtypeStruct((2, n_rows, WIDE), BF)


def qkv_body(info_ref, x_ref, gain_ref, wa, wb, wc, wd, cos_ref, sl_ref, sr_ref, nt_ref, q_ref, k_ref, v_ref, w_ref):
    @pl.when(pl.program_id(0) == 0)
    def _():
        lay(info_ref[2], (wa, wb, wc, wd), w_ref)

    n, _ = normalize(x_ref[...].astype(F32))
    normed = (n * gain_ref[...]).astype(BF)
    nt_ref[...] = normed.T
    cos, sl, sr = cos_ref[...], sl_ref[...], sr_ref[...]
    for part, ref, scale in ((0, q_ref, HD**-0.5), (1, k_ref, 1.0)):
        u = dot(normed, w_ref[:, part * D : (part + 1) * D])
        for p in range(D // PAIR):
            t = turn(u[:, p * PAIR : (p + 1) * PAIR], cos, sl, sr)
            ref[:, p * PAIR : (p + 1) * PAIR] = (t * scale).astype(BF)
    v_ref[...] = dot(normed, w_ref[:, 2 * D :]).astype(BF)


def qkv_call(info, x_ext, gain, w_parts, cos, sl, sr, deps=()):
    ext = x_ext.shape[0]
    t = ext // 3
    out = jax.ShapeDtypeStruct((ext, D), BF)
    return call(
        qkv_body,
        [info, x_ext, gain, *w_parts, cos, sl, sr],
        grid=(3,),
        in_specs=[smem(), rows(t, D), full((1, D))] + [full((D // 4, 3 * D))] * 4 + [rows(t, PAIR)] * 3,
        out_specs=[pl.BlockSpec((D, t), lambda i: (0, i))] + [rows(t, D)] * 3,
        out_shape=[jax.ShapeDtypeStruct((D, ext), BF)] + [out] * 3,
        scratch_shapes=[pltpu.VMEM((D, 3 * D), BF)],
        megabytes=18,
        deps=deps,
        cost_estimate=cost(9),
        name="qkv",
    )


def apart(u):
    head = lax.broadcasted_iota(jnp.int32, u.shape, 1) // HD
    zero = jnp.zeros_like(u)
    return jnp.concatenate([jnp.where(head == h, u, zero) for h in range(4)], axis=0)


def together(u):
    r = u.shape[0] // 4
    head = lax.broadcasted_iota(jnp.int32, (r, QUAD), 1) // HD
    out = u[:r]
    for h in range(1, 4):
        out = jnp.where(head == h, u[h * r : (h + 1) * r], out)
    return out


def repeat(u):
    return jnp.concatenate([u] * 4, axis=1)


def attend_body(info_ref, bias_ref, q_ref, k_ref, v_ref, x_ref, wa, wb, wc, wd, gain_ref,
                mixed_ref, middle_ref, n2_ref, w_ref, lse_ref):
    i = pl.program_id(0)
    last = pl.num_programs(0) * (TILE // QB) - 1

    @pl.when(i == 0)
    def _():
        lay(info_ref[2], (wa, wb, wc, wd), w_ref)

    for s in range(TILE // QB):
        b = i * (TILE // QB) + s
        start = pl.multiple_of(b * QB, QB)
        which = jnp.where(b == 0, 0, jnp.where(b == last, 2, 1))
        bias = repeat(bias_ref[which])
        for g in range(D // QUAD):
            cols = slice(g * QUAD, (g + 1) * QUAD)
            win = pl.ds(start, QB + 2 * HALF)
            q4 = apart(q_ref[pl.ds(start + HALF, QB), cols])
            scores = dot_bt(k_ref[win, cols], q4) + bias
            most = jnp.max(scores, axis=0, keepdims=True)
            e = jnp.exp(scores - most)
            total = jnp.sum(e, axis=0, keepdims=True)
            probs = (e * (1.0 / total)).astype(BF)
            o = together(dot_at(probs, v_ref[win, cols]))
            mixed_ref[s * QB : (s + 1) * QB, cols] = o.astype(BF)
            lse = most + jnp.log(total)
            for h in range(4):
                lse_ref[g, h : h + 1, s * QB : (s + 1) * QB] = lse[:, h * QB : (h + 1) * QB]
    middle = x_ref[...].astype(F32) + dot(mixed_ref[...], w_ref[...])
    middle_ref[...] = middle.astype(BF)
    n, _ = normalize(middle)
    n2_ref[...] = (n * gain_ref[...]).astype(BF)


def attend_call(info, bias, q, k, v, x, w_parts, gain, deps=()):
    n = x.shape[0]
    ext = q.shape[0]
    groups = D // QUAD
    return call(
        attend_body,
        [info, bias, q, k, v, x, *w_parts, gain],
        grid=(n // TILE,),
        in_specs=[smem(), full(bias.shape)] + [full((ext, D))] * 3 + [rows(TILE, D)] + [full((D // 4, D))] * 4 + [full((1, D))],
        out_specs=[rows(TILE, D)] * 3 + [full((D, D)), pl.BlockSpec((groups, 4, TILE), lambda i: (0, 0, i))],
        out_shape=[
            jax.ShapeDtypeStruct((n, D), BF), jax.ShapeDtypeStruct((n, D), BF), jax.ShapeDtypeStruct((n, D), BF),
            jax.ShapeDtypeStruct((D, D), BF), jax.ShapeDtypeStruct((groups, 4, n), F32),
        ],
        megabytes=12,
        deps=deps,
        cost_estimate=cost(11),
        name="attend",
    )


def hidden(n2, cot, wg, wu, wd):
    gate = dot(n2, wg)
    up = dot(n2, wu)
    ga = dot_bt(cot, wd)
    phi = 0.5 + 0.5 * lax.erf(gate * (2.0**-0.5))
    gelu = gate * phi
    act = (gelu * up).astype(BF)
    slope = phi + gate * (jnp.exp(-0.5 * gate * gate) * 0.3989422804014327)
    dgate = (ga * up * slope).astype(BF)
    dup = (ga * gelu).astype(BF)
    out = dot(act, wd)
    gn = dot_bt(dgate, wg) + dot_bt(dup, wu)
    return act, dgate, dup, out, gn


def ffn_a_body(info_ref, n2_ref, cot_ref, ga, gb, gc, gd, ua, ub, uc, ud, oa, ob, oc, od,
               out_ref, gn_ref, keep_ref, send_ref, wg_ref, wu_ref, wd_ref, acc, ad):
    i = pl.program_id(0)

    @pl.when(i == 0)
    def _():
        lay(info_ref[2], (ga, gb, gc, gd), wg_ref)
        lay(info_ref[2], (ua, ub, uc, ud), wu_ref)
        lay(info_ref[2], (oa, ob, oc, od), wd_ref)
        acc[...] = jnp.zeros_like(acc)
        ad[...] = jnp.zeros_like(ad)

    n2 = n2_ref[...]
    cot = cot_ref[...]
    nt = n2.T
    total_out = jnp.zeros((TILE, D), F32)
    total_gn = jnp.zeros((TILE, D), F32)
    for h in range(2):
        g, u = slice(h * WIDE, (h + 1) * WIDE), slice(D + h * WIDE, D + (h + 1) * WIDE)
        act, dgate, dup, out, gn = hidden(n2, cot, wg_ref[:, g], wu_ref[:, g], wd_ref[g, :])
        total_out += out
        total_gn += gn
        acc[:, g] += dot(nt, dgate)
        acc[:, u] += dot(nt, dup)
        ad[g, :] += dot_at(act, cot)
    out_ref[...] = total_out.astype(BF)
    gn_ref[...] = total_gn.astype(BF)

    @pl.when(i == pl.num_programs(0) - 1)
    def _():
        for b in range(4):
            deal(info_ref[2], acc, slice(b * WIDE, (b + 1) * WIDE), keep_ref, send_ref, b * D // 4)
        for b in range(2):
            deal(info_ref[2], ad, slice(b * WIDE, (b + 1) * WIDE), keep_ref, send_ref, (4 + b) * D // 4)


def ffn_a_call(info, n2, cot, gate_parts, up_parts, down_parts, deps=()):
    n = n2.shape[0]
    part = jax.ShapeDtypeStruct((n, D), BF)
    size = 6 * D // 4
    return call(
        ffn_a_body,
        [info, n2, cot, *gate_parts, *up_parts, *down_parts],
        grid=(n // TILE,),
        in_specs=[smem()] + [rows(TILE, D)] * 2 + [full((D // 4, D))] * 8 + [full((FF // 4, D))] * 4,
        out_specs=[rows(TILE, D)] * 2 + [full((2, size, WIDE))] * 2,
        out_shape=[part, part, piece(size), piece(size)],
        scratch_shapes=[pltpu.VMEM((D, D), BF)] * 3 + [pltpu.VMEM((D, 2 * D), F32), pltpu.VMEM((D, D), F32)],
        megabytes=24,
        deps=deps,
        cost_estimate=cost(18),
        name="ffn_a",
    )


def norm_back(grad, n, r, gain):
    e = grad * gain
    return r * (e - jnp.mean(e, axis=-1, keepdims=True) - n * jnp.mean(e * n, axis=-1, keepdims=True))


def ffn_b_body(info_ref, n2_ref, cot_ref, ia, ib, ic, id_, oa, ob, oc, od, pout_ref, pgn_ref, mid_ref, mixed_ref, wo_ref, gain_ref,
               out_ref, gmid_ref, gmix_ref, keep_ref, send_ref, w_ref, wd_ref, acc, ad, ao):
    i = pl.program_id(0)

    @pl.when(i == 0)
    def _():
        lay(info_ref[2], (ia, ib, ic, id_), w_ref)
        lay(info_ref[2], (oa, ob, oc, od), wd_ref, D // 4)
        acc[...] = jnp.zeros_like(acc)
        ao[...] = jnp.zeros_like(ao)
        ad[...] = jnp.zeros_like(ad)

    n2 = n2_ref[...]
    cot = cot_ref[...]
    act, dgate, dup, out, gn = hidden(n2, cot, w_ref[:, :WIDE], w_ref[:, WIDE:], wd_ref[...])
    nt = n2.T
    acc[:, :WIDE] += dot(nt, dgate)
    acc[:, WIDE:] += dot(nt, dup)
    ad[...] += dot_at(act, cot)
    middle = mid_ref[...].astype(F32)
    out_ref[...] = (middle + pout_ref[...].astype(F32) + out).astype(BF)
    n, r = normalize(middle)
    branch = (cot.astype(F32) + norm_back(pgn_ref[...].astype(F32) + gn, n, r, gain_ref[...])).astype(BF)
    gmid_ref[...] = branch
    gmix_ref[...] = dot_bt(branch, wo_ref[...]).astype(BF)
    ao[...] += dot_at(mixed_ref[...], branch)

    @pl.when(i == pl.num_programs(0) - 1)
    def _():
        w = info_ref[2]
        r = D // 4
        for b in range(2):
            cols = slice(b * WIDE, (b + 1) * WIDE)
            deal(w, acc, cols, keep_ref, send_ref, b * r)
            deal(w, ao, cols, keep_ref, send_ref, (2 + b) * r)
            deal(w, ad, cols, keep_ref, send_ref, 4 * r + b * r // 2)


def ffn_b_call(info, n2, cot, in_parts, down_parts, pout, pgn, middle, mixed, wo, gain, deps=()):
    n = n2.shape[0]
    size = 5 * D // 4
    return call(
        ffn_b_body,
        [info, n2, cot, *in_parts, *down_parts, pout, pgn, middle, mixed, wo, gain],
        grid=(n // TILE,),
        in_specs=[smem()] + [rows(TILE, D)] * 2 + [full((D // 4, D))] * 4 + [full((FF // 4, D))] * 4
        + [rows(TILE, D)] * 4 + [full((D, D)), full((1, D))],
        out_specs=[rows(TILE, D)] * 3 + [full((2, size, WIDE))] * 2,
        out_shape=[jax.ShapeDtypeStruct((n, D), BF)] * 3 + [piece(size), piece(size)],
        scratch_shapes=[pltpu.VMEM((D, D), BF), pltpu.VMEM((WIDE, D), BF),
                        pltpu.VMEM((D, D), F32), pltpu.VMEM((WIDE, D), F32), pltpu.VMEM((D, D), F32)],
        megabytes=24,
        deps=deps,
        cost_estimate=cost(14),
        name="ffn_b",
    )


def attend_back_body(info_ref, bias_ref, q_ref, k_ref, v_ref, g_ref, mixed_ref, lse_ref, cos_ref, sl_ref, sr_ref, nt_ref, *rest):
    dq_ref, dk_ref, dv_ref, keep_ref, send_ref, ak, av, aw = rest[-8:]
    ext = ak.shape[0]
    blocks = (ext - 2 * HALF) // QB
    ak[...] = jnp.zeros_like(ak)
    av[...] = jnp.zeros_like(av)
    zero = jnp.zeros((HALF, QUAD), BF)
    dq_ref[:HALF, :] = zero
    dq_ref[ext - HALF :, :] = zero
    prod = mixed_ref[...].astype(F32) * g_ref[...].astype(F32)
    head = lax.broadcasted_iota(jnp.int32, (8, QUAD), 1) // HD
    pick = jnp.where(head == lax.broadcasted_iota(jnp.int32, (8, QUAD), 0), 1.0, 0.0).astype(BF)
    high = prod.astype(BF)
    delta = dot_bt(pick, high) + dot_bt(pick, (prod - high.astype(F32)).astype(BF))

    def of_heads(a, start):
        return jnp.concatenate([a[h : h + 1, start : start + QB] for h in range(4)], axis=1)

    def unturn(u, at):
        cos, sl, sr = cos_ref[at, :], -sl_ref[at, :], -sr_ref[at, :]
        return jnp.concatenate([turn(u[:, c : c + PAIR], cos, sl, sr) for c in (0, PAIR)], axis=1).astype(BF)

    for b in range(blocks):
        start = b * QB
        win = slice(start, start + QB + 2 * HALF)
        here = slice(start + HALF, start + HALF + QB)
        bias = repeat(bias_ref[0 if b == 0 else 2 if b == blocks - 1 else 1])
        q4 = apart(q_ref[here, :])
        g4 = apart(g_ref[start : start + QB, :])
        kw = k_ref[win, :]
        probs = jnp.exp(dot_bt(kw, q4) + bias - of_heads(lse_ref[0], start))
        ds = (probs * (dot_bt(v_ref[win, :], g4) - of_heads(delta, start))).astype(BF)
        ak[win, :] += dot(ds, q4)
        av[win, :] += dot(probs.astype(BF), g4)
        dq_ref[here, :] = unturn(together(dot_at(ds, kw)) * HD**-0.5, here)
    dk_ref[...] = unturn(ak[...], slice(0, ext))
    dv_ref[...] = av[...].astype(BF)
    for part, ref in enumerate((dq_ref, dk_ref, dv_ref)):
        aw[...] = dot(nt_ref[...], ref[...])
        deal(info_ref[2], aw, slice(0, QUAD), keep_ref, send_ref, part * D // 4)


def attend_back_call(p, at, width, info, bias, q, k, v, g, mixed, lse, cos, sl, sr, nt, sofar, pieces, deps=()):
    n = g.shape[0]
    ext = q.shape[0]
    cols = pl.BlockSpec((ext, QUAD), lambda i: (0, p))
    inner = pl.BlockSpec((n, QUAD), lambda i: (0, p))
    own = jax.ShapeDtypeStruct((ext, D), BF)
    out = jax.ShapeDtypeStruct((2, 3 * D // 4, width), BF)
    args = [info, bias, q, k, v, g, mixed, lse, cos, sl, sr, nt]
    extra = list(sofar) + list(pieces)
    aliases = {}
    for i in range(len(sofar)):
        aliases[len(args) + i] = i
    for i in range(len(pieces)):
        aliases[len(args) + len(sofar) + i] = 3 + i
    mine = pl.BlockSpec((2, 3 * D // 4, QUAD), lambda i: (0, 0, at))
    return call(
        attend_back_body,
        args + extra,
        grid=(1,),
        in_specs=[smem(), full(bias.shape), cols, cols, cols, inner, inner, pl.BlockSpec((1, 4, n), lambda i: (p, 0, 0))]
        + [full((ext, PAIR))] * 3 + [full((D, ext))] + [pl.BlockSpec(memory_space=pl.ANY)] * len(extra),
        out_specs=[cols] * 3 + [mine] * 2,
        out_shape=[own, own, own, out, out],
        scratch_shapes=[pltpu.VMEM((ext, QUAD), F32), pltpu.VMEM((ext, QUAD), F32), pltpu.VMEM((D, QUAD), F32)],
        aliases=aliases,
        megabytes=12,
        deps=deps,
        cost_estimate=cost(4),
        name="attend_back",
    )


def last_body(info_ref, x_ref, dq_ref, dk_ref, dv_ref, rim_ref, gmid_ref, wa, wb, wc, wd, gain_ref, gin_ref, w_ref, *both):
    i = pl.program_id(0)
    start = pl.multiple_of(i * TILE, TILE)
    here = pl.ds(start + HALF, TILE)
    ext = x_ref.shape[0]

    @pl.when(i == 0)
    def _():
        lay(info_ref[2], (wa, wb, wc, wd), w_ref)
        for j, ref in enumerate((dk_ref, dv_ref)):
            cols = slice(j * D, (j + 1) * D)
            both[j][...] = ref[...]
            both[j][HALF : 2 * HALF, :] += rim_ref[:HALF, cols]
            both[j][ext - 2 * HALF : ext - HALF, :] += rim_ref[HALF:, cols]

    total = jnp.zeros((TILE, D), F32)
    for j, ref in enumerate((dq_ref, *both)):
        total += dot_bt(ref[here, :], w_ref[:, j * D : (j + 1) * D])
    n, r = normalize(x_ref[here, :].astype(F32))
    gin_ref[...] = (gmid_ref[...].astype(F32) + norm_back(total, n, r, gain_ref[...])).astype(BF)


def last_call(info, x_ext, grads, rim, gmid, w_parts, gain, deps=()):
    n = gmid.shape[0]
    ext = x_ext.shape[0]
    return call(
        last_body,
        [info, x_ext, *grads, rim, gmid, *w_parts, gain],
        grid=(n // TILE,),
        in_specs=[smem()] + [full((ext, D))] * 4 + [full((2 * HALF, 2 * D)), rows(TILE, D)] + [full((D // 4, 3 * D))] * 4 + [full((1, D))],
        out_specs=[rows(TILE, D)],
        out_shape=[jax.ShapeDtypeStruct((n, D), BF)],
        scratch_shapes=[pltpu.VMEM((D, 3 * D), BF)] + [pltpu.VMEM((ext, D), BF)] * 2,
        megabytes=16,
        deps=deps,
        cost_estimate=cost(7),
        name="last",
    )


def adam(weight, grad, first_old, second, decay_rate):
    new_first = BETA_ONE * first_old + (1.0 - BETA_ONE) * grad
    new_second = BETA_TWO * second + (1.0 - BETA_TWO) * grad * grad
    root = jnp.sqrt(new_second * (1.0 / (1.0 - BETA_TWO**STEP))) + ADAM_EPS
    change = (-LEARN_RATE / (1.0 - BETA_ONE**STEP)) * (new_first / root)
    if decay_rate:
        change = change - (LEARN_RATE * decay_rate) * weight
    return (new_first, new_second, change)


def adam_body(*refs):
    g_in, w_ref, m_ref, v_ref = refs[:4]
    g_ref, nm_ref, nv_ref, st_ref, dots_ref = refs[-5:]
    g = g_in[...].astype(F32)
    w = w_ref[...].astype(F32)
    g_ref[...] = g
    nm_ref[...], nv_ref[...], st_ref[...] = adam(w, g, m_ref[...], v_ref[...], WEIGHT_DECAY)

    @pl.when(pl.program_id(0) == 0)
    def _():
        dots_ref[...] = jnp.zeros_like(dots_ref)

    dots_ref[...] += jnp.sum(w * g, axis=1, keepdims=True)


def adam_call(grad, at, weight, first, second, wide, steps, cols, before=()):
    r, width = weight.shape
    own = pl.BlockSpec((r, wide), lambda j: (0, cols(j)))
    out = jax.ShapeDtypeStruct((r, width), F32)
    return pl.pallas_call(
        adam_body,
        grid=(steps,),
        in_specs=[pl.BlockSpec((r, wide), at)] + [own] * 3 + [pl.BlockSpec(memory_space=pl.ANY)] * len(before),
        out_specs=[own] * 4 + [full((r, 1))],
        out_shape=[out] * 4 + [jax.ShapeDtypeStruct((r, 1), F32)],
        input_output_aliases={4 + i: i for i in range(len(before))},
        compiler_params=pltpu.CompilerParams(dimension_semantics=("arbitrary",), vmem_limit_bytes=12 * 1024 * 1024),
        cost_estimate=cost(3),
        name="adam",
    )(grad, weight, first, second, *before)


def whole_adam(grad, weight, first, second):
    return adam_call(grad, lambda j: (0, j), weight, first, second, WIDE, weight.shape[1] // WIDE, lambda j: j)


CORES = [(0, 1), (1, 0), (2, 3), (3, 2)]
CHIPS = [(0, 2), (2, 0), (1, 3), (3, 1)]


def to_core(a):
    return lax.ppermute(a, "wshard", CORES)


def to_chip(a):
    return lax.ppermute(a, "wshard", CHIPS)


def after(a, first):
    return together_at([a, first])[0]


class Chain:
    def __init__(self, keep, send, halvings, seq_first=False):
        count = lax.axis_size("seq")
        self.kept = keep
        self.out = send
        plan = []
        shift = 0
        while 1 << shift < count:
            plan.append(("half" if shift < halvings else "whole", shift))
            shift += 1
        back = [("back", t) for kind, t in reversed(plan) if kind == "half"]
        plan.insert(1 if seq_first else 0, ("chip", 0))
        self.plan = [("core", 0)] + plan + back
        self.at = 0

    def done(self):
        return self.at == len(self.plan)

    def start(self):
        if self.done():
            return
        kind, shift = self.plan[self.at]
        sent = self.kept if self.out is None else self.out
        if kind == "core":
            self.flight = lax.ppermute(sent, "wshard", CORES)
        elif kind == "chip":
            self.flight = lax.ppermute(sent, "wshard", CHIPS)
        else:
            count = lax.axis_size("seq")
            self.flight = lax.ppermute(sent, "seq", [(i, i ^ (1 << shift)) for i in range(count)])

    def landing(self):
        kind, shift = self.plan[self.at]
        later = self.plan[self.at + 1] if self.at + 1 < len(self.plan) else ("end", 0)
        shape = self.kept.shape
        if kind == "back":
            shape = (2 * shape[0],) + shape[1:]
        if later[0] == "chip":
            shapes = [shape[1:]] * 2
        elif later[0] == "half":
            shapes = [shape[:-2] + (shape[-2] // 2, shape[-1])] * 2
        else:
            shapes = [shape]

        def bit(info_ref, kind, shift):
            return (info_ref[2] >> 1) & 1 if kind == "chip" else (info_ref[3] >> shift) & 1

        def body(info_ref, kept_ref, got_ref, outs):
            if kind == "back":
                r = kept_ref.shape[0]
                b = bit(info_ref, kind, shift)
                outs[0][pl.ds(pl.multiple_of(b * r, 16), r), :] = kept_ref[...]
                outs[0][pl.ds(pl.multiple_of((1 - b) * r, 16), r), :] = got_ref[...]
            elif later[0] == "chip":
                b = bit(info_ref, *later)
                outs[0][...] = sum_of(kept_ref[b], got_ref[b])
                outs[1][...] = sum_of(kept_ref[1 - b], got_ref[1 - b])
            elif later[0] == "half":
                b = bit(info_ref, *later)
                r = kept_ref.shape[-2] // 2
                for out, i in ((outs[0], b), (outs[1], 1 - b)):
                    here = pl.ds(pl.multiple_of(i * r, 16), r)
                    if len(shape) == 3:
                        out[...] = sum_of(kept_ref[:, here, :], got_ref[:, here, :])
                    else:
                        out[...] = sum_of(kept_ref[here, :], got_ref[here, :])
            else:
                outs[0][...] = sum_of(kept_ref[...], got_ref[...])

        return shapes, body

    def landed(self, outs):
        self.at += 1
        self.kept = outs[0]
        self.out = outs[1] if len(outs) > 1 else None


def sum_of(a, b):
    return (a.astype(F32) + b.astype(F32)).astype(BF)


def nothing(*refs):
    pass


def together_at(arrays):
    hbm = pl.BlockSpec(memory_space=pl.ANY)
    return pl.pallas_call(
        nothing,
        in_specs=[hbm] * len(arrays),
        out_specs=[hbm] * len(arrays),
        out_shape=[jax.ShapeDtypeStruct(a.shape, a.dtype) for a in arrays],
        input_output_aliases={i: i for i in range(len(arrays))},
        compiler_params=pltpu.CompilerParams(vmem_limit_bytes=1024 * 1024),
        name="boundary",
    )(*arrays)


def boundary(info, token, landing=(), starting=(), also=()):
    landing = [c for c in landing if not c.done()]
    plans = [c.landing() for c in landing]
    args = [info] + [a for c in landing for a in (c.kept, c.flight)]
    through = [c.out for c in starting] + list(also) + [token]
    shapes = [jax.ShapeDtypeStruct(t, BF) for p in plans for t in p[0]]
    count = len(args)

    def body(*refs):
        outs = list(refs[count + len(through) :])
        for i, (shapes_i, land) in enumerate(plans):
            land(refs[0], refs[1 + 2 * i], refs[2 + 2 * i], [outs.pop(0) for _ in shapes_i])

    hbm = pl.BlockSpec(memory_space=pl.ANY)
    outs = pl.pallas_call(
        body,
        grid=(1,),
        in_specs=[smem()] + [full(a.shape) for a in args[1:]] + [hbm] * len(through),
        out_specs=[full(t.shape) for t in shapes] + [hbm] * len(through),
        out_shape=shapes + [jax.ShapeDtypeStruct(a.shape, a.dtype) for a in through],
        input_output_aliases={count + i: len(shapes) + i for i in range(len(through))},
        compiler_params=pltpu.CompilerParams(vmem_limit_bytes=16 * 1024 * 1024),
        cost_estimate=cost(1),
        name="land",
    )(*args, *through)
    outs = list(outs)
    for c, (shapes_i, _) in zip(landing, plans):
        c.landed([outs.pop(0) for _ in shapes_i])
    for c in starting:
        c.out = outs.pop(0)
    waits = [outs[-1]]
    for c in landing + list(starting):
        waits.append(c.kept if c.out is None else c.out)
        c.start()
    return outs[:-1], tuple(waits)


def neighbours(count):
    up = [(i, i + 1) for i in range(count - 1)]
    return up, [(j, i) for i, j in up]


def shards(
    hidden_in, cotangent, block_seq, block_place, attn_in, attn_out, ffn_in, ffn_out, norm_attn, norm_ffn,
    m_attn_in, m_attn_out, m_ffn_in, m_ffn_out, m_norm_attn, m_norm_ffn,
    v_attn_in, v_attn_out, v_ffn_in, v_ffn_out, v_norm_attn, v_norm_ffn,
):
    x = hidden_in[0]
    cot = cotangent[0]
    n = x.shape[0]
    ext = n + 2 * HALF
    w = lax.axis_index("wshard")
    count = lax.axis_size("seq")
    at = lax.axis_index("seq")
    up, down = neighbours(count)

    far = to_chip(attn_in)
    mate = to_core(attn_in)
    mate, gain_own, x_low, x_high = together_at([mate, jnp.stack([norm_attn, norm_ffn]), x[:HALF], x[n - HALF :]])
    gain_far = to_chip(gain_own)
    gains = gain_own, to_core(gain_own), gain_far, to_core(gain_far)
    x_ext = jnp.concatenate([lax.ppermute(x_high, "seq", up), x, lax.ppermute(x_low, "seq", down)], axis=0)
    some, rest = D // 4, FF // 4 - D // 4

    def units(start, first, size):
        return [ffn_in[:, start + s * (FF // 4) + first :][:, :size] for s in range(4)]

    in_g = jnp.concatenate(units(0, 0, some), axis=1)
    in_u = jnp.concatenate(units(FF, 0, some), axis=1)
    in_b = jnp.concatenate(units(0, some, rest) + units(FF, some, rest), axis=1)
    out_mate, g_mate, u_mate, down_mate, b_mate = (to_core(a) for a in (attn_out, in_g, in_u, ffn_out, in_b))

    ids = block_seq[0]

    def pick(a, i):
        return lax.dynamic_index_in_dim(a, i, keepdims=False)

    own = pick(ids, at)
    left = (at > 0) & (pick(ids, jnp.maximum(at - 1, 0)) == own)
    right = (at < count - 1) & (pick(ids, jnp.minimum(at + 1, count - 1)) == own)
    info = jnp.stack([t.astype(jnp.int32) for t in (left, right, w, at)])
    key = jnp.arange(QB + 2 * HALF)[:, None]
    off = key - jnp.arange(QB)[None, :]
    band = (off >= 0) & (off <= 2 * HALF)
    bias = jnp.where(jnp.stack([band & (left | (key >= HALF)), band, band & (right | (key < QB + HALF))]), 0.0, NEG_FILL)
    pos = pick(block_place[0], at) * n - HALF + jnp.arange(ext, dtype=jnp.int32)
    lane = jnp.arange(PAIR)
    freq = THETA ** (-2.0 * (lane % (HD // 2)).astype(F32) / HD)
    angle = pos.astype(F32)[:, None] * freq[None, :]
    cos = jnp.cos(angle)
    sin = jnp.sin(angle)
    low = (lane % HD < HD // 2)[None, :]
    sl = jnp.where(low, -sin, 0.0)
    sr = jnp.where(low, 0.0, sin)
    by_owner = jnp.stack(gains)
    order = jnp.arange(4) ^ w
    gain = jnp.take(by_owner, order, axis=0).transpose(1, 0, 2).reshape(2, D).astype(F32)
    g1, g2 = gain[0:1], gain[1:2]

    far, in_g, x_ext, g1, g2, cos, sl, sr, bias, info, token, mate, out_mate, g_mate, u_mate, down_mate, b_mate = together_at(
        [far, in_g, x_ext, g1, g2, cos, sl, sr, bias, info, jnp.zeros((8, 128), F32),
         mate, out_mate, g_mate, u_mate, down_mate, b_mate]
    )
    farmate = to_core(far)
    out_far = to_chip(after(attn_out, token))
    g_far = to_chip(in_g)
    attn_parts = attn_in, mate, far, farmate
    nt, q, k, v, token = qkv_call(info, x_ext, g1, attn_parts, cos, sl, sr)
    out_far, g_far, in_u, token = together_at([out_far, g_far, in_u, token])
    out_farmate = to_core(out_far)
    out_farmate, in_u, down_own, token = together_at([out_farmate, in_u, ffn_out, token])
    u_far = to_chip(in_u)
    down_far = to_chip(down_own)
    out_parts = attn_out, out_mate, out_far, out_farmate
    mixed, middle, n2, out_w, lse, token = attend_call(info, bias, q, k, v, x, out_parts, g2, deps=(token,))
    u_far, down_far, in_b, token = together_at([u_far, down_far, in_b, token])
    g_farmate = to_core(g_far)
    b_far = to_chip(in_b)
    gate_parts = in_g, g_mate, g_far, g_farmate
    up_parts = in_u, u_mate, u_far, to_core(u_far)
    down_parts = ffn_out, down_mate, down_far, to_core(down_far)
    pout, pgn, keep, send, token = ffn_a_call(info, n2, cot, gate_parts, up_parts, down_parts, deps=(token,))
    chain_a = Chain(keep, send, 2)
    (b_far,), deps = boundary(info, token, (), (chain_a,), (b_far,))
    b_parts = in_b, b_mate, b_far, to_core(b_far)
    _, deps = boundary(info, deps[0], (chain_a,))
    block_out, gmid, gmix, keep, send, token = ffn_b_call(
        info, n2, cot, b_parts, down_parts, pout, pgn, middle, mixed, out_w, g2, deps=deps
    )
    chain_b = Chain(keep, send, 1)
    grads, pieces = (), ()

    def back(p, at, width, deps):
        nonlocal grads, pieces
        if at == 0:
            pieces = ()
        out = attend_back_call(p, at, width, info, bias, q, k, v, gmix, mixed, lse, cos, sl, sr, nt, grads, pieces, deps)
        grads, pieces = out[:3], out[3:5]
        return out[5]

    _, deps = boundary(info, token, (chain_a,), (chain_b,))
    token = back(0, 0, 2 * QUAD, deps)
    _, deps = boundary(info, token, (chain_a, chain_b))
    token = back(1, 1, 2 * QUAD, deps)
    chain_c = Chain(*pieces, 1)
    _, deps = boundary(info, token, (chain_a,), (chain_c,))
    token = back(2, 0, QUAD, deps)
    chain_d = Chain(*pieces, 1, True)
    rims = [jnp.concatenate([a[r] for a in grads[1:]], axis=1) for r in (slice(0, HALF), slice(n + HALF, ext))]
    rims, deps = boundary(info, token, (chain_a, chain_b, chain_c), (chain_d,), rims)
    rim = jnp.concatenate([lax.ppermute(rims[1], "seq", up), lax.ppermute(rims[0], "seq", down)], axis=0)
    (rim,), deps = boundary(info, deps[0], (chain_d,), (), (rim,))
    grad_in, token = last_call(info, x_ext, grads, rim, gmid, attn_parts, g1, deps=deps)
    chains = (chain_a, chain_b, chain_c, chain_d)
    while not all(c.done() for c in chains):
        _, deps = boundary(info, token, chains)
        token = deps[0]
    sum_a, sum_b, sum_c, sum_d = (c.kept for c in chains)

    r = D // 4

    def blocks(a, *at):
        return jnp.concatenate([a[i * r : (i + 1) * r] for i in at], axis=1)

    ga, gb = blocks(sum_a, 0, 1), sum_b[:r]
    ua, ub = blocks(sum_a, 2, 3), sum_b[r : 2 * r]
    g_ffn_in = jnp.concatenate(
        [t for a, b in ((ga, gb), (ua, ub)) for s in range(4)
         for t in (a[:, s * some : (s + 1) * some], b[:, s * rest : (s + 1) * rest])], axis=1
    )
    g_ffn_out = jnp.concatenate(
        [blocks(sum_a, 4, 5), jnp.concatenate([sum_b[4 * r : 4 * r + rest], sum_b[4 * r + rest :]], axis=1)], axis=0
    )
    res_ffn_in = whole_adam(g_ffn_in, ffn_in, m_ffn_in, v_ffn_in)
    res_attn_out = whole_adam(blocks(sum_b, 2, 3), attn_out, m_attn_out, v_attn_out)
    res_ffn_out = whole_adam(g_ffn_out, ffn_out, m_ffn_out, v_ffn_out)
    own_attn = attn_in, m_attn_in, v_attn_in, QUAD
    most = adam_call(sum_c, lambda j: (j // 2, j % 2), *own_attn, 6, lambda j: 3 * (j // 2) + j % 2)
    res_attn_in = adam_call(sum_d, lambda j: (j, 0), *own_attn, 3, lambda j: 3 * j + 2, most[:4])
    res_attn_in = list(res_attn_in[:4]) + [res_attn_in[4] + most[4]]
    results = [res_attn_in, res_attn_out, res_ffn_in, res_ffn_out]
    for res, own_gain, m, v_ in ((res_attn_in, norm_attn, m_norm_attn, v_norm_attn), (res_ffn_in, norm_ffn, m_norm_ffn, v_norm_ffn)):
        wide = own_gain.astype(F32)
        g = res[4][:, 0] / wide
        results.append((g,) + adam(wide, g, m, v_, 0.0))
    return (block_out[None], grad_in[None]) + tuple(res[i] for i in range(4) for res in results)


def solution(mesh):
    big = P("wshard", "seq", None)
    mat = P("wshard", None)
    vec = P("wshard")
    group = (mat, mat, mat, mat, vec, vec)
    in_specs = (big, big, mat, mat) + group * 3
    out_specs = (big, big) + group * 4
    return jax.shard_map(shards, mesh=mesh, in_specs=in_specs, out_specs=out_specs, check_vma=False)
```

time: 454 us -> 282 us (0.62)
  waiting for transfers between devices: 233 us -> 90.9 us
  starting transfers between devices: 12.4 us -> 52.2 us
  blocking collectives: 35.1 us -> 0 us
  Pallas kernels: 120 us -> 104 us
  between operations: 19 us -> 4.93 us
  other arithmetic: 21.1 us -> 11.1 us
    psum x1 -> x0, waiting for transfers between devices: 87.6 us -> none  [shards(): shard_grads.append(lax.psum(s, 'seq').astype(F32))]
    ppermute x4 -> x50, waiting for transfers between devices: 7.27 us -> 90.9 us  [the longest x17 48.4 us: start(): lax.ppermute(sent, 'seq', [(i, i ^ 1 << shift) for i in range(count)])]
    reduce_scatter x4 -> x0, waiting for transfers between devices: 77.4 us -> none  [shards(): lax.psum_scatter(g.astype(BF), 'wshard', scatter_dimension=0, tiled=True)]
    all_gather x4 -> x0, waiting for transfers between devices: 57.7 us -> none  [shards(): lax.all_gather(w, 'wshard', axis=0, tiled=True)]
    ppermute x4 -> x50, starting transfers between devices: 12 us -> 52.2 us  [the longest x17 25.7 us: start(): lax.ppermute(sent, 'seq', [(i, i ^ 1 << shift) for i in range(count)])]
    psum x1 -> x0, blocking collectives: 22.6 us -> none  [shards(): shard_grads.append(lax.psum(s, 'seq').astype(F32))]
    pallas_call x8 -> x31, Pallas kernels: 120 us -> 104 us  [the longest x8 78 us: call(): pl.pallas_call(wrapped, in_specs=list(in_specs) + [pl.BlockSpec(memory_sp...]
    unnamed x2 -> x0, blocking collectives: 12.6 us -> none
  transfers between devices with their start and end apart: 13 -> 50, of which waited for: 9 -> 18; matrix products, arithmetic and copies ran while one was open for 4% -> 7% of each run, Pallas kernels for 15% -> 32%
where the time goes in v2:
time: 282 us; the launch traced here: 278 us
  Pallas kernels  104 us (37%)
  waiting for transfers between devices  90.9 us (32%)
  starting transfers between devices  52.2 us (19%)
  local copies, waits for them, and re-layouts  15.4 us (5%)
  other arithmetic  11.1 us (4%)
  between operations  4.93 us (2%)
    pallas_call x8, Pallas kernels, call(): pl.pallas_call(wrapped, in_specs=list(in_specs) + [pl.BlockSpec(memory_sp...  78 us
    ppermute x17, waiting for transfers between devices, start(): lax.ppermute(sent, 'seq', [(i, i ^ 1 << shift) for i in range(count)])  48.4 us
    ppermute x17, starting transfers between devices, start(): lax.ppermute(sent, 'seq', [(i, i ^ 1 << shift) for i in range(count)])  25.7 us
    ppermute x7, waiting for transfers between devices, to_chip(): return lax.ppermute(a, 'wshard', CHIPS)  16.3 us
    pallas_call x5, Pallas kernels, adam_call(): pl.pallas_call(adam_body, grid=(steps,), in_specs=[pl.BlockSpec((r, wide)...  15.8 us
    ppermute x4, waiting for transfers between devices, start(): self.flight = lax.ppermute(sent, 'wshard', CHIPS)  12.8 us
    pallas_call x12, Pallas kernels, boundary(): pl.pallas_call(body, grid=(1,), in_specs=[smem()] + [full(a.shape) for a...  9.84 us
    ppermute x7, starting transfers between devices, to_chip(): return lax.ppermute(a, 'wshard', CHIPS)  8.32 us
  transfers between devices with their start and end apart: 50, of which 18 were waited for; matrix products, arithmetic and copies ran while one was open for 7% of the time, Pallas kernels for 32%

profile of v2, /device:TPU:0, one launch (start us, length us, event | category | flops | bytes accessed | tf_op | source)
XLA Modules:
  0.0 278.1 jit_solution(16522997396897420790)
XLA Ops:
  1.2 2.6 collective-permute-start
  5.4 1.4 constant_dynamic-slice_fusion.2
  12.6 1.6 fusion.24
  15.2 2.0 fusion.23
  17.2 2.2 fusion
  20.1 4.2 %collective-permute-done.5 = bf16[2,192]{1,0:T(2,128)(2,1)S(1)} collective-permute-done((bf16[2,192]{1,0:T(2,128)(2,1)S(1)}, bf16[2,192]{1,0:T(2,128)(2,1)S(1)}, u32[]{:S(2)}, u32[]{:S(2)}) %collective-permute-start.5) | collective-permute-done | bytes 800 | tf_op jit(solution)/shard_map/ppermute | solution.py:527
  24.4 1.9 concatenate.39.refs_2_
  26.3 4.3 %collective-permute-start.2 = (bf16[64,768]{1,0:T(8,128)(2,1)S(1)}, bf16[64,768]{1,0:T(8,128)(2,1)}, u32[]{:S(2)}, u32[]{:S(2)}) collective-permute-start(bf16[64,768]{1,0:T(8,128)(2,1)S(1)} %get-tuple-element.178), channel_id=1, source_target_pairs={{0,4},{4,8},{8,12},{12,16},{16,20},{20,24},{24,28},{1,5},{5,9},{9,... | collective-permute-start | bytes 294920 | tf_op jit(solution)/shard_map/ppermute | solution.py:693
  30.6 1.5 collective-permute-start.3
  34.8 2.7 collective-permute-done.3
  37.5 1.6 pad_maximum_fusion.refs_2_
  40.2 1.6 collective-permute-start.13
  42.3 7.4 %qkv.1 = (bf16[768,1152]{1,0:T(8,128)(2,1)S(1)}, bf16[1152,768]{1,0:T(8,128)(2,1)S(1)}, bf16[1152,768]{1,0:T(8,128)(2,1)S(1)}, bf16[1152,768]{1,0:T(8,128)(2,1)S(1)}, f32[8,128]{1,0:T(8,128)S(1)}) custom-call(s32[4]{0:T(128)S(1)} %get-tuple-element.182.refs_0_, bf16[1152,768]{1,0:T(8,128)(2,1)S(1)} %get-tuple-element.184.refs_1_, ...), custom_call_target="tpu_custom_call" | custom-call | flops 9900000256 | tf_op jit(solution)/shard_map/qkv/pallas_call | solution.py:56
  50.1 5.9 %collective-permute-done.14.refs_1_ = bf16[192,768]{1,0:T(8,128)(2,1)S(1)} collective-permute-done((bf16[192,768]{1,0:T(8,128)(2,1)S(1)}, bf16[192,768]{1,0:T(8,128)(2,1)S(1)}, u32[]{:S(2)}, u32[]{:S(2)}) %collective-permute-start.14) | collective-permute-done | bytes 294944 | tf_op jit(solution)/shard_map/ppermute | solution.py:527
  56.1 1.5 collective-permute-done.15.refs_0_
  57.6 1.5 collective-permute-start.16
  59.6 10.6 %attend.1 = (bf16[1024,768]{1,0:T(8,128)(2,1)S(1)}, bf16[1024,768]{1,0:T(8,128)(2,1)S(1)}, bf16[1024,768]{1,0:T(8,128)(2,1)S(1)}, bf16[768,768]{1,0:T(8,128)(2,1...) custom-call(s32[4]{0:T(128)S(1)} %get-tuple-element.182.refs_0_, f32[3,256,128]{2,1,0:T(8,128)S(1)} %get-tuple-element.183.refs_1_, ...), custom_call_target="tpu_custom_call" | custom-call | flops 12099999744 | tf_op jit(solution)/shard_map/attend/pallas_call | solution.py:56
  70.3 5.9 %collective-permute-done.17.refs_1_ = bf16[288,768]{1,0:T(8,128)(2,1)S(1)} collective-permute-done((bf16[288,768]{1,0:T(8,128)(2,1)S(1)}, bf16[288,768]{1,0:T(8,128)(2,1)S(1)}, u32[]{:S(2)}, u32[]{:S(2)}) %collective-permute-start.17) | collective-permute-done | bytes 442400 | tf_op jit(solution)/shard_map/ppermute | solution.py:527
  76.7 1.5 collective-permute-start.21
  78.8 17.5 %ffn_a.1 = (bf16[1024,768]{1,0:T(8,128)(2,1)S(1)}, bf16[1024,768]{1,0:T(8,128)(2,1)S(1)}, bf16[2,1152,384]{2,1,0:T(8,128)(2,1)S(1)}, bf16[2,1152,384]{2,1,0:T(8,128)(2,1)S(1)}, f32[8,128]{1,0:T(8,128)S(1)}) custom-call(s32[4]{0:T(128)S(1)} %get-tuple-element.182.refs_0_, bf16[1024,768]{1,0:T(8,128)(2,1)S(1)} %get-tuple-element.205.refs_1_, ...), custom_call_target="tpu_custom_call" | custom-call | flops 19800000512 | tf_op jit(solution)/shard_map/ffn_a/pallas_call | solution.py:56
  97.5 3.2 %collective-permute-done.23.refs_2_ = bf16[2,1152,384]{2,1,0:T(8,128)(2,1)S(1)} collective-permute-done((bf16[2,1152,384]{2,1,0:T(8,128)(2,1)S(1)}, bf16[2,1152,384]{2,1,0:T(8,128)(2,1)S(1)}, u32[]{:S(2)}, u32[]{:S(2)}) %collective-permute-start.23) | collective-permute-done | bytes 1769504 | tf_op jit(solution)/shard_map/ppermute | solution.py:558
  100.7 1.0 land.13
  101.6 1.6 collective-permute-start.24
  103.2 14.3 %ffn_b.1 = (bf16[1024,768]{1,0:T(8,128)(2,1)}, bf16[1024,768]{1,0:T(8,128)(2,1)S(1)}, bf16[1024,768]{1,0:T(8,128)(2,1)S(1)}, bf16[2,960,384]{2,1,0:T(8,128)(2,1)...) custom-call(s32[4]{0:T(128)S(1)} %get-tuple-element.182.refs_0_, bf16[1024,768]{1,0:T(8,128)(2,1)S(1)} %copy-done.18, ...), custom_call_target="tpu_custom_call" | custom-call | flops 15399999488 | tf_op jit(solution)/shard_map/ffn_b/pallas_call | solution.py:56
  117.5 5.9 %collective-permute-done.24.refs_2_ = bf16[1152,384]{1,0:T(8,128)(2,1)S(1)} collective-permute-done((bf16[1152,384]{1,0:T(8,128)(2,1)S(1)}, bf16[1152,384]{1,0:T(8,128)(2,1)S(1)}, u32[]{:S(2)}, u32[]{:S(2)}) %collective-permute-start.24) | collective-permute-done | bytes 884768 | tf_op jit(solution)/shard_map/ppermute | solution.py:560
  124.2 1.9 collective-permute-start.25
  126.1 6.5 %attend_back.3 = (bf16[1152,768]{1,0:T(8,128)(2,1)S(1)}, bf16[1152,768]{1,0:T(8,128)(2,1)S(1)}, bf16[1152,768]{1,0:T(8,128)(2,1)S(1)}, bf16[2,576,512]{2,1,0:T(8...) custom-call(s32[4]{0:T(128)S(1)} %get-tuple-element.182.refs_0_, ...), custom_call_target="tpu_custom_call" | custom-call | flops 4400000000 | tf_op jit(solution)/shard_map/attend_back/pallas_call | solution.py:56
  132.6 4.3 %collective-permute-done.25.refs_2_ = bf16[576,384]{1,0:T(8,128)(2,1)S(1)} collective-permute-done((bf16[576,384]{1,0:T(8,128)(2,1)S(1)}, bf16[576,384]{1,0:T(8,128)(2,1)S(1)}, u32[]{:S(2)}, u32[]{:S(2)}) %collective-permute-start.25) | collective-permute-done | bytes 442400 | tf_op jit(solution)/shard_map/ppermute | solution.py:563
  136.9 1.0 land.15
  137.9 1.6 collective-permute-start.27
  139.5 1.5 collective-permute-start.29
  141.0 6.9 %attend_back.4 = (bf16[1152,768]{1,0:T(8,128)(2,1)S(1)}, bf16[1152,768]{1,0:T(8,128)(2,1)S(1)}, bf16[1152,768]{1,0:T(8,128)(2,1)S(1)}, bf16[2,576,512]{2,1,0:T(8...) custom-call(s32[4]{0:T(128)S(1)} %get-tuple-element.182.refs_0_, ...), custom_call_target="tpu_custom_call", output_to_operand_aliasing={{0}: (12, {}), {1}: (13, {}), {2}: (14, {}), {3}: (15, {}),... | custom-call | flops 4400000000 | tf_op jit(solution)/shard_map/attend_back/pallas_call | solution.py:56
  148.5 2.0 collective-permute-start.28
  150.5 6.5 %attend_back.5 = (bf16[1152,768]{1,0:T(8,128)(2,1)S(1)}, bf16[1152,768]{1,0:T(8,128)(2,1)S(1)}, bf16[1152,768]{1,0:T(8,128)(2,1)S(1)}, bf16[2,576,256]{2,1,0:T(8...) custom-call(s32[4]{0:T(128)S(1)} %get-tuple-element.182.refs_0_, ...), custom_call_target="tpu_custom_call", output_to_operand_aliasing={{0}: (12, {}), {1}: (13, {}), {2}: (14, {})} | custom-call | flops 4400000000 | tf_op jit(solution)/shard_map/attend_back/pallas_call | solution.py:56
  157.1 3.6 %collective-permute-done.28.refs_2_ = bf16[288,384]{1,0:T(8,128)(2,1)S(1)} collective-permute-done((bf16[288,384]{1,0:T(8,128)(2,1)S(1)}, bf16[288,384]{1,0:T(8,128)(2,1)S(1)}, u32[]{:S(2)}, u32[]{:S(2)}) %collective-permute-start.28) | collective-permute-done | bytes 221216 | tf_op jit(solution)/shard_map/ppermute | solution.py:563
  160.7 1.0 land.17
  161.8 3.5 %collective-permute-start.32 = (bf16[64,1536]{1,0:T(8,128)(2,1)S(1)}, bf16[64,1536]{1,0:T(8,128)(2,1)S(1)}, u32[]{:S(2)}, u32[]{:S(2)}) collective-permute-start(bf16[64,1536]{1,0:T(8,128)(2,1)S(1)} %get-tuple-element.270), channel_id=1, source_target_pairs={{0,4},{4,8},{8,12},{12,16},{16,20},{20,24},{24,28},{1,5},{5,9},{9,... | collective-permute-start | bytes 589832 | tf_op jit(solution)/shard_map/ppermute | solution.py:782
  165.4 1.3 collective-permute-start.33
  166.7 2.1 collective-permute-start.34
  169.5 5.3 %collective-permute-done.32 = bf16[64,1536]{1,0:T(8,128)(2,1)S(1)} collective-permute-done((bf16[64,1536]{1,0:T(8,128)(2,1)S(1)}, bf16[64,1536]{1,0:T(8,128)(2,1)S(1)}, u32[]{:S(2)}, u32[]{:S(2)}) %collective-permute-start.32) | collective-permute-done | bytes 196640 | tf_op jit(solution)/shard_map/ppermute | solution.py:782
  176.0 2.5 collective-permute-start.37
  178.6 8.3 %last.1 = (bf16[1024,768]{1,0:T(8,128)(2,1)}, f32[8,128]{1,0:T(8,128)S(1)}) custom-call(s32[4]{0:T(128)S(1)} %get-tuple-element.182.refs_0_, bf16[1152,768]{1,0:T(8,128)(2,1)S(1)} %get-tuple-element.184.refs_1_, bf16[1152,768]{1,0:T(8,128)(2,1)S(1)} %get-tuple-element.261.refs_2_, bf16[1152,768]{1,0:T(8,128)(2,1)S(1)} %get-tuple-element.262.refs_3_, ...), custom_call_target="tpu_custom_call" | custom-call | flops 7699999744 | tf_op jit(solution)/shard_map/last/pallas_call | solution.py:56
  186.9 2.3 collective-permute-done.36.refs_6_
  190.0 2.7 collective-permute-start.38
  192.7 1.0 collective-permute-start.40
  194.3 4.6 %collective-permute-done.41.refs_8_ = bf16[288,256]{1,0:T(8,128)(2,1)S(1)} collective-permute-done((bf16[288,256]{1,0:T(8,128)(2,1)S(1)}, bf16[288,256]{1,0:T(8,128)(2,1)S(1)}, u32[]{:S(2)}, u32[]{:S(2)}) %collective-permute-start.41) | collective-permute-done | bytes 147488 | tf_op jit(solution)/shard_map/ppermute | solution.py:560
  198.9 9.5 %collective-permute-done.40.refs_6_ = bf16[288,512]{1,0:T(8,128)(2,1)S(1)} collective-permute-done((bf16[288,512]{1,0:T(8,128)(2,1)S(1)}, bf16[288,512]{1,0:T(8,128)(2,1)S(1)}, u32[]{:S(2)}, u32[]{:S(2)}) %collective-permute-start.40) | collective-permute-done | bytes 294944 | tf_op jit(solution)/shard_map/ppermute | solution.py:563
  209.2 1.7 collective-permute-start.42
  210.9 2.9 %collective-permute-start.43 = (bf16[288,512]{1,0:T(8,128)(2,1)S(1)}, bf16[288,512]{1,0:T(8,128)(2,1)S(1)}, u32[]{:S(2)}, u32[]{:S(2)}) collective-permute-start(bf16[288,512]{1,0:T(8,128)(2,1)S(1)} %get-tuple-element.293.refs_3_), channel_id=1, source_target_pairs={{0,8},{4,12},{8,0},{12,4},{16,24},{20,28},{24,16},{28,20},{1,9},{5... | collective-permute-start | bytes 884744 | tf_op jit(solution)/shard_map/ppermute | solution.py:563
  213.8 15.0 %collective-permute-done.44.refs_6_ = bf16[288,256]{1,0:T(8,128)(2,1)S(1)} collective-permute-done((bf16[288,256]{1,0:T(8,128)(2,1)S(1)}, bf16[288,256]{1,0:T(8,128)(2,1)S(1)}, u32[]{:S(2)}, u32[]{:S(2)}) %collective-permute-start.44) | collective-permute-done | bytes 147488 | tf_op jit(solution)/shard_map/ppermute | solution.py:563
  229.6 2.5 collective-permute-start.46
  232.9 1.4 collective-permute-start.47
  234.3 16.0 %collective-permute-done.47.refs_6_ = bf16[288,256]{1,0:T(8,128)(2,1)S(1)} collective-permute-done((bf16[288,256]{1,0:T(8,128)(2,1)S(1)}, bf16[288,256]{1,0:T(8,128)(2,1)S(1)}, u32[]{:S(2)}, u32[]{:S(2)}) %collective-permute-start.47) | collective-permute-done | bytes 147488 | tf_op jit(solution)/shard_map/ppermute | solution.py:563
  252.0 1.0 collective-permute-start.49
  253.0 1.0 collective-permute-start.48
  254.1 2.1 adam.7
  256.2 2.7 adam.9
  258.9 1.4 concatenate.44.refs_0_
  260.4 1.5 copy-done.6
  261.9 1.5 copy-done.7
  263.3 4.8 %adam.8 = (f32[192,2304]{1,0:T(8,128)}, f32[192,2304]{1,0:T(8,128)}, f32[192,2304]{1,0:T(8,128)}, f32[192,2304]{1,0:T(8,128)}, f32[192,1]{1,0:T(8,128)S(1)}) custom-call(bf16[192,2304]{1,0:T(8,128)(2,1)S(1)} %concatenate.44.refs_0_, bf16[192,2304]{1,0:T(8,128)(2,1)S(1)} %copy-done.1, f32[192,2304]{1,0:T(8,128)S(1)} %copy-done.6, f32[192,2304]{1,0:T(8,128)S(1)} %copy-done.7), custom_call_target="tpu_custom_call" | custom-call | flops 3300000000 | tf_op jit(solution)/shard_map/adam/pallas_call | solution.py:501
  268.9 1.1 land.23
  271.0 3.9 %adam.5 = (f32[192,2304]{1,0:T(8,128)}, f32[192,2304]{1,0:T(8,128)}, f32[192,2304]{1,0:T(8,128)}, f32[192,2304]{1,0:T(8,128)}, f32[192,1]{1,0:T(8,128)S(1)}) custom-call(bf16[576,512]{1,0:T(8,128)(2,1)S(1)} %get-tuple-element.304.refs_0_, bf16[192,2304]{1,0:T(8,128)(2,1)S(1)} %copy-done.14, f32[192,2304]{1,0:T(8,128)S(1)} %copy-done.8, f32[192,2304]{1,0:T(8,128)S(1)} %copy-done.9), custom_call_target="tpu_custom_call" | custom-call | flops 3300000000 | tf_op jit(solution)/shard_map/adam/pallas_call | solution.py:501
  274.9 2.3 adam.6
  (180 shorter events, 25.3 us)
Async XLA Ops:
  0.7 18.7 %collective-permute-start.1 = (bf16[192,2304]{1,0:T(8,128)(2,1)}, bf16[192,2304]{1,0:T(8,128)(2,1)S(1)}, u32[]{:S(2)}, u32[]{:S(2)}) collective-permute-start(bf16[192,2304]{1,0:T(8,128)(2,1)} %refs_1_.6), channel_id=1, source_target_pairs={{0,1},{1,0},{2,3},{3,2},{4,5},{5,4},{6,7},{7,6},{8,9},{9,8},{10,11... | collective-permute-start | bytes 2654216 | tf_op jit(solution)/shard_map/ppermute | solution.py:523
  1.2 38.0 %collective-permute-start = (bf16[192,2304]{1,0:T(8,128)(2,1)}, bf16[192,2304]{1,0:T(8,128)(2,1)}, u32[]{:S(2)}, u32[]{:S(2)}) collective-permute-start(bf16[192,2304]{1,0:T(8,128)(2,1)} %refs_1_.6), channel_id=1, source_target_pairs={{0,2},{2,0},{1,3},{3,1},{4,6},{6,4},{5,7},{7,5},{8,10},{10,8},{9,1... | collective-permute-start | bytes 2654216 | tf_op jit(solution)/shard_map/ppermute | solution.py:527
  3.8 30.5 %collective-permute-start.7 = (bf16[192,768]{1,0:T(8,128)(2,1)}, bf16[192,768]{1,0:T(8,128)(2,1)}, u32[]{:S(2)}, u32[]{:S(2)}) collective-permute-start(bf16[192,768]{1,0:T(8,128)(2,1)} %refs_1_.7), channel_id=1, source_target_pairs={{0,1},{1,0},{2,3},{3,2},{4,5},{5,4},{6,7},{7,6},{8,9},{9,8},{10,11... | collective-permute-start | bytes 884744 | tf_op jit(solution)/shard_map/ppermute | solution.py:523
  3.9 35.3 %collective-permute-start.10 = (bf16[288,768]{1,0:T(8,128)(2,1)}, bf16[288,768]{1,0:T(8,128)(2,1)}, u32[]{:S(2)}, u32[]{:S(2)}) collective-permute-start(bf16[288,768]{1,0:T(8,128)(2,1)} %refs_1_.9), channel_id=1, source_target_pairs={{0,1},{1,0},{2,3},{3,2},{4,5},{5,4},{6,7},{7,6},{8,9},{9,8},{10,11... | collective-permute-start | bytes 1327112 | tf_op jit(solution)/shard_map/ppermute | solution.py:523
  12.5 4.6 %copy-start.27 = (pred[128]{0:T(512)(128)(4,1)S(1)}, pred[128]{0:T(512)(128)(4,1)}, u32[]{:S(2)}) copy-start(pred[128]{0:T(512)(128)(4,1)} %fusion.15) | copy-start | bytes 388
  12.5 4.6 %copy-start.28 = (f32[128]{0:T(128)S(1)}, f32[128]{0:T(128)}, u32[]{:S(2)}) copy-start(f32[128]{0:T(128)} %fusion.14) | copy-start | bytes 1540
  19.4 4.9 %collective-permute-start.5 = (bf16[2,192]{1,0:T(2,128)(2,1)S(1)}, bf16[2,192]{1,0:T(2,128)(2,1)S(1)}, u32[]{:S(2)}, u32[]{:S(2)}) collective-permute-start(bf16[2,192]{1,0:T(2,128)(2,1)S(1)} %get-tuple-element.180), channel_id=1, source_target_pairs={{0,2},{2,0},{1,3},{3,1},{4,6},{6,4},{5,7},{7,5},{8,10},{10,8},{9,1... | collective-permute-start | bytes 2312 | tf_op jit(solution)/shard_map/ppermute | solution.py:527
  20.0 6.2 %collective-permute-start.4 = (bf16[2,192]{1,0:T(2,128)(2,1)S(1)}, bf16[2,192]{1,0:T(2,128)(2,1)}, u32[]{:S(2)}, u32[]{:S(2)}) collective-permute-start(bf16[2,192]{1,0:T(2,128)(2,1)S(1)} %get-tuple-element.180), channel_id=1, source_target_pairs={{0,1},{1,0},{2,3},{3,2},{4,5},{5,4},{6,7},{7,6},{8,9},{9,8},{10,11... | collective-permute-start | bytes 2312 | tf_op jit(solution)/shard_map/ppermute | solution.py:523
  24.3 7.7 %copy-start.26 = (bf16[2,192]{1,0:T(2,128)(2,1)}, bf16[2,192]{1,0:T(2,128)(2,1)S(1)}, u32[]{:S(2)}) copy-start(bf16[2,192]{1,0:T(2,128)(2,1)S(1)} %collective-permute-done.5) | copy-start | bytes 2308
  24.3 6.3 %collective-permute-start.6 = (bf16[2,192]{1,0:T(2,128)(2,1)S(1)}, bf16[2,192]{1,0:T(2,128)(2,1)}, u32[]{:S(2)}, u32[]{:S(2)}) collective-permute-start(bf16[2,192]{1,0:T(2,128)(2,1)S(1)} %collective-permute-done.5), channel_id=1, source_target_pairs={{0,1},{1,0},{2,3},{3,2},{4,5},{5,4},{6,7},{7,6},{8,9},{9,8},{10,11... | collective-permute-start | bytes 2312 | tf_op jit(solution)/shard_map/ppermute | solution.py:523
  26.3 8.3 %collective-permute-start.2 = (bf16[64,768]{1,0:T(8,128)(2,1)S(1)}, bf16[64,768]{1,0:T(8,128)(2,1)}, u32[]{:S(2)}, u32[]{:S(2)}) collective-permute-start(bf16[64,768]{1,0:T(8,128)(2,1)S(1)} %get-tuple-element.178), channel_id=1, source_target_pairs={{0,4},{4,8},{8,12},{12,16},{16,20},{20,24},{24,28},{1,5},{5,9},{9,... | collective-permute-start | bytes 294920 | tf_op jit(solution)/shard_map/ppermute | solution.py:693
  30.6 6.9 %collective-permute-start.3 = (bf16[64,768]{1,0:T(8,128)(2,1)S(1)}, bf16[64,768]{1,0:T(8,128)(2,1)}, u32[]{:S(2)}, u32[]{:S(2)}) collective-permute-start(bf16[64,768]{1,0:T(8,128)(2,1)S(1)} %get-tuple-element.179), channel_id=1, source_target_pairs={{4,0},{8,4},{12,8},{16,12},{20,16},{24,20},{28,24},{5,1},{9,5},{13... | collective-permute-start | bytes 294920 | tf_op jit(solution)/shard_map/ppermute | solution.py:693
  34.3 4.9 %collective-permute-start.11 = (bf16[192,768]{1,0:T(8,128)(2,1)}, bf16[192,768]{1,0:T(8,128)(2,1)S(1)}, u32[]{:S(2)}, u32[]{:S(2)}) collective-permute-start(bf16[192,768]{1,0:T(8,128)(2,1)} %concatenate.39.refs_2_), channel_id=1, source_target_pairs={{0,1},{1,0},{2,3},{3,2},{4,5},{5,4},{6,7},{7,6},{8,9},{9,8},{10,11... | collective-permute-start | bytes 884744 | tf_op jit(solution)/shard_map/ppermute | solution.py:523
  34.5 4.6 %collective-permute-start.8 = (bf16[192,768]{1,0:T(8,128)(2,1)}, bf16[192,768]{1,0:T(8,128)(2,1)S(1)}, u32[]{:S(2)}, u32[]{:S(2)}) collective-permute-start(bf16[192,768]{1,0:T(8,128)(2,1)} %pad_maximum_fusion.2.refs_1_), channel_id=1, source_target_pairs={{0,1},{1,0},{2,3},{3,2},{4,5},{5,4},{6,7},{7,6},{8,9},{9,8},{10,11... | collective-permute-start | bytes 884744 | tf_op jit(solution)/shard_map/ppermute | solution.py:523
  37.5 1.7 collective-permute-start.9
  39.2 3.1 %copy-start.13 = (bf16[192,2304]{1,0:T(8,128)(2,1)S(1)}, bf16[192,2304]{1,0:T(8,128)(2,1)}, u32[]{:S(2)}) copy-start(bf16[192,2304]{1,0:T(8,128)(2,1)} %refs_1_.6) | copy-start | bytes 2654212
  39.3 3.0 %collective-permute-start.12 = (bf16[192,2304]{1,0:T(8,128)(2,1)}, bf16[192,2304]{1,0:T(8,128)(2,1)S(1)}, u32[]{:S(2)}, u32[]{:S(2)}) collective-permute-start(bf16[192,2304]{1,0:T(8,128)(2,1)} %get-tuple-element.187.refs_5_.refs_9_), channel_id=1, source_target_pairs={{0,1},{1,0},{2,3},{3,2},{4,5},{5,4},{6,7},{7,6},{8,9},{9,8},{10,11... | collective-permute-start | bytes 2654216 | tf_op jit(solution)/shard_map/ppermute | solution.py:523
  40.2 9.9 %collective-permute-start.13 = (bf16[192,768]{1,0:T(8,128)(2,1)S(1)}, bf16[192,768]{1,0:T(8,128)(2,1)S(1)}, u32[]{:S(2)}, u32[]{:S(2)}) collective-permute-start(bf16[192,768]{1,0:T(8,128)(2,1)S(1)} %get-tuple-element.196), channel_id=1, source_target_pairs={{0,2},{2,0},{1,3},{3,1},{4,6},{6,4},{5,7},{7,5},{8,10},{10,8},{9,1... | collective-permute-start | bytes 884744 | tf_op jit(solution)/shard_map/ppermute | solution.py:527
  41.8 14.2 %collective-permute-start.14 = (bf16[192,768]{1,0:T(8,128)(2,1)S(1)}, bf16[192,768]{1,0:T(8,128)(2,1)S(1)}, u32[]{:S(2)}, u32[]{:S(2)}) collective-permute-start(bf16[192,768]{1,0:T(8,128)(2,1)S(1)} %get-tuple-element.197.refs_3_), channel_id=1, source_target_pairs={{0,2},{2,0},{1,3},{3,1},{4,6},{6,4},{5,7},{7,5},{8,10},{10,8},{9,1... | collective-permute-start | bytes 884744 | tf_op jit(solution)/shard_map/ppermute | solution.py:527
  42.3 13.7 %copy-start.4 = (bf16[288,768]{1,0:T(8,128)(2,1)S(1)}, bf16[288,768]{1,0:T(8,128)(2,1)}, u32[]{:S(2)}) copy-start(bf16[288,768]{1,0:T(8,128)(2,1)} %refs_1_.9) | copy-start | bytes 1327108
  49.7 9.9 %copy-start = (bf16[1,1024,768]{2,1,0:T(8,128)(2,1)S(1)}, bf16[1,1024,768]{2,1,0:T(8,128)(2,1)}, u32[]{:S(2)}) copy-start(bf16[1,1024,768]{2,1,0:T(8,128)(2,1)} %param.22) | copy-start | bytes 4718596
  56.0 1.6 collective-permute-start.15
  57.6 12.7 %collective-permute-start.16 = (bf16[192,768]{1,0:T(8,128)(2,1)S(1)}, bf16[192,768]{1,0:T(8,128)(2,1)S(1)}, u32[]{:S(2)}, u32[]{:S(2)}) collective-permute-start(bf16[192,768]{1,0:T(8,128)(2,1)S(1)} %get-tuple-element.206.refs_7_), channel_id=1, source_target_pairs={{0,2},{2,0},{1,3},{3,1},{4,6},{6,4},{5,7},{7,5},{8,10},{10,8},{9,1... | collective-permute-start | bytes 884744 | tf_op jit(solution)/shard_map/ppermute | solution.py:527
  59.1 17.0 %collective-permute-start.17 = (bf16[288,768]{1,0:T(8,128)(2,1)S(1)}, bf16[288,768]{1,0:T(8,128)(2,1)S(1)}, u32[]{:S(2)}, u32[]{:S(2)}) collective-permute-start(bf16[288,768]{1,0:T(8,128)(2,1)S(1)} %get-tuple-element.207), channel_id=1, source_target_pairs={{0,2},{2,0},{1,3},{3,1},{4,6},{6,4},{5,7},{7,5},{8,10},{10,8},{9,1... | collective-permute-start | bytes 1327112 | tf_op jit(solution)/shard_map/ppermute | solution.py:527
  59.6 16.5 %copy-start.3 = (bf16[192,768]{1,0:T(8,128)(2,1)S(1)}, bf16[192,768]{1,0:T(8,128)(2,1)}, u32[]{:S(2)}) copy-start(bf16[192,768]{1,0:T(8,128)(2,1)} %concatenate.39.refs_2_) | copy-start | bytes 884740
  59.6 19.1 %copy-start.10 = (bf16[1,1024,768]{2,1,0:T(8,128)(2,1)S(1)}, bf16[1,1024,768]{2,1,0:T(8,128)(2,1)}, u32[]{:S(2)}) copy-start(bf16[1,1024,768]{2,1,0:T(8,128)(2,1)} %param.23) | copy-start | bytes 4718596
  70.2 26.1 %copy-start.17 = (bf16[1024,768]{1,0:T(8,128)(2,1)}, bf16[1024,768]{1,0:T(8,128)(2,1)S(1)}, u32[]{:S(2)}) copy-start(bf16[1024,768]{1,0:T(8,128)(2,1)S(1)} %get-tuple-element.205.refs_1_) | copy-start | bytes 4718596
  76.1 2.6 collective-permute-start.20
  76.1 2.2 collective-permute-start.18
  76.6 2.1 collective-permute-start.19
  76.7 19.7 %collective-permute-start.21 = (bf16[192,768]{1,0:T(8,128)(2,1)S(1)}, bf16[192,768]{1,0:T(8,128)(2,1)S(1)}, u32[]{:S(2)}, u32[]{:S(2)}) collective-permute-start(bf16[192,768]{1,0:T(8,128)(2,1)S(1)} %get-tuple-element.209.refs_3_), channel_id=1, source_target_pairs={{0,2},{2,0},{1,3},{3,1},{4,6},{6,4},{5,7},{7,5},{8,10},{10,8},{9,1... | collective-permute-start | bytes 884744 | tf_op jit(solution)/shard_map/ppermute | solution.py:527
  96.9 3.8 %collective-permute-start.23 = (bf16[2,1152,384]{2,1,0:T(8,128)(2,1)S(1)}, bf16[2,1152,384]{2,1,0:T(8,128)(2,1)S(1)}, u32[]{:S(2)}, u32[]{:S(2)}) collective-permute-start(bf16[2,1152,384]{2,1,0:T(8,128)(2,1)S(1)} %get-tuple-element.227), channel_id=1, source_target_pairs={{0,1},{1,0},{2,3},{3,2},{4,5},{5,4},{6,7},{7,6},{8,9},{9,8},{10,11... | collective-permute-start | bytes 5308424 | tf_op jit(solution)/shard_map/ppermute | solution.py:558
  97.1 6.1 %collective-permute-start.22 = (bf16[192,768]{1,0:T(8,128)(2,1)S(1)}, bf16[192,768]{1,0:T(8,128)(2,1)S(1)}, u32[]{:S(2)}, u32[]{:S(2)}) collective-permute-start(bf16[192,768]{1,0:T(8,128)(2,1)S(1)} %get-tuple-element.220.refs_5_), channel_id=1, source_target_pairs={{0,1},{1,0},{2,3},{3,2},{4,5},{5,4},{6,7},{7,6},{8,9},{9,8},{10,11... | collective-permute-start | bytes 884744 | tf_op jit(solution)/shard_map/ppermute | solution.py:523
  101.6 21.8 %collective-permute-start.24 = (bf16[1152,384]{1,0:T(8,128)(2,1)S(1)}, bf16[1152,384]{1,0:T(8,128)(2,1)S(1)}, u32[]{:S(2)}, u32[]{:S(2)}) collective-permute-start(bf16[1152,384]{1,0:T(8,128)(2,1)S(1)} %get-tuple-element.230.refs_18_), channel_id=1, source_target_pairs={{0,2},{2,0},{1,3},{3,1},{4,6},{6,4},{5,7},{7,5},{8,10},{10,8},{9,1... | collective-permute-start | bytes 2654216 | tf_op jit(solution)/shard_map/ppermute | solution.py:560
  124.1 12.7 %collective-permute-start.26 = (bf16[2,960,384]{2,1,0:T(8,128)(2,1)S(1)}, bf16[2,960,384]{2,1,0:T(8,128)(2,1)S(1)}, u32[]{:S(2)}, u32[]{:S(2)}) collective-permute-start(bf16[2,960,384]{2,1,0:T(8,128)(2,1)S(1)} %get-tuple-element.240.refs_14_), channel_id=1, source_target_pairs={{0,1},{1,0},{2,3},{3,2},{4,5},{5,4},{6,7},{7,6},{8,9},{9,8},{10,11... | collective-permute-start | bytes 4423688 | tf_op jit(solution)/shard_map/ppermute | solution.py:558
  124.2 12.6 %collective-permute-start.25 = (bf16[576,384]{1,0:T(8,128)(2,1)S(1)}, bf16[576,384]{1,0:T(8,128)(2,1)S(1)}, u32[]{:S(2)}, u32[]{:S(2)}) collective-permute-start(bf16[576,384]{1,0:T(8,128)(2,1)S(1)} %get-tuple-element.239.refs_13_), channel_id=1, source_target_pairs={{0,4},{4,0},{8,12},{12,8},{16,20},{20,16},{24,28},{28,24},{1,5},{5... | collective-permute-start | bytes 1327112 | tf_op jit(solution)/shard_map/ppermute | solution.py:563
  137.9 10.0 %collective-permute-start.27 = (bf16[288,384]{1,0:T(8,128)(2,1)S(1)}, bf16[288,384]{1,0:T(8,128)(2,1)S(1)}, u32[]{:S(2)}, u32[]{:S(2)}) collective-permute-start(bf16[288,384]{1,0:T(8,128)(2,1)S(1)} %get-tuple-element.250.refs_18_), channel_id=1, source_target_pairs={{0,8},{4,12},{8,0},{12,4},{16,24},{20,28},{24,16},{28,20},{1,9},{5... | collective-permute-start | bytes 663560 | tf_op jit(solution)/shard_map/ppermute | solution.py:563
  139.5 21.2 %collective-permute-start.29 = (bf16[960,384]{1,0:T(8,128)(2,1)S(1)}, bf16[960,384]{1,0:T(8,128)(2,1)S(1)}, u32[]{:S(2)}, u32[]{:S(2)}) collective-permute-start(bf16[960,384]{1,0:T(8,128)(2,1)S(1)} %get-tuple-element.251.refs_19_), channel_id=1, source_target_pairs={{0,2},{2,0},{1,3},{3,1},{4,6},{6,4},{5,7},{7,5},{8,10},{10,8},{9,1... | collective-permute-start | bytes 2211848 | tf_op jit(solution)/shard_map/ppermute | solution.py:560
  148.5 12.2 %collective-permute-start.28 = (bf16[288,384]{1,0:T(8,128)(2,1)S(1)}, bf16[288,384]{1,0:T(8,128)(2,1)S(1)}, u32[]{:S(2)}, u32[]{:S(2)}) collective-permute-start(bf16[288,384]{1,0:T(8,128)(2,1)S(1)} %get-tuple-element.259.refs_16_.refs_1_), channel_id=1, source_target_pairs={{0,16},{4,20},{8,24},{12,28},{16,0},{20,4},{24,8},{28,12},{1,17},{... | collective-permute-start | bytes 663560 | tf_op jit(solution)/shard_map/ppermute | solution.py:563
  150.5 10.2 %collective-permute-start.30 = (bf16[2,576,512]{2,1,0:T(8,128)(2,1)S(1)}, bf16[2,576,512]{2,1,0:T(8,128)(2,1)S(1)}, u32[]{:S(2)}, u32[]{:S(2)}) collective-permute-start(bf16[2,576,512]{2,1,0:T(8,128)(2,1)S(1)} %get-tuple-element.260.refs_17_), channel_id=1, source_target_pairs={{0,1},{1,0},{2,3},{3,2},{4,5},{5,4},{6,7},{7,6},{8,9},{9,8},{10,11... | collective-permute-start | bytes 3538952 | tf_op jit(solution)/shard_map/ppermute | solution.py:558
  161.7 13.6 %collective-permute-start.31 = (bf16[2,576,256]{2,1,0:T(8,128)(2,1)S(1)}, bf16[2,576,256]{2,1,0:T(8,128)(2,1)S(1)}, u32[]{:S(2)}, u32[]{:S(2)}) collective-permute-start(bf16[2,576,256]{2,1,0:T(8,128)(2,1)S(1)} %get-tuple-element.269), channel_id=1, source_target_pairs={{0,1},{1,0},{2,3},{3,2},{4,5},{5,4},{6,7},{7,6},{8,9},{9,8},{10,11... | collective-permute-start | bytes 1769480 | tf_op jit(solution)/shard_map/ppermute | solution.py:558
  161.8 12.9 %collective-permute-start.32 = (bf16[64,1536]{1,0:T(8,128)(2,1)S(1)}, bf16[64,1536]{1,0:T(8,128)(2,1)S(1)}, u32[]{:S(2)}, u32[]{:S(2)}) collective-permute-start(bf16[64,1536]{1,0:T(8,128)(2,1)S(1)} %get-tuple-element.270), channel_id=1, source_target_pairs={{0,4},{4,8},{8,12},{12,16},{16,20},{20,24},{24,28},{1,5},{5,9},{9,... | collective-permute-start | bytes 589832 | tf_op jit(solution)/shard_map/ppermute | solution.py:782
  165.4 9.9 %collective-permute-start.33 = (bf16[64,1536]{1,0:T(8,128)(2,1)S(1)}, bf16[64,1536]{1,0:T(8,128)(2,1)S(1)}, u32[]{:S(2)}, u32[]{:S(2)}) collective-permute-start(bf16[64,1536]{1,0:T(8,128)(2,1)S(1)} %get-tuple-element.271), channel_id=1, source_target_pairs={{4,0},{8,4},{12,8},{16,12},{20,16},{24,20},{28,24},{5,1},{9,5},{13... | collective-permute-start | bytes 589832 | tf_op jit(solution)/shard_map/ppermute | solution.py:782
  166.7 20.2 %collective-permute-start.34 = (bf16[288,384]{1,0:T(8,128)(2,1)S(1)}, bf16[288,384]{1,0:T(8,128)(2,1)S(1)}, u32[]{:S(2)}, u32[]{:S(2)}) collective-permute-start(bf16[288,384]{1,0:T(8,128)(2,1)S(1)} %get-tuple-element.278.refs_1_), channel_id=1, source_target_pairs={{0,8},{4,12},{8,0},{12,4},{16,24},{20,28},{24,16},{28,20},{1,9},{5... | collective-permute-start | bytes 663560 | tf_op jit(solution)/shard_map/ppermute | solution.py:563
  168.8 18.1 %collective-permute-start.35 = (bf16[480,384]{1,0:T(8,128)(2,1)S(1)}, bf16[480,384]{1,0:T(8,128)(2,1)S(1)}, u32[]{:S(2)}, u32[]{:S(2)}) collective-permute-start(bf16[480,384]{1,0:T(8,128)(2,1)S(1)} %get-tuple-element.280), channel_id=1, source_target_pairs={{0,4},{4,0},{8,12},{12,8},{16,20},{20,16},{24,28},{28,24},{1,5},{5... | collective-permute-start | bytes 1105928 | tf_op jit(solution)/shard_map/ppermute | solution.py:563
  174.8 14.4 %collective-permute-start.36 = (bf16[576,512]{1,0:T(8,128)(2,1)S(1)}, bf16[576,512]{1,0:T(8,128)(2,1)S(1)}, u32[]{:S(2)}, u32[]{:S(2)}) collective-permute-start(bf16[576,512]{1,0:T(8,128)(2,1)S(1)} %get-tuple-element.282), channel_id=1, source_target_pairs={{0,2},{2,0},{1,3},{3,1},{4,6},{6,4},{5,7},{7,5},{8,10},{10,8},{9,1... | collective-permute-start | bytes 1769480 | tf_op jit(solution)/shard_map/ppermute | solution.py:560
  176.0 13.1 %collective-permute-start.37 = (bf16[2,288,256]{2,1,0:T(8,128)(2,1)S(1)}, bf16[2,288,256]{2,1,0:T(8,128)(2,1)S(1)}, u32[]{:S(2)}, u32[]{:S(2)}) collective-permute-start(bf16[2,288,256]{2,1,0:T(8,128)(2,1)S(1)} %get-tuple-element.276.refs_13_), channel_id=1, source_target_pairs={{0,4},{4,0},{8,12},{12,8},{16,20},{20,16},{24,28},{28,24},{1,5},{5... | collective-permute-start | bytes 884744 | tf_op jit(solution)/shard_map/ppermute | solution.py:563
  190.0 18.3 %collective-permute-start.38 = (bf16[576,384]{1,0:T(8,128)(2,1)S(1)}, bf16[576,384]{1,0:T(8,128)(2,1)S(1)}, u32[]{:S(2)}, u32[]{:S(2)}) collective-permute-start(bf16[576,384]{1,0:T(8,128)(2,1)S(1)} %get-tuple-element.285.refs_1_), channel_id=1, source_target_pairs={{0,4},{4,0},{8,12},{12,8},{16,20},{20,16},{24,28},{28,24},{1,5},{5... | collective-permute-start | bytes 1327112 | tf_op jit(solution)/shard_map/ppermute | solution.py:563
  192.7 15.6 %collective-permute-start.39 = (bf16[480,384]{1,0:T(8,128)(2,1)S(1)}, bf16[480,384]{1,0:T(8,128)(2,1)S(1)}, u32[]{:S(2)}, u32[]{:S(2)}) collective-permute-start(bf16[480,384]{1,0:T(8,128)(2,1)S(1)} %get-tuple-element.286.refs_3_), channel_id=1, source_target_pairs={{0,8},{4,12},{8,0},{12,4},{16,24},{20,28},{24,16},{28,20},{1,9},{5... | collective-permute-start | bytes 1105928 | tf_op jit(solution)/shard_map/ppermute | solution.py:563
  192.7 15.6 %collective-permute-start.40 = (bf16[288,512]{1,0:T(8,128)(2,1)S(1)}, bf16[288,512]{1,0:T(8,128)(2,1)S(1)}, u32[]{:S(2)}, u32[]{:S(2)}) collective-permute-start(bf16[288,512]{1,0:T(8,128)(2,1)S(1)} %get-tuple-element.288), channel_id=1, source_target_pairs={{0,4},{4,0},{8,12},{12,8},{16,20},{20,16},{24,28},{28,24},{1,5},{5... | collective-permute-start | bytes 884744 | tf_op jit(solution)/shard_map/ppermute | solution.py:563
  193.8 5.1 %collective-permute-start.41 = (bf16[288,256]{1,0:T(8,128)(2,1)S(1)}, bf16[288,256]{1,0:T(8,128)(2,1)S(1)}, u32[]{:S(2)}, u32[]{:S(2)}) collective-permute-start(bf16[288,256]{1,0:T(8,128)(2,1)S(1)} %get-tuple-element.290), channel_id=1, source_target_pairs={{0,2},{2,0},{1,3},{3,1},{4,6},{6,4},{5,7},{7,5},{8,10},{10,8},{9,1... | collective-permute-start | bytes 442376 | tf_op jit(solution)/shard_map/ppermute | solution.py:560
  209.2 19.7 %collective-permute-start.42 = (bf16[480,384]{1,0:T(8,128)(2,1)S(1)}, bf16[480,384]{1,0:T(8,128)(2,1)S(1)}, u32[]{:S(2)}, u32[]{:S(2)}) collective-permute-start(bf16[480,384]{1,0:T(8,128)(2,1)S(1)} %get-tuple-element.292.refs_1_), channel_id=1, source_target_pairs={{0,16},{4,20},{8,24},{12,28},{16,0},{20,4},{24,8},{28,12},{1,17},{... | collective-permute-start | bytes 1105928 | tf_op jit(solution)/shard_map/ppermute | solution.py:563
  210.9 17.9 %collective-permute-start.43 = (bf16[288,512]{1,0:T(8,128)(2,1)S(1)}, bf16[288,512]{1,0:T(8,128)(2,1)S(1)}, u32[]{:S(2)}, u32[]{:S(2)}) collective-permute-start(bf16[288,512]{1,0:T(8,128)(2,1)S(1)} %get-tuple-element.293.refs_3_), channel_id=1, source_target_pairs={{0,8},{4,12},{8,0},{12,4},{16,24},{20,28},{24,16},{28,20},{1,9},{5... | collective-permute-start | bytes 884744 | tf_op jit(solution)/shard_map/ppermute | solution.py:563
  213.8 15.0 %collective-permute-start.44 = (bf16[288,256]{1,0:T(8,128)(2,1)S(1)}, bf16[288,256]{1,0:T(8,128)(2,1)S(1)}, u32[]{:S(2)}, u32[]{:S(2)}) collective-permute-start(bf16[288,256]{1,0:T(8,128)(2,1)S(1)} %get-tuple-element.294.refs_5_), channel_id=1, source_target_pairs={{0,8},{4,12},{8,0},{12,4},{16,24},{20,28},{24,16},{28,20},{1,9},{5... | collective-permute-start | bytes 442376 | tf_op jit(solution)/shard_map/ppermute | solution.py:563
  229.6 20.7 %collective-permute-start.46 = (bf16[288,512]{1,0:T(8,128)(2,1)S(1)}, bf16[288,512]{1,0:T(8,128)(2,1)S(1)}, u32[]{:S(2)}, u32[]{:S(2)}) collective-permute-start(bf16[288,512]{1,0:T(8,128)(2,1)S(1)} %get-tuple-element.297.refs_3_), channel_id=1, source_target_pairs={{0,16},{4,20},{8,24},{12,28},{16,0},{20,4},{24,8},{28,12},{1,17},{... | collective-permute-start | bytes 884744 | tf_op jit(solution)/shard_map/ppermute | solution.py:563
  232.1 18.2 %collective-permute-start.45 = (bf16[480,384]{1,0:T(8,128)(2,1)S(1)}, bf16[480,384]{1,0:T(8,128)(2,1)S(1)}, u32[]{:S(2)}, u32[]{:S(2)}) collective-permute-start(bf16[480,384]{1,0:T(8,128)(2,1)S(1)} %get-tuple-element.296.refs_1_), channel_id=1, source_target_pairs={{0,4},{4,0},{8,12},{12,8},{16,20},{20,16},{24,28},{28,24},{1,5},{5... | collective-permute-start | bytes 1105928 | tf_op jit(solution)/shard_map/ppermute | solution.py:563
  232.9 17.4 %collective-permute-start.47 = (bf16[288,256]{1,0:T(8,128)(2,1)S(1)}, bf16[288,256]{1,0:T(8,128)(2,1)S(1)}, u32[]{:S(2)}, u32[]{:S(2)}) collective-permute-start(bf16[288,256]{1,0:T(8,128)(2,1)S(1)} %get-tuple-element.298.refs_5_), channel_id=1, source_target_pairs={{0,16},{4,20},{8,24},{12,28},{16,0},{20,4},{24,8},{28,12},{1,17},{... | collective-permute-start | bytes 442376 | tf_op jit(solution)/shard_map/ppermute | solution.py:563
  251.0 3.0 %copy-start.15 = (f32[192,768]{1,0:T(8,128)S(1)}, f32[192,768]{1,0:T(8,128)}, u32[]{:S(2)}) copy-start(f32[192,768]{1,0:T(8,128)} %refs_2_.8) | copy-start | bytes 1769476
  252.0 16.9 %collective-permute-start.49 = (bf16[288,256]{1,0:T(8,128)(2,1)S(1)}, bf16[288,256]{1,0:T(8,128)(2,1)}, u32[]{:S(2)}, u32[]{:S(2)}) collective-permute-start(bf16[288,256]{1,0:T(8,128)(2,1)S(1)} %get-tuple-element.301.refs_3_), channel_id=1, source_target_pairs={{0,4},{4,0},{8,12},{12,8},{16,20},{20,16},{24,28},{28,24},{1,5},{5... | collective-permute-start | bytes 442376 | tf_op jit(solution)/shard_map/ppermute | solution.py:563
  253.0 15.9 %collective-permute-start.48 = (bf16[288,512]{1,0:T(8,128)(2,1)S(1)}, bf16[288,512]{1,0:T(8,128)(2,1)S(1)}, u32[]{:S(2)}, u32[]{:S(2)}) collective-permute-start(bf16[288,512]{1,0:T(8,128)(2,1)S(1)} %get-tuple-element.300.refs_1_), channel_id=1, source_target_pairs={{0,4},{4,0},{8,12},{12,8},{16,20},{20,16},{24,28},{28,24},{1,5},{5... | collective-permute-start | bytes 884744 | tf_op jit(solution)/shard_map/ppermute | solution.py:563
  263.3 4.9 %copy-start.22 = (f32[192]{0:T(256)S(1)}, f32[192]{0:T(256)}, u32[]{:S(2)}) copy-start(f32[192]{0:T(256)} %param.43) | copy-start | bytes 2308
  263.3 5.0 %copy-start.23 = (f32[192]{0:T(256)S(1)}, f32[192]{0:T(256)}, u32[]{:S(2)}) copy-start(f32[192]{0:T(256)} %param.37) | copy-start | bytes 2308
  263.3 5.0 %copy-start.29 = (bf16[192]{0:T(256)(128)(2,1)S(1)}, bf16[192]{0:T(256)(128)(2,1)}, u32[]{:S(2)}) copy-start(bf16[192]{0:T(256)(128)(2,1)} %param.31) | copy-start | bytes 1156
  263.3 6.7 %copy-start.14 = (bf16[192,2304]{1,0:T(8,128)(2,1)S(1)}, bf16[192,2304]{1,0:T(8,128)(2,1)}, u32[]{:S(2)}) copy-start(bf16[192,2304]{1,0:T(8,128)(2,1)} %refs_1_.6) | copy-start | bytes 2654212
  (17 other events, 36.0 us)

commit v3 on v2

v3 whole, which is shorter than its diff:
```python
import functools

import jax
import jax.numpy as jnp
import numpy as np
from jax import lax
from jax.experimental import pallas as pl
from jax.experimental.pallas import tpu as pltpu
from jax.sharding import PartitionSpec as P

D = 768
FF = 1152
HEADS = 12
HD = 64
HALF = 64
STEP = 10
PAIR = 2 * HD
QB = 128
TILE = 256
WIDE = 384
QUAD = 4 * HD

NORM_EPS = 1e-05
BETA_ONE = 0.9
BETA_TWO = 0.98
LEARN_RATE = 0.05
WEIGHT_DECAY = 0.01
ADAM_EPS = 1e-06
NEG_FILL = -1e30
THETA = 10000.0
BF = jnp.bfloat16
F32 = jnp.float32


def dot(left, right):
    return lax.dot_general(left, right, (((1,), (0,)), ((), ())), preferred_element_type=F32)


def dot_bt(left, right):
    return lax.dot_general(left, right, (((1,), (1,)), ((), ())), preferred_element_type=F32)


def dot_at(left, right):
    return lax.dot_general(left, right, (((0,), (0,)), ((), ())), preferred_element_type=F32)


def call(body, args, in_specs, out_specs, out_shape, megabytes, deps=(), aliases=None, **kw):
    first = len(args)
    n_out = len(out_shape)

    def wrapped(*refs):
        refs = refs[:first] + refs[first + len(deps) :]
        token = refs[first + n_out]
        token[...] = jnp.zeros_like(token)
        body(*refs[: first + n_out], *refs[first + n_out + 1 :])

    return pl.pallas_call(
        wrapped,
        in_specs=list(in_specs) + [pl.BlockSpec(memory_space=pl.ANY)] * len(deps),
        out_specs=list(out_specs) + [full((8, 128))],
        out_shape=list(out_shape) + [jax.ShapeDtypeStruct((8, 128), F32)],
        input_output_aliases=aliases or {},
        compiler_params=pltpu.CompilerParams(
            dimension_semantics=("arbitrary",), vmem_limit_bytes=megabytes * 1024 * 1024
        ),
        **kw,
    )(*args, *deps)


def full(shape):
    return pl.BlockSpec(shape, lambda i: (0,) * len(shape))


def rows(tile, width):
    return pl.BlockSpec((tile, width), lambda i: (i, 0))


def cost(microseconds):
    return pl.CostEstimate(flops=int(microseconds * 1.1e9), bytes_accessed=0, transcendentals=0)


def normalize(x):
    mean = jnp.mean(x, axis=-1, keepdims=True)
    centered = x - mean
    var = jnp.mean(centered * centered, axis=-1, keepdims=True)
    r = lax.rsqrt(var + NORM_EPS)
    return centered * r, r


def signed(sin):
    first = lax.broadcasted_iota(jnp.int32, sin.shape, 1) % HD < HD // 2
    zero = jnp.zeros_like(sin)
    return jnp.where(first, -sin, zero), jnp.where(first, zero, sin)


def turn(u, cos, sin_left, sin_right):
    return u * cos + pltpu.roll(u, PAIR - HD // 2, 1) * sin_left + pltpu.roll(u, HD // 2, 1) * sin_right


def blocks_of(info_ref):
    return (info_ref.shape[0] - 2) // 2


def sides(info_ref):
    count = blocks_of(info_ref)
    at = info_ref[1]
    own = info_ref[2 + at]
    left = (at > 0) & (info_ref[2 + jnp.maximum(at - 1, 0)] == own)
    right = (at < count - 1) & (info_ref[2 + jnp.minimum(at + 1, count - 1)] == own)
    return left, right


def bias_of(b, last, left, right):
    shape = (QB + 2 * HALF, QB)
    key = lax.broadcasted_iota(jnp.int32, shape, 0)
    off = key - lax.broadcasted_iota(jnp.int32, shape, 1)
    low = jnp.where((b > 0) | left, 0, HALF)
    high = jnp.where((b < last) | right, QB + 2 * HALF, QB + HALF)
    ok = (off >= 0) & (off <= 2 * HALF) & (key >= low) & (key < high)
    return jnp.where(ok, 0.0, NEG_FILL)


def lay(w, parts, out_ref, bit=0):
    r = out_ref.shape[0] // 4
    for i, ref in enumerate(parts):
        start = (w ^ i) * r
        if isinstance(ref, tuple):
            half = r // 2
            for j, a in enumerate(ref):
                out_ref[pl.ds(pl.multiple_of(start + (bit ^ j) * half, 16), half), :] = a[...]
        else:
            out_ref[pl.ds(pl.multiple_of(start, 32), r), :] = ref[...]


def deal(w, acc, cols, keep_ref, send_ref, at):
    r = acc.shape[0] // 4
    c = w & 1
    for x in range(2):
        keep_ref[x, at : at + r, :] = acc[pl.ds(pl.multiple_of((2 * x + c) * r, 32), r), cols].astype(BF)
        send_ref[x, at : at + r, :] = acc[pl.ds(pl.multiple_of((2 * x + 1 - c) * r, 32), r), cols].astype(BF)


def smem():
    return pl.BlockSpec(memory_space=pltpu.SMEM)


def piece(n_rows):
    return jax.ShapeDtypeStruct((2, n_rows, WIDE), BF)


def qkv_body(info_ref, x_ref, low_ref, high_ref, gain_a, gain_b, gain_c, gain_d, wa, wb, wc, wd, far_ref, near_ref,
             nt_ref, q_ref, k_ref, v_ref, cos_ref, sin_ref, gain_ref, w_ref, x_ext):
    t = q_ref.shape[0]
    i = pl.program_id(0)

    @pl.when(i == 0)
    def _():
        lay(info_ref[0], (wa, wb, wc, wd), w_ref)
        end = x_ext.shape[0] - HALF
        x_ext[:HALF, :] = low_ref[...]
        x_ext[HALF:end, :] = x_ref[...]
        x_ext[end:, :] = high_ref[...]
        r = D // 4
        for p, ref in enumerate((gain_a, gain_b, gain_c, gain_d)):
            gains = ref[...].astype(F32)
            for owner in range(4):

                @pl.when((info_ref[0] ^ p) == owner)
                def _():
                    gain_ref[:2, owner * r : (owner + 1) * r] = gains


    place = info_ref[2 + blocks_of(info_ref) + info_ref[1]]
    c2, s2 = far_ref[0, pl.ds(place, 1), :], far_ref[1, pl.ds(place, 1), :]
    c1, s1 = near_ref[0], near_ref[1]
    cos = c1 * c2 - s1 * s2
    sin = s1 * c2 + c1 * s2
    cos_ref[...] = cos
    sin_ref[...] = sin
    sl, sr = signed(sin)
    n, _ = normalize(x_ext[pl.ds(pl.multiple_of(i * t, 128), t), :].astype(F32))
    normed = (n * gain_ref[0:1, :]).astype(BF)
    nt_ref[...] = normed.T
    for part, ref, scale in ((0, q_ref, HD**-0.5), (1, k_ref, 1.0)):
        u = dot(normed, w_ref[:, part * D : (part + 1) * D])
        for p in range(D // PAIR):
            r = turn(u[:, p * PAIR : (p + 1) * PAIR], cos, sl, sr)
            ref[:, p * PAIR : (p + 1) * PAIR] = (r * scale).astype(BF)
    v_ref[...] = dot(normed, w_ref[:, 2 * D :]).astype(BF)


def angle_tables(n, ext):
    freq = THETA ** (-2.0 * (np.arange(PAIR) % (HD // 2)) / HD)

    def table(positions):
        angle = positions[:, None] * freq[None, :]
        return jnp.asarray(np.stack([np.cos(angle), np.sin(angle)]).astype(np.float32))

    return table(np.arange(4.0) * n), table(np.arange(float(ext)) - HALF)


def qkv_call(info, x, low, high, gains, w_parts, deps=()):
    n = x.shape[0]
    ext = n + 2 * HALF
    t = ext // 3
    out = jax.ShapeDtypeStruct((ext, D), BF)
    table = jax.ShapeDtypeStruct((ext, PAIR), F32)
    far, near = angle_tables(n, ext)
    return call(
        qkv_body,
        [info, x, low, high, *gains, *w_parts, far, near],
        grid=(3,),
        in_specs=[smem(), full((n, D)), full((HALF, D)), full((HALF, D))] + [full((2, D // 4))] * 4 + [full((D // 4, 3 * D))] * 4
        + [full(far.shape), pl.BlockSpec((2, t, PAIR), lambda i: (0, i, 0))],
        out_specs=[pl.BlockSpec((D, t), lambda i: (0, i))] + [rows(t, D)] * 3 + [rows(t, PAIR)] * 2 + [full((8, D))],
        out_shape=[jax.ShapeDtypeStruct((D, ext), BF)] + [out] * 3 + [table] * 2 + [jax.ShapeDtypeStruct((8, D), F32)],
        scratch_shapes=[pltpu.VMEM((D, 3 * D), BF), pltpu.VMEM((ext, D), BF)],
        megabytes=20,
        deps=deps,
        cost_estimate=cost(9),
        name="qkv",
    )


def apart(u):
    head = lax.broadcasted_iota(jnp.int32, u.shape, 1) // HD
    zero = jnp.zeros_like(u)
    return jnp.concatenate([jnp.where(head == h, u, zero) for h in range(4)], axis=0)


def together(u):
    r = u.shape[0] // 4
    head = lax.broadcasted_iota(jnp.int32, (r, QUAD), 1) // HD
    out = u[:r]
    for h in range(1, 4):
        out = jnp.where(head == h, u[h * r : (h + 1) * r], out)
    return out


def repeat(u):
    return jnp.concatenate([u] * 4, axis=1)


def attend_body(info_ref, q_ref, k_ref, v_ref, x_ref, wa, wb, wc, wd, gain_ref,
                mixed_ref, middle_ref, n2_ref, w_ref, lse_ref):
    i = pl.program_id(0)
    last = pl.num_programs(0) * (TILE // QB) - 1
    left, right = sides(info_ref)

    @pl.when(i == 0)
    def _():
        lay(info_ref[0], (wa, wb, wc, wd), w_ref)

    for s in range(TILE // QB):
        b = i * (TILE // QB) + s
        start = pl.multiple_of(b * QB, QB)
        bias = repeat(bias_of(b, last, left, right))
        for g in range(D // QUAD):
            cols = slice(g * QUAD, (g + 1) * QUAD)
            win = pl.ds(start, QB + 2 * HALF)
            q4 = apart(q_ref[pl.ds(start + HALF, QB), cols])
            scores = dot_bt(k_ref[win, cols], q4) + bias
            most = jnp.max(scores, axis=0, keepdims=True)
            e = jnp.exp(scores - most)
            total = jnp.sum(e, axis=0, keepdims=True)
            probs = (e * (1.0 / total)).astype(BF)
            o = together(dot_at(probs, v_ref[win, cols]))
            mixed_ref[s * QB : (s + 1) * QB, cols] = o.astype(BF)
            lse = most + jnp.log(total)
            for h in range(4):
                lse_ref[g, h : h + 1, s * QB : (s + 1) * QB] = lse[:, h * QB : (h + 1) * QB]
    middle = x_ref[...].astype(F32) + dot(mixed_ref[...], w_ref[...])
    middle_ref[...] = middle.astype(BF)
    n, _ = normalize(middle)
    n2_ref[...] = (n * gain_ref[1:2, :]).astype(BF)


def attend_call(info, q, k, v, x, w_parts, gain, deps=()):
    n = x.shape[0]
    ext = q.shape[0]
    groups = D // QUAD
    return call(
        attend_body,
        [info, q, k, v, x, *w_parts, gain],
        grid=(n // TILE,),
        in_specs=[smem()] + [full((ext, D))] * 3 + [rows(TILE, D)] + [full((D // 4, D))] * 4 + [full((8, D))],
        out_specs=[rows(TILE, D)] * 3 + [full((D, D)), pl.BlockSpec((groups, 4, TILE), lambda i: (0, 0, i))],
        out_shape=[
            jax.ShapeDtypeStruct((n, D), BF), jax.ShapeDtypeStruct((n, D), BF), jax.ShapeDtypeStruct((n, D), BF),
            jax.ShapeDtypeStruct((D, D), BF), jax.ShapeDtypeStruct((groups, 4, n), F32),
        ],
        megabytes=12,
        deps=deps,
        cost_estimate=cost(11),
        name="attend",
    )


def hidden(n2, cot, wg, wu, wd):
    gate = dot(n2, wg)
    up = dot(n2, wu)
    ga = dot_bt(cot, wd)
    phi = 0.5 + 0.5 * lax.erf(gate * (2.0**-0.5))
    gelu = gate * phi
    act = (gelu * up).astype(BF)
    slope = phi + gate * (jnp.exp(-0.5 * gate * gate) * 0.3989422804014327)
    dgate = (ga * up * slope).astype(BF)
    dup = (ga * gelu).astype(BF)
    out = dot(act, wd)
    gn = dot_bt(dgate, wg) + dot_bt(dup, wu)
    return act, dgate, dup, out, gn


def ffn_a_body(info_ref, n2_ref, cot_ref, ga, gb, gc, gd, ge, gf, ua, ub, uc, ud, oa, ob, oc, od,
               out_ref, gn_ref, keep_ref, send_ref, wg_ref, wu_ref, wd_ref, acc, ad):
    i = pl.program_id(0)

    @pl.when(i == 0)
    def _():
        lay(info_ref[0], (ga, gb, (gc, gd), (ge, gf)), wg_ref, info_ref[1] & 1)
        lay(info_ref[0], (ua, ub, uc, ud), wu_ref)
        lay(info_ref[0], (oa, ob, oc, od), wd_ref)
        acc[...] = jnp.zeros_like(acc)
        ad[...] = jnp.zeros_like(ad)

    n2 = n2_ref[...]
    cot = cot_ref[...]
    nt = n2.T
    total_out = jnp.zeros((TILE, D), F32)
    total_gn = jnp.zeros((TILE, D), F32)
    for h in range(2):
        g, u = slice(h * WIDE, (h + 1) * WIDE), slice(D + h * WIDE, D + (h + 1) * WIDE)
        act, dgate, dup, out, gn = hidden(n2, cot, wg_ref[:, g], wu_ref[:, g], wd_ref[g, :])
        total_out += out
        total_gn += gn
        acc[:, g] += dot(nt, dgate)
        acc[:, u] += dot(nt, dup)
        ad[g, :] += dot_at(act, cot)
    out_ref[...] = total_out.astype(BF)
    gn_ref[...] = total_gn.astype(BF)

    @pl.when(i == pl.num_programs(0) - 1)
    def _():
        for b in range(4):
            deal(info_ref[0], acc, slice(b * WIDE, (b + 1) * WIDE), keep_ref, send_ref, b * D // 4)
        for b in range(2):
            deal(info_ref[0], ad, slice(b * WIDE, (b + 1) * WIDE), keep_ref, send_ref, (4 + b) * D // 4)


def ffn_a_call(info, n2, cot, gate_parts, up_parts, down_parts, deps=()):
    n = n2.shape[0]
    part = jax.ShapeDtypeStruct((n, D), BF)
    size = 6 * D // 4
    return call(
        ffn_a_body,
        [info, n2, cot, *gate_parts, *up_parts, *down_parts],
        grid=(n // TILE,),
        in_specs=[smem()] + [rows(TILE, D)] * 2 + [full((D // 4, D))] * 2 + [full((D // 8, D))] * 4
        + [full((D // 4, D))] * 8,
        out_specs=[rows(TILE, D)] * 2 + [full((2, size, WIDE))] * 2,
        out_shape=[part, part, piece(size), piece(size)],
        scratch_shapes=[pltpu.VMEM((D, D), BF)] * 3 + [pltpu.VMEM((D, 2 * D), F32), pltpu.VMEM((D, D), F32)],
        megabytes=24,
        deps=deps,
        cost_estimate=cost(18),
        name="ffn_a",
    )


def norm_back(grad, n, r, gain):
    e = grad * gain
    return r * (e - jnp.mean(e, axis=-1, keepdims=True) - n * jnp.mean(e * n, axis=-1, keepdims=True))


def ffn_b_body(info_ref, n2_ref, cot_ref, ia, ib, ic, id_, oa, ob, oc, od, pout_ref, pgn_ref, mid_ref, mixed_ref, wo_ref, gain_ref,
               out_ref, gmid_ref, gmix_ref, keep_ref, send_ref, w_ref, wd_ref, acc, ad, ao):
    i = pl.program_id(0)

    @pl.when(i == 0)
    def _():
        lay(info_ref[0], (ia, ib, ic, id_), w_ref)
        lay(info_ref[0], (oa, ob, oc, od), wd_ref)
        acc[...] = jnp.zeros_like(acc)
        ao[...] = jnp.zeros_like(ao)
        ad[...] = jnp.zeros_like(ad)

    n2 = n2_ref[...]
    cot = cot_ref[...]
    act, dgate, dup, out, gn = hidden(n2, cot, w_ref[:, :WIDE], w_ref[:, WIDE:], wd_ref[...])
    nt = n2.T
    acc[:, :WIDE] += dot(nt, dgate)
    acc[:, WIDE:] += dot(nt, dup)
    ad[...] += dot_at(act, cot)
    middle = mid_ref[...].astype(F32)
    out_ref[...] = (middle + pout_ref[...].astype(F32) + out).astype(BF)
    n, r = normalize(middle)
    branch = (cot.astype(F32) + norm_back(pgn_ref[...].astype(F32) + gn, n, r, gain_ref[1:2, :])).astype(BF)
    gmid_ref[...] = branch
    gmix_ref[...] = dot_bt(branch, wo_ref[...]).astype(BF)
    ao[...] += dot_at(mixed_ref[...], branch)

    @pl.when(i == pl.num_programs(0) - 1)
    def _():
        w = info_ref[0]
        r = D // 4
        for b in range(2):
            cols = slice(b * WIDE, (b + 1) * WIDE)
            deal(w, acc, cols, keep_ref, send_ref, b * r)
            deal(w, ao, cols, keep_ref, send_ref, (2 + b) * r)
            deal(w, ad, cols, keep_ref, send_ref, 4 * r + b * r // 2)


def ffn_b_call(info, n2, cot, in_parts, down_parts, pout, pgn, middle, mixed, wo, gain, deps=()):
    n = n2.shape[0]
    size = 5 * D // 4
    return call(
        ffn_b_body,
        [info, n2, cot, *in_parts, *down_parts, pout, pgn, middle, mixed, wo, gain],
        grid=(n // TILE,),
        in_specs=[smem()] + [rows(TILE, D)] * 2 + [full((D // 4, D))] * 4 + [full((WIDE // 4, D))] * 4
        + [rows(TILE, D)] * 4 + [full((D, D)), full((8, D))],
        out_specs=[rows(TILE, D)] * 3 + [full((2, size, WIDE))] * 2,
        out_shape=[jax.ShapeDtypeStruct((n, D), BF)] * 3 + [piece(size), piece(size)],
        scratch_shapes=[pltpu.VMEM((D, D), BF), pltpu.VMEM((WIDE, D), BF),
                        pltpu.VMEM((D, D), F32), pltpu.VMEM((WIDE, D), F32), pltpu.VMEM((D, D), F32)],
        megabytes=24,
        deps=deps,
        cost_estimate=cost(14),
        name="ffn_b",
    )


def attend_back_body(info_ref, q_ref, k_ref, v_ref, g_ref, mixed_ref, lse_ref, cos_ref, sin_ref, nt_ref, *rest):
    dq_ref, dk_ref, dv_ref, keep_ref, send_ref, ak, av, aw = rest[-8:]
    ext = ak.shape[0]
    blocks = (ext - 2 * HALF) // QB
    left, right = sides(info_ref)
    ak[...] = jnp.zeros_like(ak)
    av[...] = jnp.zeros_like(av)
    zero = jnp.zeros((HALF, QUAD), BF)
    dq_ref[:HALF, :] = zero
    dq_ref[ext - HALF :, :] = zero
    prod = mixed_ref[...].astype(F32) * g_ref[...].astype(F32)
    head = lax.broadcasted_iota(jnp.int32, (8, QUAD), 1) // HD
    pick = jnp.where(head == lax.broadcasted_iota(jnp.int32, (8, QUAD), 0), 1.0, 0.0).astype(BF)
    high = prod.astype(BF)
    delta = dot_bt(pick, high) + dot_bt(pick, (prod - high.astype(F32)).astype(BF))

    def of_heads(a, start):
        return jnp.concatenate([a[h : h + 1, start : start + QB] for h in range(4)], axis=1)

    def unturn(u, at):
        cos = cos_ref[at, :]
        sl, sr = signed(-sin_ref[at, :])
        return jnp.concatenate([turn(u[:, c : c + PAIR], cos, sl, sr) for c in (0, PAIR)], axis=1).astype(BF)

    for b in range(blocks):
        start = b * QB
        win = slice(start, start + QB + 2 * HALF)
        here = slice(start + HALF, start + HALF + QB)
        bias = repeat(bias_of(b, blocks - 1, left, right))
        q4 = apart(q_ref[here, :])
        g4 = apart(g_ref[start : start + QB, :])
        kw = k_ref[win, :]
        probs = jnp.exp(dot_bt(kw, q4) + bias - of_heads(lse_ref[0], start))
        ds = (probs * (dot_bt(v_ref[win, :], g4) - of_heads(delta, start))).astype(BF)
        ak[win, :] += dot(ds, q4)
        av[win, :] += dot(probs.astype(BF), g4)
        dq_ref[here, :] = unturn(together(dot_at(ds, kw)) * HD**-0.5, here)
    dk_ref[...] = unturn(ak[...], slice(0, ext))
    dv_ref[...] = av[...].astype(BF)
    for part, ref in enumerate((dq_ref, dk_ref, dv_ref)):
        aw[...] = dot(nt_ref[...], ref[...])
        deal(info_ref[0], aw, slice(0, QUAD), keep_ref, send_ref, part * D // 4)


def attend_back_call(p, at, width, info, q, k, v, g, mixed, lse, cos, sin, nt, sofar, pieces, deps=()):
    n = g.shape[0]
    ext = q.shape[0]
    cols = pl.BlockSpec((ext, QUAD), lambda i: (0, p))
    inner = pl.BlockSpec((n, QUAD), lambda i: (0, p))
    own = jax.ShapeDtypeStruct((ext, D), BF)
    out = jax.ShapeDtypeStruct((2, 3 * D // 4, width), BF)
    args = [info, q, k, v, g, mixed, lse, cos, sin, nt]
    extra = list(sofar) + list(pieces)
    aliases = {}
    for i in range(len(sofar)):
        aliases[len(args) + i] = i
    for i in range(len(pieces)):
        aliases[len(args) + len(sofar) + i] = 3 + i
    mine = pl.BlockSpec((2, 3 * D // 4, QUAD), lambda i: (0, 0, at))
    return call(
        attend_back_body,
        args + extra,
        grid=(1,),
        in_specs=[smem(), cols, cols, cols, inner, inner, pl.BlockSpec((1, 4, n), lambda i: (p, 0, 0))]
        + [full((ext, PAIR))] * 2 + [full((D, ext))] + [pl.BlockSpec(memory_space=pl.ANY)] * len(extra),
        out_specs=[cols] * 3 + [mine] * 2,
        out_shape=[own, own, own, out, out],
        scratch_shapes=[pltpu.VMEM((ext, QUAD), F32), pltpu.VMEM((ext, QUAD), F32), pltpu.VMEM((D, QUAD), F32)],
        aliases=aliases,
        megabytes=12,
        deps=deps,
        cost_estimate=cost(4),
        name="attend_back",
    )


def last_body(info_ref, x_ref, dq_ref, dk_ref, dv_ref, rim_low, rim_high, gmid_ref, wa, wb, wc, wd, gain_ref, gin_ref, w_ref, *both):
    i = pl.program_id(0)
    start = pl.multiple_of(i * TILE, TILE)
    here = pl.ds(start + HALF, TILE)
    ext = dk_ref.shape[0]

    @pl.when(i == 0)
    def _():
        lay(info_ref[0], (wa, wb, wc, wd), w_ref)
        for j, ref in enumerate((dk_ref, dv_ref)):
            cols = slice(j * D, (j + 1) * D)
            both[j][...] = ref[...]
            both[j][HALF : 2 * HALF, :] += rim_low[:, cols]
            both[j][ext - 2 * HALF : ext - HALF, :] += rim_high[:, cols]

    total = jnp.zeros((TILE, D), F32)
    for j, ref in enumerate((dq_ref, *both)):
        total += dot_bt(ref[here, :], w_ref[:, j * D : (j + 1) * D])
    n, r = normalize(x_ref[...].astype(F32))
    gin_ref[...] = (gmid_ref[...].astype(F32) + norm_back(total, n, r, gain_ref[0:1, :])).astype(BF)


def last_call(info, x, grads, rims, gmid, w_parts, gain, deps=()):
    n = gmid.shape[0]
    ext = grads[0].shape[0]
    return call(
        last_body,
        [info, x, *grads, *rims, gmid, *w_parts, gain],
        grid=(n // TILE,),
        in_specs=[smem(), rows(TILE, D)] + [full((ext, D))] * 3 + [full((HALF, 2 * D))] * 2 + [rows(TILE, D)]
        + [full((D // 4, 3 * D))] * 4 + [full((8, D))],
        out_specs=[rows(TILE, D)],
        out_shape=[jax.ShapeDtypeStruct((n, D), BF)],
        scratch_shapes=[pltpu.VMEM((D, 3 * D), BF)] + [pltpu.VMEM((ext, D), BF)] * 2,
        megabytes=16,
        deps=deps,
        cost_estimate=cost(7),
        name="last",
    )


def adam(weight, grad, first_old, second, decay_rate):
    new_first = BETA_ONE * first_old + (1.0 - BETA_ONE) * grad
    new_second = BETA_TWO * second + (1.0 - BETA_TWO) * grad * grad
    root = jnp.sqrt(new_second * (1.0 / (1.0 - BETA_TWO**STEP))) + ADAM_EPS
    change = (-LEARN_RATE / (1.0 - BETA_ONE**STEP)) * (new_first / root)
    if decay_rate:
        change = change - (LEARN_RATE * decay_rate) * weight
    return (new_first, new_second, change)


def adam_body(count, *refs):
    grads, (w_ref, m_ref, v_ref, g_ref, nm_ref, nv_ref, st_ref, dots_ref) = refs[:count], refs[count:]
    g = jnp.concatenate([r[...] for r in grads], axis=1).astype(F32)
    w = w_ref[...].astype(F32)
    g_ref[...] = g
    nm_ref[...], nv_ref[...], st_ref[...] = adam(w, g, m_ref[...], v_ref[...], WEIGHT_DECAY)

    @pl.when(pl.program_id(0) == 0)
    def _():
        dots_ref[...] = jnp.zeros_like(dots_ref)

    dots_ref[...] += jnp.sum(w * g, axis=1, keepdims=True)


def adam_call(grads, weight, first, second, megabytes=60):
    r, width = weight.shape
    own = pl.BlockSpec((r, D), lambda j: (0, j))
    out = jax.ShapeDtypeStruct((r, width), F32)
    return pl.pallas_call(
        functools.partial(adam_body, len(grads)),
        grid=(width // D,),
        in_specs=[pl.BlockSpec((r, wide), at) for _, wide, at in grads] + [own] * 3,
        out_specs=[own] * 4 + [full((r, 1))],
        out_shape=[out] * 4 + [jax.ShapeDtypeStruct((r, 1), F32)],
        compiler_params=pltpu.CompilerParams(dimension_semantics=("arbitrary",), vmem_limit_bytes=megabytes * 1024 * 1024),
        cost_estimate=cost(3),
        name="adam",
    )(*[g for g, _, _ in grads], weight, first, second)


CORES = [(0, 1), (1, 0), (2, 3), (3, 2)]
CHIPS = [(0, 2), (2, 0), (1, 3), (3, 1)]


def to_core(a):
    return lax.ppermute(a, "wshard", CORES)


def to_chip(a):
    return lax.ppermute(a, "wshard", CHIPS)


def copy_body(*refs):
    for a, b in zip(refs[: len(refs) // 2], refs[len(refs) // 2 :]):
        b[...] = a[...]


def copies(arrays):
    return pl.pallas_call(
        copy_body,
        grid=(1,),
        in_specs=[full(a.shape) for a in arrays],
        out_specs=[full(a.shape) for a in arrays],
        out_shape=[jax.ShapeDtypeStruct(a.shape, a.dtype) for a in arrays],
        compiler_params=pltpu.CompilerParams(vmem_limit_bytes=8 * 1024 * 1024),
        name="copies",
    )(*arrays)


def after(a, first):
    return together_at([a, first])[0]


class Chain:
    def __init__(self, keep, send):
        count = lax.axis_size("seq")
        whole = []
        shift = 2
        while 1 << shift < count:
            whole.append(("whole", shift))
            shift += 1
        self.plan = [("core", 0), ("one", 0), ("two", 0), ("half", 1)] + whole + [("back", 1), ("end", 0)]
        self.at = 0
        self.kept = [keep]
        self.sends = [send]
        self.rows, self.columns = keep.shape[1:]

    def done(self):
        return self.at == len(self.plan)

    def start(self):
        if self.done():
            return
        kind, shift = self.plan[self.at]

        def along_seq(a):
            count = lax.axis_size("seq")
            return lax.ppermute(a, "seq", [(i, i ^ (1 << shift)) for i in range(count)])

        if kind == "core":
            ways = [to_core]
        elif kind == "one":
            ways = [to_chip, along_seq]
        elif kind == "two":
            ways = [along_seq, to_chip]
        else:
            ways = [along_seq]
        self.flights = [way(a) for way, a in zip(ways, self.sends)]

    def landing(self):
        kind, _ = self.plan[self.at]
        q, c = self.rows // 4, self.columns
        shapes = {
            "core": [(2 * q, c), (2, q, c)] * 2, "one": [(q, c)] * 4, "two": [(q, c)] * 2,
            "half": [(q, c)], "whole": [(q, c)], "back": [(2 * q, c)], "end": [(4 * q, c)],
        }[kind]

        def body(info_ref, ins, outs):
            bx, by, bz = (info_ref[0] >> 1) & 1, info_ref[1] & 1, (info_ref[1] >> 1) & 1

            def at(i, base=0):
                return pl.ds(pl.multiple_of(base + i * q, 16), q)

            if kind == "core":
                keep, got = ins
                for out, i in ((outs[0], bx), (outs[2], 1 - bx)):
                    out[...] = sum_of(keep[i, : 2 * q, :], got[i, : 2 * q, :])
                for out, i in ((outs[1], by), (outs[3], 1 - by)):
                    out[...] = sum_of(keep[:, at(i, 2 * q), :], got[:, at(i, 2 * q), :])
            elif kind == "one":
                for out, i in ((outs[0], by), (outs[2], 1 - by)):
                    out[...] = sum_of(ins[0][at(i), :], ins[2][at(i), :])
                for out, i in ((outs[1], bx), (outs[3], 1 - bx)):
                    out[...] = sum_of(ins[1][i], ins[3][i])
            elif kind == "two":
                first = sum_of(ins[0][...], ins[2][...])
                second = sum_of(ins[1][...], ins[3][...])
                put_by(bz, outs, first, second, slice(0, c))
            elif kind == "back":
                outs[0][at(bz), :] = ins[0][...]
                outs[0][at(1 - bz), :] = ins[1][...]
            elif kind == "end":
                for half in range(2):
                    outs[0][at(by, 2 * q * half), :] = ins[0][half * q : (half + 1) * q, :]
                    outs[0][at(1 - by, 2 * q * half), :] = ins[1][half * q : (half + 1) * q, :]
            else:
                outs[0][...] = sum_of(ins[0][...], ins[1][...])

        return self.kept + self.flights, shapes, body

    def landed(self, outs):
        kind, _ = self.plan[self.at]
        self.at += 1
        pairs = {"core": 2, "one": 2, "two": 1}.get(kind)
        self.kept = outs[:pairs] if pairs else outs
        self.sends = outs[pairs:] if pairs else outs


def put_by(bit, outs, first, second, cols):
    @pl.when(bit == 0)
    def _():
        outs[0][:, cols] = first
        outs[1][:, cols] = second

    @pl.when(bit != 0)
    def _():
        outs[0][:, cols] = second
        outs[1][:, cols] = first


class Joined(Chain):
    def __init__(self, first, second):
        self.both = (first, second)
        self.plan, self.at, self.rows = second.plan, second.at, second.rows
        self.columns = first.columns + second.columns

    def landing(self):
        if self.both is None:
            return Chain.landing(self)
        plans = [c.landing() for c in self.both]
        q = self.rows // 4

        def body(info_ref, ins, outs):
            bz = (info_ref[1] >> 1) & 1
            start = 0
            for i, c in enumerate(self.widths):
                a = ins[4 * i : 4 * i + 4]
                first = sum_of(a[0][...], a[2][...])
                second = sum_of(a[1][...], a[3][...])
                put_by(bz, outs, first, second, slice(start, start + c))
                start += c

        self.widths = [c.columns for c in self.both]
        return plans[0][0] + plans[1][0], [(q, self.columns)] * 2, body

    def landed(self, outs):
        self.both = None
        Chain.landed(self, outs)


def sum_of(a, b):
    return (a.astype(F32) + b.astype(F32)).astype(BF)


def nothing(*refs):
    pass


def together_at(arrays, seen=()):
    hbm = pl.BlockSpec(memory_space=pl.ANY)
    return pl.pallas_call(
        nothing,
        in_specs=[hbm] * (len(arrays) + len(seen)),
        out_specs=[hbm] * len(arrays),
        out_shape=[jax.ShapeDtypeStruct(a.shape, a.dtype) for a in arrays],
        input_output_aliases={i: i for i in range(len(arrays))},
        compiler_params=pltpu.CompilerParams(vmem_limit_bytes=1024 * 1024),
        name="boundary",
    )(*arrays, *seen)


def boundary(info, token, landing=(), starting=(), also=()):
    landing = [c for c in landing if not c.done()]
    plans = [c.landing() for c in landing]
    args = [info] + [a for p in plans for a in p[0]]
    through = [c.sends[0] for c in starting] + list(also) + [token]
    shapes = [jax.ShapeDtypeStruct(t, BF) for p in plans for t in p[1]]
    count = len(args)

    def body(*refs):
        ins = list(refs[1:count])
        outs = list(refs[count + len(through) :])
        for operands, shapes_i, land in plans:
            land(refs[0], [ins.pop(0) for _ in operands], [outs.pop(0) for _ in shapes_i])

    hbm = pl.BlockSpec(memory_space=pl.ANY)
    outs = pl.pallas_call(
        body,
        grid=(1,),
        in_specs=[smem()] + [full(a.shape) for a in args[1:]] + [hbm] * len(through),
        out_specs=[full(t.shape) for t in shapes] + [hbm] * len(through),
        out_shape=shapes + [jax.ShapeDtypeStruct(a.shape, a.dtype) for a in through],
        input_output_aliases={count + i: len(shapes) + i for i in range(len(through))},
        compiler_params=pltpu.CompilerParams(vmem_limit_bytes=16 * 1024 * 1024),
        cost_estimate=cost(1),
        name="land",
    )(*args, *through)
    outs = list(outs)
    for c, p in zip(landing, plans):
        c.landed([outs.pop(0) for _ in p[1]])
    for c in starting:
        c.sends = [outs.pop(0)]
    waits = [outs[-1]]
    for c in landing + list(starting):
        waits.append(c.sends[0])
        c.start()
    return outs[:-1], tuple(waits)


def neighbours(count):
    up = [(i, i + 1) for i in range(count - 1)]
    return up, [(j, i) for i, j in up]


def shards(
    hidden_in, cotangent, block_seq, block_place, attn_in, attn_out, ffn_in, ffn_out, norm_attn, norm_ffn,
    m_attn_in, m_attn_out, m_ffn_in, m_ffn_out, m_norm_attn, m_norm_ffn,
    v_attn_in, v_attn_out, v_ffn_in, v_ffn_out, v_norm_attn, v_norm_ffn,
):
    x = hidden_in[0]
    cot = cotangent[0]
    n = x.shape[0]
    ext = n + 2 * HALF
    w = lax.axis_index("wshard")
    count = lax.axis_size("seq")
    at = lax.axis_index("seq")
    up, down = neighbours(count)

    far = to_chip(attn_in)
    mate = to_core(attn_in)
    gain_own = jnp.stack([norm_attn, norm_ffn])
    gain_far, gain_mate = to_chip(gain_own), to_core(gain_own)
    x_low, x_high = lax.ppermute(x[n - HALF :], "seq", up), lax.ppermute(x[:HALF], "seq", down)
    attn_out_own, down_a, down_b = copies([attn_out, ffn_out[: D // 4], ffn_out[D // 4 :]])
    info = jnp.concatenate([jnp.stack([w, at]).astype(jnp.int32), block_seq[0], block_place[0]])
    some, rest = D // 4, FF // 4 - D // 4

    def units(start, first, size):
        return [ffn_in[:, start + s * (FF // 4) + first :][:, :size] for s in range(4)]

    in_g = jnp.concatenate(units(0, 0, some), axis=1)
    in_u = jnp.concatenate(units(FF, 0, some), axis=1)
    in_b = jnp.concatenate(units(0, some, rest) + units(FF, some, rest), axis=1)
    out_mate, g_mate, u_mate, da_mate, db_mate, b_mate = (to_core(a) for a in (attn_out_own, in_g, in_u, down_a, down_b, in_b))

    g_half = lax.dynamic_slice_in_dim(in_g, (at & 1) * (D // 8), D // 8, 0)
    (token,) = together_at(
        [jnp.zeros((8, 128), F32)], [x_low, x_high, info, mate, out_mate, g_mate, u_mate, da_mate, db_mate, b_mate]
    )
    far, g_half, attn_out_own, token = together_at([far, g_half, attn_out_own, token], [gain_far, gain_mate])
    farmate = to_core(far)
    out_far = to_chip(attn_out_own)
    g_mine = to_chip(g_half)
    attn_parts = attn_in, mate, far, farmate
    gains = gain_own, gain_mate, gain_far, to_core(gain_far)
    nt, q, k, v, cos, sin, gain, token = qkv_call(info, x, x_low, x_high, gains, attn_parts)
    out_far, g_mine, in_u, token = together_at([out_far, g_mine, in_u, token])
    out_farmate = to_core(out_far)
    out_farmate, in_u, down_a, token = together_at([out_farmate, in_u, down_a, token])
    u_far = to_chip(in_u)
    da_far = to_chip(down_a)
    g_other = lax.ppermute(g_mine, "seq", [(i, i ^ 1) for i in range(count)])
    out_parts = attn_out, out_mate, out_far, out_farmate
    mixed, middle, n2, out_w, lse, token = attend_call(info, q, k, v, x, out_parts, gain, deps=(token,))
    g_other, u_far, da_far, in_b, down_b, token = together_at([g_other, u_far, da_far, in_b, down_b, token])
    b_far = to_chip(in_b)
    db_far = to_chip(down_b)
    gate_parts = in_g, g_mate, g_mine, g_other, to_core(g_mine), to_core(g_other)
    up_parts = in_u, u_mate, u_far, to_core(u_far)
    down_parts = down_a, da_mate, da_far, to_core(da_far)
    pout, pgn, keep, send, token = ffn_a_call(info, n2, cot, gate_parts, up_parts, down_parts, deps=(token,))
    chain_a = Chain(keep, send)
    (b_far, db_far), deps = boundary(info, token, (), (chain_a,), (b_far, db_far))
    b_parts = in_b, b_mate, b_far, to_core(b_far)
    db_parts = down_b, db_mate, db_far, to_core(db_far)
    _, deps = boundary(info, deps[0], (chain_a,))
    block_out, gmid, gmix, keep, send, token = ffn_b_call(
        info, n2, cot, b_parts, db_parts, pout, pgn, middle, mixed, out_w, gain, deps=deps
    )
    chain_b = Chain(keep, send)
    grads, pieces = (), ()

    def back(p, at, width, deps):
        nonlocal grads, pieces
        if at == 0:
            pieces = ()
        out = attend_back_call(p, at, width, info, q, k, v, gmix, mixed, lse, cos, sin, nt, grads, pieces, deps)
        grads, pieces = out[:3], out[3:5]
        return out[5]

    _, deps = boundary(info, token, (chain_a,), (chain_b,))
    token = back(0, 0, 2 * QUAD, deps)
    _, deps = boundary(info, token, (chain_a, chain_b))
    token = back(1, 1, 2 * QUAD, deps)
    chain_c = Chain(*pieces)
    _, deps = boundary(info, token, (chain_a, chain_b), (chain_c,))
    token = back(2, 0, QUAD, deps)
    chain_d = Chain(*pieces)
    _, deps = boundary(info, token, (chain_a, chain_b, chain_c), (chain_d,))
    rims = [jnp.concatenate([a[r] for a in grads[1:]], axis=1) for r in (slice(0, HALF), slice(n + HALF, ext))]
    rims, deps = boundary(info, deps[0], (chain_b, chain_c, chain_d), (), rims)
    rims = lax.ppermute(rims[1], "seq", up), lax.ppermute(rims[0], "seq", down)
    rims, deps = boundary(info, deps[0], (chain_a, chain_b, chain_d), (), rims)
    grad_in, token = last_call(info, x, grads, rims, gmid, attn_parts, gain, deps=deps)
    chains = (chain_a, chain_b, Joined(chain_c, chain_d))
    sum_b = late_b = sum_a = None
    while not all(c.done() for c in chains):
        also = ()
        if chain_a.done() and chain_b.done():
            also = (chain_b.kept[0], chain_a.kept[0])
        through, deps = boundary(info, token, chains, (), also)
        token = deps[0]
        if also:
            chain_b.kept, chain_a.kept = through[:1], through[1:2]
            sum_b = through[0] if sum_b is None else sum_b
            if not chains[2].done():
                late_b, sum_a = through
    sum_c = chains[2].kept[0]

    r = D // 4

    def blocks(a, *at):
        return jnp.concatenate([a[i * r : (i + 1) * r] for i in at], axis=1)

    ga, gb = blocks(sum_a, 0, 1), late_b[:r]
    ua, ub = blocks(sum_a, 2, 3), late_b[r : 2 * r]
    g_ffn_in = jnp.concatenate(
        [t for a, b in ((ga, gb), (ua, ub)) for s in range(4)
         for t in (a[:, s * some : (s + 1) * some], b[:, s * rest : (s + 1) * rest])], axis=1
    )
    g_ffn_out = jnp.concatenate(
        [blocks(sum_a, 4, 5), jnp.concatenate([sum_b[4 * r : 4 * r + rest], sum_b[4 * r + rest :]], axis=1)], axis=0
    )
    res_ffn_in = adam_call([(g_ffn_in, D, lambda j: (0, j))], ffn_in, m_ffn_in, v_ffn_in)
    res_attn_out = adam_call([(blocks(sum_b, 2, 3), D, lambda j: (0, j))], attn_out, m_attn_out, v_attn_out)
    res_ffn_out = adam_call([(g_ffn_out, D, lambda j: (0, j))], ffn_out, m_ffn_out, v_ffn_out)
    res_attn_in = adam_call([(sum_c, D, lambda j: (j, 0))], attn_in, m_attn_in, v_attn_in, 20)
    results = [res_attn_in, res_attn_out, res_ffn_in, res_ffn_out]
    for res, own_gain, m, v_ in ((res_attn_in, norm_attn, m_norm_attn, v_norm_attn), (res_ffn_in, norm_ffn, m_norm_ffn, v_norm_ffn)):
        wide = own_gain.astype(F32)
        g = res[4][:, 0] / wide
        results.append((g,) + adam(wide, g, m, v_, 0.0))
    return (block_out[None], grad_in[None]) + tuple(res[i] for i in range(4) for res in results)


def solution(mesh):
    big = P("wshard", "seq", None)
    mat = P("wshard", None)
    vec = P("wshard")
    group = (mat, mat, mat, mat, vec, vec)
    in_specs = (big, big, mat, mat) + group * 3
    out_specs = (big, big) + group * 4
    return jax.shard_map(shards, mesh=mesh, in_specs=in_specs, out_specs=out_specs, check_vma=False)
```

time: 282 us -> 244 us (0.87)
  waiting for transfers between devices: 90.9 us -> 46.5 us
  starting transfers between devices: 52.2 us -> 62 us
  other arithmetic: 11.1 us -> 6.32 us
  between operations: 4.93 us -> 1.64 us
    ppermute x27 -> x23, waiting for transfers between devices: 67 us -> 32.9 us  [the longest x20 32.9 us: along_seq(): return lax.ppermute(a, 'seq', [(i, i ^ 1 << shift) for i in range(count)])]
    ppermute x7 -> x16, starting transfers between devices: 8.32 us -> 17.9 us  [to_chip(): return lax.ppermute(a, 'wshard', CHIPS)]
    ppermute x7 -> x16, waiting for transfers between devices: 16.3 us -> 9.05 us  [to_chip(): return lax.ppermute(a, 'wshard', CHIPS)]
    ppermute x1, waiting for transfers between devices: 5.31 us -> 0.01 us  [shards(): lax.ppermute(rims[1], 'seq', up)]
    pallas_call x11 -> x10, Pallas kernels: 15.8 us -> 18.7 us  [the longest x4 18.7 us: adam_call(): pl.pallas_call(functools.partial(adam_body, len(grads)), grid=(width // D...]
    unnamed x64 -> x60, local copies, waits for them, and re-layouts: 4.39 us -> 6.69 us
    ppermute x27 -> x23, starting transfers between devices: 36 us -> 35.3 us  [the longest x20 27 us: along_seq(): return lax.ppermute(a, 'seq', [(i, i ^ 1 << shift) for i in range(count)])]
    pallas_call x12 -> x13, Pallas kernels: 9.84 us -> 10.1 us  [boundary(): pl.pallas_call(body, grid=(1,), in_specs=[smem()] + [full(a.shape) for a...]
  transfers between devices with their start and end apart: 50 -> 62, of which waited for: 18 -> 19; matrix products, arithmetic and copies ran while one was open for 7% -> 6% of each run, Pallas kernels for 32% -> 39%
where the time goes in v3:
time: 244 us; the launch traced here: 241 us
  Pallas kernels  106 us (43%)
  starting transfers between devices  62 us (25%)
  waiting for transfers between devices  46.5 us (19%)
  local copies, waits for them, and re-layouts  17.9 us (7%)
  other arithmetic  6.32 us (3%)
    pallas_call x8, Pallas kernels, call(): pl.pallas_call(wrapped, in_specs=list(in_specs) + [pl.BlockSpec(memory_sp...  77.5 us
    ppermute x20, waiting for transfers between devices, along_seq(): return lax.ppermute(a, 'seq', [(i, i ^ 1 << shift) for i in range(count)])  32.9 us
    ppermute x20, starting transfers between devices, along_seq(): return lax.ppermute(a, 'seq', [(i, i ^ 1 << shift) for i in range(count)])  27 us
    pallas_call x4, Pallas kernels, adam_call(): pl.pallas_call(functools.partial(adam_body, len(grads)), grid=(width // D...  18.7 us
    ppermute x16, starting transfers between devices, to_chip(): return lax.ppermute(a, 'wshard', CHIPS)  17.9 us
    pallas_call x13, Pallas kernels, boundary(): pl.pallas_call(body, grid=(1,), in_specs=[smem()] + [full(a.shape) for a...  10.1 us
    ppermute x16, waiting for transfers between devices, to_chip(): return lax.ppermute(a, 'wshard', CHIPS)  9.05 us
    unnamed x60, local copies, waits for them, and re-layouts  6.69 us
  transfers between devices with their start and end apart: 62, of which 19 were waited for; matrix products, arithmetic and copies ran while one was open for 6% of the time, Pallas kernels for 39%

profile of v3, /device:TPU:0, one launch (start us, length us, event | category | flops | bytes accessed | tf_op | source)
XLA Modules:
  0.0 240.7 jit_solution(6463695940933901372)
XLA Ops:
  0.7 3.0 %collective-permute-start.6 = (bf16[192,2304]{1,0:T(8,128)(2,1)}, bf16[192,2304]{1,0:T(8,128)(2,1)S(1)}, u32[]{:S(2)}, u32[]{:S(2)}) collective-permute-start(bf16[192,2304]{1,0:T(8,128)(2,1)} %refs_1_.4), channel_id=1, source_target_pairs={{0,2},{2,0},{1,3},{3,1},{4,6},{6,4},{5,7},{7,5},{8,10},{10,8},{9,1... | collective-permute-start | bytes 2654216 | tf_op jit(solution)/shard_map/ppermute | solution.py:599
  4.6 1.3 collective-permute-start.1
  5.9 4.6 %collective-permute-start = (bf16[64,768]{1,0:T(8,128)(2,1)S(1)}, bf16[64,768]{1,0:T(8,128)(2,1)S(1)}, u32[]{:S(2)}, u32[]{:S(2)}) collective-permute-start(bf16[64,768]{1,0:T(8,128)(2,1)S(1)} %get-tuple-element.357), channel_id=1, source_target_pairs={{0,4},{4,8},{8,12},{12,16},{16,20},{20,24},{24,28},{1,5},{5,9},{9,... | collective-permute-start | bytes 294920 | tf_op jit(solution)/shard_map/ppermute | solution.py:832
  11.4 1.0 slice.202.refs_1_
  13.5 1.1 fusion.11
  17.9 1.1 concatenate.36.refs_3_
  19.1 1.2 pad_maximum_fusion.refs_3_
  21.0 1.2 pad_maximum_fusion.1.refs_2_
  23.9 2.4 collective-permute-done.3.refs_4_.refs_6_
  27.1 1.8 collective-permute-start.14
  29.0 7.7 %qkv.1 = (bf16[768,1152]{1,0:T(8,128)(2,1)S(1)}, bf16[1152,768]{1,0:T(8,128)(2,1)S(1)}, bf16[1152,768]{1,0:T(8,128)(2,1)S(1)}, bf16[1152,768]{1,0:T(8,128)(2,1)S...) custom-call(s32[18]{0:T(128)S(1)} %pad_add_fusion.refs_3_.refs_0_, ...), custom_call_target="tpu_custom_call" | custom-call | flops 9900000256 | tf_op jit(solution)/shard_map/qkv/pallas_call | solution.py:57
  36.7 2.4 collective-permute-done.14.refs_0_
  39.1 2.4 %collective-permute-start.17 = (bf16[96,768]{1,0:T(8,128)(2,1)S(1)}, bf16[96,768]{1,0:T(8,128)(2,1)S(1)}, u32[]{:S(2)}, u32[]{:S(2)}) collective-permute-start(bf16[96,768]{1,0:T(8,128)(2,1)S(1)} %get-tuple-element.202.refs_5_), channel_id=1, source_target_pairs={{0,4},{4,0},{8,12},{12,8},{16,20},{20,16},{24,28},{28,24},{1,5},{5... | collective-permute-start | bytes 442376 | tf_op jit(solution)/shard_map/ppermute | solution.py:861
  42.0 1.5 collective-permute-start.19
  43.5 10.6 %attend.1 = (bf16[1024,768]{1,0:T(8,128)(2,1)S(1)}, bf16[1024,768]{1,0:T(8,128)(2,1)S(1)}, bf16[1024,768]{1,0:T(8,128)(2,1)S(1)}, bf16[768,768]{1,0:T(8,128)(2,1...) custom-call(s32[18]{0:T(128)S(1)} %pad_add_fusion.refs_3_.refs_0_, ...), custom_call_target="tpu_custom_call" | custom-call | flops 12099999744 | tf_op jit(solution)/shard_map/attend/pallas_call | solution.py:57
  54.1 2.8 %collective-permute-done.19.refs_2_ = bf16[192,768]{1,0:T(8,128)(2,1)S(1)} collective-permute-done((bf16[192,768]{1,0:T(8,128)(2,1)S(1)}, bf16[192,768]{1,0:T(8,128)(2,1)S(1)}, u32[]{:S(2)}, u32[]{:S(2)}) %collective-permute-start.19) | collective-permute-done | bytes 294944 | tf_op jit(solution)/shard_map/ppermute | solution.py:599
  60.0 17.3 %ffn_a.1 = (bf16[1024,768]{1,0:T(8,128)(2,1)S(1)}, bf16[1024,768]{1,0:T(8,128)(2,1)S(1)}, bf16[2,1152,384]{2,1,0:T(8,128)(2,1)S(1)}, bf16[2,1152,384]{2,1,0:T(8,128)(2,1)S(1)}, f32[8,128]{1,0:T(8,128)S(1)}) custom-call(s32[18]{0:T(128)S(1)} %pad_add_fusion.refs_3_.refs_0_, bf16[1024,768]{1,0:T(8,128)(2,1)S(1)} %get-tuple-element.201.refs_1_, ...), custom_call_target="tpu_custom_call" | custom-call | flops 19800000512 | tf_op jit(solution)/shard_map/ffn_a/pallas_call | solution.py:57
  78.5 3.1 %collective-permute-done.28.refs_2_ = bf16[2,1152,384]{2,1,0:T(8,128)(2,1)S(1)} collective-permute-done((bf16[2,1152,384]{2,1,0:T(8,128)(2,1)S(1)}, bf16[2,1152,384]{2,1,0:T(8,128)(2,1)S(1)}, u32[]{:S(2)}, u32[]{:S(2)}) %collective-permute-start.28) | collective-permute-done | bytes 1769504 | tf_op jit(solution)/shard_map/ppermute | solution.py:595
  81.7 1.0 land.14
  82.6 1.5 collective-permute-start.30
  84.2 1.2 collective-permute-start.29
  85.4 14.5 %ffn_b.1 = (bf16[1024,768]{1,0:T(8,128)(2,1)}, bf16[1024,768]{1,0:T(8,128)(2,1)S(1)}, bf16[1024,768]{1,0:T(8,128)(2,1)S(1)}, bf16[2,960,384]{2,1,0:T(8,128)(2,1)...) custom-call(s32[18]{0:T(128)S(1)} %pad_add_fusion.refs_3_.refs_0_, ...), custom_call_target="tpu_custom_call" | custom-call | flops 15399999488 | tf_op jit(solution)/shard_map/ffn_b/pallas_call | solution.py:57
  102.2 6.6 %attend_back.3 = (bf16[1152,768]{1,0:T(8,128)(2,1)S(1)}, bf16[1152,768]{1,0:T(8,128)(2,1)S(1)}, bf16[1152,768]{1,0:T(8,128)(2,1)S(1)}, bf16[2,576,512]{2,1,0:T(8...) custom-call(s32[18]{0:T(128)S(1)} %pad_add_fusion.refs_3_.refs_0_, ...), custom_call_target="tpu_custom_call" | custom-call | flops 4400000000 | tf_op jit(solution)/shard_map/attend_back/pallas_call | solution.py:57
  109.2 1.2 land.16
  110.4 1.6 collective-permute-start.34
  112.1 1.1 collective-permute-start.36
  113.2 1.2 collective-permute-start.35
  114.4 6.5 %attend_back.4 = (bf16[1152,768]{1,0:T(8,128)(2,1)S(1)}, bf16[1152,768]{1,0:T(8,128)(2,1)S(1)}, bf16[1152,768]{1,0:T(8,128)(2,1)S(1)}, bf16[2,576,512]{2,1,0:T(8...) custom-call(s32[18]{0:T(128)S(1)} %pad_add_fusion.refs_3_.refs_0_, ...), custom_call_target="tpu_custom_call", output_to_operand_aliasing={{0}: (10, {}), {1}: (11, {}), {2}: (12, {}), {3}: (13, {}),... | custom-call | flops 4400000000 | tf_op jit(solution)/shard_map/attend_back/pallas_call | solution.py:57
  121.8 1.2 collective-permute-done.35.refs_5_
  123.9 1.3 collective-permute-start.39
  125.7 1.7 collective-permute-start.37
  127.3 6.8 %attend_back.5 = (bf16[1152,768]{1,0:T(8,128)(2,1)S(1)}, bf16[1152,768]{1,0:T(8,128)(2,1)S(1)}, bf16[1152,768]{1,0:T(8,128)(2,1)S(1)}, bf16[2,576,256]{2,1,0:T(8...) custom-call(s32[18]{0:T(128)S(1)} %pad_add_fusion.refs_3_.refs_0_, ...), custom_call_target="tpu_custom_call", output_to_operand_aliasing={{0}: (10, {}), {1}: (11, {}), {2}: (12, {})} | custom-call | flops 4400000000 | tf_op jit(solution)/shard_map/attend_back/pallas_call | solution.py:57
  134.1 4.3 %collective-permute-done.37.refs_2_ = bf16[288,384]{1,0:T(8,128)(2,1)S(1)} collective-permute-done((bf16[288,384]{1,0:T(8,128)(2,1)S(1)}, bf16[288,384]{1,0:T(8,128)(2,1)S(1)}, u32[]{:S(2)}, u32[]{:S(2)}) %collective-permute-start.37) | collective-permute-done | bytes 221216 | tf_op jit(solution)/shard_map/ppermute | solution.py:647
  138.4 1.0 land.18
  140.4 1.5 collective-permute-start.44
  142.0 2.0 collective-permute-start.41
  144.0 5.5 %collective-permute-done.42.refs_2_ = bf16[240,384]{1,0:T(8,128)(2,1)S(1)} collective-permute-done((bf16[240,384]{1,0:T(8,128)(2,1)S(1)}, bf16[240,384]{1,0:T(8,128)(2,1)S(1)}, u32[]{:S(2)}, u32[]{:S(2)}) %collective-permute-start.42) | collective-permute-done | bytes 184352 | tf_op jit(solution)/shard_map/ppermute | solution.py:647
  150.4 3.4 %collective-permute-start.49 = (bf16[64,1536]{1,0:T(8,128)(2,1)S(1)}, bf16[64,1536]{1,0:T(8,128)(2,1)S(1)}, u32[]{:S(2)}, u32[]{:S(2)}) collective-permute-start(bf16[64,1536]{1,0:T(8,128)(2,1)S(1)} %get-tuple-element.290), channel_id=1, source_target_pairs={{0,4},{4,8},{8,12},{12,16},{16,20},{20,24},{24,28},{1,5},{5,9},{9,... | collective-permute-start | bytes 589832 | tf_op jit(solution)/shard_map/ppermute | solution.py:901
  153.8 1.3 collective-permute-start.50
  155.1 1.3 collective-permute-start.47
  156.4 2.9 %collective-permute-start.46 = (bf16[240,384]{1,0:T(8,128)(2,1)S(1)}, bf16[240,384]{1,0:T(8,128)(2,1)S(1)}, u32[]{:S(2)}, u32[]{:S(2)}) collective-permute-start(bf16[240,384]{1,0:T(8,128)(2,1)S(1)} %get-tuple-element.285.refs_3_), channel_id=1, source_target_pairs={{0,16},{4,20},{8,24},{12,28},{16,0},{20,4},{24,8},{28,12},{1,17},{... | collective-permute-start | bytes 552968 | tf_op jit(solution)/shard_map/ppermute | solution.py:647
  160.4 2.6 %collective-permute-start.53 = (bf16[144,512]{1,0:T(8,128)(2,1)S(1)}, bf16[144,512]{1,0:T(8,128)(2,1)S(1)}, u32[]{:S(2)}, u32[]{:S(2)}) collective-permute-start(bf16[144,512]{1,0:T(8,128)(2,1)S(1)} %get-tuple-element.303), channel_id=1, source_target_pairs={{0,4},{4,0},{8,12},{12,8},{16,20},{20,16},{24,28},{28,24},{1,5},{5... | collective-permute-start | bytes 442376 | tf_op jit(solution)/shard_map/ppermute | solution.py:647
  163.0 3.4 %collective-permute-done.48.refs_8_ = bf16[2,144,256]{2,1,0:T(8,128)(2,1)S(1)} collective-permute-done((bf16[2,144,256]{2,1,0:T(8,128)(2,1)S(1)}, bf16[2,144,256]{2,1,0:T(8,128)(2,1)S(1)}, u32[]{:S(2)}, u32[]{:S(2)}) %collective-permute-start.48) | collective-permute-done | bytes 147488 | tf_op jit(solution)/shard_map/ppermute | solution.py:647
  166.4 1.2 collective-permute-start.54
  167.6 1.6 collective-permute-done.46.refs_4_
  169.9 1.3 collective-permute-start.56
  171.9 1.3 collective-permute-start.51
  173.2 7.6 %last.1 = (bf16[1024,768]{1,0:T(8,128)(2,1)}, f32[8,128]{1,0:T(8,128)S(1)}) custom-call(s32[18]{0:T(128)S(1)} %pad_add_fusion.refs_3_.refs_0_, bf16[1024,768]{1,0:T(8,128)(2,1)S(1)} %bitcast.14, bf16[1152,768]{1,0:T(8,128)(2,1)S(1)} %get-tuple-element.266.refs_2_, bf16[1152,768]{1,0:T(8,128)(2,1)S(1)} %get-tuple-element.267.refs_3_, ...), custom_call_target="tpu_custom_call" | custom-call | flops 7699999744 | tf_op jit(solution)/shard_map/last/pallas_call | solution.py:57
  180.9 1.7 collective-permute-done.51.refs_2_
  183.4 1.1 collective-permute-start.57
  184.5 1.0 collective-permute-start.58
  185.5 5.0 %collective-permute-done.58.refs_4_ = bf16[144,768]{1,0:T(8,128)(2,1)S(1)} collective-permute-done((bf16[144,768]{1,0:T(8,128)(2,1)S(1)}, bf16[144,768]{1,0:T(8,128)(2,1)S(1)}, u32[]{:S(2)}, u32[]{:S(2)}) %collective-permute-start.58) | collective-permute-done | bytes 221216 | tf_op jit(solution)/shard_map/ppermute | solution.py:647
  191.7 3.7 %collective-permute-start.59 = (bf16[144,768]{1,0:T(8,128)(2,1)S(1)}, bf16[144,768]{1,0:T(8,128)(2,1)S(1)}, u32[]{:S(2)}, u32[]{:S(2)}) collective-permute-start(bf16[144,768]{1,0:T(8,128)(2,1)S(1)} %get-tuple-element.313.refs_1_), channel_id=1, source_target_pairs={{0,16},{4,20},{8,24},{12,28},{16,0},{20,4},{24,8},{28,12},{1,17},{... | collective-permute-start | bytes 663560 | tf_op jit(solution)/shard_map/ppermute | solution.py:647
  195.3 8.0 %collective-permute-done.59.refs_2_ = bf16[144,768]{1,0:T(8,128)(2,1)S(1)} collective-permute-done((bf16[144,768]{1,0:T(8,128)(2,1)S(1)}, bf16[144,768]{1,0:T(8,128)(2,1)S(1)}, u32[]{:S(2)}, u32[]{:S(2)}) %collective-permute-start.59) | collective-permute-done | bytes 221216 | tf_op jit(solution)/shard_map/ppermute | solution.py:647
  204.9 3.2 %adam.5 = (f32[192,768]{1,0:T(8,128)}, f32[192,768]{1,0:T(8,128)}, f32[192,768]{1,0:T(8,128)}, f32[192,768]{1,0:T(8,128)}, f32[192,1]{1,0:T(8,128)}) custom-call(bf16[192,768]{1,0:T(8,128)(2,1)} %pad_maximum_fusion.2.refs_0_, bf16[192,768]{1,0:T(8,128)(2,1)} %refs_1_.5, f32[192,768]{1,0:T(8,128)} %refs_2_.5, f32[192,768]{1,0:T(8,128)} %refs_3_.5), custom_call_target="tpu_custom_call" | custom-call | flops 3300000000 | tf_op jit(solution)/shard_map/adam/pallas_call | solution.py:578
  208.8 1.6 collective-permute-done.60.refs_2_
  212.6 1.9 collective-permute-start.61
  214.6 2.2 concatenate.40.refs_0_
  216.8 7.1 %adam.6 = (f32[192,2304]{1,0:T(8,128)}, f32[192,2304]{1,0:T(8,128)}, f32[192,2304]{1,0:T(8,128)}, f32[192,2304]{1,0:T(8,128)}, f32[192,1]{1,0:T(8,128)}) custom-call(bf16[192,2304]{1,0:T(8,128)(2,1)} %concatenate.40.refs_0_, bf16[192,2304]{1,0:T(8,128)(2,1)} %refs_1_.6, f32[192,2304]{1,0:T(8,128)} %refs_2_.6, f32[192,2304]{1,0:T(8,128)} %refs_3_.6), custom_call_target="tpu_custom_call" | custom-call | flops 3300000000 | tf_op jit(solution)/shard_map/adam/pallas_call | solution.py:578
  223.9 1.0 reduce.1
  226.4 4.1 %adam.7 = (f32[288,768]{1,0:T(8,128)}, f32[288,768]{1,0:T(8,128)}, f32[288,768]{1,0:T(8,128)}, f32[288,768]{1,0:T(8,128)}, f32[288,1]{1,0:T(8,128)}) custom-call(bf16[288,768]{1,0:T(8,128)(2,1)} %maximum_maximum_fusion.refs_0_, bf16[288,768]{1,0:T(8,128)(2,1)} %refs_1_.7, f32[288,768]{1,0:T(8,128)} %refs_2_.7, f32[288,768]{1,0:T(8,128)} %refs_3_.7), custom_call_target="tpu_custom_call" | custom-call | flops 3300000000 | tf_op jit(solution)/shard_map/adam/pallas_call | solution.py:578
  231.2 1.0 copy-done.15
  234.2 1.2 copy-done.11
  235.4 4.3 %adam.4 = (f32[192,2304]{1,0:T(8,128)}, f32[192,2304]{1,0:T(8,128)}, f32[192,2304]{1,0:T(8,128)}, f32[192,2304]{1,0:T(8,128)}, f32[192,1]{1,0:T(8,128)S(1)}) custom-call(bf16[576,768]{1,0:T(8,128)(2,1)S(1)} %get-tuple-element.325.refs_0_, bf16[192,2304]{1,0:T(8,128)(2,1)S(1)} %copy-done.11, f32[192,2304]{1,0:T(8,128)S(1)} %copy-done.7, f32[192,2304]{1,0:T(8,128)S(1)} %copy-done.8), custom_call_target="tpu_custom_call" | custom-call | flops 3300000000 | tf_op jit(solution)/shard_map/adam/pallas_call | solution.py:578
  (180 shorter events, 35.0 us)
Async XLA Ops:
  0.7 25.7 %collective-permute-start.6 = (bf16[192,2304]{1,0:T(8,128)(2,1)}, bf16[192,2304]{1,0:T(8,128)(2,1)S(1)}, u32[]{:S(2)}, u32[]{:S(2)}) collective-permute-start(bf16[192,2304]{1,0:T(8,128)(2,1)} %refs_1_.4), channel_id=1, source_target_pairs={{0,2},{2,0},{1,3},{3,1},{4,6},{6,4},{5,7},{7,5},{8,10},{10,8},{9,1... | collective-permute-start | bytes 2654216 | tf_op jit(solution)/shard_map/ppermute | solution.py:599
  3.7 20.2 %collective-permute-start.5 = (bf16[192,2304]{1,0:T(8,128)(2,1)}, bf16[192,2304]{1,0:T(8,128)(2,1)S(1)}, u32[]{:S(2)}, u32[]{:S(2)}) collective-permute-start(bf16[192,2304]{1,0:T(8,128)(2,1)} %refs_1_.4), channel_id=1, source_target_pairs={{0,1},{1,0},{2,3},{3,2},{4,5},{5,4},{6,7},{7,6},{8,9},{9,8},{10,11... | collective-permute-start | bytes 2654216 | tf_op jit(solution)/shard_map/ppermute | solution.py:595
  4.6 10.0 %collective-permute-start.1 = (bf16[64,768]{1,0:T(8,128)(2,1)S(1)}, bf16[64,768]{1,0:T(8,128)(2,1)S(1)}, u32[]{:S(2)}, u32[]{:S(2)}) collective-permute-start(bf16[64,768]{1,0:T(8,128)(2,1)S(1)} %get-tuple-element.356), channel_id=1, source_target_pairs={{4,0},{8,4},{12,8},{16,12},{20,16},{24,20},{28,24},{5,1},{9,5},{13... | collective-permute-start | bytes 294920 | tf_op jit(solution)/shard_map/ppermute | solution.py:832
  5.9 9.8 %collective-permute-start = (bf16[64,768]{1,0:T(8,128)(2,1)S(1)}, bf16[64,768]{1,0:T(8,128)(2,1)S(1)}, u32[]{:S(2)}, u32[]{:S(2)}) collective-permute-start(bf16[64,768]{1,0:T(8,128)(2,1)S(1)} %get-tuple-element.357), channel_id=1, source_target_pairs={{0,4},{4,8},{8,12},{12,16},{16,20},{20,24},{24,28},{1,5},{5,9},{9,... | collective-permute-start | bytes 294920 | tf_op jit(solution)/shard_map/ppermute | solution.py:832
  13.4 6.9 %collective-permute-start.11 = (bf16[96,768]{1,0:T(8,128)(2,1)S(1)}, bf16[96,768]{1,0:T(8,128)(2,1)S(1)}, u32[]{:S(2)}, u32[]{:S(2)}) collective-permute-start(bf16[96,768]{1,0:T(8,128)(2,1)S(1)} %get-tuple-element.187.refs_4_), channel_id=1, source_target_pairs={{0,1},{1,0},{2,3},{3,2},{4,5},{5,4},{6,7},{7,6},{8,9},{9,8},{10,11... | collective-permute-start | bytes 442376 | tf_op jit(solution)/shard_map/ppermute | solution.py:595
  15.3 5.6 %collective-permute-start.7 = (bf16[192,768]{1,0:T(8,128)(2,1)S(1)}, bf16[192,768]{1,0:T(8,128)(2,1)S(1)}, u32[]{:S(2)}, u32[]{:S(2)}) collective-permute-start(bf16[192,768]{1,0:T(8,128)(2,1)S(1)} %get-tuple-element.185.refs_2_), channel_id=1, source_target_pairs={{0,1},{1,0},{2,3},{3,2},{4,5},{5,4},{6,7},{7,6},{8,9},{9,8},{10,11... | collective-permute-start | bytes 884744 | tf_op jit(solution)/shard_map/ppermute | solution.py:595
  16.4 5.8 %collective-permute-start.10 = (bf16[192,768]{1,0:T(8,128)(2,1)S(1)}, bf16[192,768]{1,0:T(8,128)(2,1)S(1)}, u32[]{:S(2)}, u32[]{:S(2)}) collective-permute-start(bf16[192,768]{1,0:T(8,128)(2,1)S(1)} %get-tuple-element.186.refs_2_), channel_id=1, source_target_pairs={{0,1},{1,0},{2,3},{3,2},{4,5},{5,4},{6,7},{7,6},{8,9},{9,8},{10,11... | collective-permute-start | bytes 884744 | tf_op jit(solution)/shard_map/ppermute | solution.py:595
  20.3 2.4 collective-permute-start.12
  20.9 2.1 collective-permute-start.8
  22.2 1.7 collective-permute-start.9
  22.7 3.6 %collective-permute-start.3 = (bf16[2,192]{1,0:T(2,128)(2,1)S(1)}, bf16[2,192]{1,0:T(2,128)(2,1)S(1)}, u32[]{:S(2)}, u32[]{:S(2)}) collective-permute-start(bf16[2,192]{1,0:T(2,128)(2,1)S(1)} %pad_maximum_fusion.5.refs_4_), channel_id=1, source_target_pairs={{0,2},{2,0},{1,3},{3,1},{4,6},{6,4},{5,7},{7,5},{8,10},{10,8},{9,1... | collective-permute-start | bytes 2312 | tf_op jit(solution)/shard_map/ppermute | solution.py:599
  23.0 3.4 %collective-permute-start.2 = (bf16[2,192]{1,0:T(2,128)(2,1)S(1)}, bf16[2,192]{1,0:T(2,128)(2,1)S(1)}, u32[]{:S(2)}, u32[]{:S(2)}) collective-permute-start(bf16[2,192]{1,0:T(2,128)(2,1)S(1)} %pad_maximum_fusion.5.refs_4_), channel_id=1, source_target_pairs={{0,1},{1,0},{2,3},{3,2},{4,5},{5,4},{6,7},{7,6},{8,9},{9,8},{10,11... | collective-permute-start | bytes 2312 | tf_op jit(solution)/shard_map/ppermute | solution.py:595
  26.4 2.6 %collective-permute-start.13 = (bf16[192,2304]{1,0:T(8,128)(2,1)S(1)}, bf16[192,2304]{1,0:T(8,128)(2,1)S(1)}, u32[]{:S(2)}, u32[]{:S(2)}) collective-permute-start(bf16[192,2304]{1,0:T(8,128)(2,1)S(1)} %get-tuple-element.188.refs_10_), channel_id=1, source_target_pairs={{0,1},{1,0},{2,3},{3,2},{4,5},{5,4},{6,7},{7,6},{8,9},{9,8},{10,11... | collective-permute-start | bytes 2654216 | tf_op jit(solution)/shard_map/ppermute | solution.py:595
  26.4 2.5 %collective-permute-start.4 = (bf16[2,192]{1,0:T(2,128)(2,1)S(1)}, bf16[2,192]{1,0:T(2,128)(2,1)S(1)}, u32[]{:S(2)}, u32[]{:S(2)}) collective-permute-start(bf16[2,192]{1,0:T(2,128)(2,1)S(1)} %collective-permute-done.3.refs_4_.refs_6_), channel_id=1, source_target_pairs={{0,1},{1,0},{2,3},{3,2},{4,5},{5,4},{6,7},{7,6},{8,9},{9,8},{10,11... | collective-permute-start | bytes 2312 | tf_op jit(solution)/shard_map/ppermute | solution.py:595
  26.9 9.8 %collective-permute-start.15 = (bf16[96,768]{1,0:T(8,128)(2,1)S(1)}, bf16[96,768]{1,0:T(8,128)(2,1)S(1)}, u32[]{:S(2)}, u32[]{:S(2)}) collective-permute-start(bf16[96,768]{1,0:T(8,128)(2,1)S(1)} %get-tuple-element.193), channel_id=1, source_target_pairs={{0,2},{2,0},{1,3},{3,1},{4,6},{6,4},{5,7},{7,5},{8,10},{10,8},{9,1... | collective-permute-start | bytes 442376 | tf_op jit(solution)/shard_map/ppermute | solution.py:599
  27.1 12.0 %collective-permute-start.14 = (bf16[192,768]{1,0:T(8,128)(2,1)S(1)}, bf16[192,768]{1,0:T(8,128)(2,1)S(1)}, u32[]{:S(2)}, u32[]{:S(2)}) collective-permute-start(bf16[192,768]{1,0:T(8,128)(2,1)S(1)} %get-tuple-element.192), channel_id=1, source_target_pairs={{0,2},{2,0},{1,3},{3,1},{4,6},{6,4},{5,7},{7,5},{8,10},{10,8},{9,1... | collective-permute-start | bytes 884744 | tf_op jit(solution)/shard_map/ppermute | solution.py:599
  29.0 14.5 %copy-start.1 = (bf16[192,768]{1,0:T(8,128)(2,1)S(1)}, bf16[192,768]{1,0:T(8,128)(2,1)}, u32[]{:S(2)}) copy-start(bf16[192,768]{1,0:T(8,128)(2,1)} %refs_1_.5) | copy-start | bytes 884740
  39.1 2.4 %collective-permute-start.16 = (bf16[192,768]{1,0:T(8,128)(2,1)S(1)}, bf16[192,768]{1,0:T(8,128)(2,1)S(1)}, u32[]{:S(2)}, u32[]{:S(2)}) collective-permute-start(bf16[192,768]{1,0:T(8,128)(2,1)S(1)} %get-tuple-element.195.refs_7_), channel_id=1, source_target_pairs={{0,1},{1,0},{2,3},{3,2},{4,5},{5,4},{6,7},{7,6},{8,9},{9,8},{10,11... | collective-permute-start | bytes 884744 | tf_op jit(solution)/shard_map/ppermute | solution.py:595
  39.1 15.0 %collective-permute-start.17 = (bf16[96,768]{1,0:T(8,128)(2,1)S(1)}, bf16[96,768]{1,0:T(8,128)(2,1)S(1)}, u32[]{:S(2)}, u32[]{:S(2)}) collective-permute-start(bf16[96,768]{1,0:T(8,128)(2,1)S(1)} %get-tuple-element.202.refs_5_), channel_id=1, source_target_pairs={{0,4},{4,0},{8,12},{12,8},{16,20},{20,16},{24,28},{28,24},{1,5},{5... | collective-permute-start | bytes 442376 | tf_op jit(solution)/shard_map/ppermute | solution.py:861
  41.5 12.6 %collective-permute-start.18 = (bf16[192,768]{1,0:T(8,128)(2,1)S(1)}, bf16[192,768]{1,0:T(8,128)(2,1)S(1)}, u32[]{:S(2)}, u32[]{:S(2)}) collective-permute-start(bf16[192,768]{1,0:T(8,128)(2,1)S(1)} %get-tuple-element.203.refs_9_), channel_id=1, source_target_pairs={{0,2},{2,0},{1,3},{3,1},{4,6},{6,4},{5,7},{7,5},{8,10},{10,8},{9,1... | collective-permute-start | bytes 884744 | tf_op jit(solution)/shard_map/ppermute | solution.py:599
  42.0 14.9 %collective-permute-start.19 = (bf16[192,768]{1,0:T(8,128)(2,1)S(1)}, bf16[192,768]{1,0:T(8,128)(2,1)S(1)}, u32[]{:S(2)}, u32[]{:S(2)}) collective-permute-start(bf16[192,768]{1,0:T(8,128)(2,1)S(1)} %get-tuple-element.204.refs_13_), channel_id=1, source_target_pairs={{0,2},{2,0},{1,3},{3,1},{4,6},{6,4},{5,7},{7,5},{8,10},{10,8},{9,1... | collective-permute-start | bytes 884744 | tf_op jit(solution)/shard_map/ppermute | solution.py:599
  43.5 16.5 %copy-start.9 = (bf16[1,1024,768]{2,1,0:T(8,128)(2,1)S(1)}, bf16[1,1024,768]{2,1,0:T(8,128)(2,1)}, u32[]{:S(2)}) copy-start(bf16[1,1024,768]{2,1,0:T(8,128)(2,1)} %param.25) | copy-start | bytes 4718596
  57.0 3.1 %collective-permute-start.22 = (bf16[192,768]{1,0:T(8,128)(2,1)S(1)}, bf16[192,768]{1,0:T(8,128)(2,1)S(1)}, u32[]{:S(2)}, u32[]{:S(2)}) collective-permute-start(bf16[192,768]{1,0:T(8,128)(2,1)S(1)} %get-tuple-element.208.refs_11_), channel_id=1, source_target_pairs={{0,1},{1,0},{2,3},{3,2},{4,5},{5,4},{6,7},{7,6},{8,9},{9,8},{10,11... | collective-permute-start | bytes 884744 | tf_op jit(solution)/shard_map/ppermute | solution.py:595
  57.0 3.1 %collective-permute-start.23 = (bf16[192,768]{1,0:T(8,128)(2,1)S(1)}, bf16[192,768]{1,0:T(8,128)(2,1)S(1)}, u32[]{:S(2)}, u32[]{:S(2)}) collective-permute-start(bf16[192,768]{1,0:T(8,128)(2,1)S(1)} %get-tuple-element.209.refs_15_), channel_id=1, source_target_pairs={{0,1},{1,0},{2,3},{3,2},{4,5},{5,4},{6,7},{7,6},{8,9},{9,8},{10,11... | collective-permute-start | bytes 884744 | tf_op jit(solution)/shard_map/ppermute | solution.py:595
  57.5 1.7 collective-permute-start.20
  57.5 2.5 %collective-permute-start.21 = (bf16[96,768]{1,0:T(8,128)(2,1)S(1)}, bf16[96,768]{1,0:T(8,128)(2,1)S(1)}, u32[]{:S(2)}, u32[]{:S(2)}) collective-permute-start(bf16[96,768]{1,0:T(8,128)(2,1)S(1)} %get-tuple-element.207.refs_6_), channel_id=1, source_target_pairs={{0,1},{1,0},{2,3},{3,2},{4,5},{5,4},{6,7},{7,6},{8,9},{9,8},{10,11... | collective-permute-start | bytes 442376 | tf_op jit(solution)/shard_map/ppermute | solution.py:595
  58.0 19.3 %collective-permute-start.25 = (bf16[96,768]{1,0:T(8,128)(2,1)S(1)}, bf16[96,768]{1,0:T(8,128)(2,1)S(1)}, u32[]{:S(2)}, u32[]{:S(2)}) collective-permute-start(bf16[96,768]{1,0:T(8,128)(2,1)S(1)} %get-tuple-element.212.refs_7_), channel_id=1, source_target_pairs={{0,2},{2,0},{1,3},{3,1},{4,6},{6,4},{5,7},{7,5},{8,10},{10,8},{9,1... | collective-permute-start | bytes 442376 | tf_op jit(solution)/shard_map/ppermute | solution.py:599
  59.2 18.2 %collective-permute-start.24 = (bf16[192,768]{1,0:T(8,128)(2,1)S(1)}, bf16[192,768]{1,0:T(8,128)(2,1)S(1)}, u32[]{:S(2)}, u32[]{:S(2)}) collective-permute-start(bf16[192,768]{1,0:T(8,128)(2,1)S(1)} %get-tuple-element.206.refs_3_), channel_id=1, source_target_pairs={{0,2},{2,0},{1,3},{3,1},{4,6},{6,4},{5,7},{7,5},{8,10},{10,8},{9,1... | collective-permute-start | bytes 884744 | tf_op jit(solution)/shard_map/ppermute | solution.py:599
  77.9 3.8 %collective-permute-start.28 = (bf16[2,1152,384]{2,1,0:T(8,128)(2,1)S(1)}, bf16[2,1152,384]{2,1,0:T(8,128)(2,1)S(1)}, u32[]{:S(2)}, u32[]{:S(2)}) collective-permute-start(bf16[2,1152,384]{2,1,0:T(8,128)(2,1)S(1)} %get-tuple-element.222), channel_id=1, source_target_pairs={{0,1},{1,0},{2,3},{3,2},{4,5},{5,4},{6,7},{7,6},{8,9},{9,8},{10,11... | collective-permute-start | bytes 5308424 | tf_op jit(solution)/shard_map/ppermute | solution.py:595
  78.0 7.4 %collective-permute-start.26 = (bf16[192,768]{1,0:T(8,128)(2,1)S(1)}, bf16[192,768]{1,0:T(8,128)(2,1)S(1)}, u32[]{:S(2)}, u32[]{:S(2)}) collective-permute-start(bf16[192,768]{1,0:T(8,128)(2,1)S(1)} %get-tuple-element.214.refs_5_), channel_id=1, source_target_pairs={{0,1},{1,0},{2,3},{3,2},{4,5},{5,4},{6,7},{7,6},{8,9},{9,8},{10,11... | collective-permute-start | bytes 884744 | tf_op jit(solution)/shard_map/ppermute | solution.py:595
  78.5 6.9 %collective-permute-start.27 = (bf16[96,768]{1,0:T(8,128)(2,1)S(1)}, bf16[96,768]{1,0:T(8,128)(2,1)S(1)}, u32[]{:S(2)}, u32[]{:S(2)}) collective-permute-start(bf16[96,768]{1,0:T(8,128)(2,1)S(1)} %get-tuple-element.215.refs_9_), channel_id=1, source_target_pairs={{0,1},{1,0},{2,3},{3,2},{4,5},{5,4},{6,7},{7,6},{8,9},{9,8},{10,11... | collective-permute-start | bytes 442376 | tf_op jit(solution)/shard_map/ppermute | solution.py:595
  82.6 17.3 %collective-permute-start.30 = (bf16[2,288,384]{2,1,0:T(8,128)(2,1)S(1)}, bf16[2,288,384]{2,1,0:T(8,128)(2,1)S(1)}, u32[]{:S(2)}, u32[]{:S(2)}) collective-permute-start(bf16[2,288,384]{2,1,0:T(8,128)(2,1)S(1)} %get-tuple-element.234), channel_id=1, source_target_pairs={{0,4},{4,0},{8,12},{12,8},{16,20},{20,16},{24,28},{28,24},{1,5},{5... | collective-permute-start | bytes 1327112 | tf_op jit(solution)/shard_map/ppermute | solution.py:647
  84.2 15.8 %collective-permute-start.29 = (bf16[576,384]{1,0:T(8,128)(2,1)S(1)}, bf16[576,384]{1,0:T(8,128)(2,1)S(1)}, u32[]{:S(2)}, u32[]{:S(2)}) collective-permute-start(bf16[576,384]{1,0:T(8,128)(2,1)S(1)} %get-tuple-element.225.refs_18_), channel_id=1, source_target_pairs={{0,2},{2,0},{1,3},{3,1},{4,6},{6,4},{5,7},{7,5},{8,10},{10,8},{9,1... | collective-permute-start | bytes 1327112 | tf_op jit(solution)/shard_map/ppermute | solution.py:599
  100.7 8.5 %collective-permute-start.33 = (bf16[2,960,384]{2,1,0:T(8,128)(2,1)S(1)}, bf16[2,960,384]{2,1,0:T(8,128)(2,1)S(1)}, u32[]{:S(2)}, u32[]{:S(2)}) collective-permute-start(bf16[2,960,384]{2,1,0:T(8,128)(2,1)S(1)} %get-tuple-element.239.refs_12_), channel_id=1, source_target_pairs={{0,1},{1,0},{2,3},{3,2},{4,5},{5,4},{6,7},{7,6},{8,9},{9,8},{10,11... | collective-permute-start | bytes 4423688 | tf_op jit(solution)/shard_map/ppermute | solution.py:595
  100.8 8.0 %collective-permute-start.32 = (bf16[288,384]{1,0:T(8,128)(2,1)S(1)}, bf16[288,384]{1,0:T(8,128)(2,1)S(1)}, u32[]{:S(2)}, u32[]{:S(2)}) collective-permute-start(bf16[288,384]{1,0:T(8,128)(2,1)S(1)} %get-tuple-element.247), channel_id=1, source_target_pairs={{0,2},{2,0},{1,3},{3,1},{4,6},{6,4},{5,7},{7,5},{8,10},{10,8},{9,1... | collective-permute-start | bytes 663560 | tf_op jit(solution)/shard_map/ppermute | solution.py:599
  101.7 7.5 %collective-permute-start.31 = (bf16[288,384]{1,0:T(8,128)(2,1)S(1)}, bf16[288,384]{1,0:T(8,128)(2,1)S(1)}, u32[]{:S(2)}, u32[]{:S(2)}) collective-permute-start(bf16[288,384]{1,0:T(8,128)(2,1)S(1)} %get-tuple-element.238.refs_11_), channel_id=1, source_target_pairs={{0,4},{4,0},{8,12},{12,8},{16,20},{20,16},{24,28},{28,24},{1,5},{5... | collective-permute-start | bytes 663560 | tf_op jit(solution)/shard_map/ppermute | solution.py:647
  110.4 10.5 %collective-permute-start.34 = (bf16[288,384]{1,0:T(8,128)(2,1)S(1)}, bf16[288,384]{1,0:T(8,128)(2,1)S(1)}, u32[]{:S(2)}, u32[]{:S(2)}) collective-permute-start(bf16[288,384]{1,0:T(8,128)(2,1)S(1)} %get-tuple-element.251.refs_16_), channel_id=1, source_target_pairs={{0,8},{4,12},{8,0},{12,4},{16,24},{20,28},{24,16},{28,20},{1,9},{5... | collective-permute-start | bytes 663560 | tf_op jit(solution)/shard_map/ppermute | solution.py:647
  112.1 9.7 %collective-permute-start.36 = (bf16[2,240,384]{2,1,0:T(8,128)(2,1)S(1)}, bf16[2,240,384]{2,1,0:T(8,128)(2,1)S(1)}, u32[]{:S(2)}, u32[]{:S(2)}) collective-permute-start(bf16[2,240,384]{2,1,0:T(8,128)(2,1)S(1)} %get-tuple-element.259), channel_id=1, source_target_pairs={{0,4},{4,0},{8,12},{12,8},{16,20},{20,16},{24,28},{28,24},{1,5},{5... | collective-permute-start | bytes 1105928 | tf_op jit(solution)/shard_map/ppermute | solution.py:647
  113.2 9.8 %collective-permute-start.35 = (bf16[480,384]{1,0:T(8,128)(2,1)S(1)}, bf16[480,384]{1,0:T(8,128)(2,1)S(1)}, u32[]{:S(2)}, u32[]{:S(2)}) collective-permute-start(bf16[480,384]{1,0:T(8,128)(2,1)S(1)} %get-tuple-element.252.refs_17_), channel_id=1, source_target_pairs={{0,2},{2,0},{1,3},{3,1},{4,6},{6,4},{5,7},{7,5},{8,10},{10,8},{9,1... | collective-permute-start | bytes 1105928 | tf_op jit(solution)/shard_map/ppermute | solution.py:599
  123.8 14.7 %collective-permute-start.40 = (bf16[2,576,512]{2,1,0:T(8,128)(2,1)S(1)}, bf16[2,576,512]{2,1,0:T(8,128)(2,1)S(1)}, u32[]{:S(2)}, u32[]{:S(2)}) collective-permute-start(bf16[2,576,512]{2,1,0:T(8,128)(2,1)S(1)} %get-tuple-element.265.refs_16_), channel_id=1, source_target_pairs={{0,1},{1,0},{2,3},{3,2},{4,5},{5,4},{6,7},{7,6},{8,9},{9,8},{10,11... | collective-permute-start | bytes 3538952 | tf_op jit(solution)/shard_map/ppermute | solution.py:595
  123.9 10.3 %collective-permute-start.39 = (bf16[240,384]{1,0:T(8,128)(2,1)S(1)}, bf16[240,384]{1,0:T(8,128)(2,1)S(1)}, u32[]{:S(2)}, u32[]{:S(2)}) collective-permute-start(bf16[240,384]{1,0:T(8,128)(2,1)S(1)} %get-tuple-element.271), channel_id=1, source_target_pairs={{0,2},{2,0},{1,3},{3,1},{4,6},{6,4},{5,7},{7,5},{8,10},{10,8},{9,1... | collective-permute-start | bytes 552968 | tf_op jit(solution)/shard_map/ppermute | solution.py:599
  125.1 9.0 %collective-permute-start.38 = (bf16[240,384]{1,0:T(8,128)(2,1)S(1)}, bf16[240,384]{1,0:T(8,128)(2,1)S(1)}, u32[]{:S(2)}, u32[]{:S(2)}) collective-permute-start(bf16[240,384]{1,0:T(8,128)(2,1)S(1)} %get-tuple-element.264.refs_15_), channel_id=1, source_target_pairs={{0,4},{4,0},{8,12},{12,8},{16,20},{20,16},{24,28},{28,24},{1,5},{5... | collective-permute-start | bytes 552968 | tf_op jit(solution)/shard_map/ppermute | solution.py:647
  125.7 12.7 %collective-permute-start.37 = (bf16[288,384]{1,0:T(8,128)(2,1)S(1)}, bf16[288,384]{1,0:T(8,128)(2,1)S(1)}, u32[]{:S(2)}, u32[]{:S(2)}) collective-permute-start(bf16[288,384]{1,0:T(8,128)(2,1)S(1)} %get-tuple-element.263.refs_14_.refs_1_), channel_id=1, source_target_pairs={{0,16},{4,20},{8,24},{12,28},{16,0},{20,4},{24,8},{28,12},{1,17},{... | collective-permute-start | bytes 663560 | tf_op jit(solution)/shard_map/ppermute | solution.py:647
  139.4 10.1 %collective-permute-start.45 = (bf16[2,576,256]{2,1,0:T(8,128)(2,1)S(1)}, bf16[2,576,256]{2,1,0:T(8,128)(2,1)S(1)}, u32[]{:S(2)}, u32[]{:S(2)}) collective-permute-start(bf16[2,576,256]{2,1,0:T(8,128)(2,1)S(1)} %get-tuple-element.283), channel_id=1, source_target_pairs={{0,1},{1,0},{2,3},{3,2},{4,5},{5,4},{6,7},{7,6},{8,9},{9,8},{10,11... | collective-permute-start | bytes 1769480 | tf_op jit(solution)/shard_map/ppermute | solution.py:595
  139.6 10.0 %collective-permute-start.43 = (bf16[288,512]{1,0:T(8,128)(2,1)S(1)}, bf16[288,512]{1,0:T(8,128)(2,1)S(1)}, u32[]{:S(2)}, u32[]{:S(2)}) collective-permute-start(bf16[288,512]{1,0:T(8,128)(2,1)S(1)} %get-tuple-element.280), channel_id=1, source_target_pairs={{0,2},{2,0},{1,3},{3,1},{4,6},{6,4},{5,7},{7,5},{8,10},{10,8},{9,1... | collective-permute-start | bytes 884744 | tf_op jit(solution)/shard_map/ppermute | solution.py:599
  140.4 9.1 %collective-permute-start.44 = (bf16[2,144,512]{2,1,0:T(8,128)(2,1)S(1)}, bf16[2,144,512]{2,1,0:T(8,128)(2,1)S(1)}, u32[]{:S(2)}, u32[]{:S(2)}) collective-permute-start(bf16[2,144,512]{2,1,0:T(8,128)(2,1)S(1)} %get-tuple-element.281), channel_id=1, source_target_pairs={{0,4},{4,0},{8,12},{12,8},{16,20},{20,16},{24,28},{28,24},{1,5},{5... | collective-permute-start | bytes 884744 | tf_op jit(solution)/shard_map/ppermute | solution.py:647
  141.9 7.6 %collective-permute-start.42 = (bf16[240,384]{1,0:T(8,128)(2,1)S(1)}, bf16[240,384]{1,0:T(8,128)(2,1)S(1)}, u32[]{:S(2)}, u32[]{:S(2)}) collective-permute-start(bf16[240,384]{1,0:T(8,128)(2,1)S(1)} %get-tuple-element.277), channel_id=1, source_target_pairs={{0,8},{4,12},{8,0},{12,4},{16,24},{20,28},{24,16},{28,20},{1,9},{5... | collective-permute-start | bytes 552968 | tf_op jit(solution)/shard_map/ppermute | solution.py:647
  142.0 17.3 %collective-permute-start.41 = (bf16[288,384]{1,0:T(8,128)(2,1)S(1)}, bf16[288,384]{1,0:T(8,128)(2,1)S(1)}, u32[]{:S(2)}, u32[]{:S(2)}) collective-permute-start(bf16[288,384]{1,0:T(8,128)(2,1)S(1)} %get-tuple-element.275.refs_1_), channel_id=1, source_target_pairs={{0,8},{4,12},{8,0},{12,4},{16,24},{20,28},{24,16},{28,20},{1,9},{5... | collective-permute-start | bytes 663560 | tf_op jit(solution)/shard_map/ppermute | solution.py:647
  150.4 18.7 %collective-permute-start.49 = (bf16[64,1536]{1,0:T(8,128)(2,1)S(1)}, bf16[64,1536]{1,0:T(8,128)(2,1)S(1)}, u32[]{:S(2)}, u32[]{:S(2)}) collective-permute-start(bf16[64,1536]{1,0:T(8,128)(2,1)S(1)} %get-tuple-element.290), channel_id=1, source_target_pairs={{0,4},{4,8},{8,12},{12,16},{16,20},{20,24},{24,28},{1,5},{5,9},{9,... | collective-permute-start | bytes 589832 | tf_op jit(solution)/shard_map/ppermute | solution.py:901
  153.8 15.3 %collective-permute-start.50 = (bf16[64,1536]{1,0:T(8,128)(2,1)S(1)}, bf16[64,1536]{1,0:T(8,128)(2,1)S(1)}, u32[]{:S(2)}, u32[]{:S(2)}) collective-permute-start(bf16[64,1536]{1,0:T(8,128)(2,1)S(1)} %get-tuple-element.291), channel_id=1, source_target_pairs={{4,0},{8,4},{12,8},{16,12},{20,16},{24,20},{28,24},{5,1},{9,5},{13... | collective-permute-start | bytes 589832 | tf_op jit(solution)/shard_map/ppermute | solution.py:901
  155.1 5.2 %collective-permute-start.47 = (bf16[288,256]{1,0:T(8,128)(2,1)S(1)}, bf16[288,256]{1,0:T(8,128)(2,1)S(1)}, u32[]{:S(2)}, u32[]{:S(2)}) collective-permute-start(bf16[288,256]{1,0:T(8,128)(2,1)S(1)} %get-tuple-element.288), channel_id=1, source_target_pairs={{0,2},{2,0},{1,3},{3,1},{4,6},{6,4},{5,7},{7,5},{8,10},{10,8},{9,1... | collective-permute-start | bytes 442376 | tf_op jit(solution)/shard_map/ppermute | solution.py:599
  156.4 12.8 %collective-permute-start.46 = (bf16[240,384]{1,0:T(8,128)(2,1)S(1)}, bf16[240,384]{1,0:T(8,128)(2,1)S(1)}, u32[]{:S(2)}, u32[]{:S(2)}) collective-permute-start(bf16[240,384]{1,0:T(8,128)(2,1)S(1)} %get-tuple-element.285.refs_3_), channel_id=1, source_target_pairs={{0,16},{4,20},{8,24},{12,28},{16,0},{20,4},{24,8},{28,12},{1,17},{... | collective-permute-start | bytes 552968 | tf_op jit(solution)/shard_map/ppermute | solution.py:647
  159.3 7.1 %collective-permute-start.48 = (bf16[2,144,256]{2,1,0:T(8,128)(2,1)S(1)}, bf16[2,144,256]{2,1,0:T(8,128)(2,1)S(1)}, u32[]{:S(2)}, u32[]{:S(2)}) collective-permute-start(bf16[2,144,256]{2,1,0:T(8,128)(2,1)S(1)} %get-tuple-element.289), channel_id=1, source_target_pairs={{0,4},{4,0},{8,12},{12,8},{16,20},{20,16},{24,28},{28,24},{1,5},{5... | collective-permute-start | bytes 442376 | tf_op jit(solution)/shard_map/ppermute | solution.py:647
  160.4 11.6 %collective-permute-start.53 = (bf16[144,512]{1,0:T(8,128)(2,1)S(1)}, bf16[144,512]{1,0:T(8,128)(2,1)S(1)}, u32[]{:S(2)}, u32[]{:S(2)}) collective-permute-start(bf16[144,512]{1,0:T(8,128)(2,1)S(1)} %get-tuple-element.303), channel_id=1, source_target_pairs={{0,4},{4,0},{8,12},{12,8},{16,20},{20,16},{24,28},{28,24},{1,5},{5... | collective-permute-start | bytes 442376 | tf_op jit(solution)/shard_map/ppermute | solution.py:647
  166.4 14.5 %collective-permute-start.54 = (bf16[144,512]{1,0:T(8,128)(2,1)S(1)}, bf16[144,512]{1,0:T(8,128)(2,1)S(1)}, u32[]{:S(2)}, u32[]{:S(2)}) collective-permute-start(bf16[144,512]{1,0:T(8,128)(2,1)S(1)} %get-tuple-element.304), channel_id=1, source_target_pairs={{0,2},{2,0},{1,3},{3,1},{4,6},{6,4},{5,7},{7,5},{8,10},{10,8},{9,1... | collective-permute-start | bytes 442376 | tf_op jit(solution)/shard_map/ppermute | solution.py:599
  169.9 11.0 %collective-permute-start.56 = (bf16[144,256]{1,0:T(8,128)(2,1)S(1)}, bf16[144,256]{1,0:T(8,128)(2,1)S(1)}, u32[]{:S(2)}, u32[]{:S(2)}) collective-permute-start(bf16[144,256]{1,0:T(8,128)(2,1)S(1)} %get-tuple-element.307), channel_id=1, source_target_pairs={{0,2},{2,0},{1,3},{3,1},{4,6},{6,4},{5,7},{7,5},{8,10},{10,8},{9,1... | collective-permute-start | bytes 221192 | tf_op jit(solution)/shard_map/ppermute | solution.py:599
  171.1 9.7 %collective-permute-start.55 = (bf16[144,256]{1,0:T(8,128)(2,1)S(1)}, bf16[144,256]{1,0:T(8,128)(2,1)S(1)}, u32[]{:S(2)}, u32[]{:S(2)}) collective-permute-start(bf16[144,256]{1,0:T(8,128)(2,1)S(1)} %get-tuple-element.299.refs_16_), channel_id=1, source_target_pairs={{0,4},{4,0},{8,12},{12,8},{16,20},{20,16},{24,28},{28,24},{1,5},{5... | collective-permute-start | bytes 221192 | tf_op jit(solution)/shard_map/ppermute | solution.py:647
  171.1 9.7 %collective-permute-start.52 = (bf16[240,384]{1,0:T(8,128)(2,1)S(1)}, bf16[240,384]{1,0:T(8,128)(2,1)S(1)}, u32[]{:S(2)}, u32[]{:S(2)}) collective-permute-start(bf16[240,384]{1,0:T(8,128)(2,1)S(1)} %get-tuple-element.298.refs_15_.refs_3_), channel_id=1, source_target_pairs={{0,8},{4,12},{8,0},{12,4},{16,24},{20,28},{24,16},{28,20},{1,9},{5... | collective-permute-start | bytes 552968 | tf_op jit(solution)/shard_map/ppermute | solution.py:647
  171.9 10.7 %collective-permute-start.51 = (bf16[576,384]{1,0:T(8,128)(2,1)S(1)}, bf16[576,384]{1,0:T(8,128)(2,1)S(1)}, u32[]{:S(2)}, u32[]{:S(2)}) collective-permute-start(bf16[576,384]{1,0:T(8,128)(2,1)S(1)} %get-tuple-element.297.refs_14_.refs_1_), channel_id=1, source_target_pairs={{0,4},{4,0},{8,12},{12,8},{16,20},{20,16},{24,28},{28,24},{1,5},{5... | collective-permute-start | bytes 1327112 | tf_op jit(solution)/shard_map/ppermute | solution.py:647
  183.4 7.6 %collective-permute-start.57 = (bf16[480,384]{1,0:T(8,128)(2,1)S(1)}, bf16[480,384]{1,0:T(8,128)(2,1)S(1)}, u32[]{:S(2)}, u32[]{:S(2)}) collective-permute-start(bf16[480,384]{1,0:T(8,128)(2,1)S(1)} %get-tuple-element.309.refs_1_), channel_id=1, source_target_pairs={{0,4},{4,0},{8,12},{12,8},{16,20},{20,16},{24,28},{28,24},{1,5},{5... | collective-permute-start | bytes 1105928 | tf_op jit(solution)/shard_map/ppermute | solution.py:647
  184.5 5.9 %collective-permute-start.58 = (bf16[144,768]{1,0:T(8,128)(2,1)S(1)}, bf16[144,768]{1,0:T(8,128)(2,1)S(1)}, u32[]{:S(2)}, u32[]{:S(2)}) collective-permute-start(bf16[144,768]{1,0:T(8,128)(2,1)S(1)} %get-tuple-element.311), channel_id=1, source_target_pairs={{0,8},{4,12},{8,0},{12,4},{16,24},{20,28},{24,16},{28,20},{1,9},{5... | collective-permute-start | bytes 663560 | tf_op jit(solution)/shard_map/ppermute | solution.py:647
  191.7 11.7 %collective-permute-start.59 = (bf16[144,768]{1,0:T(8,128)(2,1)S(1)}, bf16[144,768]{1,0:T(8,128)(2,1)S(1)}, u32[]{:S(2)}, u32[]{:S(2)}) collective-permute-start(bf16[144,768]{1,0:T(8,128)(2,1)S(1)} %get-tuple-element.313.refs_1_), channel_id=1, source_target_pairs={{0,16},{4,20},{8,24},{12,28},{16,0},{20,4},{24,8},{28,12},{1,17},{... | collective-permute-start | bytes 663560 | tf_op jit(solution)/shard_map/ppermute | solution.py:647
  204.0 6.4 %collective-permute-start.60 = (bf16[144,768]{1,0:T(8,128)(2,1)S(1)}, bf16[144,768]{1,0:T(8,128)(2,1)S(1)}, u32[]{:S(2)}, u32[]{:S(2)}) collective-permute-start(bf16[144,768]{1,0:T(8,128)(2,1)S(1)} %get-tuple-element.317.refs_1_), channel_id=1, source_target_pairs={{0,8},{4,12},{8,0},{12,4},{16,24},{20,28},{24,16},{28,20},{1,9},{5... | collective-permute-start | bytes 663560 | tf_op jit(solution)/shard_map/ppermute | solution.py:647
  212.6 17.8 %collective-permute-start.61 = (bf16[288,768]{1,0:T(8,128)(2,1)S(1)}, bf16[288,768]{1,0:T(8,128)(2,1)S(1)}, u32[]{:S(2)}, u32[]{:S(2)}) collective-permute-start(bf16[288,768]{1,0:T(8,128)(2,1)S(1)} %get-tuple-element.321.refs_1_), channel_id=1, source_target_pairs={{0,4},{4,0},{8,12},{12,8},{16,20},{20,16},{24,28},{28,24},{1,5},{5... | collective-permute-start | bytes 1327112 | tf_op jit(solution)/shard_map/ppermute | solution.py:647
  (28 other events, 140.0 us)

commit v4 on v3

--- a/solution.py
+++ b/solution.py
@@ -18,6 +18,7 @@
 QB = 128
 TILE = 256
 WIDE = 384
+ADAM_MB = 60
 QUAD = 4 * HD
 
 NORM_EPS = 1e-05
@@ -557,34 +558,33 @@
     return (new_first, new_second, change)
 
 
-def adam_body(count, *refs):
-    grads, (w_ref, m_ref, v_ref, g_ref, nm_ref, nv_ref, st_ref, dots_ref) = refs[:count], refs[count:]
-    g = jnp.concatenate([r[...] for r in grads], axis=1).astype(F32)
-    w = w_ref[...].astype(F32)
-    g_ref[...] = g
-    nm_ref[...], nv_ref[...], st_ref[...] = adam(w, g, m_ref[...], v_ref[...], WEIGHT_DECAY)
-
-    @pl.when(pl.program_id(0) == 0)
-    def _():
-        dots_ref[...] = jnp.zeros_like(dots_ref)
-
-    dots_ref[...] += jnp.sum(w * g, axis=1, keepdims=True)
-
-
-def adam_call(grads, weight, first, second, megabytes=60):
+def adam_call(info, assemble, grads, weight, first, second, rows_at_once, deps=()):
     r, width = weight.shape
-    own = pl.BlockSpec((r, D), lambda j: (0, j))
+    own = rows(rows_at_once, width)
     out = jax.ShapeDtypeStruct((r, width), F32)
+    count = len(grads)
+
+    def body(info_ref, *refs):
+        blocks = refs[:count]
+        w_ref, m_ref, v_ref = refs[count : count + 3]
+        g_ref, nm_ref, nv_ref, st_ref, dots_ref = refs[-5:]
+        assemble(pl.program_id(0), info_ref, blocks, g_ref)
+        g = g_ref[...]
+        w = w_ref[...].astype(F32)
+        nm_ref[...], nv_ref[...], st_ref[...] = adam(w, g, m_ref[...], v_ref[...], WEIGHT_DECAY)
+        dots_ref[...] = jnp.sum(w * g, axis=1, keepdims=True)
+
     return pl.pallas_call(
-        functools.partial(adam_body, len(grads)),
-        grid=(width // D,),
-        in_specs=[pl.BlockSpec((r, wide), at) for _, wide, at in grads] + [own] * 3,
-        out_specs=[own] * 4 + [full((r, 1))],
+        body,
+        grid=(r // rows_at_once,),
+        in_specs=[smem()] + [pl.BlockSpec(shape, at) for _, shape, at in grads] + [own] * 3
+        + [pl.BlockSpec(memory_space=pl.ANY)] * len(deps),
+        out_specs=[own] * 4 + [rows(rows_at_once, 1)],
         out_shape=[out] * 4 + [jax.ShapeDtypeStruct((r, 1), F32)],
-        compiler_params=pltpu.CompilerParams(dimension_semantics=("arbitrary",), vmem_limit_bytes=megabytes * 1024 * 1024),
+        compiler_params=pltpu.CompilerParams(dimension_semantics=("arbitrary",), vmem_limit_bytes=ADAM_MB * 1024 * 1024),
         cost_estimate=cost(3),
         name="adam",
-    )(*[g for g, _, _ in grads], weight, first, second)
+    )(info, *[g for g, _, _ in grads], weight, first, second, *deps)
 
 
 CORES = [(0, 1), (1, 0), (2, 3), (3, 2)]
@@ -895,45 +895,81 @@
     _, deps = boundary(info, token, (chain_a, chain_b), (chain_c,))
     token = back(2, 0, QUAD, deps)
     chain_d = Chain(*pieces)
-    _, deps = boundary(info, token, (chain_a, chain_b, chain_c), (chain_d,))
+    _, deps = boundary(info, token, (chain_b, chain_c), (chain_d,))
     rims = [jnp.concatenate([a[r] for a in grads[1:]], axis=1) for r in (slice(0, HALF), slice(n + HALF, ext))]
-    rims, deps = boundary(info, deps[0], (chain_b, chain_c, chain_d), (), rims)
+    rims, deps = boundary(info, deps[0], (chain_a, chain_b, chain_c, chain_d), (), rims)
     rims = lax.ppermute(rims[1], "seq", up), lax.ppermute(rims[0], "seq", down)
     rims, deps = boundary(info, deps[0], (chain_a, chain_b, chain_d), (), rims)
     grad_in, token = last_call(info, x, grads, rims, gmid, attn_parts, gain, deps=deps)
-    chains = (chain_a, chain_b, Joined(chain_c, chain_d))
-    sum_b = late_b = sum_a = None
-    while not all(c.done() for c in chains):
-        also = ()
-        if chain_a.done() and chain_b.done():
-            also = (chain_b.kept[0], chain_a.kept[0])
-        through, deps = boundary(info, token, chains, (), also)
+    chain_c = Joined(chain_c, chain_d)
+    chains = (chain_a, chain_b, chain_c)
+    while chain_c.at < len(chain_c.plan) - 1:
+        _, deps = boundary(info, token, chains)
         token = deps[0]
-        if also:
-            chain_b.kept, chain_a.kept = through[:1], through[1:2]
-            sum_b = through[0] if sum_b is None else sum_b
-            if not chains[2].done():
-                late_b, sum_a = through
-    sum_c = chains[2].kept[0]
+    sum_a, sum_b = chain_a.kept[0], chain_b.kept[0]
 
     r = D // 4
-
-    def blocks(a, *at):
-        return jnp.concatenate([a[i * r : (i + 1) * r] for i in at], axis=1)
-
-    ga, gb = blocks(sum_a, 0, 1), late_b[:r]
-    ua, ub = blocks(sum_a, 2, 3), late_b[r : 2 * r]
-    g_ffn_in = jnp.concatenate(
-        [t for a, b in ((ga, gb), (ua, ub)) for s in range(4)
-         for t in (a[:, s * some : (s + 1) * some], b[:, s * rest : (s + 1) * rest])], axis=1
-    )
-    g_ffn_out = jnp.concatenate(
-        [blocks(sum_a, 4, 5), jnp.concatenate([sum_b[4 * r : 4 * r + rest], sum_b[4 * r + rest :]], axis=1)], axis=0
-    )
-    res_ffn_in = adam_call([(g_ffn_in, D, lambda j: (0, j))], ffn_in, m_ffn_in, v_ffn_in)
-    res_attn_out = adam_call([(blocks(sum_b, 2, 3), D, lambda j: (0, j))], attn_out, m_attn_out, v_attn_out)
-    res_ffn_out = adam_call([(g_ffn_out, D, lambda j: (0, j))], ffn_out, m_ffn_out, v_ffn_out)
-    res_attn_in = adam_call([(sum_c, D, lambda j: (j, 0))], attn_in, m_attn_in, v_attn_in, 20)
+    third = FF // 12
+
+    def block_rows(a, first, step, columns):
+        return a, (step, columns), lambda i: (first // step + i, 0)
+
+    def lay_out(i, info_ref, refs, out):
+        for b, ref in enumerate(refs):
+            out[:, b * WIDE : (b + 1) * WIDE] = ref[...].astype(F32)
+
+    res_attn_out = adam_call(
+        info, lay_out, [block_rows(sum_b, (2 + b) * r, r // 2, WIDE) for b in range(2)], attn_out, m_attn_out, v_attn_out, r // 2
+    )
+
+    def lay_down(i, info_ref, refs, out):
+        for b in range(2):
+            out[:, b * WIDE : (b + 1) * WIDE] = jnp.where(i < 2, refs[b][...], refs[2 + b][...]).astype(F32)
+
+    res_ffn_out = adam_call(
+        info, lay_down,
+        [(sum_a, (third, WIDE), lambda i, b=b: ((4 + b) * (r // third) + jnp.minimum(i, 1), 0)) for b in range(2)]
+        + [(sum_b, (third, WIDE), lambda i, b=b: (4 * (r // third) + b, 0)) for b in range(2)],
+        ffn_out, m_ffn_out, v_ffn_out, third,
+    )
+
+    def lay_units(i, info_ref, refs, out):
+        for half in range(2):
+            of_a = jnp.concatenate([refs[2 * half][...], refs[2 * half + 1][...]], axis=1).astype(F32)
+            of_b = refs[4 + half][...].astype(F32)
+            for s in range(4):
+                start = half * FF + s * (some + rest)
+                out[:, start : start + some] = of_a[:, s * some : (s + 1) * some]
+                out[:, start + some : start + some + rest] = of_b[:, s * rest : (s + 1) * rest]
+
+    step = r // 4
+    res_ffn_in = adam_call(
+        info, lay_units,
+        [block_rows(sum_a, b * r, step, WIDE) for b in range(4)] + [block_rows(sum_b, b * r, step, WIDE) for b in range(2)],
+        ffn_in, m_ffn_in, v_ffn_in, step, deps=(token,),
+    )
+
+    def row_of(part, i):
+        at = part * r + i * step
+        return at // (2 * r * 3 // 4), (at % (2 * r * 3 // 4)) // (r * 3 // 4), at % (r * 3 // 4)
+
+    def source(part):
+        def at(i):
+            half, _, row = row_of(part, i)
+            return (half * (r * 3 // 4) + row) // step, 0
+
+        return at
+
+    def lay_parts(i, info_ref, refs, out):
+        for part in range(3):
+            mine = row_of(part, i)[1] == (info_ref[1] & 1)
+            out[:, part * D : (part + 1) * D] = jnp.where(mine, refs[part][...], refs[3 + part][...]).astype(F32)
+
+    res_attn_in = adam_call(
+        info, lay_parts,
+        [(a, (step, D), source(part)) for a in (chain_c.kept[0], chain_c.flights[0]) for part in range(3)],
+        attn_in, m_attn_in, v_attn_in, step,
+    )
     results = [res_attn_in, res_attn_out, res_ffn_in, res_ffn_out]
     for res, own_gain, m, v_ in ((res_attn_in, norm_attn, m_norm_attn, v_norm_attn), (res_ffn_in, norm_ffn, m_norm_ffn, v_norm_ffn)):
         wide = own_gain.astype(F32)

time: 244 us -> 231 us (0.947)
  local copies, waits for them, and re-layouts: 17.9 us -> 10.6 us
  waiting for transfers between devices: 46.5 us -> 41.8 us
    ppermute x20, waiting for transfers between devices: 32.9 us -> 27.4 us  [along_seq(): return lax.ppermute(a, 'seq', [(i, i ^ 1 << shift) for i in range(count)])]
    pallas_call x4, Pallas kernels: 18.7 us -> 21.3 us  [adam_call(): pl.pallas_call(body, grid=(r // rows_at_once,), in_specs=[smem()] + [pl.B...]
    pallas_call x13 -> x12, Pallas kernels: 10.1 us -> 9.73 us  [boundary(): pl.pallas_call(body, grid=(1,), in_specs=[smem()] + [full(a.shape) for a...]
  transfers between devices with their start and end apart: 62 -> 62, of which waited for: 19 -> 20; matrix products, arithmetic and copies ran while one was open for 6% -> 4% of each run, Pallas kernels for 39% -> 41%
where the time goes in v4:
time: 231 us; the launch traced here: 227 us
  Pallas kernels  108 us (47%)
  starting transfers between devices  59.7 us (26%)
  waiting for transfers between devices  41.8 us (18%)
  local copies, waits for them, and re-layouts  10.6 us (5%)
  other arithmetic  5.68 us (2%)
    pallas_call x8, Pallas kernels, call(): pl.pallas_call(wrapped, in_specs=list(in_specs) + [pl.BlockSpec(memory_sp...  77 us
    ppermute x20, waiting for transfers between devices, along_seq(): return lax.ppermute(a, 'seq', [(i, i ^ 1 << shift) for i in range(count)])  27.4 us
    ppermute x20, starting transfers between devices, along_seq(): return lax.ppermute(a, 'seq', [(i, i ^ 1 << shift) for i in range(count)])  25.2 us
    pallas_call x4, Pallas kernels, adam_call(): pl.pallas_call(body, grid=(r // rows_at_once,), in_specs=[smem()] + [pl.B...  21.3 us
    ppermute x16, starting transfers between devices, to_chip(): return lax.ppermute(a, 'wshard', CHIPS)  17.5 us
    ppermute x16, waiting for transfers between devices, to_chip(): return lax.ppermute(a, 'wshard', CHIPS)  9.81 us
    pallas_call x12, Pallas kernels, boundary(): pl.pallas_call(body, grid=(1,), in_specs=[smem()] + [full(a.shape) for a...  9.73 us
  transfers between devices with their start and end apart: 62, of which 20 were waited for; matrix products, arithmetic and copies ran while one was open for 4% of the time, Pallas kernels for 41%

profile of v4, /device:TPU:0, one launch (start us, length us, event | category | flops | bytes accessed | tf_op | source)
XLA Modules:
  0.0 227.4 jit_solution(1324372900995085165)
XLA Ops:
  0.7 3.0 %collective-permute-start.6 = (bf16[192,2304]{1,0:T(8,128)(2,1)}, bf16[192,2304]{1,0:T(8,128)(2,1)S(1)}, u32[]{:S(2)}, u32[]{:S(2)}) collective-permute-start(bf16[192,2304]{1,0:T(8,128)(2,1)} %refs_6_.3), channel_id=1, source_target_pairs={{0,2},{2,0},{1,3},{3,1},{4,6},{6,4},{5,7},{7,5},{8,10},{10,8},{9,1... | collective-permute-start | bytes 2654216 | tf_op jit(solution)/shard_map/ppermute | solution.py:599
  3.7 1.0 slice_bitcast_fusion
  4.6 1.3 collective-permute-start.1
  5.9 4.6 %collective-permute-start = (bf16[64,768]{1,0:T(8,128)(2,1)S(1)}, bf16[64,768]{1,0:T(8,128)(2,1)S(1)}, u32[]{:S(2)}, u32[]{:S(2)}) collective-permute-start(bf16[64,768]{1,0:T(8,128)(2,1)S(1)} %get-tuple-element.347), channel_id=1, source_target_pairs={{0,4},{4,8},{8,12},{12,16},{16,20},{20,24},{24,28},{1,5},{5,9},{9,... | collective-permute-start | bytes 294920 | tf_op jit(solution)/shard_map/ppermute | solution.py:832
  10.5 0.9 slice.115.refs_2_
  11.5 1.0 slice.114.refs_1_
  12.5 1.0 copy-done
  13.6 1.1 fusion.9
  17.3 1.1 concatenate.21.refs_3_
  18.5 1.2 pad_maximum_fusion.refs_3_
  20.4 1.2 pad_maximum_fusion.1.refs_2_
  23.3 2.4 %collective-permute-done.3.refs_4_.refs_6_ = bf16[2,192]{1,0:T(2,128)(2,1)S(1)} collective-permute-done((bf16[2,192]{1,0:T(2,128)(2,1)S(1)}, bf16[2,192]{1,0:T(2,128)(2,1)S(1)}, u32[]{:S(2)}, u32[]{:S(2)}) %collective-permute-start.3) | collective-permute-done | bytes 800 | tf_op jit(solution)/shard_map/ppermute | solution.py:599
  26.5 1.8 collective-permute-start.14
  28.4 7.5 %qkv.1 = (bf16[768,1152]{1,0:T(8,128)(2,1)S(1)}, bf16[1152,768]{1,0:T(8,128)(2,1)S(1)}, bf16[1152,768]{1,0:T(8,128)(2,1)S(1)}, bf16[1152,768]{1,0:T(8,128)(2,1)S...) custom-call(s32[18]{0:T(128)S(1)} %pad_add_fusion.refs_3_.refs_0_.info_ref, ...), custom_call_target="tpu_custom_call" | custom-call | flops 9900000256 | tf_op jit(solution)/shard_map/qkv/pallas_call | solution.py:58
  35.9 2.5 %collective-permute-done.14.refs_0_ = bf16[192,768]{1,0:T(8,128)(2,1)S(1)} collective-permute-done((bf16[192,768]{1,0:T(8,128)(2,1)S(1)}, bf16[192,768]{1,0:T(8,128)(2,1)S(1)}, u32[]{:S(2)}, u32[]{:S(2)}) %collective-permute-start.14) | collective-permute-done | bytes 294944 | tf_op jit(solution)/shard_map/ppermute | solution.py:599
  38.5 2.4 %collective-permute-start.17 = (bf16[96,768]{1,0:T(8,128)(2,1)S(1)}, bf16[96,768]{1,0:T(8,128)(2,1)S(1)}, u32[]{:S(2)}, u32[]{:S(2)}) collective-permute-start(bf16[96,768]{1,0:T(8,128)(2,1)S(1)} %get-tuple-element.197.refs_5_), channel_id=1, source_target_pairs={{0,4},{4,0},{8,12},{12,8},{16,20},{20,16},{24,28},{28,24},{1,5},{5... | collective-permute-start | bytes 442376 | tf_op jit(solution)/shard_map/ppermute | solution.py:861
  41.4 1.5 collective-permute-start.19
  42.9 10.6 %attend.1 = (bf16[1024,768]{1,0:T(8,128)(2,1)S(1)}, bf16[1024,768]{1,0:T(8,128)(2,1)S(1)}, bf16[1024,768]{1,0:T(8,128)(2,1)S(1)}, bf16[768,768]{1,0:T(8,128)(2,1...) custom-call(s32[18]{0:T(128)S(1)} %pad_add_fusion.refs_3_.refs_0_.info_ref, ...), custom_call_target="tpu_custom_call" | custom-call | flops 12099999744 | tf_op jit(solution)/shard_map/attend/pallas_call | solution.py:58
  53.5 2.8 %collective-permute-done.19.refs_2_ = bf16[192,768]{1,0:T(8,128)(2,1)S(1)} collective-permute-done((bf16[192,768]{1,0:T(8,128)(2,1)S(1)}, bf16[192,768]{1,0:T(8,128)(2,1)S(1)}, u32[]{:S(2)}, u32[]{:S(2)}) %collective-permute-start.19) | collective-permute-done | bytes 294944 | tf_op jit(solution)/shard_map/ppermute | solution.py:599
  59.4 17.2 %ffn_a.1 = (bf16[1024,768]{1,0:T(8,128)(2,1)S(1)}, bf16[1024,768]{1,0:T(8,128)(2,1)S(1)}, bf16[2,1152,384]{2,1,0:T(8,128)(2,1)S(1)}, bf16[2,1152,384]{2,1,0:T(8,128)(2,1)S(1)}, f32[8,128]{1,0:T(8,128)S(1)}) custom-call(s32[18]{0:T(128)S(1)} %pad_add_fusion.refs_3_.refs_0_.info_ref, bf16[1024,768]{1,0:T(8,128)(2,1)S(1)} %get-tuple-element.196.refs_1_, ...), custom_call_target="tpu_custom_call" | custom-call | flops 19800000512 | tf_op jit(solution)/shard_map/ffn_a/pallas_call | solution.py:58
  77.9 3.1 %collective-permute-done.28.refs_2_ = bf16[2,1152,384]{2,1,0:T(8,128)(2,1)S(1)} collective-permute-done((bf16[2,1152,384]{2,1,0:T(8,128)(2,1)S(1)}, bf16[2,1152,384]{2,1,0:T(8,128)(2,1)S(1)}, u32[]{:S(2)}, u32[]{:S(2)}) %collective-permute-start.28) | collective-permute-done | bytes 1769504 | tf_op jit(solution)/shard_map/ppermute | solution.py:595
  81.0 1.0 land.13
  82.0 1.5 collective-permute-start.30
  83.5 1.2 collective-permute-start.29
  84.7 14.3 %ffn_b.1 = (bf16[1024,768]{1,0:T(8,128)(2,1)}, bf16[1024,768]{1,0:T(8,128)(2,1)S(1)}, bf16[1024,768]{1,0:T(8,128)(2,1)S(1)}, bf16[2,960,384]{2,1,0:T(8,128)(2,1)...) custom-call(s32[18]{0:T(128)S(1)} %pad_add_fusion.refs_3_.refs_0_.info_ref, ...), custom_call_target="tpu_custom_call" | custom-call | flops 15399999488 | tf_op jit(solution)/shard_map/ffn_b/pallas_call | solution.py:58
  101.3 6.5 %attend_back.3 = (bf16[1152,768]{1,0:T(8,128)(2,1)S(1)}, bf16[1152,768]{1,0:T(8,128)(2,1)S(1)}, bf16[1152,768]{1,0:T(8,128)(2,1)S(1)}, bf16[2,576,512]{2,1,0:T(8...) custom-call(s32[18]{0:T(128)S(1)} %pad_add_fusion.refs_3_.refs_0_.info_ref, ...), custom_call_target="tpu_custom_call" | custom-call | flops 4400000000 | tf_op jit(solution)/shard_map/attend_back/pallas_call | solution.py:58
  108.3 1.5 land.15
  109.7 1.6 collective-permute-start.34
  111.4 1.1 collective-permute-start.36
  112.5 1.2 collective-permute-start.35
  113.7 6.6 %attend_back.4 = (bf16[1152,768]{1,0:T(8,128)(2,1)S(1)}, bf16[1152,768]{1,0:T(8,128)(2,1)S(1)}, bf16[1152,768]{1,0:T(8,128)(2,1)S(1)}, bf16[2,576,512]{2,1,0:T(8...) custom-call(s32[18]{0:T(128)S(1)} %pad_add_fusion.refs_3_.refs_0_.in, ...), custom_call_target="tpu_custom_call", output_to_operand_aliasing={{0}: (10, {}), {1}: (11, {}), {2}: (12, {}), {3}: (13, {}),... | custom-call | flops 4400000000 | tf_op jit(solution)/shard_map/attend_back/pallas_call | solution.py:58
  121.1 1.2 collective-permute-done.35.refs_5_
  123.2 1.3 collective-permute-start.39
  125.0 1.7 collective-permute-start.37
  126.6 6.7 %attend_back.5 = (bf16[1152,768]{1,0:T(8,128)(2,1)S(1)}, bf16[1152,768]{1,0:T(8,128)(2,1)S(1)}, bf16[1152,768]{1,0:T(8,128)(2,1)S(1)}, bf16[2,576,256]{2,1,0:T(8...) custom-call(s32[18]{0:T(128)S(1)} %pad_add_fusion.refs_3_.refs_0_.in, ...), custom_call_target="tpu_custom_call", output_to_operand_aliasing={{0}: (10, {}), {1}: (11, {}), {2}: (12, {})} | custom-call | flops 4400000000 | tf_op jit(solution)/shard_map/attend_back/pallas_call | solution.py:58
  133.4 1.0 land.17
  135.4 1.2 collective-permute-start.43
  136.6 1.7 collective-permute-start.41
  138.3 4.8 %collective-permute-done.41.refs_4_ = bf16[240,384]{1,0:T(8,128)(2,1)S(1)} collective-permute-done((bf16[240,384]{1,0:T(8,128)(2,1)S(1)}, bf16[240,384]{1,0:T(8,128)(2,1)S(1)}, u32[]{:S(2)}, u32[]{:S(2)}) %collective-permute-start.41) | collective-permute-done | bytes 184352 | tf_op jit(solution)/shard_map/ppermute | solution.py:647
  144.5 0.9 land.18
  145.4 1.3 collective-permute-start.47
  146.6 1.4 collective-permute-start.45
  148.0 3.4 %collective-permute-start.49 = (bf16[64,1536]{1,0:T(8,128)(2,1)S(1)}, bf16[64,1536]{1,0:T(8,128)(2,1)S(1)}, u32[]{:S(2)}, u32[]{:S(2)}) collective-permute-start(bf16[64,1536]{1,0:T(8,128)(2,1)S(1)} %get-tuple-element.285), channel_id=1, source_target_pairs={{0,4},{4,8},{8,12},{12,16},{16,20},{20,24},{24,28},{1,5},{5,9},{9,... | collective-permute-start | bytes 589832 | tf_op jit(solution)/shard_map/ppermute | solution.py:901
  151.4 1.3 collective-permute-start.50
  152.7 2.7 %collective-permute-start.48 = (bf16[2,144,256]{2,1,0:T(8,128)(2,1)S(1)}, bf16[2,144,256]{2,1,0:T(8,128)(2,1)S(1)}, u32[]{:S(2)}, u32[]{:S(2)}) collective-permute-start(bf16[2,144,256]{2,1,0:T(8,128)(2,1)S(1)} %get-tuple-element.284), channel_id=1, source_target_pairs={{0,4},{4,0},{8,12},{12,8},{16,20},{20,16},{24,28},{28,24},{1,5},{5... | collective-permute-start | bytes 442376 | tf_op jit(solution)/shard_map/ppermute | solution.py:647
  155.8 6.2 %collective-permute-done.48.refs_8_ = bf16[2,144,256]{2,1,0:T(8,128)(2,1)S(1)} collective-permute-done((bf16[2,144,256]{2,1,0:T(8,128)(2,1)S(1)}, bf16[2,144,256]{2,1,0:T(8,128)(2,1)S(1)}, u32[]{:S(2)}, u32[]{:S(2)}) %collective-permute-start.48) | collective-permute-done | bytes 147488 | tf_op jit(solution)/shard_map/ppermute | solution.py:647
  162.0 2.5 %collective-permute-start.53 = (bf16[144,512]{1,0:T(8,128)(2,1)S(1)}, bf16[144,512]{1,0:T(8,128)(2,1)S(1)}, u32[]{:S(2)}, u32[]{:S(2)}) collective-permute-start(bf16[144,512]{1,0:T(8,128)(2,1)S(1)} %get-tuple-element.298), channel_id=1, source_target_pairs={{0,4},{4,0},{8,12},{12,8},{16,20},{20,16},{24,28},{28,24},{1,5},{5... | collective-permute-start | bytes 442376 | tf_op jit(solution)/shard_map/ppermute | solution.py:647
  164.4 2.2 collective-permute-done.46.refs_4_
  168.2 1.3 collective-permute-start.56
  169.5 1.1 collective-permute-start.52
  171.5 7.5 %last.1 = (bf16[1024,768]{1,0:T(8,128)(2,1)}, f32[8,128]{1,0:T(8,128)S(1)}) custom-call(s32[18]{0:T(128)S(1)} %pad_add_fusion.refs_3_.refs_0_.info_ref, bf16[1024,768]{1,0:T(8,128)(2,1)S(1)} %bitcast.14, bf16[1152,768]{1,0:T(8,128)(2,1)S(1)} %get-tuple-element.261.refs_2_, bf16[1152,768]{1,0:T(8,128)(2,1)S(1)} %get-tuple-element.262.refs_3_, ...), custom_call_target="tpu_custom_call" | custom-call | flops 7699999744 | tf_op jit(solution)/shard_map/last/pallas_call | solution.py:58
  179.1 1.8 collective-permute-done.51.refs_2_
  181.7 1.0 collective-permute-start.57
  182.7 1.7 collective-permute-start.58
  184.4 4.2 %collective-permute-done.58.refs_4_ = bf16[144,768]{1,0:T(8,128)(2,1)S(1)} collective-permute-done((bf16[144,768]{1,0:T(8,128)(2,1)S(1)}, bf16[144,768]{1,0:T(8,128)(2,1)S(1)}, u32[]{:S(2)}, u32[]{:S(2)}) %collective-permute-start.58) | collective-permute-done | bytes 221216 | tf_op jit(solution)/shard_map/ppermute | solution.py:647
  190.8 2.7 %collective-permute-start.59 = (bf16[144,768]{1,0:T(8,128)(2,1)S(1)}, bf16[144,768]{1,0:T(8,128)(2,1)S(1)}, u32[]{:S(2)}, u32[]{:S(2)}) collective-permute-start(bf16[144,768]{1,0:T(8,128)(2,1)S(1)} %get-tuple-element.308.refs_1_), channel_id=1, source_target_pairs={{0,16},{4,20},{8,24},{12,28},{16,0},{20,4},{24,8},{28,12},{1,17},{... | collective-permute-start | bytes 663560 | tf_op jit(solution)/shard_map/ppermute | solution.py:647
  193.6 2.9 %adam.5 = (f32[192,768]{1,0:T(8,128)}, f32[192,768]{1,0:T(8,128)}, f32[192,768]{1,0:T(8,128)}, f32[192,768]{1,0:T(8,128)}, f32[192,1]{1,0:T(8,128)}) custom-call(s32[18]{0:T(128)} %copy-done.7, bf16[960,384]{1,0:T(8,128)(2,1)} %copy-done.16, bf16[960,384]{1,0:T(8,128)(2,1)} %copy-done.16, bf16[192,768]{1,0:T(8,128)(2,1)} %refs_2_.1, f32[192,768]{1,0:T(8,128)} %refs_3_.1, ...), custom_call_target="tpu_custom_call" | custom-call | flops 3300000000 | tf_op jit(solution)/shard_map/adam/pallas_call | solution.py:577
  196.5 4.3 %collective-permute-done.59.refs_2_ = bf16[144,768]{1,0:T(8,128)(2,1)S(1)} collective-permute-done((bf16[144,768]{1,0:T(8,128)(2,1)S(1)}, bf16[144,768]{1,0:T(8,128)(2,1)S(1)}, u32[]{:S(2)}, u32[]{:S(2)}) %collective-permute-start.59) | collective-permute-done | bytes 221216 | tf_op jit(solution)/shard_map/ppermute | solution.py:647
  201.5 4.7 %adam.7 = (f32[288,768]{1,0:T(8,128)}, f32[288,768]{1,0:T(8,128)}, f32[288,768]{1,0:T(8,128)}, f32[288,768]{1,0:T(8,128)}, f32[288,1]{1,0:T(8,128)}) custom-call(s32[18]{0:T(128)} %copy-done.7, bf16[1152,384]{1,0:T(8,128)(2,1)} %copy-done.15, bf16[1152,384]{1,0:T(8,128)(2,1)} %copy-done.15, bf16[960,384]{1,0:T(8,128)(2,1)} %copy-done.16, ...), custom_call_target="tpu_custom_call" | custom-call | flops 3300000000 | tf_op jit(solution)/shard_map/adam/pallas_call | solution.py:577
  206.2 1.2 collective-permute-done.60.refs_2_
  209.3 6.7 %adam.6 = (f32[192,2304]{1,0:T(8,128)}, f32[192,2304]{1,0:T(8,128)}, f32[192,2304]{1,0:T(8,128)}, f32[192,2304]{1,0:T(8,128)}, f32[192,1]{1,0:T(8,128)}) custom-call(s32[18]{0:T(128)} %copy-done.7, bf16[1152,384]{1,0:T(8,128)(2,1)} %copy-done.15, bf16[1152,384]{1,0:T(8,128)(2,1)} %copy-done.15, bf16[1152,384]{1,0:T(8,128)(2,1)} %copy-done.15, ...), custom_call_target="tpu_custom_call" | custom-call | flops 3300000000 | tf_op jit(solution)/shard_map/adam/pallas_call | solution.py:577
  216.1 1.0 reduce.1
  218.7 6.9 %adam.4 = (f32[192,2304]{1,0:T(8,128)}, f32[192,2304]{1,0:T(8,128)}, f32[192,2304]{1,0:T(8,128)}, f32[192,2304]{1,0:T(8,128)}, f32[192,1]{1,0:T(8,128)}) custom-call(s32[18]{0:T(128)} %copy-done.7, bf16[288,768]{1,0:T(8,128)(2,1)} %copy-done.12, bf16[288,768]{1,0:T(8,128)(2,1)} %copy-done.12, bf16[288,768]{1,0:T(8,128)(2,1)} %copy-done.12, ...), custom_call_target="tpu_custom_call" | custom-call | flops 3300000000 | tf_op jit(solution)/shard_map/adam/pallas_call | solution.py:577
  225.6 1.0 reduce
  (171 shorter events, 28.7 us)
Async XLA Ops:
  0.7 25.1 %collective-permute-start.6 = (bf16[192,2304]{1,0:T(8,128)(2,1)}, bf16[192,2304]{1,0:T(8,128)(2,1)S(1)}, u32[]{:S(2)}, u32[]{:S(2)}) collective-permute-start(bf16[192,2304]{1,0:T(8,128)(2,1)} %refs_6_.3), channel_id=1, source_target_pairs={{0,2},{2,0},{1,3},{3,1},{4,6},{6,4},{5,7},{7,5},{8,10},{10,8},{9,1... | collective-permute-start | bytes 2654216 | tf_op jit(solution)/shard_map/ppermute | solution.py:599
  3.7 19.6 %collective-permute-start.5 = (bf16[192,2304]{1,0:T(8,128)(2,1)}, bf16[192,2304]{1,0:T(8,128)(2,1)S(1)}, u32[]{:S(2)}, u32[]{:S(2)}) collective-permute-start(bf16[192,2304]{1,0:T(8,128)(2,1)} %refs_6_.3), channel_id=1, source_target_pairs={{0,1},{1,0},{2,3},{3,2},{4,5},{5,4},{6,7},{7,6},{8,9},{9,8},{10,11... | collective-permute-start | bytes 2654216 | tf_op jit(solution)/shard_map/ppermute | solution.py:595
  4.6 10.0 %collective-permute-start.1 = (bf16[64,768]{1,0:T(8,128)(2,1)S(1)}, bf16[64,768]{1,0:T(8,128)(2,1)S(1)}, u32[]{:S(2)}, u32[]{:S(2)}) collective-permute-start(bf16[64,768]{1,0:T(8,128)(2,1)S(1)} %get-tuple-element.346), channel_id=1, source_target_pairs={{4,0},{8,4},{12,8},{16,12},{20,16},{24,20},{28,24},{5,1},{9,5},{13... | collective-permute-start | bytes 294920 | tf_op jit(solution)/shard_map/ppermute | solution.py:832
  5.9 9.8 %collective-permute-start = (bf16[64,768]{1,0:T(8,128)(2,1)S(1)}, bf16[64,768]{1,0:T(8,128)(2,1)S(1)}, u32[]{:S(2)}, u32[]{:S(2)}) collective-permute-start(bf16[64,768]{1,0:T(8,128)(2,1)S(1)} %get-tuple-element.347), channel_id=1, source_target_pairs={{0,4},{4,8},{8,12},{12,16},{16,20},{20,24},{24,28},{1,5},{5,9},{9,... | collective-permute-start | bytes 294920 | tf_op jit(solution)/shard_map/ppermute | solution.py:832
  13.5 6.2 %collective-permute-start.11 = (bf16[96,768]{1,0:T(8,128)(2,1)S(1)}, bf16[96,768]{1,0:T(8,128)(2,1)S(1)}, u32[]{:S(2)}, u32[]{:S(2)}) collective-permute-start(bf16[96,768]{1,0:T(8,128)(2,1)S(1)} %get-tuple-element.182.refs_4_), channel_id=1, source_target_pairs={{0,1},{1,0},{2,3},{3,2},{4,5},{5,4},{6,7},{7,6},{8,9},{9,8},{10,11... | collective-permute-start | bytes 442376 | tf_op jit(solution)/shard_map/ppermute | solution.py:595
  15.3 5.0 %collective-permute-start.7 = (bf16[192,768]{1,0:T(8,128)(2,1)S(1)}, bf16[192,768]{1,0:T(8,128)(2,1)S(1)}, u32[]{:S(2)}, u32[]{:S(2)}) collective-permute-start(bf16[192,768]{1,0:T(8,128)(2,1)S(1)} %get-tuple-element.180.refs_2_), channel_id=1, source_target_pairs={{0,1},{1,0},{2,3},{3,2},{4,5},{5,4},{6,7},{7,6},{8,9},{9,8},{10,11... | collective-permute-start | bytes 884744 | tf_op jit(solution)/shard_map/ppermute | solution.py:595
  16.4 5.1 %collective-permute-start.10 = (bf16[192,768]{1,0:T(8,128)(2,1)S(1)}, bf16[192,768]{1,0:T(8,128)(2,1)S(1)}, u32[]{:S(2)}, u32[]{:S(2)}) collective-permute-start(bf16[192,768]{1,0:T(8,128)(2,1)S(1)} %get-tuple-element.181.refs_2_), channel_id=1, source_target_pairs={{0,1},{1,0},{2,3},{3,2},{4,5},{5,4},{6,7},{7,6},{8,9},{9,8},{10,11... | collective-permute-start | bytes 884744 | tf_op jit(solution)/shard_map/ppermute | solution.py:595
  19.7 2.4 %collective-permute-start.12 = (bf16[192,768]{1,0:T(8,128)(2,1)S(1)}, bf16[192,768]{1,0:T(8,128)(2,1)S(1)}, u32[]{:S(2)}, u32[]{:S(2)}) collective-permute-start(bf16[192,768]{1,0:T(8,128)(2,1)S(1)} %concatenate.21.refs_3_), channel_id=1, source_target_pairs={{0,1},{1,0},{2,3},{3,2},{4,5},{5,4},{6,7},{7,6},{8,9},{9,8},{10,11... | collective-permute-start | bytes 884744 | tf_op jit(solution)/shard_map/ppermute | solution.py:595
  20.3 2.1 collective-permute-start.8
  21.5 1.7 collective-permute-start.9
  22.1 3.6 %collective-permute-start.3 = (bf16[2,192]{1,0:T(2,128)(2,1)S(1)}, bf16[2,192]{1,0:T(2,128)(2,1)S(1)}, u32[]{:S(2)}, u32[]{:S(2)}) collective-permute-start(bf16[2,192]{1,0:T(2,128)(2,1)S(1)} %pad_maximum_fusion.4.refs_4_), channel_id=1, source_target_pairs={{0,2},{2,0},{1,3},{3,1},{4,6},{6,4},{5,7},{7,5},{8,10},{10,8},{9,1... | collective-permute-start | bytes 2312 | tf_op jit(solution)/shard_map/ppermute | solution.py:599
  22.3 3.4 %collective-permute-start.2 = (bf16[2,192]{1,0:T(2,128)(2,1)S(1)}, bf16[2,192]{1,0:T(2,128)(2,1)S(1)}, u32[]{:S(2)}, u32[]{:S(2)}) collective-permute-start(bf16[2,192]{1,0:T(2,128)(2,1)S(1)} %pad_maximum_fusion.4.refs_4_), channel_id=1, source_target_pairs={{0,1},{1,0},{2,3},{3,2},{4,5},{5,4},{6,7},{7,6},{8,9},{9,8},{10,11... | collective-permute-start | bytes 2312 | tf_op jit(solution)/shard_map/ppermute | solution.py:595
  22.4 166.8 %copy-start.7 = (s32[18]{0:T(128)}, s32[18]{0:T(128)S(1)}, u32[]{:S(2)}) copy-start(s32[18]{0:T(128)S(1)} %pad_add_fusion.refs_3_.refs_0_.info_ref) | copy-start | bytes 220
  25.7 2.6 %collective-permute-start.13 = (bf16[192,2304]{1,0:T(8,128)(2,1)S(1)}, bf16[192,2304]{1,0:T(8,128)(2,1)S(1)}, u32[]{:S(2)}, u32[]{:S(2)}) collective-permute-start(bf16[192,2304]{1,0:T(8,128)(2,1)S(1)} %get-tuple-element.183.refs_10_), channel_id=1, source_target_pairs={{0,1},{1,0},{2,3},{3,2},{4,5},{5,4},{6,7},{7,6},{8,9},{9,8},{10,11... | collective-permute-start | bytes 2654216 | tf_op jit(solution)/shard_map/ppermute | solution.py:595
  25.8 2.5 %collective-permute-start.4 = (bf16[2,192]{1,0:T(2,128)(2,1)S(1)}, bf16[2,192]{1,0:T(2,128)(2,1)S(1)}, u32[]{:S(2)}, u32[]{:S(2)}) collective-permute-start(bf16[2,192]{1,0:T(2,128)(2,1)S(1)} %collective-permute-done.3.refs_4_.refs_6_), channel_id=1, source_target_pairs={{0,1},{1,0},{2,3},{3,2},{4,5},{5,4},{6,7},{7,6},{8,9},{9,8},{10,11... | collective-permute-start | bytes 2312 | tf_op jit(solution)/shard_map/ppermute | solution.py:595
  26.3 9.6 %collective-permute-start.15 = (bf16[96,768]{1,0:T(8,128)(2,1)S(1)}, bf16[96,768]{1,0:T(8,128)(2,1)S(1)}, u32[]{:S(2)}, u32[]{:S(2)}) collective-permute-start(bf16[96,768]{1,0:T(8,128)(2,1)S(1)} %get-tuple-element.188), channel_id=1, source_target_pairs={{0,2},{2,0},{1,3},{3,1},{4,6},{6,4},{5,7},{7,5},{8,10},{10,8},{9,1... | collective-permute-start | bytes 442376 | tf_op jit(solution)/shard_map/ppermute | solution.py:599
  26.5 12.0 %collective-permute-start.14 = (bf16[192,768]{1,0:T(8,128)(2,1)S(1)}, bf16[192,768]{1,0:T(8,128)(2,1)S(1)}, u32[]{:S(2)}, u32[]{:S(2)}) collective-permute-start(bf16[192,768]{1,0:T(8,128)(2,1)S(1)} %get-tuple-element.187), channel_id=1, source_target_pairs={{0,2},{2,0},{1,3},{3,1},{4,6},{6,4},{5,7},{7,5},{8,10},{10,8},{9,1... | collective-permute-start | bytes 884744 | tf_op jit(solution)/shard_map/ppermute | solution.py:599
  38.5 2.4 %collective-permute-start.16 = (bf16[192,768]{1,0:T(8,128)(2,1)S(1)}, bf16[192,768]{1,0:T(8,128)(2,1)S(1)}, u32[]{:S(2)}, u32[]{:S(2)}) collective-permute-start(bf16[192,768]{1,0:T(8,128)(2,1)S(1)} %get-tuple-element.190.refs_7_), channel_id=1, source_target_pairs={{0,1},{1,0},{2,3},{3,2},{4,5},{5,4},{6,7},{7,6},{8,9},{9,8},{10,11... | collective-permute-start | bytes 884744 | tf_op jit(solution)/shard_map/ppermute | solution.py:595
  38.5 15.0 %collective-permute-start.17 = (bf16[96,768]{1,0:T(8,128)(2,1)S(1)}, bf16[96,768]{1,0:T(8,128)(2,1)S(1)}, u32[]{:S(2)}, u32[]{:S(2)}) collective-permute-start(bf16[96,768]{1,0:T(8,128)(2,1)S(1)} %get-tuple-element.197.refs_5_), channel_id=1, source_target_pairs={{0,4},{4,0},{8,12},{12,8},{16,20},{20,16},{24,28},{28,24},{1,5},{5... | collective-permute-start | bytes 442376 | tf_op jit(solution)/shard_map/ppermute | solution.py:861
  40.9 12.6 %collective-permute-start.18 = (bf16[192,768]{1,0:T(8,128)(2,1)S(1)}, bf16[192,768]{1,0:T(8,128)(2,1)S(1)}, u32[]{:S(2)}, u32[]{:S(2)}) collective-permute-start(bf16[192,768]{1,0:T(8,128)(2,1)S(1)} %get-tuple-element.198.refs_9_), channel_id=1, source_target_pairs={{0,2},{2,0},{1,3},{3,1},{4,6},{6,4},{5,7},{7,5},{8,10},{10,8},{9,1... | collective-permute-start | bytes 884744 | tf_op jit(solution)/shard_map/ppermute | solution.py:599
  41.4 14.9 %collective-permute-start.19 = (bf16[192,768]{1,0:T(8,128)(2,1)S(1)}, bf16[192,768]{1,0:T(8,128)(2,1)S(1)}, u32[]{:S(2)}, u32[]{:S(2)}) collective-permute-start(bf16[192,768]{1,0:T(8,128)(2,1)S(1)} %get-tuple-element.199.refs_13_), channel_id=1, source_target_pairs={{0,2},{2,0},{1,3},{3,1},{4,6},{6,4},{5,7},{7,5},{8,10},{10,8},{9,1... | collective-permute-start | bytes 884744 | tf_op jit(solution)/shard_map/ppermute | solution.py:599
  42.9 16.5 %copy-start.10 = (bf16[1,1024,768]{2,1,0:T(8,128)(2,1)S(1)}, bf16[1,1024,768]{2,1,0:T(8,128)(2,1)}, u32[]{:S(2)}) copy-start(bf16[1,1024,768]{2,1,0:T(8,128)(2,1)} %param.25) | copy-start | bytes 4718596
  56.3 3.1 %collective-permute-start.22 = (bf16[192,768]{1,0:T(8,128)(2,1)S(1)}, bf16[192,768]{1,0:T(8,128)(2,1)S(1)}, u32[]{:S(2)}, u32[]{:S(2)}) collective-permute-start(bf16[192,768]{1,0:T(8,128)(2,1)S(1)} %get-tuple-element.203.refs_11_), channel_id=1, source_target_pairs={{0,1},{1,0},{2,3},{3,2},{4,5},{5,4},{6,7},{7,6},{8,9},{9,8},{10,11... | collective-permute-start | bytes 884744 | tf_op jit(solution)/shard_map/ppermute | solution.py:595
  56.3 3.1 %collective-permute-start.23 = (bf16[192,768]{1,0:T(8,128)(2,1)S(1)}, bf16[192,768]{1,0:T(8,128)(2,1)S(1)}, u32[]{:S(2)}, u32[]{:S(2)}) collective-permute-start(bf16[192,768]{1,0:T(8,128)(2,1)S(1)} %get-tuple-element.204.refs_15_), channel_id=1, source_target_pairs={{0,1},{1,0},{2,3},{3,2},{4,5},{5,4},{6,7},{7,6},{8,9},{9,8},{10,11... | collective-permute-start | bytes 884744 | tf_op jit(solution)/shard_map/ppermute | solution.py:595
  56.9 1.7 collective-permute-start.20
  56.9 2.5 %collective-permute-start.21 = (bf16[96,768]{1,0:T(8,128)(2,1)S(1)}, bf16[96,768]{1,0:T(8,128)(2,1)S(1)}, u32[]{:S(2)}, u32[]{:S(2)}) collective-permute-start(bf16[96,768]{1,0:T(8,128)(2,1)S(1)} %get-tuple-element.202.refs_6_), channel_id=1, source_target_pairs={{0,1},{1,0},{2,3},{3,2},{4,5},{5,4},{6,7},{7,6},{8,9},{9,8},{10,11... | collective-permute-start | bytes 442376 | tf_op jit(solution)/shard_map/ppermute | solution.py:595
  57.4 19.3 %collective-permute-start.25 = (bf16[96,768]{1,0:T(8,128)(2,1)S(1)}, bf16[96,768]{1,0:T(8,128)(2,1)S(1)}, u32[]{:S(2)}, u32[]{:S(2)}) collective-permute-start(bf16[96,768]{1,0:T(8,128)(2,1)S(1)} %get-tuple-element.207.refs_7_), channel_id=1, source_target_pairs={{0,2},{2,0},{1,3},{3,1},{4,6},{6,4},{5,7},{7,5},{8,10},{10,8},{9,1... | collective-permute-start | bytes 442376 | tf_op jit(solution)/shard_map/ppermute | solution.py:599
  58.6 18.1 %collective-permute-start.24 = (bf16[192,768]{1,0:T(8,128)(2,1)S(1)}, bf16[192,768]{1,0:T(8,128)(2,1)S(1)}, u32[]{:S(2)}, u32[]{:S(2)}) collective-permute-start(bf16[192,768]{1,0:T(8,128)(2,1)S(1)} %get-tuple-element.201.refs_3_), channel_id=1, source_target_pairs={{0,2},{2,0},{1,3},{3,1},{4,6},{6,4},{5,7},{7,5},{8,10},{10,8},{9,1... | collective-permute-start | bytes 884744 | tf_op jit(solution)/shard_map/ppermute | solution.py:599
  77.2 3.8 %collective-permute-start.28 = (bf16[2,1152,384]{2,1,0:T(8,128)(2,1)S(1)}, bf16[2,1152,384]{2,1,0:T(8,128)(2,1)S(1)}, u32[]{:S(2)}, u32[]{:S(2)}) collective-permute-start(bf16[2,1152,384]{2,1,0:T(8,128)(2,1)S(1)} %get-tuple-element.217), channel_id=1, source_target_pairs={{0,1},{1,0},{2,3},{3,2},{4,5},{5,4},{6,7},{7,6},{8,9},{9,8},{10,11... | collective-permute-start | bytes 5308424 | tf_op jit(solution)/shard_map/ppermute | solution.py:595
  77.3 7.4 %collective-permute-start.26 = (bf16[192,768]{1,0:T(8,128)(2,1)S(1)}, bf16[192,768]{1,0:T(8,128)(2,1)S(1)}, u32[]{:S(2)}, u32[]{:S(2)}) collective-permute-start(bf16[192,768]{1,0:T(8,128)(2,1)S(1)} %get-tuple-element.209.refs_5_), channel_id=1, source_target_pairs={{0,1},{1,0},{2,3},{3,2},{4,5},{5,4},{6,7},{7,6},{8,9},{9,8},{10,11... | collective-permute-start | bytes 884744 | tf_op jit(solution)/shard_map/ppermute | solution.py:595
  77.8 6.9 %collective-permute-start.27 = (bf16[96,768]{1,0:T(8,128)(2,1)S(1)}, bf16[96,768]{1,0:T(8,128)(2,1)S(1)}, u32[]{:S(2)}, u32[]{:S(2)}) collective-permute-start(bf16[96,768]{1,0:T(8,128)(2,1)S(1)} %get-tuple-element.210.refs_9_), channel_id=1, source_target_pairs={{0,1},{1,0},{2,3},{3,2},{4,5},{5,4},{6,7},{7,6},{8,9},{9,8},{10,11... | collective-permute-start | bytes 442376 | tf_op jit(solution)/shard_map/ppermute | solution.py:595
  82.0 17.0 %collective-permute-start.30 = (bf16[2,288,384]{2,1,0:T(8,128)(2,1)S(1)}, bf16[2,288,384]{2,1,0:T(8,128)(2,1)S(1)}, u32[]{:S(2)}, u32[]{:S(2)}) collective-permute-start(bf16[2,288,384]{2,1,0:T(8,128)(2,1)S(1)} %get-tuple-element.229), channel_id=1, source_target_pairs={{0,4},{4,0},{8,12},{12,8},{16,20},{20,16},{24,28},{28,24},{1,5},{5... | collective-permute-start | bytes 1327112 | tf_op jit(solution)/shard_map/ppermute | solution.py:647
  83.5 15.5 %collective-permute-start.29 = (bf16[576,384]{1,0:T(8,128)(2,1)S(1)}, bf16[576,384]{1,0:T(8,128)(2,1)S(1)}, u32[]{:S(2)}, u32[]{:S(2)}) collective-permute-start(bf16[576,384]{1,0:T(8,128)(2,1)S(1)} %get-tuple-element.220.refs_18_), channel_id=1, source_target_pairs={{0,2},{2,0},{1,3},{3,1},{4,6},{6,4},{5,7},{7,5},{8,10},{10,8},{9,1... | collective-permute-start | bytes 1327112 | tf_op jit(solution)/shard_map/ppermute | solution.py:599
  99.8 8.5 %collective-permute-start.33 = (bf16[2,960,384]{2,1,0:T(8,128)(2,1)S(1)}, bf16[2,960,384]{2,1,0:T(8,128)(2,1)S(1)}, u32[]{:S(2)}, u32[]{:S(2)}) collective-permute-start(bf16[2,960,384]{2,1,0:T(8,128)(2,1)S(1)} %get-tuple-element.234.refs_12_), channel_id=1, source_target_pairs={{0,1},{1,0},{2,3},{3,2},{4,5},{5,4},{6,7},{7,6},{8,9},{9,8},{10,11... | collective-permute-start | bytes 4423688 | tf_op jit(solution)/shard_map/ppermute | solution.py:595
  99.9 8.0 %collective-permute-start.32 = (bf16[288,384]{1,0:T(8,128)(2,1)S(1)}, bf16[288,384]{1,0:T(8,128)(2,1)S(1)}, u32[]{:S(2)}, u32[]{:S(2)}) collective-permute-start(bf16[288,384]{1,0:T(8,128)(2,1)S(1)} %get-tuple-element.242), channel_id=1, source_target_pairs={{0,2},{2,0},{1,3},{3,1},{4,6},{6,4},{5,7},{7,5},{8,10},{10,8},{9,1... | collective-permute-start | bytes 663560 | tf_op jit(solution)/shard_map/ppermute | solution.py:599
  100.8 7.5 %collective-permute-start.31 = (bf16[288,384]{1,0:T(8,128)(2,1)S(1)}, bf16[288,384]{1,0:T(8,128)(2,1)S(1)}, u32[]{:S(2)}, u32[]{:S(2)}) collective-permute-start(bf16[288,384]{1,0:T(8,128)(2,1)S(1)} %get-tuple-element.233.refs_11_), channel_id=1, source_target_pairs={{0,4},{4,0},{8,12},{12,8},{16,20},{20,16},{24,28},{28,24},{1,5},{5... | collective-permute-start | bytes 663560 | tf_op jit(solution)/shard_map/ppermute | solution.py:647
  109.7 10.5 %collective-permute-start.34 = (bf16[288,384]{1,0:T(8,128)(2,1)S(1)}, bf16[288,384]{1,0:T(8,128)(2,1)S(1)}, u32[]{:S(2)}, u32[]{:S(2)}) collective-permute-start(bf16[288,384]{1,0:T(8,128)(2,1)S(1)} %get-tuple-element.246.refs_16_), channel_id=1, source_target_pairs={{0,8},{4,12},{8,0},{12,4},{16,24},{20,28},{24,16},{28,20},{1,9},{5... | collective-permute-start | bytes 663560 | tf_op jit(solution)/shard_map/ppermute | solution.py:647
  111.4 9.7 %collective-permute-start.36 = (bf16[2,240,384]{2,1,0:T(8,128)(2,1)S(1)}, bf16[2,240,384]{2,1,0:T(8,128)(2,1)S(1)}, u32[]{:S(2)}, u32[]{:S(2)}) collective-permute-start(bf16[2,240,384]{2,1,0:T(8,128)(2,1)S(1)} %get-tuple-element.254), channel_id=1, source_target_pairs={{0,4},{4,0},{8,12},{12,8},{16,20},{20,16},{24,28},{28,24},{1,5},{5... | collective-permute-start | bytes 1105928 | tf_op jit(solution)/shard_map/ppermute | solution.py:647
  112.5 9.8 %collective-permute-start.35 = (bf16[480,384]{1,0:T(8,128)(2,1)S(1)}, bf16[480,384]{1,0:T(8,128)(2,1)S(1)}, u32[]{:S(2)}, u32[]{:S(2)}) collective-permute-start(bf16[480,384]{1,0:T(8,128)(2,1)S(1)} %get-tuple-element.247.refs_17_), channel_id=1, source_target_pairs={{0,2},{2,0},{1,3},{3,1},{4,6},{6,4},{5,7},{7,5},{8,10},{10,8},{9,1... | collective-permute-start | bytes 1105928 | tf_op jit(solution)/shard_map/ppermute | solution.py:599
  123.1 10.3 %collective-permute-start.40 = (bf16[2,576,512]{2,1,0:T(8,128)(2,1)S(1)}, bf16[2,576,512]{2,1,0:T(8,128)(2,1)S(1)}, u32[]{:S(2)}, u32[]{:S(2)}) collective-permute-start(bf16[2,576,512]{2,1,0:T(8,128)(2,1)S(1)} %get-tuple-element.260.refs_16_), channel_id=1, source_target_pairs={{0,1},{1,0},{2,3},{3,2},{4,5},{5,4},{6,7},{7,6},{8,9},{9,8},{10,11... | collective-permute-start | bytes 3538952 | tf_op jit(solution)/shard_map/ppermute | solution.py:595
  123.2 10.2 %collective-permute-start.39 = (bf16[240,384]{1,0:T(8,128)(2,1)S(1)}, bf16[240,384]{1,0:T(8,128)(2,1)S(1)}, u32[]{:S(2)}, u32[]{:S(2)}) collective-permute-start(bf16[240,384]{1,0:T(8,128)(2,1)S(1)} %get-tuple-element.266), channel_id=1, source_target_pairs={{0,2},{2,0},{1,3},{3,1},{4,6},{6,4},{5,7},{7,5},{8,10},{10,8},{9,1... | collective-permute-start | bytes 552968 | tf_op jit(solution)/shard_map/ppermute | solution.py:599
  124.4 8.9 %collective-permute-start.38 = (bf16[240,384]{1,0:T(8,128)(2,1)S(1)}, bf16[240,384]{1,0:T(8,128)(2,1)S(1)}, u32[]{:S(2)}, u32[]{:S(2)}) collective-permute-start(bf16[240,384]{1,0:T(8,128)(2,1)S(1)} %get-tuple-element.259.refs_15_), channel_id=1, source_target_pairs={{0,4},{4,0},{8,12},{12,8},{16,20},{20,16},{24,28},{28,24},{1,5},{5... | collective-permute-start | bytes 552968 | tf_op jit(solution)/shard_map/ppermute | solution.py:647
  125.0 13.4 %collective-permute-start.37 = (bf16[288,384]{1,0:T(8,128)(2,1)S(1)}, bf16[288,384]{1,0:T(8,128)(2,1)S(1)}, u32[]{:S(2)}, u32[]{:S(2)}) collective-permute-start(bf16[288,384]{1,0:T(8,128)(2,1)S(1)} %get-tuple-element.258.refs_14_.refs_1_), channel_id=1, source_target_pairs={{0,16},{4,20},{8,24},{12,28},{16,0},{20,4},{24,8},{28,12},{1,17},{... | collective-permute-start | bytes 663560 | tf_op jit(solution)/shard_map/ppermute | solution.py:647
  134.3 10.1 %collective-permute-start.44 = (bf16[2,576,256]{2,1,0:T(8,128)(2,1)S(1)}, bf16[2,576,256]{2,1,0:T(8,128)(2,1)S(1)}, u32[]{:S(2)}, u32[]{:S(2)}) collective-permute-start(bf16[2,576,256]{2,1,0:T(8,128)(2,1)S(1)} %get-tuple-element.277), channel_id=1, source_target_pairs={{0,1},{1,0},{2,3},{3,2},{4,5},{5,4},{6,7},{7,6},{8,9},{9,8},{10,11... | collective-permute-start | bytes 1769480 | tf_op jit(solution)/shard_map/ppermute | solution.py:595
  134.4 9.5 %collective-permute-start.42 = (bf16[288,512]{1,0:T(8,128)(2,1)S(1)}, bf16[288,512]{1,0:T(8,128)(2,1)S(1)}, u32[]{:S(2)}, u32[]{:S(2)}) collective-permute-start(bf16[288,512]{1,0:T(8,128)(2,1)S(1)} %get-tuple-element.274), channel_id=1, source_target_pairs={{0,2},{2,0},{1,3},{3,1},{4,6},{6,4},{5,7},{7,5},{8,10},{10,8},{9,1... | collective-permute-start | bytes 884744 | tf_op jit(solution)/shard_map/ppermute | solution.py:599
  135.4 9.1 %collective-permute-start.43 = (bf16[2,144,512]{2,1,0:T(8,128)(2,1)S(1)}, bf16[2,144,512]{2,1,0:T(8,128)(2,1)S(1)}, u32[]{:S(2)}, u32[]{:S(2)}) collective-permute-start(bf16[2,144,512]{2,1,0:T(8,128)(2,1)S(1)} %get-tuple-element.275), channel_id=1, source_target_pairs={{0,4},{4,0},{8,12},{12,8},{16,20},{20,16},{24,28},{28,24},{1,5},{5... | collective-permute-start | bytes 884744 | tf_op jit(solution)/shard_map/ppermute | solution.py:647
  136.6 6.5 %collective-permute-start.41 = (bf16[240,384]{1,0:T(8,128)(2,1)S(1)}, bf16[240,384]{1,0:T(8,128)(2,1)S(1)}, u32[]{:S(2)}, u32[]{:S(2)}) collective-permute-start(bf16[240,384]{1,0:T(8,128)(2,1)S(1)} %get-tuple-element.271), channel_id=1, source_target_pairs={{0,8},{4,12},{8,0},{12,4},{16,24},{20,28},{24,16},{28,20},{1,9},{5... | collective-permute-start | bytes 552968 | tf_op jit(solution)/shard_map/ppermute | solution.py:647
  145.4 10.0 %collective-permute-start.47 = (bf16[288,256]{1,0:T(8,128)(2,1)S(1)}, bf16[288,256]{1,0:T(8,128)(2,1)S(1)}, u32[]{:S(2)}, u32[]{:S(2)}) collective-permute-start(bf16[288,256]{1,0:T(8,128)(2,1)S(1)} %get-tuple-element.283), channel_id=1, source_target_pairs={{0,2},{2,0},{1,3},{3,1},{4,6},{6,4},{5,7},{7,5},{8,10},{10,8},{9,1... | collective-permute-start | bytes 442376 | tf_op jit(solution)/shard_map/ppermute | solution.py:599
  146.6 20.8 %collective-permute-start.45 = (bf16[288,384]{1,0:T(8,128)(2,1)S(1)}, bf16[288,384]{1,0:T(8,128)(2,1)S(1)}, u32[]{:S(2)}, u32[]{:S(2)}) collective-permute-start(bf16[288,384]{1,0:T(8,128)(2,1)S(1)} %get-tuple-element.279.refs_1_), channel_id=1, source_target_pairs={{0,8},{4,12},{8,0},{12,4},{16,24},{20,28},{24,16},{28,20},{1,9},{5... | collective-permute-start | bytes 663560 | tf_op jit(solution)/shard_map/ppermute | solution.py:647
  148.0 19.4 %collective-permute-start.49 = (bf16[64,1536]{1,0:T(8,128)(2,1)S(1)}, bf16[64,1536]{1,0:T(8,128)(2,1)S(1)}, u32[]{:S(2)}, u32[]{:S(2)}) collective-permute-start(bf16[64,1536]{1,0:T(8,128)(2,1)S(1)} %get-tuple-element.285), channel_id=1, source_target_pairs={{0,4},{4,8},{8,12},{12,16},{16,20},{20,24},{24,28},{1,5},{5,9},{9,... | collective-permute-start | bytes 589832 | tf_op jit(solution)/shard_map/ppermute | solution.py:901
  151.4 16.1 %collective-permute-start.50 = (bf16[64,1536]{1,0:T(8,128)(2,1)S(1)}, bf16[64,1536]{1,0:T(8,128)(2,1)S(1)}, u32[]{:S(2)}, u32[]{:S(2)}) collective-permute-start(bf16[64,1536]{1,0:T(8,128)(2,1)S(1)} %get-tuple-element.286), channel_id=1, source_target_pairs={{4,0},{8,4},{12,8},{16,12},{20,16},{24,20},{28,24},{5,1},{9,5},{13... | collective-permute-start | bytes 589832 | tf_op jit(solution)/shard_map/ppermute | solution.py:901
  152.7 9.2 %collective-permute-start.48 = (bf16[2,144,256]{2,1,0:T(8,128)(2,1)S(1)}, bf16[2,144,256]{2,1,0:T(8,128)(2,1)S(1)}, u32[]{:S(2)}, u32[]{:S(2)}) collective-permute-start(bf16[2,144,256]{2,1,0:T(8,128)(2,1)S(1)} %get-tuple-element.284), channel_id=1, source_target_pairs={{0,4},{4,0},{8,12},{12,8},{16,20},{20,16},{24,28},{28,24},{1,5},{5... | collective-permute-start | bytes 442376 | tf_op jit(solution)/shard_map/ppermute | solution.py:647
  155.4 11.2 %collective-permute-start.46 = (bf16[240,384]{1,0:T(8,128)(2,1)S(1)}, bf16[240,384]{1,0:T(8,128)(2,1)S(1)}, u32[]{:S(2)}, u32[]{:S(2)}) collective-permute-start(bf16[240,384]{1,0:T(8,128)(2,1)S(1)} %get-tuple-element.280.refs_3_), channel_id=1, source_target_pairs={{0,16},{4,20},{8,24},{12,28},{16,0},{20,4},{24,8},{28,12},{1,17},{... | collective-permute-start | bytes 552968 | tf_op jit(solution)/shard_map/ppermute | solution.py:647
  162.0 8.6 %collective-permute-start.53 = (bf16[144,512]{1,0:T(8,128)(2,1)S(1)}, bf16[144,512]{1,0:T(8,128)(2,1)S(1)}, u32[]{:S(2)}, u32[]{:S(2)}) collective-permute-start(bf16[144,512]{1,0:T(8,128)(2,1)S(1)} %get-tuple-element.298), channel_id=1, source_target_pairs={{0,4},{4,0},{8,12},{12,8},{16,20},{20,16},{24,28},{28,24},{1,5},{5... | collective-permute-start | bytes 442376 | tf_op jit(solution)/shard_map/ppermute | solution.py:647
  166.6 12.4 %collective-permute-start.54 = (bf16[144,512]{1,0:T(8,128)(2,1)S(1)}, bf16[144,512]{1,0:T(8,128)(2,1)S(1)}, u32[]{:S(2)}, u32[]{:S(2)}) collective-permute-start(bf16[144,512]{1,0:T(8,128)(2,1)S(1)} %get-tuple-element.299), channel_id=1, source_target_pairs={{0,2},{2,0},{1,3},{3,1},{4,6},{6,4},{5,7},{7,5},{8,10},{10,8},{9,1... | collective-permute-start | bytes 442376 | tf_op jit(solution)/shard_map/ppermute | solution.py:599
  168.2 10.8 %collective-permute-start.56 = (bf16[144,256]{1,0:T(8,128)(2,1)S(1)}, bf16[144,256]{1,0:T(8,128)(2,1)S(1)}, u32[]{:S(2)}, u32[]{:S(2)}) collective-permute-start(bf16[144,256]{1,0:T(8,128)(2,1)S(1)} %get-tuple-element.302), channel_id=1, source_target_pairs={{0,2},{2,0},{1,3},{3,1},{4,6},{6,4},{5,7},{7,5},{8,10},{10,8},{9,1... | collective-permute-start | bytes 221192 | tf_op jit(solution)/shard_map/ppermute | solution.py:599
  169.5 9.6 %collective-permute-start.55 = (bf16[144,256]{1,0:T(8,128)(2,1)S(1)}, bf16[144,256]{1,0:T(8,128)(2,1)S(1)}, u32[]{:S(2)}, u32[]{:S(2)}) collective-permute-start(bf16[144,256]{1,0:T(8,128)(2,1)S(1)} %get-tuple-element.294.refs_16_), channel_id=1, source_target_pairs={{0,4},{4,0},{8,12},{12,8},{16,20},{20,16},{24,28},{28,24},{1,5},{5... | collective-permute-start | bytes 221192 | tf_op jit(solution)/shard_map/ppermute | solution.py:647
  169.5 9.6 %collective-permute-start.52 = (bf16[240,384]{1,0:T(8,128)(2,1)S(1)}, bf16[240,384]{1,0:T(8,128)(2,1)S(1)}, u32[]{:S(2)}, u32[]{:S(2)}) collective-permute-start(bf16[240,384]{1,0:T(8,128)(2,1)S(1)} %get-tuple-element.293.refs_15_.refs_3_), channel_id=1, source_target_pairs={{0,8},{4,12},{8,0},{12,4},{16,24},{20,28},{24,16},{28,20},{1,9},{5... | collective-permute-start | bytes 552968 | tf_op jit(solution)/shard_map/ppermute | solution.py:647
  170.6 10.3 %collective-permute-start.51 = (bf16[576,384]{1,0:T(8,128)(2,1)S(1)}, bf16[576,384]{1,0:T(8,128)(2,1)S(1)}, u32[]{:S(2)}, u32[]{:S(2)}) collective-permute-start(bf16[576,384]{1,0:T(8,128)(2,1)S(1)} %get-tuple-element.292.refs_14_.refs_1_), channel_id=1, source_target_pairs={{0,4},{4,0},{8,12},{12,8},{16,20},{20,16},{24,28},{28,24},{1,5},{5... | collective-permute-start | bytes 1327112 | tf_op jit(solution)/shard_map/ppermute | solution.py:647
  181.7 7.6 %collective-permute-start.57 = (bf16[480,384]{1,0:T(8,128)(2,1)S(1)}, bf16[480,384]{1,0:T(8,128)(2,1)S(1)}, u32[]{:S(2)}, u32[]{:S(2)}) collective-permute-start(bf16[480,384]{1,0:T(8,128)(2,1)S(1)} %get-tuple-element.304.refs_1_), channel_id=1, source_target_pairs={{0,4},{4,0},{8,12},{12,8},{16,20},{20,16},{24,28},{28,24},{1,5},{5... | collective-permute-start | bytes 1105928 | tf_op jit(solution)/shard_map/ppermute | solution.py:647
  182.7 5.9 %collective-permute-start.58 = (bf16[144,768]{1,0:T(8,128)(2,1)S(1)}, bf16[144,768]{1,0:T(8,128)(2,1)S(1)}, u32[]{:S(2)}, u32[]{:S(2)}) collective-permute-start(bf16[144,768]{1,0:T(8,128)(2,1)S(1)} %get-tuple-element.306), channel_id=1, source_target_pairs={{0,8},{4,12},{8,0},{12,4},{16,24},{20,28},{24,16},{28,20},{1,9},{5... | collective-permute-start | bytes 663560 | tf_op jit(solution)/shard_map/ppermute | solution.py:647
  190.8 10.0 %collective-permute-start.59 = (bf16[144,768]{1,0:T(8,128)(2,1)S(1)}, bf16[144,768]{1,0:T(8,128)(2,1)S(1)}, u32[]{:S(2)}, u32[]{:S(2)}) collective-permute-start(bf16[144,768]{1,0:T(8,128)(2,1)S(1)} %get-tuple-element.308.refs_1_), channel_id=1, source_target_pairs={{0,16},{4,20},{8,24},{12,28},{16,0},{20,4},{24,8},{28,12},{1,17},{... | collective-permute-start | bytes 663560 | tf_op jit(solution)/shard_map/ppermute | solution.py:647
  201.4 6.0 %collective-permute-start.60 = (bf16[144,768]{1,0:T(8,128)(2,1)S(1)}, bf16[144,768]{1,0:T(8,128)(2,1)S(1)}, u32[]{:S(2)}, u32[]{:S(2)}) collective-permute-start(bf16[144,768]{1,0:T(8,128)(2,1)S(1)} %get-tuple-element.310.refs_1_), channel_id=1, source_target_pairs={{0,8},{4,12},{8,0},{12,4},{16,24},{20,28},{24,16},{28,20},{1,9},{5... | collective-permute-start | bytes 663560 | tf_op jit(solution)/shard_map/ppermute | solution.py:647
  208.6 9.4 %collective-permute-start.61 = (bf16[288,768]{1,0:T(8,128)(2,1)S(1)}, bf16[288,768]{1,0:T(8,128)(2,1)S(1)}, u32[]{:S(2)}, u32[]{:S(2)}) collective-permute-start(bf16[288,768]{1,0:T(8,128)(2,1)S(1)} %get-tuple-element.312.refs_0_.refs_1_.refs_2_), channel_id=1, source_target_pairs={{0,4},{4,0},{8,12},{12,8},{16,20},{20,16},{24,28},{28,24},{1,5},{5... | collective-permute-start | bytes 1327112 | tf_op jit(solution)/shard_map/ppermute | solution.py:647
  (28 other events, 167.9 us)

commit v5 on v4

--- a/solution.py
+++ b/solution.py
@@ -297,19 +297,20 @@
     )
 
 
-def hidden(n2, cot, wg, wu, wd):
-    gate = dot(n2, wg)
-    up = dot(n2, wu)
+def hidden(n2, cot, both, wd):
+    gate_up = jnp.concatenate([dot(n2, w[...]) for w in both], axis=1)
+    half = gate_up.shape[1] // 2
+    gate, up = gate_up[:, :half], gate_up[:, half:]
     ga = dot_bt(cot, wd)
     phi = 0.5 + 0.5 * lax.erf(gate * (2.0**-0.5))
     gelu = gate * phi
     act = (gelu * up).astype(BF)
     slope = phi + gate * (jnp.exp(-0.5 * gate * gate) * 0.3989422804014327)
-    dgate = (ga * up * slope).astype(BF)
-    dup = (ga * gelu).astype(BF)
+    grads = jnp.concatenate([(ga * up * slope).astype(BF), (ga * gelu).astype(BF)], axis=1)
     out = dot(act, wd)
-    gn = dot_bt(dgate, wg) + dot_bt(dup, wu)
-    return act, dgate, dup, out, gn
+    size = grads.shape[1] // len(both)
+    gn = sum(dot_bt(grads[:, i * size : (i + 1) * size], w[...]) for i, w in enumerate(both))
+    return act, grads, out, gn
 
 
 def ffn_a_body(info_ref, n2_ref, cot_ref, ga, gb, gc, gd, ge, gf, ua, ub, uc, ud, oa, ob, oc, od,
@@ -327,16 +328,9 @@
     n2 = n2_ref[...]
     cot = cot_ref[...]
     nt = n2.T
-    total_out = jnp.zeros((TILE, D), F32)
-    total_gn = jnp.zeros((TILE, D), F32)
-    for h in range(2):
-        g, u = slice(h * WIDE, (h + 1) * WIDE), slice(D + h * WIDE, D + (h + 1) * WIDE)
-        act, dgate, dup, out, gn = hidden(n2, cot, wg_ref[:, g], wu_ref[:, g], wd_ref[g, :])
-        total_out += out
-        total_gn += gn
-        acc[:, g] += dot(nt, dgate)
-        acc[:, u] += dot(nt, dup)
-        ad[g, :] += dot_at(act, cot)
+    act, grads, total_out, total_gn = hidden(n2, cot, (wg_ref, wu_ref), wd_ref[...])
+    acc[...] += dot(nt, grads)
+    ad[...] += dot_at(act, cot)
     out_ref[...] = total_out.astype(BF)
     gn_ref[...] = total_gn.astype(BF)
 
@@ -387,10 +381,8 @@
 
     n2 = n2_ref[...]
     cot = cot_ref[...]
-    act, dgate, dup, out, gn = hidden(n2, cot, w_ref[:, :WIDE], w_ref[:, WIDE:], wd_ref[...])
-    nt = n2.T
-    acc[:, :WIDE] += dot(nt, dgate)
-    acc[:, WIDE:] += dot(nt, dup)
+    act, grads, out, gn = hidden(n2, cot, (w_ref,), wd_ref[...])
+    acc[...] += dot(n2.T, grads)
     ad[...] += dot_at(act, cot)
     middle = mid_ref[...].astype(F32)
     out_ref[...] = (middle + pout_ref[...].astype(F32) + out).astype(BF)

time: 231 us -> 227 us (0.983)
  Pallas kernels: 108 us -> 104 us
    pallas_call x8, Pallas kernels: 77 us -> 73.3 us  [call(): pl.pallas_call(wrapped, in_specs=list(in_specs) + [pl.BlockSpec(memory_sp...]
  transfers between devices with their start and end apart: 62 -> 62, of which waited for: 20 -> 20; matrix products, arithmetic and copies ran while one was open for 4% -> 5% of each run, Pallas kernels for 41% -> 40%
where the time goes in v5:
time: 227 us; the launch traced here: 223 us
  Pallas kernels  104 us (46%)
  starting transfers between devices  59.7 us (26%)
  waiting for transfers between devices  41.5 us (18%)
  local copies, waits for them, and re-layouts  10.6 us (5%)
  other arithmetic  5.68 us (3%)
    pallas_call x8, Pallas kernels, call(): pl.pallas_call(wrapped, in_specs=list(in_specs) + [pl.BlockSpec(memory_sp...  73.3 us
    ppermute x20, waiting for transfers between devices, along_seq(): return lax.ppermute(a, 'seq', [(i, i ^ 1 << shift) for i in range(count)])  27.4 us
    ppermute x20, starting transfers between devices, along_seq(): return lax.ppermute(a, 'seq', [(i, i ^ 1 << shift) for i in range(count)])  25.1 us
    pallas_call x4, Pallas kernels, adam_call(): pl.pallas_call(body, grid=(r // rows_at_once,), in_specs=[smem()] + [pl.B...  21.3 us
    ppermute x16, starting transfers between devices, to_chip(): return lax.ppermute(a, 'wshard', CHIPS)  17.5 us
    pallas_call x12, Pallas kernels, boundary(): pl.pallas_call(body, grid=(1,), in_specs=[smem()] + [full(a.shape) for a...  9.54 us
    ppermute x16, waiting for transfers between devices, to_chip(): return lax.ppermute(a, 'wshard', CHIPS)  9.47 us
    ppermute x21, waiting for transfers between devices, to_core(): return lax.ppermute(a, 'wshard', CORES)  4.6 us
  transfers between devices with their start and end apart: 62, of which 20 were waited for; matrix products, arithmetic and copies ran while one was open for 5% of the time, Pallas kernels for 40%

profile of v5, /device:TPU:0, one launch (start us, length us, event | category | flops | bytes accessed | tf_op | source)
XLA Modules:
  0.0 223.3 jit_solution(8204606046917918585)
XLA Ops:
  0.7 3.0 %collective-permute-start.6 = (bf16[192,2304]{1,0:T(8,128)(2,1)}, bf16[192,2304]{1,0:T(8,128)(2,1)S(1)}, u32[]{:S(2)}, u32[]{:S(2)}) collective-permute-start(bf16[192,2304]{1,0:T(8,128)(2,1)} %refs_6_.3), channel_id=1, source_target_pairs={{0,2},{2,0},{1,3},{3,1},{4,6},{6,4},{5,7},{7,5},{8,10},{10,8},{9,1... | collective-permute-start | bytes 2654216 | tf_op jit(solution)/shard_map/ppermute | solution.py:591
  3.7 1.0 slice_bitcast_fusion
  4.6 1.3 collective-permute-start.1
  5.9 4.6 %collective-permute-start = (bf16[64,768]{1,0:T(8,128)(2,1)S(1)}, bf16[64,768]{1,0:T(8,128)(2,1)S(1)}, u32[]{:S(2)}, u32[]{:S(2)}) collective-permute-start(bf16[64,768]{1,0:T(8,128)(2,1)S(1)} %get-tuple-element.347), channel_id=1, source_target_pairs={{0,4},{4,8},{8,12},{12,16},{16,20},{20,24},{24,28},{1,5},{5,9},{9,... | collective-permute-start | bytes 294920 | tf_op jit(solution)/shard_map/ppermute | solution.py:824
  10.5 0.9 slice.115.refs_2_
  11.5 1.0 slice.114.refs_1_
  12.5 1.0 copy-done
  13.6 1.1 fusion.9
  17.3 1.1 concatenate.21.refs_3_
  18.5 1.2 pad_maximum_fusion.refs_3_
  20.4 1.2 pad_maximum_fusion.1.refs_2_
  23.3 2.4 %collective-permute-done.3.refs_4_.refs_6_ = bf16[2,192]{1,0:T(2,128)(2,1)S(1)} collective-permute-done((bf16[2,192]{1,0:T(2,128)(2,1)S(1)}, bf16[2,192]{1,0:T(2,128)(2,1)S(1)}, u32[]{:S(2)}, u32[]{:S(2)}) %collective-permute-start.3) | collective-permute-done | bytes 800 | tf_op jit(solution)/shard_map/ppermute | solution.py:591
  26.5 1.8 collective-permute-start.14
  28.4 7.9 %qkv.1 = (bf16[768,1152]{1,0:T(8,128)(2,1)S(1)}, bf16[1152,768]{1,0:T(8,128)(2,1)S(1)}, bf16[1152,768]{1,0:T(8,128)(2,1)S(1)}, bf16[1152,768]{1,0:T(8,128)(2,1)S...) custom-call(s32[18]{0:T(128)S(1)} %pad_add_fusion.refs_3_.refs_0_.info_ref, ...), custom_call_target="tpu_custom_call" | custom-call | flops 9900000256 | tf_op jit(solution)/shard_map/qkv/pallas_call | solution.py:58
  36.3 2.2 collective-permute-done.14.refs_0_
  38.5 2.4 %collective-permute-start.17 = (bf16[96,768]{1,0:T(8,128)(2,1)S(1)}, bf16[96,768]{1,0:T(8,128)(2,1)S(1)}, u32[]{:S(2)}, u32[]{:S(2)}) collective-permute-start(bf16[96,768]{1,0:T(8,128)(2,1)S(1)} %get-tuple-element.197.refs_5_), channel_id=1, source_target_pairs={{0,4},{4,0},{8,12},{12,8},{16,20},{20,16},{24,28},{28,24},{1,5},{5... | collective-permute-start | bytes 442376 | tf_op jit(solution)/shard_map/ppermute | solution.py:853
  41.4 1.5 collective-permute-start.19
  42.9 10.6 %attend.1 = (bf16[1024,768]{1,0:T(8,128)(2,1)S(1)}, bf16[1024,768]{1,0:T(8,128)(2,1)S(1)}, bf16[1024,768]{1,0:T(8,128)(2,1)S(1)}, bf16[768,768]{1,0:T(8,128)(2,1...) custom-call(s32[18]{0:T(128)S(1)} %pad_add_fusion.refs_3_.refs_0_.info_ref, ...), custom_call_target="tpu_custom_call" | custom-call | flops 12099999744 | tf_op jit(solution)/shard_map/attend/pallas_call | solution.py:58
  53.5 2.8 %collective-permute-done.19.refs_2_ = bf16[192,768]{1,0:T(8,128)(2,1)S(1)} collective-permute-done((bf16[192,768]{1,0:T(8,128)(2,1)S(1)}, bf16[192,768]{1,0:T(8,128)(2,1)S(1)}, u32[]{:S(2)}, u32[]{:S(2)}) %collective-permute-start.19) | collective-permute-done | bytes 294944 | tf_op jit(solution)/shard_map/ppermute | solution.py:591
  59.4 14.0 %ffn_a.1 = (bf16[1024,768]{1,0:T(8,128)(2,1)S(1)}, bf16[1024,768]{1,0:T(8,128)(2,1)S(1)}, bf16[2,1152,384]{2,1,0:T(8,128)(2,1)S(1)}, bf16[2,1152,384]{2,1,0:T(8,128)(2,1)S(1)}, f32[8,128]{1,0:T(8,128)S(1)}) custom-call(s32[18]{0:T(128)S(1)} %pad_add_fusion.refs_3_.refs_0_.info_ref, bf16[1024,768]{1,0:T(8,128)(2,1)S(1)} %get-tuple-element.196.refs_1_, ...), custom_call_target="tpu_custom_call" | custom-call | flops 19800000512 | tf_op jit(solution)/shard_map/ffn_a/pallas_call | solution.py:58
  74.6 3.1 %collective-permute-done.28.refs_2_ = bf16[2,1152,384]{2,1,0:T(8,128)(2,1)S(1)} collective-permute-done((bf16[2,1152,384]{2,1,0:T(8,128)(2,1)S(1)}, bf16[2,1152,384]{2,1,0:T(8,128)(2,1)S(1)}, u32[]{:S(2)}, u32[]{:S(2)}) %collective-permute-start.28) | collective-permute-done | bytes 1769504 | tf_op jit(solution)/shard_map/ppermute | solution.py:587
  77.7 1.0 land.13
  78.7 1.5 collective-permute-start.30
  80.2 1.2 collective-permute-start.29
  81.4 13.5 %ffn_b.1 = (bf16[1024,768]{1,0:T(8,128)(2,1)}, bf16[1024,768]{1,0:T(8,128)(2,1)S(1)}, bf16[1024,768]{1,0:T(8,128)(2,1)S(1)}, bf16[2,960,384]{2,1,0:T(8,128)(2,1)...) custom-call(s32[18]{0:T(128)S(1)} %pad_add_fusion.refs_3_.refs_0_.info_ref, ...), custom_call_target="tpu_custom_call" | custom-call | flops 15399999488 | tf_op jit(solution)/shard_map/ffn_b/pallas_call | solution.py:58
  97.2 6.5 %attend_back.3 = (bf16[1152,768]{1,0:T(8,128)(2,1)S(1)}, bf16[1152,768]{1,0:T(8,128)(2,1)S(1)}, bf16[1152,768]{1,0:T(8,128)(2,1)S(1)}, bf16[2,576,512]{2,1,0:T(8...) custom-call(s32[18]{0:T(128)S(1)} %pad_add_fusion.refs_3_.refs_0_.info_ref, ...), custom_call_target="tpu_custom_call" | custom-call | flops 4400000000 | tf_op jit(solution)/shard_map/attend_back/pallas_call | solution.py:58
  104.2 1.3 land.15
  105.5 1.6 collective-permute-start.34
  107.1 1.1 collective-permute-start.36
  108.2 1.2 collective-permute-start.35
  109.4 6.5 %attend_back.4 = (bf16[1152,768]{1,0:T(8,128)(2,1)S(1)}, bf16[1152,768]{1,0:T(8,128)(2,1)S(1)}, bf16[1152,768]{1,0:T(8,128)(2,1)S(1)}, bf16[2,576,512]{2,1,0:T(8...) custom-call(s32[18]{0:T(128)S(1)} %pad_add_fusion.refs_3_.refs_0_.in, ...), custom_call_target="tpu_custom_call", output_to_operand_aliasing={{0}: (10, {}), {1}: (11, {}), {2}: (12, {}), {3}: (13, {}),... | custom-call | flops 4400000000 | tf_op jit(solution)/shard_map/attend_back/pallas_call | solution.py:58
  116.8 1.2 collective-permute-done.35.refs_5_
  118.9 1.2 collective-permute-start.39
  120.7 1.7 collective-permute-start.37
  122.3 6.8 %attend_back.5 = (bf16[1152,768]{1,0:T(8,128)(2,1)S(1)}, bf16[1152,768]{1,0:T(8,128)(2,1)S(1)}, bf16[1152,768]{1,0:T(8,128)(2,1)S(1)}, bf16[2,576,256]{2,1,0:T(8...) custom-call(s32[18]{0:T(128)S(1)} %pad_add_fusion.refs_3_.refs_0_.in, ...), custom_call_target="tpu_custom_call", output_to_operand_aliasing={{0}: (10, {}), {1}: (11, {}), {2}: (12, {})} | custom-call | flops 4400000000 | tf_op jit(solution)/shard_map/attend_back/pallas_call | solution.py:58
  129.2 1.0 land.17
  130.2 0.9 collective-permute-start.42
  131.2 1.2 collective-permute-start.43
  132.4 1.7 collective-permute-start.41
  134.1 4.8 %collective-permute-done.41.refs_4_ = bf16[240,384]{1,0:T(8,128)(2,1)S(1)} collective-permute-done((bf16[240,384]{1,0:T(8,128)(2,1)S(1)}, bf16[240,384]{1,0:T(8,128)(2,1)S(1)}, u32[]{:S(2)}, u32[]{:S(2)}) %collective-permute-start.41) | collective-permute-done | bytes 184352 | tf_op jit(solution)/shard_map/ppermute | solution.py:639
  141.2 1.2 collective-permute-start.47
  142.4 1.4 collective-permute-start.45
  143.8 3.4 %collective-permute-start.49 = (bf16[64,1536]{1,0:T(8,128)(2,1)S(1)}, bf16[64,1536]{1,0:T(8,128)(2,1)S(1)}, u32[]{:S(2)}, u32[]{:S(2)}) collective-permute-start(bf16[64,1536]{1,0:T(8,128)(2,1)S(1)} %get-tuple-element.285), channel_id=1, source_target_pairs={{0,4},{4,8},{8,12},{12,16},{16,20},{20,24},{24,28},{1,5},{5,9},{9,... | collective-permute-start | bytes 589832 | tf_op jit(solution)/shard_map/ppermute | solution.py:893
  147.2 1.3 collective-permute-start.50
  148.5 2.7 %collective-permute-start.48 = (bf16[2,144,256]{2,1,0:T(8,128)(2,1)S(1)}, bf16[2,144,256]{2,1,0:T(8,128)(2,1)S(1)}, u32[]{:S(2)}, u32[]{:S(2)}) collective-permute-start(bf16[2,144,256]{2,1,0:T(8,128)(2,1)S(1)} %get-tuple-element.284), channel_id=1, source_target_pairs={{0,4},{4,0},{8,12},{12,8},{16,20},{20,16},{24,28},{28,24},{1,5},{5... | collective-permute-start | bytes 442376 | tf_op jit(solution)/shard_map/ppermute | solution.py:639
  151.6 6.2 %collective-permute-done.48.refs_8_ = bf16[2,144,256]{2,1,0:T(8,128)(2,1)S(1)} collective-permute-done((bf16[2,144,256]{2,1,0:T(8,128)(2,1)S(1)}, bf16[2,144,256]{2,1,0:T(8,128)(2,1)S(1)}, u32[]{:S(2)}, u32[]{:S(2)}) %collective-permute-start.48) | collective-permute-done | bytes 147488 | tf_op jit(solution)/shard_map/ppermute | solution.py:639
  157.7 2.5 %collective-permute-start.53 = (bf16[144,512]{1,0:T(8,128)(2,1)S(1)}, bf16[144,512]{1,0:T(8,128)(2,1)S(1)}, u32[]{:S(2)}, u32[]{:S(2)}) collective-permute-start(bf16[144,512]{1,0:T(8,128)(2,1)S(1)} %get-tuple-element.298), channel_id=1, source_target_pairs={{0,4},{4,0},{8,12},{12,8},{16,20},{20,16},{24,28},{28,24},{1,5},{5... | collective-permute-start | bytes 442376 | tf_op jit(solution)/shard_map/ppermute | solution.py:639
  160.2 2.2 collective-permute-done.46.refs_4_
  164.0 1.3 collective-permute-start.56
  165.2 1.1 collective-permute-start.52
  167.3 7.5 %last.1 = (bf16[1024,768]{1,0:T(8,128)(2,1)}, f32[8,128]{1,0:T(8,128)S(1)}) custom-call(s32[18]{0:T(128)S(1)} %pad_add_fusion.refs_3_.refs_0_.info_ref, bf16[1024,768]{1,0:T(8,128)(2,1)S(1)} %bitcast.14, bf16[1152,768]{1,0:T(8,128)(2,1)S(1)} %get-tuple-element.261.refs_2_, bf16[1152,768]{1,0:T(8,128)(2,1)S(1)} %get-tuple-element.262.refs_3_, ...), custom_call_target="tpu_custom_call" | custom-call | flops 7699999744 | tf_op jit(solution)/shard_map/last/pallas_call | solution.py:58
  174.8 1.8 collective-permute-done.51.refs_2_
  177.5 1.0 collective-permute-start.57
  178.5 1.7 collective-permute-start.58
  180.2 4.2 %collective-permute-done.58.refs_4_ = bf16[144,768]{1,0:T(8,128)(2,1)S(1)} collective-permute-done((bf16[144,768]{1,0:T(8,128)(2,1)S(1)}, bf16[144,768]{1,0:T(8,128)(2,1)S(1)}, u32[]{:S(2)}, u32[]{:S(2)}) %collective-permute-start.58) | collective-permute-done | bytes 221216 | tf_op jit(solution)/shard_map/ppermute | solution.py:639
  186.6 2.8 %collective-permute-start.59 = (bf16[144,768]{1,0:T(8,128)(2,1)S(1)}, bf16[144,768]{1,0:T(8,128)(2,1)S(1)}, u32[]{:S(2)}, u32[]{:S(2)}) collective-permute-start(bf16[144,768]{1,0:T(8,128)(2,1)S(1)} %get-tuple-element.308.refs_1_), channel_id=1, source_target_pairs={{0,16},{4,20},{8,24},{12,28},{16,0},{20,4},{24,8},{28,12},{1,17},{... | collective-permute-start | bytes 663560 | tf_op jit(solution)/shard_map/ppermute | solution.py:639
  189.4 2.9 %adam.5 = (f32[192,768]{1,0:T(8,128)}, f32[192,768]{1,0:T(8,128)}, f32[192,768]{1,0:T(8,128)}, f32[192,768]{1,0:T(8,128)}, f32[192,1]{1,0:T(8,128)}) custom-call(s32[18]{0:T(128)} %copy-done.7, bf16[960,384]{1,0:T(8,128)(2,1)} %copy-done.16, bf16[960,384]{1,0:T(8,128)(2,1)} %copy-done.16, bf16[192,768]{1,0:T(8,128)(2,1)} %refs_2_.1, f32[192,768]{1,0:T(8,128)} %refs_3_.1, ...), custom_call_target="tpu_custom_call" | custom-call | flops 3300000000 | tf_op jit(solution)/shard_map/adam/pallas_call | solution.py:569
  192.3 4.3 %collective-permute-done.59.refs_2_ = bf16[144,768]{1,0:T(8,128)(2,1)S(1)} collective-permute-done((bf16[144,768]{1,0:T(8,128)(2,1)S(1)}, bf16[144,768]{1,0:T(8,128)(2,1)S(1)}, u32[]{:S(2)}, u32[]{:S(2)}) %collective-permute-start.59) | collective-permute-done | bytes 221216 | tf_op jit(solution)/shard_map/ppermute | solution.py:639
  197.3 4.7 %adam.7 = (f32[288,768]{1,0:T(8,128)}, f32[288,768]{1,0:T(8,128)}, f32[288,768]{1,0:T(8,128)}, f32[288,768]{1,0:T(8,128)}, f32[288,1]{1,0:T(8,128)}) custom-call(s32[18]{0:T(128)} %copy-done.7, bf16[1152,384]{1,0:T(8,128)(2,1)} %copy-done.15, bf16[1152,384]{1,0:T(8,128)(2,1)} %copy-done.15, bf16[960,384]{1,0:T(8,128)(2,1)} %copy-done.16, ...), custom_call_target="tpu_custom_call" | custom-call | flops 3300000000 | tf_op jit(solution)/shard_map/adam/pallas_call | solution.py:569
  202.0 1.2 collective-permute-done.60.refs_2_
  205.1 6.7 %adam.6 = (f32[192,2304]{1,0:T(8,128)}, f32[192,2304]{1,0:T(8,128)}, f32[192,2304]{1,0:T(8,128)}, f32[192,2304]{1,0:T(8,128)}, f32[192,1]{1,0:T(8,128)}) custom-call(s32[18]{0:T(128)} %copy-done.7, bf16[1152,384]{1,0:T(8,128)(2,1)} %copy-done.15, bf16[1152,384]{1,0:T(8,128)(2,1)} %copy-done.15, bf16[1152,384]{1,0:T(8,128)(2,1)} %copy-done.15, ...), custom_call_target="tpu_custom_call" | custom-call | flops 3300000000 | tf_op jit(solution)/shard_map/adam/pallas_call | solution.py:569
  211.8 1.0 reduce.1
  214.5 6.9 %adam.4 = (f32[192,2304]{1,0:T(8,128)}, f32[192,2304]{1,0:T(8,128)}, f32[192,2304]{1,0:T(8,128)}, f32[192,2304]{1,0:T(8,128)}, f32[192,1]{1,0:T(8,128)}) custom-call(s32[18]{0:T(128)} %copy-done.7, bf16[288,768]{1,0:T(8,128)(2,1)} %copy-done.12, bf16[288,768]{1,0:T(8,128)(2,1)} %copy-done.12, bf16[288,768]{1,0:T(8,128)(2,1)} %copy-done.12, ...), custom_call_target="tpu_custom_call" | custom-call | flops 3300000000 | tf_op jit(solution)/shard_map/adam/pallas_call | solution.py:569
  221.4 1.0 reduce
  (171 shorter events, 28.7 us)
Async XLA Ops:
  0.7 25.1 %collective-permute-start.6 = (bf16[192,2304]{1,0:T(8,128)(2,1)}, bf16[192,2304]{1,0:T(8,128)(2,1)S(1)}, u32[]{:S(2)}, u32[]{:S(2)}) collective-permute-start(bf16[192,2304]{1,0:T(8,128)(2,1)} %refs_6_.3), channel_id=1, source_target_pairs={{0,2},{2,0},{1,3},{3,1},{4,6},{6,4},{5,7},{7,5},{8,10},{10,8},{9,1... | collective-permute-start | bytes 2654216 | tf_op jit(solution)/shard_map/ppermute | solution.py:591
  3.7 19.6 %collective-permute-start.5 = (bf16[192,2304]{1,0:T(8,128)(2,1)}, bf16[192,2304]{1,0:T(8,128)(2,1)S(1)}, u32[]{:S(2)}, u32[]{:S(2)}) collective-permute-start(bf16[192,2304]{1,0:T(8,128)(2,1)} %refs_6_.3), channel_id=1, source_target_pairs={{0,1},{1,0},{2,3},{3,2},{4,5},{5,4},{6,7},{7,6},{8,9},{9,8},{10,11... | collective-permute-start | bytes 2654216 | tf_op jit(solution)/shard_map/ppermute | solution.py:587
  4.6 10.0 %collective-permute-start.1 = (bf16[64,768]{1,0:T(8,128)(2,1)S(1)}, bf16[64,768]{1,0:T(8,128)(2,1)S(1)}, u32[]{:S(2)}, u32[]{:S(2)}) collective-permute-start(bf16[64,768]{1,0:T(8,128)(2,1)S(1)} %get-tuple-element.346), channel_id=1, source_target_pairs={{4,0},{8,4},{12,8},{16,12},{20,16},{24,20},{28,24},{5,1},{9,5},{13... | collective-permute-start | bytes 294920 | tf_op jit(solution)/shard_map/ppermute | solution.py:824
  5.9 9.8 %collective-permute-start = (bf16[64,768]{1,0:T(8,128)(2,1)S(1)}, bf16[64,768]{1,0:T(8,128)(2,1)S(1)}, u32[]{:S(2)}, u32[]{:S(2)}) collective-permute-start(bf16[64,768]{1,0:T(8,128)(2,1)S(1)} %get-tuple-element.347), channel_id=1, source_target_pairs={{0,4},{4,8},{8,12},{12,16},{16,20},{20,24},{24,28},{1,5},{5,9},{9,... | collective-permute-start | bytes 294920 | tf_op jit(solution)/shard_map/ppermute | solution.py:824
  13.5 6.2 %collective-permute-start.11 = (bf16[96,768]{1,0:T(8,128)(2,1)S(1)}, bf16[96,768]{1,0:T(8,128)(2,1)S(1)}, u32[]{:S(2)}, u32[]{:S(2)}) collective-permute-start(bf16[96,768]{1,0:T(8,128)(2,1)S(1)} %get-tuple-element.182.refs_4_), channel_id=1, source_target_pairs={{0,1},{1,0},{2,3},{3,2},{4,5},{5,4},{6,7},{7,6},{8,9},{9,8},{10,11... | collective-permute-start | bytes 442376 | tf_op jit(solution)/shard_map/ppermute | solution.py:587
  15.3 5.0 %collective-permute-start.7 = (bf16[192,768]{1,0:T(8,128)(2,1)S(1)}, bf16[192,768]{1,0:T(8,128)(2,1)S(1)}, u32[]{:S(2)}, u32[]{:S(2)}) collective-permute-start(bf16[192,768]{1,0:T(8,128)(2,1)S(1)} %get-tuple-element.180.refs_2_), channel_id=1, source_target_pairs={{0,1},{1,0},{2,3},{3,2},{4,5},{5,4},{6,7},{7,6},{8,9},{9,8},{10,11... | collective-permute-start | bytes 884744 | tf_op jit(solution)/shard_map/ppermute | solution.py:587
  16.4 5.1 %collective-permute-start.10 = (bf16[192,768]{1,0:T(8,128)(2,1)S(1)}, bf16[192,768]{1,0:T(8,128)(2,1)S(1)}, u32[]{:S(2)}, u32[]{:S(2)}) collective-permute-start(bf16[192,768]{1,0:T(8,128)(2,1)S(1)} %get-tuple-element.181.refs_2_), channel_id=1, source_target_pairs={{0,1},{1,0},{2,3},{3,2},{4,5},{5,4},{6,7},{7,6},{8,9},{9,8},{10,11... | collective-permute-start | bytes 884744 | tf_op jit(solution)/shard_map/ppermute | solution.py:587
  19.7 2.4 %collective-permute-start.12 = (bf16[192,768]{1,0:T(8,128)(2,1)S(1)}, bf16[192,768]{1,0:T(8,128)(2,1)S(1)}, u32[]{:S(2)}, u32[]{:S(2)}) collective-permute-start(bf16[192,768]{1,0:T(8,128)(2,1)S(1)} %concatenate.21.refs_3_), channel_id=1, source_target_pairs={{0,1},{1,0},{2,3},{3,2},{4,5},{5,4},{6,7},{7,6},{8,9},{9,8},{10,11... | collective-permute-start | bytes 884744 | tf_op jit(solution)/shard_map/ppermute | solution.py:587
  20.3 2.1 collective-permute-start.8
  21.5 1.7 collective-permute-start.9
  22.1 3.6 %collective-permute-start.3 = (bf16[2,192]{1,0:T(2,128)(2,1)S(1)}, bf16[2,192]{1,0:T(2,128)(2,1)S(1)}, u32[]{:S(2)}, u32[]{:S(2)}) collective-permute-start(bf16[2,192]{1,0:T(2,128)(2,1)S(1)} %pad_maximum_fusion.4.refs_4_), channel_id=1, source_target_pairs={{0,2},{2,0},{1,3},{3,1},{4,6},{6,4},{5,7},{7,5},{8,10},{10,8},{9,1... | collective-permute-start | bytes 2312 | tf_op jit(solution)/shard_map/ppermute | solution.py:591
  22.3 3.4 %collective-permute-start.2 = (bf16[2,192]{1,0:T(2,128)(2,1)S(1)}, bf16[2,192]{1,0:T(2,128)(2,1)S(1)}, u32[]{:S(2)}, u32[]{:S(2)}) collective-permute-start(bf16[2,192]{1,0:T(2,128)(2,1)S(1)} %pad_maximum_fusion.4.refs_4_), channel_id=1, source_target_pairs={{0,1},{1,0},{2,3},{3,2},{4,5},{5,4},{6,7},{7,6},{8,9},{9,8},{10,11... | collective-permute-start | bytes 2312 | tf_op jit(solution)/shard_map/ppermute | solution.py:587
  22.4 162.6 %copy-start.7 = (s32[18]{0:T(128)}, s32[18]{0:T(128)S(1)}, u32[]{:S(2)}) copy-start(s32[18]{0:T(128)S(1)} %pad_add_fusion.refs_3_.refs_0_.info_ref) | copy-start | bytes 220
  25.7 2.6 %collective-permute-start.13 = (bf16[192,2304]{1,0:T(8,128)(2,1)S(1)}, bf16[192,2304]{1,0:T(8,128)(2,1)S(1)}, u32[]{:S(2)}, u32[]{:S(2)}) collective-permute-start(bf16[192,2304]{1,0:T(8,128)(2,1)S(1)} %get-tuple-element.183.refs_10_), channel_id=1, source_target_pairs={{0,1},{1,0},{2,3},{3,2},{4,5},{5,4},{6,7},{7,6},{8,9},{9,8},{10,11... | collective-permute-start | bytes 2654216 | tf_op jit(solution)/shard_map/ppermute | solution.py:587
  25.8 2.5 %collective-permute-start.4 = (bf16[2,192]{1,0:T(2,128)(2,1)S(1)}, bf16[2,192]{1,0:T(2,128)(2,1)S(1)}, u32[]{:S(2)}, u32[]{:S(2)}) collective-permute-start(bf16[2,192]{1,0:T(2,128)(2,1)S(1)} %collective-permute-done.3.refs_4_.refs_6_), channel_id=1, source_target_pairs={{0,1},{1,0},{2,3},{3,2},{4,5},{5,4},{6,7},{7,6},{8,9},{9,8},{10,11... | collective-permute-start | bytes 2312 | tf_op jit(solution)/shard_map/ppermute | solution.py:587
  26.3 10.0 %collective-permute-start.15 = (bf16[96,768]{1,0:T(8,128)(2,1)S(1)}, bf16[96,768]{1,0:T(8,128)(2,1)S(1)}, u32[]{:S(2)}, u32[]{:S(2)}) collective-permute-start(bf16[96,768]{1,0:T(8,128)(2,1)S(1)} %get-tuple-element.188), channel_id=1, source_target_pairs={{0,2},{2,0},{1,3},{3,1},{4,6},{6,4},{5,7},{7,5},{8,10},{10,8},{9,1... | collective-permute-start | bytes 442376 | tf_op jit(solution)/shard_map/ppermute | solution.py:591
  26.5 12.0 %collective-permute-start.14 = (bf16[192,768]{1,0:T(8,128)(2,1)S(1)}, bf16[192,768]{1,0:T(8,128)(2,1)S(1)}, u32[]{:S(2)}, u32[]{:S(2)}) collective-permute-start(bf16[192,768]{1,0:T(8,128)(2,1)S(1)} %get-tuple-element.187), channel_id=1, source_target_pairs={{0,2},{2,0},{1,3},{3,1},{4,6},{6,4},{5,7},{7,5},{8,10},{10,8},{9,1... | collective-permute-start | bytes 884744 | tf_op jit(solution)/shard_map/ppermute | solution.py:591
  38.5 2.4 %collective-permute-start.16 = (bf16[192,768]{1,0:T(8,128)(2,1)S(1)}, bf16[192,768]{1,0:T(8,128)(2,1)S(1)}, u32[]{:S(2)}, u32[]{:S(2)}) collective-permute-start(bf16[192,768]{1,0:T(8,128)(2,1)S(1)} %get-tuple-element.190.refs_7_), channel_id=1, source_target_pairs={{0,1},{1,0},{2,3},{3,2},{4,5},{5,4},{6,7},{7,6},{8,9},{9,8},{10,11... | collective-permute-start | bytes 884744 | tf_op jit(solution)/shard_map/ppermute | solution.py:587
  38.5 15.0 %collective-permute-start.17 = (bf16[96,768]{1,0:T(8,128)(2,1)S(1)}, bf16[96,768]{1,0:T(8,128)(2,1)S(1)}, u32[]{:S(2)}, u32[]{:S(2)}) collective-permute-start(bf16[96,768]{1,0:T(8,128)(2,1)S(1)} %get-tuple-element.197.refs_5_), channel_id=1, source_target_pairs={{0,4},{4,0},{8,12},{12,8},{16,20},{20,16},{24,28},{28,24},{1,5},{5... | collective-permute-start | bytes 442376 | tf_op jit(solution)/shard_map/ppermute | solution.py:853
  40.9 12.6 %collective-permute-start.18 = (bf16[192,768]{1,0:T(8,128)(2,1)S(1)}, bf16[192,768]{1,0:T(8,128)(2,1)S(1)}, u32[]{:S(2)}, u32[]{:S(2)}) collective-permute-start(bf16[192,768]{1,0:T(8,128)(2,1)S(1)} %get-tuple-element.198.refs_9_), channel_id=1, source_target_pairs={{0,2},{2,0},{1,3},{3,1},{4,6},{6,4},{5,7},{7,5},{8,10},{10,8},{9,1... | collective-permute-start | bytes 884744 | tf_op jit(solution)/shard_map/ppermute | solution.py:591
  41.4 14.9 %collective-permute-start.19 = (bf16[192,768]{1,0:T(8,128)(2,1)S(1)}, bf16[192,768]{1,0:T(8,128)(2,1)S(1)}, u32[]{:S(2)}, u32[]{:S(2)}) collective-permute-start(bf16[192,768]{1,0:T(8,128)(2,1)S(1)} %get-tuple-element.199.refs_13_), channel_id=1, source_target_pairs={{0,2},{2,0},{1,3},{3,1},{4,6},{6,4},{5,7},{7,5},{8,10},{10,8},{9,1... | collective-permute-start | bytes 884744 | tf_op jit(solution)/shard_map/ppermute | solution.py:591
  42.9 16.5 %copy-start.10 = (bf16[1,1024,768]{2,1,0:T(8,128)(2,1)S(1)}, bf16[1,1024,768]{2,1,0:T(8,128)(2,1)}, u32[]{:S(2)}) copy-start(bf16[1,1024,768]{2,1,0:T(8,128)(2,1)} %param.25) | copy-start | bytes 4718596
  56.3 3.1 %collective-permute-start.22 = (bf16[192,768]{1,0:T(8,128)(2,1)S(1)}, bf16[192,768]{1,0:T(8,128)(2,1)S(1)}, u32[]{:S(2)}, u32[]{:S(2)}) collective-permute-start(bf16[192,768]{1,0:T(8,128)(2,1)S(1)} %get-tuple-element.203.refs_11_), channel_id=1, source_target_pairs={{0,1},{1,0},{2,3},{3,2},{4,5},{5,4},{6,7},{7,6},{8,9},{9,8},{10,11... | collective-permute-start | bytes 884744 | tf_op jit(solution)/shard_map/ppermute | solution.py:587
  56.3 3.1 %collective-permute-start.23 = (bf16[192,768]{1,0:T(8,128)(2,1)S(1)}, bf16[192,768]{1,0:T(8,128)(2,1)S(1)}, u32[]{:S(2)}, u32[]{:S(2)}) collective-permute-start(bf16[192,768]{1,0:T(8,128)(2,1)S(1)} %get-tuple-element.204.refs_15_), channel_id=1, source_target_pairs={{0,1},{1,0},{2,3},{3,2},{4,5},{5,4},{6,7},{7,6},{8,9},{9,8},{10,11... | collective-permute-start | bytes 884744 | tf_op jit(solution)/shard_map/ppermute | solution.py:587
  56.9 1.7 collective-permute-start.20
  56.9 2.5 %collective-permute-start.21 = (bf16[96,768]{1,0:T(8,128)(2,1)S(1)}, bf16[96,768]{1,0:T(8,128)(2,1)S(1)}, u32[]{:S(2)}, u32[]{:S(2)}) collective-permute-start(bf16[96,768]{1,0:T(8,128)(2,1)S(1)} %get-tuple-element.202.refs_6_), channel_id=1, source_target_pairs={{0,1},{1,0},{2,3},{3,2},{4,5},{5,4},{6,7},{7,6},{8,9},{9,8},{10,11... | collective-permute-start | bytes 442376 | tf_op jit(solution)/shard_map/ppermute | solution.py:587
  57.4 16.0 %collective-permute-start.25 = (bf16[96,768]{1,0:T(8,128)(2,1)S(1)}, bf16[96,768]{1,0:T(8,128)(2,1)S(1)}, u32[]{:S(2)}, u32[]{:S(2)}) collective-permute-start(bf16[96,768]{1,0:T(8,128)(2,1)S(1)} %get-tuple-element.207.refs_7_), channel_id=1, source_target_pairs={{0,2},{2,0},{1,3},{3,1},{4,6},{6,4},{5,7},{7,5},{8,10},{10,8},{9,1... | collective-permute-start | bytes 442376 | tf_op jit(solution)/shard_map/ppermute | solution.py:591
  58.6 14.8 %collective-permute-start.24 = (bf16[192,768]{1,0:T(8,128)(2,1)S(1)}, bf16[192,768]{1,0:T(8,128)(2,1)S(1)}, u32[]{:S(2)}, u32[]{:S(2)}) collective-permute-start(bf16[192,768]{1,0:T(8,128)(2,1)S(1)} %get-tuple-element.201.refs_3_), channel_id=1, source_target_pairs={{0,2},{2,0},{1,3},{3,1},{4,6},{6,4},{5,7},{7,5},{8,10},{10,8},{9,1... | collective-permute-start | bytes 884744 | tf_op jit(solution)/shard_map/ppermute | solution.py:591
  74.0 3.8 %collective-permute-start.28 = (bf16[2,1152,384]{2,1,0:T(8,128)(2,1)S(1)}, bf16[2,1152,384]{2,1,0:T(8,128)(2,1)S(1)}, u32[]{:S(2)}, u32[]{:S(2)}) collective-permute-start(bf16[2,1152,384]{2,1,0:T(8,128)(2,1)S(1)} %get-tuple-element.217), channel_id=1, source_target_pairs={{0,1},{1,0},{2,3},{3,2},{4,5},{5,4},{6,7},{7,6},{8,9},{9,8},{10,11... | collective-permute-start | bytes 5308424 | tf_op jit(solution)/shard_map/ppermute | solution.py:587
  74.0 7.4 %collective-permute-start.26 = (bf16[192,768]{1,0:T(8,128)(2,1)S(1)}, bf16[192,768]{1,0:T(8,128)(2,1)S(1)}, u32[]{:S(2)}, u32[]{:S(2)}) collective-permute-start(bf16[192,768]{1,0:T(8,128)(2,1)S(1)} %get-tuple-element.209.refs_5_), channel_id=1, source_target_pairs={{0,1},{1,0},{2,3},{3,2},{4,5},{5,4},{6,7},{7,6},{8,9},{9,8},{10,11... | collective-permute-start | bytes 884744 | tf_op jit(solution)/shard_map/ppermute | solution.py:587
  74.5 6.9 %collective-permute-start.27 = (bf16[96,768]{1,0:T(8,128)(2,1)S(1)}, bf16[96,768]{1,0:T(8,128)(2,1)S(1)}, u32[]{:S(2)}, u32[]{:S(2)}) collective-permute-start(bf16[96,768]{1,0:T(8,128)(2,1)S(1)} %get-tuple-element.210.refs_9_), channel_id=1, source_target_pairs={{0,1},{1,0},{2,3},{3,2},{4,5},{5,4},{6,7},{7,6},{8,9},{9,8},{10,11... | collective-permute-start | bytes 442376 | tf_op jit(solution)/shard_map/ppermute | solution.py:587
  78.7 16.2 %collective-permute-start.30 = (bf16[2,288,384]{2,1,0:T(8,128)(2,1)S(1)}, bf16[2,288,384]{2,1,0:T(8,128)(2,1)S(1)}, u32[]{:S(2)}, u32[]{:S(2)}) collective-permute-start(bf16[2,288,384]{2,1,0:T(8,128)(2,1)S(1)} %get-tuple-element.229), channel_id=1, source_target_pairs={{0,4},{4,0},{8,12},{12,8},{16,20},{20,16},{24,28},{28,24},{1,5},{5... | collective-permute-start | bytes 1327112 | tf_op jit(solution)/shard_map/ppermute | solution.py:639
  80.2 14.7 %collective-permute-start.29 = (bf16[576,384]{1,0:T(8,128)(2,1)S(1)}, bf16[576,384]{1,0:T(8,128)(2,1)S(1)}, u32[]{:S(2)}, u32[]{:S(2)}) collective-permute-start(bf16[576,384]{1,0:T(8,128)(2,1)S(1)} %get-tuple-element.220.refs_18_), channel_id=1, source_target_pairs={{0,2},{2,0},{1,3},{3,1},{4,6},{6,4},{5,7},{7,5},{8,10},{10,8},{9,1... | collective-permute-start | bytes 1327112 | tf_op jit(solution)/shard_map/ppermute | solution.py:591
  95.7 8.5 %collective-permute-start.33 = (bf16[2,960,384]{2,1,0:T(8,128)(2,1)S(1)}, bf16[2,960,384]{2,1,0:T(8,128)(2,1)S(1)}, u32[]{:S(2)}, u32[]{:S(2)}) collective-permute-start(bf16[2,960,384]{2,1,0:T(8,128)(2,1)S(1)} %get-tuple-element.234.refs_12_), channel_id=1, source_target_pairs={{0,1},{1,0},{2,3},{3,2},{4,5},{5,4},{6,7},{7,6},{8,9},{9,8},{10,11... | collective-permute-start | bytes 4423688 | tf_op jit(solution)/shard_map/ppermute | solution.py:587
  95.8 8.0 %collective-permute-start.32 = (bf16[288,384]{1,0:T(8,128)(2,1)S(1)}, bf16[288,384]{1,0:T(8,128)(2,1)S(1)}, u32[]{:S(2)}, u32[]{:S(2)}) collective-permute-start(bf16[288,384]{1,0:T(8,128)(2,1)S(1)} %get-tuple-element.242), channel_id=1, source_target_pairs={{0,2},{2,0},{1,3},{3,1},{4,6},{6,4},{5,7},{7,5},{8,10},{10,8},{9,1... | collective-permute-start | bytes 663560 | tf_op jit(solution)/shard_map/ppermute | solution.py:591
  96.7 7.5 %collective-permute-start.31 = (bf16[288,384]{1,0:T(8,128)(2,1)S(1)}, bf16[288,384]{1,0:T(8,128)(2,1)S(1)}, u32[]{:S(2)}, u32[]{:S(2)}) collective-permute-start(bf16[288,384]{1,0:T(8,128)(2,1)S(1)} %get-tuple-element.233.refs_11_), channel_id=1, source_target_pairs={{0,4},{4,0},{8,12},{12,8},{16,20},{20,16},{24,28},{28,24},{1,5},{5... | collective-permute-start | bytes 663560 | tf_op jit(solution)/shard_map/ppermute | solution.py:639
  105.5 10.5 %collective-permute-start.34 = (bf16[288,384]{1,0:T(8,128)(2,1)S(1)}, bf16[288,384]{1,0:T(8,128)(2,1)S(1)}, u32[]{:S(2)}, u32[]{:S(2)}) collective-permute-start(bf16[288,384]{1,0:T(8,128)(2,1)S(1)} %get-tuple-element.246.refs_16_), channel_id=1, source_target_pairs={{0,8},{4,12},{8,0},{12,4},{16,24},{20,28},{24,16},{28,20},{1,9},{5... | collective-permute-start | bytes 663560 | tf_op jit(solution)/shard_map/ppermute | solution.py:639
  107.1 9.7 %collective-permute-start.36 = (bf16[2,240,384]{2,1,0:T(8,128)(2,1)S(1)}, bf16[2,240,384]{2,1,0:T(8,128)(2,1)S(1)}, u32[]{:S(2)}, u32[]{:S(2)}) collective-permute-start(bf16[2,240,384]{2,1,0:T(8,128)(2,1)S(1)} %get-tuple-element.254), channel_id=1, source_target_pairs={{0,4},{4,0},{8,12},{12,8},{16,20},{20,16},{24,28},{28,24},{1,5},{5... | collective-permute-start | bytes 1105928 | tf_op jit(solution)/shard_map/ppermute | solution.py:639
  108.2 9.8 %collective-permute-start.35 = (bf16[480,384]{1,0:T(8,128)(2,1)S(1)}, bf16[480,384]{1,0:T(8,128)(2,1)S(1)}, u32[]{:S(2)}, u32[]{:S(2)}) collective-permute-start(bf16[480,384]{1,0:T(8,128)(2,1)S(1)} %get-tuple-element.247.refs_17_), channel_id=1, source_target_pairs={{0,2},{2,0},{1,3},{3,1},{4,6},{6,4},{5,7},{7,5},{8,10},{10,8},{9,1... | collective-permute-start | bytes 1105928 | tf_op jit(solution)/shard_map/ppermute | solution.py:591
  118.8 10.3 %collective-permute-start.40 = (bf16[2,576,512]{2,1,0:T(8,128)(2,1)S(1)}, bf16[2,576,512]{2,1,0:T(8,128)(2,1)S(1)}, u32[]{:S(2)}, u32[]{:S(2)}) collective-permute-start(bf16[2,576,512]{2,1,0:T(8,128)(2,1)S(1)} %get-tuple-element.260.refs_16_), channel_id=1, source_target_pairs={{0,1},{1,0},{2,3},{3,2},{4,5},{5,4},{6,7},{7,6},{8,9},{9,8},{10,11... | collective-permute-start | bytes 3538952 | tf_op jit(solution)/shard_map/ppermute | solution.py:587
  118.9 10.2 %collective-permute-start.39 = (bf16[240,384]{1,0:T(8,128)(2,1)S(1)}, bf16[240,384]{1,0:T(8,128)(2,1)S(1)}, u32[]{:S(2)}, u32[]{:S(2)}) collective-permute-start(bf16[240,384]{1,0:T(8,128)(2,1)S(1)} %get-tuple-element.266), channel_id=1, source_target_pairs={{0,2},{2,0},{1,3},{3,1},{4,6},{6,4},{5,7},{7,5},{8,10},{10,8},{9,1... | collective-permute-start | bytes 552968 | tf_op jit(solution)/shard_map/ppermute | solution.py:591
  120.1 9.0 %collective-permute-start.38 = (bf16[240,384]{1,0:T(8,128)(2,1)S(1)}, bf16[240,384]{1,0:T(8,128)(2,1)S(1)}, u32[]{:S(2)}, u32[]{:S(2)}) collective-permute-start(bf16[240,384]{1,0:T(8,128)(2,1)S(1)} %get-tuple-element.259.refs_15_), channel_id=1, source_target_pairs={{0,4},{4,0},{8,12},{12,8},{16,20},{20,16},{24,28},{28,24},{1,5},{5... | collective-permute-start | bytes 552968 | tf_op jit(solution)/shard_map/ppermute | solution.py:639
  120.7 13.4 %collective-permute-start.37 = (bf16[288,384]{1,0:T(8,128)(2,1)S(1)}, bf16[288,384]{1,0:T(8,128)(2,1)S(1)}, u32[]{:S(2)}, u32[]{:S(2)}) collective-permute-start(bf16[288,384]{1,0:T(8,128)(2,1)S(1)} %get-tuple-element.258.refs_14_.refs_1_), channel_id=1, source_target_pairs={{0,16},{4,20},{8,24},{12,28},{16,0},{20,4},{24,8},{28,12},{1,17},{... | collective-permute-start | bytes 663560 | tf_op jit(solution)/shard_map/ppermute | solution.py:639
  130.1 10.2 %collective-permute-start.44 = (bf16[2,576,256]{2,1,0:T(8,128)(2,1)S(1)}, bf16[2,576,256]{2,1,0:T(8,128)(2,1)S(1)}, u32[]{:S(2)}, u32[]{:S(2)}) collective-permute-start(bf16[2,576,256]{2,1,0:T(8,128)(2,1)S(1)} %get-tuple-element.277), channel_id=1, source_target_pairs={{0,1},{1,0},{2,3},{3,2},{4,5},{5,4},{6,7},{7,6},{8,9},{9,8},{10,11... | collective-permute-start | bytes 1769480 | tf_op jit(solution)/shard_map/ppermute | solution.py:587
  130.2 9.5 %collective-permute-start.42 = (bf16[288,512]{1,0:T(8,128)(2,1)S(1)}, bf16[288,512]{1,0:T(8,128)(2,1)S(1)}, u32[]{:S(2)}, u32[]{:S(2)}) collective-permute-start(bf16[288,512]{1,0:T(8,128)(2,1)S(1)} %get-tuple-element.274), channel_id=1, source_target_pairs={{0,2},{2,0},{1,3},{3,1},{4,6},{6,4},{5,7},{7,5},{8,10},{10,8},{9,1... | collective-permute-start | bytes 884744 | tf_op jit(solution)/shard_map/ppermute | solution.py:591
  131.2 9.1 %collective-permute-start.43 = (bf16[2,144,512]{2,1,0:T(8,128)(2,1)S(1)}, bf16[2,144,512]{2,1,0:T(8,128)(2,1)S(1)}, u32[]{:S(2)}, u32[]{:S(2)}) collective-permute-start(bf16[2,144,512]{2,1,0:T(8,128)(2,1)S(1)} %get-tuple-element.275), channel_id=1, source_target_pairs={{0,4},{4,0},{8,12},{12,8},{16,20},{20,16},{24,28},{28,24},{1,5},{5... | collective-permute-start | bytes 884744 | tf_op jit(solution)/shard_map/ppermute | solution.py:639
  132.4 6.5 %collective-permute-start.41 = (bf16[240,384]{1,0:T(8,128)(2,1)S(1)}, bf16[240,384]{1,0:T(8,128)(2,1)S(1)}, u32[]{:S(2)}, u32[]{:S(2)}) collective-permute-start(bf16[240,384]{1,0:T(8,128)(2,1)S(1)} %get-tuple-element.271), channel_id=1, source_target_pairs={{0,8},{4,12},{8,0},{12,4},{16,24},{20,28},{24,16},{28,20},{1,9},{5... | collective-permute-start | bytes 552968 | tf_op jit(solution)/shard_map/ppermute | solution.py:639
  141.2 10.0 %collective-permute-start.47 = (bf16[288,256]{1,0:T(8,128)(2,1)S(1)}, bf16[288,256]{1,0:T(8,128)(2,1)S(1)}, u32[]{:S(2)}, u32[]{:S(2)}) collective-permute-start(bf16[288,256]{1,0:T(8,128)(2,1)S(1)} %get-tuple-element.283), channel_id=1, source_target_pairs={{0,2},{2,0},{1,3},{3,1},{4,6},{6,4},{5,7},{7,5},{8,10},{10,8},{9,1... | collective-permute-start | bytes 442376 | tf_op jit(solution)/shard_map/ppermute | solution.py:591
  142.4 20.8 %collective-permute-start.45 = (bf16[288,384]{1,0:T(8,128)(2,1)S(1)}, bf16[288,384]{1,0:T(8,128)(2,1)S(1)}, u32[]{:S(2)}, u32[]{:S(2)}) collective-permute-start(bf16[288,384]{1,0:T(8,128)(2,1)S(1)} %get-tuple-element.279.refs_1_), channel_id=1, source_target_pairs={{0,8},{4,12},{8,0},{12,4},{16,24},{20,28},{24,16},{28,20},{1,9},{5... | collective-permute-start | bytes 663560 | tf_op jit(solution)/shard_map/ppermute | solution.py:639
  143.8 19.4 %collective-permute-start.49 = (bf16[64,1536]{1,0:T(8,128)(2,1)S(1)}, bf16[64,1536]{1,0:T(8,128)(2,1)S(1)}, u32[]{:S(2)}, u32[]{:S(2)}) collective-permute-start(bf16[64,1536]{1,0:T(8,128)(2,1)S(1)} %get-tuple-element.285), channel_id=1, source_target_pairs={{0,4},{4,8},{8,12},{12,16},{16,20},{20,24},{24,28},{1,5},{5,9},{9,... | collective-permute-start | bytes 589832 | tf_op jit(solution)/shard_map/ppermute | solution.py:893
  147.2 16.1 %collective-permute-start.50 = (bf16[64,1536]{1,0:T(8,128)(2,1)S(1)}, bf16[64,1536]{1,0:T(8,128)(2,1)S(1)}, u32[]{:S(2)}, u32[]{:S(2)}) collective-permute-start(bf16[64,1536]{1,0:T(8,128)(2,1)S(1)} %get-tuple-element.286), channel_id=1, source_target_pairs={{4,0},{8,4},{12,8},{16,12},{20,16},{24,20},{28,24},{5,1},{9,5},{13... | collective-permute-start | bytes 589832 | tf_op jit(solution)/shard_map/ppermute | solution.py:893
  148.5 9.2 %collective-permute-start.48 = (bf16[2,144,256]{2,1,0:T(8,128)(2,1)S(1)}, bf16[2,144,256]{2,1,0:T(8,128)(2,1)S(1)}, u32[]{:S(2)}, u32[]{:S(2)}) collective-permute-start(bf16[2,144,256]{2,1,0:T(8,128)(2,1)S(1)} %get-tuple-element.284), channel_id=1, source_target_pairs={{0,4},{4,0},{8,12},{12,8},{16,20},{20,16},{24,28},{28,24},{1,5},{5... | collective-permute-start | bytes 442376 | tf_op jit(solution)/shard_map/ppermute | solution.py:639
  151.2 11.2 %collective-permute-start.46 = (bf16[240,384]{1,0:T(8,128)(2,1)S(1)}, bf16[240,384]{1,0:T(8,128)(2,1)S(1)}, u32[]{:S(2)}, u32[]{:S(2)}) collective-permute-start(bf16[240,384]{1,0:T(8,128)(2,1)S(1)} %get-tuple-element.280.refs_3_), channel_id=1, source_target_pairs={{0,16},{4,20},{8,24},{12,28},{16,0},{20,4},{24,8},{28,12},{1,17},{... | collective-permute-start | bytes 552968 | tf_op jit(solution)/shard_map/ppermute | solution.py:639
  157.7 8.6 %collective-permute-start.53 = (bf16[144,512]{1,0:T(8,128)(2,1)S(1)}, bf16[144,512]{1,0:T(8,128)(2,1)S(1)}, u32[]{:S(2)}, u32[]{:S(2)}) collective-permute-start(bf16[144,512]{1,0:T(8,128)(2,1)S(1)} %get-tuple-element.298), channel_id=1, source_target_pairs={{0,4},{4,0},{8,12},{12,8},{16,20},{20,16},{24,28},{28,24},{1,5},{5... | collective-permute-start | bytes 442376 | tf_op jit(solution)/shard_map/ppermute | solution.py:639
  162.4 12.4 %collective-permute-start.54 = (bf16[144,512]{1,0:T(8,128)(2,1)S(1)}, bf16[144,512]{1,0:T(8,128)(2,1)S(1)}, u32[]{:S(2)}, u32[]{:S(2)}) collective-permute-start(bf16[144,512]{1,0:T(8,128)(2,1)S(1)} %get-tuple-element.299), channel_id=1, source_target_pairs={{0,2},{2,0},{1,3},{3,1},{4,6},{6,4},{5,7},{7,5},{8,10},{10,8},{9,1... | collective-permute-start | bytes 442376 | tf_op jit(solution)/shard_map/ppermute | solution.py:591
  164.0 10.8 %collective-permute-start.56 = (bf16[144,256]{1,0:T(8,128)(2,1)S(1)}, bf16[144,256]{1,0:T(8,128)(2,1)S(1)}, u32[]{:S(2)}, u32[]{:S(2)}) collective-permute-start(bf16[144,256]{1,0:T(8,128)(2,1)S(1)} %get-tuple-element.302), channel_id=1, source_target_pairs={{0,2},{2,0},{1,3},{3,1},{4,6},{6,4},{5,7},{7,5},{8,10},{10,8},{9,1... | collective-permute-start | bytes 221192 | tf_op jit(solution)/shard_map/ppermute | solution.py:591
  165.2 9.6 %collective-permute-start.55 = (bf16[144,256]{1,0:T(8,128)(2,1)S(1)}, bf16[144,256]{1,0:T(8,128)(2,1)S(1)}, u32[]{:S(2)}, u32[]{:S(2)}) collective-permute-start(bf16[144,256]{1,0:T(8,128)(2,1)S(1)} %get-tuple-element.294.refs_16_), channel_id=1, source_target_pairs={{0,4},{4,0},{8,12},{12,8},{16,20},{20,16},{24,28},{28,24},{1,5},{5... | collective-permute-start | bytes 221192 | tf_op jit(solution)/shard_map/ppermute | solution.py:639
  165.2 9.6 %collective-permute-start.52 = (bf16[240,384]{1,0:T(8,128)(2,1)S(1)}, bf16[240,384]{1,0:T(8,128)(2,1)S(1)}, u32[]{:S(2)}, u32[]{:S(2)}) collective-permute-start(bf16[240,384]{1,0:T(8,128)(2,1)S(1)} %get-tuple-element.293.refs_15_.refs_3_), channel_id=1, source_target_pairs={{0,8},{4,12},{8,0},{12,4},{16,24},{20,28},{24,16},{28,20},{1,9},{5... | collective-permute-start | bytes 552968 | tf_op jit(solution)/shard_map/ppermute | solution.py:639
  166.4 10.3 %collective-permute-start.51 = (bf16[576,384]{1,0:T(8,128)(2,1)S(1)}, bf16[576,384]{1,0:T(8,128)(2,1)S(1)}, u32[]{:S(2)}, u32[]{:S(2)}) collective-permute-start(bf16[576,384]{1,0:T(8,128)(2,1)S(1)} %get-tuple-element.292.refs_14_.refs_1_), channel_id=1, source_target_pairs={{0,4},{4,0},{8,12},{12,8},{16,20},{20,16},{24,28},{28,24},{1,5},{5... | collective-permute-start | bytes 1327112 | tf_op jit(solution)/shard_map/ppermute | solution.py:639
  177.5 7.6 %collective-permute-start.57 = (bf16[480,384]{1,0:T(8,128)(2,1)S(1)}, bf16[480,384]{1,0:T(8,128)(2,1)S(1)}, u32[]{:S(2)}, u32[]{:S(2)}) collective-permute-start(bf16[480,384]{1,0:T(8,128)(2,1)S(1)} %get-tuple-element.304.refs_1_), channel_id=1, source_target_pairs={{0,4},{4,0},{8,12},{12,8},{16,20},{20,16},{24,28},{28,24},{1,5},{5... | collective-permute-start | bytes 1105928 | tf_op jit(solution)/shard_map/ppermute | solution.py:639
  178.5 5.9 %collective-permute-start.58 = (bf16[144,768]{1,0:T(8,128)(2,1)S(1)}, bf16[144,768]{1,0:T(8,128)(2,1)S(1)}, u32[]{:S(2)}, u32[]{:S(2)}) collective-permute-start(bf16[144,768]{1,0:T(8,128)(2,1)S(1)} %get-tuple-element.306), channel_id=1, source_target_pairs={{0,8},{4,12},{8,0},{12,4},{16,24},{20,28},{24,16},{28,20},{1,9},{5... | collective-permute-start | bytes 663560 | tf_op jit(solution)/shard_map/ppermute | solution.py:639
  186.6 9.9 %collective-permute-start.59 = (bf16[144,768]{1,0:T(8,128)(2,1)S(1)}, bf16[144,768]{1,0:T(8,128)(2,1)S(1)}, u32[]{:S(2)}, u32[]{:S(2)}) collective-permute-start(bf16[144,768]{1,0:T(8,128)(2,1)S(1)} %get-tuple-element.308.refs_1_), channel_id=1, source_target_pairs={{0,16},{4,20},{8,24},{12,28},{16,0},{20,4},{24,8},{28,12},{1,17},{... | collective-permute-start | bytes 663560 | tf_op jit(solution)/shard_map/ppermute | solution.py:639
  197.2 6.0 %collective-permute-start.60 = (bf16[144,768]{1,0:T(8,128)(2,1)S(1)}, bf16[144,768]{1,0:T(8,128)(2,1)S(1)}, u32[]{:S(2)}, u32[]{:S(2)}) collective-permute-start(bf16[144,768]{1,0:T(8,128)(2,1)S(1)} %get-tuple-element.310.refs_1_), channel_id=1, source_target_pairs={{0,8},{4,12},{8,0},{12,4},{16,24},{20,28},{24,16},{28,20},{1,9},{5... | collective-permute-start | bytes 663560 | tf_op jit(solution)/shard_map/ppermute | solution.py:639
  204.4 9.3 %collective-permute-start.61 = (bf16[288,768]{1,0:T(8,128)(2,1)S(1)}, bf16[288,768]{1,0:T(8,128)(2,1)S(1)}, u32[]{:S(2)}, u32[]{:S(2)}) collective-permute-start(bf16[288,768]{1,0:T(8,128)(2,1)S(1)} %get-tuple-element.312.refs_0_.refs_1_.refs_2_), channel_id=1, source_target_pairs={{0,4},{4,0},{8,12},{12,8},{16,20},{20,16},{24,28},{28,24},{1,5},{5... | collective-permute-start | bytes 1327112 | tf_op jit(solution)/shard_map/ppermute | solution.py:639
  (28 other events, 167.9 us)

commit v6 on v5

--- a/solution.py
+++ b/solution.py
@@ -17,6 +17,7 @@
 PAIR = 2 * HD
 QB = 128
 TILE = 256
+ATILE = 512
 WIDE = 384
 ADAM_MB = 60
 QUAD = 4 * HD
@@ -245,15 +246,15 @@
 def attend_body(info_ref, q_ref, k_ref, v_ref, x_ref, wa, wb, wc, wd, gain_ref,
                 mixed_ref, middle_ref, n2_ref, w_ref, lse_ref):
     i = pl.program_id(0)
-    last = pl.num_programs(0) * (TILE // QB) - 1
+    last = pl.num_programs(0) * (ATILE // QB) - 1
     left, right = sides(info_ref)
 
     @pl.when(i == 0)
     def _():
         lay(info_ref[0], (wa, wb, wc, wd), w_ref)
 
-    for s in range(TILE // QB):
-        b = i * (TILE // QB) + s
+    for s in range(ATILE // QB):
+        b = i * (ATILE // QB) + s
         start = pl.multiple_of(b * QB, QB)
         bias = repeat(bias_of(b, last, left, right))
         for g in range(D // QUAD):
@@ -283,14 +284,14 @@
     return call(
         attend_body,
         [info, q, k, v, x, *w_parts, gain],
-        grid=(n // TILE,),
-        in_specs=[smem()] + [full((ext, D))] * 3 + [rows(TILE, D)] + [full((D // 4, D))] * 4 + [full((8, D))],
-        out_specs=[rows(TILE, D)] * 3 + [full((D, D)), pl.BlockSpec((groups, 4, TILE), lambda i: (0, 0, i))],
+        grid=(n // ATILE,),
+        in_specs=[smem()] + [full((ext, D))] * 3 + [rows(ATILE, D)] + [full((D // 4, D))] * 4 + [full((8, D))],
+        out_specs=[rows(ATILE, D)] * 3 + [full((D, D)), pl.BlockSpec((groups, 4, ATILE), lambda i: (0, 0, i))],
         out_shape=[
             jax.ShapeDtypeStruct((n, D), BF), jax.ShapeDtypeStruct((n, D), BF), jax.ShapeDtypeStruct((n, D), BF),
             jax.ShapeDtypeStruct((D, D), BF), jax.ShapeDtypeStruct((groups, 4, n), F32),
         ],
-        megabytes=12,
+        megabytes=16,
         deps=deps,
         cost_estimate=cost(11),
         name="attend",
@@ -838,17 +839,17 @@
     (token,) = together_at(
         [jnp.zeros((8, 128), F32)], [x_low, x_high, info, mate, out_mate, g_mate, u_mate, da_mate, db_mate, b_mate]
     )
-    far, g_half, attn_out_own, token = together_at([far, g_half, attn_out_own, token], [gain_far, gain_mate])
+    far, g_half, in_u, attn_out_own, token = together_at([far, g_half, in_u, attn_out_own, token], [gain_far, gain_mate])
     farmate = to_core(far)
     out_far = to_chip(attn_out_own)
     g_mine = to_chip(g_half)
+    u_far = to_chip(in_u)
     attn_parts = attn_in, mate, far, farmate
     gains = gain_own, gain_mate, gain_far, to_core(gain_far)
     nt, q, k, v, cos, sin, gain, token = qkv_call(info, x, x_low, x_high, gains, attn_parts)
-    out_far, g_mine, in_u, token = together_at([out_far, g_mine, in_u, token])
+    out_far, g_mine, token = together_at([out_far, g_mine, token])
     out_farmate = to_core(out_far)
-    out_farmate, in_u, down_a, token = together_at([out_farmate, in_u, down_a, token])
-    u_far = to_chip(in_u)
+    out_farmate, down_a, token = together_at([out_farmate, down_a, token])
     da_far = to_chip(down_a)
     g_other = lax.ppermute(g_mine, "seq", [(i, i ^ 1) for i in range(count)])
     out_parts = attn_out, out_mate, out_far, out_farmate

time: 227 us -> 225 us (level)
  no operation moved by 1% of the time
where the time goes in v6:
time: 225 us; the launch traced here: 222 us
  Pallas kernels  102 us (45%)
  starting transfers between devices  59.9 us (27%)
  waiting for transfers between devices  41.9 us (19%)
  local copies, waits for them, and re-layouts  10.6 us (5%)
  other arithmetic  5.68 us (3%)
    pallas_call x8, Pallas kernels, call(): pl.pallas_call(wrapped, in_specs=list(in_specs) + [pl.BlockSpec(memory_sp...  71.3 us
    ppermute x20, waiting for transfers between devices, along_seq(): return lax.ppermute(a, 'seq', [(i, i ^ 1 << shift) for i in range(count)])  27.3 us
    ppermute x20, starting transfers between devices, along_seq(): return lax.ppermute(a, 'seq', [(i, i ^ 1 << shift) for i in range(count)])  25.4 us
    pallas_call x4, Pallas kernels, adam_call(): pl.pallas_call(body, grid=(r // rows_at_once,), in_specs=[smem()] + [pl.B...  21.3 us
    ppermute x16, starting transfers between devices, to_chip(): return lax.ppermute(a, 'wshard', CHIPS)  17 us
    ppermute x16, waiting for transfers between devices, to_chip(): return lax.ppermute(a, 'wshard', CHIPS)  9.74 us
    pallas_call x12, Pallas kernels, boundary(): pl.pallas_call(body, grid=(1,), in_specs=[smem()] + [full(a.shape) for a...  9.73 us
    ppermute x21, waiting for transfers between devices, to_core(): return lax.ppermute(a, 'wshard', CORES)  4.85 us
  transfers between devices with their start and end apart: 62, of which 20 were waited for; matrix products, arithmetic and copies ran while one was open for 5% of the time, Pallas kernels for 40%

profile of v6, /device:TPU:0, one launch (start us, length us, event | category | flops | bytes accessed | tf_op | source)
XLA Modules:
  0.0 222.0 jit_solution(4549025967631531045)
XLA Ops:
  0.7 3.0 %collective-permute-start.6 = (bf16[192,2304]{1,0:T(8,128)(2,1)}, bf16[192,2304]{1,0:T(8,128)(2,1)S(1)}, u32[]{:S(2)}, u32[]{:S(2)}) collective-permute-start(bf16[192,2304]{1,0:T(8,128)(2,1)} %refs_6_.3), channel_id=1, source_target_pairs={{0,2},{2,0},{1,3},{3,1},{4,6},{6,4},{5,7},{7,5},{8,10},{10,8},{9,1... | collective-permute-start | bytes 2654216 | tf_op jit(solution)/shard_map/ppermute | solution.py:592
  3.7 1.0 slice_bitcast_fusion
  4.6 1.3 collective-permute-start.1
  5.9 4.6 %collective-permute-start = (bf16[64,768]{1,0:T(8,128)(2,1)S(1)}, bf16[64,768]{1,0:T(8,128)(2,1)S(1)}, u32[]{:S(2)}, u32[]{:S(2)}) collective-permute-start(bf16[64,768]{1,0:T(8,128)(2,1)S(1)} %get-tuple-element.345), channel_id=1, source_target_pairs={{0,4},{4,8},{8,12},{12,16},{16,20},{20,24},{24,28},{1,5},{5,9},{9,... | collective-permute-start | bytes 294920 | tf_op jit(solution)/shard_map/ppermute | solution.py:825
  10.5 0.9 slice.119.refs_2_
  11.5 1.0 slice.118.refs_1_
  12.5 1.0 copy-done
  13.6 1.1 fusion.9
  17.3 1.1 concatenate.21.refs_3_
  18.5 1.2 pad_maximum_fusion.refs_3_
  20.4 1.2 pad_maximum_fusion.1.refs_2_
  23.3 2.4 %collective-permute-done.3.refs_5_.refs_6_ = bf16[2,192]{1,0:T(2,128)(2,1)S(1)} collective-permute-done((bf16[2,192]{1,0:T(2,128)(2,1)S(1)}, bf16[2,192]{1,0:T(2,128)(2,1)S(1)}, u32[]{:S(2)}, u32[]{:S(2)}) %collective-permute-start.3) | collective-permute-done | bytes 800 | tf_op jit(solution)/shard_map/ppermute | solution.py:592
  26.5 1.8 collective-permute-start.14
  28.4 7.5 %qkv.1 = (bf16[768,1152]{1,0:T(8,128)(2,1)S(1)}, bf16[1152,768]{1,0:T(8,128)(2,1)S(1)}, bf16[1152,768]{1,0:T(8,128)(2,1)S(1)}, bf16[1152,768]{1,0:T(8,128)(2,1)S...) custom-call(s32[18]{0:T(128)S(1)} %pad_add_fusion.refs_3_.refs_0_.info_ref, ...), custom_call_target="tpu_custom_call" | custom-call | flops 9900000256 | tf_op jit(solution)/shard_map/qkv/pallas_call | solution.py:59
  35.9 2.5 %collective-permute-done.14.refs_0_ = bf16[192,768]{1,0:T(8,128)(2,1)S(1)} collective-permute-done((bf16[192,768]{1,0:T(8,128)(2,1)S(1)}, bf16[192,768]{1,0:T(8,128)(2,1)S(1)}, u32[]{:S(2)}, u32[]{:S(2)}) %collective-permute-start.14) | collective-permute-done | bytes 294944 | tf_op jit(solution)/shard_map/ppermute | solution.py:592
  38.7 2.7 %collective-permute-start.17 = (bf16[96,768]{1,0:T(8,128)(2,1)S(1)}, bf16[96,768]{1,0:T(8,128)(2,1)S(1)}, u32[]{:S(2)}, u32[]{:S(2)}) collective-permute-start(bf16[96,768]{1,0:T(8,128)(2,1)S(1)} %get-tuple-element.195.refs_5_), channel_id=1, source_target_pairs={{0,4},{4,0},{8,12},{12,8},{16,20},{20,16},{24,28},{28,24},{1,5},{5... | collective-permute-start | bytes 442376 | tf_op jit(solution)/shard_map/ppermute | solution.py:854
  41.4 1.5 collective-permute-start.19
  42.9 9.0 %attend.1 = (bf16[1024,768]{1,0:T(8,128)(2,1)S(1)}, bf16[1024,768]{1,0:T(8,128)(2,1)S(1)}, bf16[1024,768]{1,0:T(8,128)(2,1)S(1)}, bf16[768,768]{1,0:T(8,128)(2,1...) custom-call(s32[18]{0:T(128)S(1)} %pad_add_fusion.refs_3_.refs_0_.info_ref, ...), custom_call_target="tpu_custom_call" | custom-call | flops 12099999744 | tf_op jit(solution)/shard_map/attend/pallas_call | solution.py:59
  51.9 2.3 %collective-permute-done.19.refs_2_ = bf16[192,768]{1,0:T(8,128)(2,1)S(1)} collective-permute-done((bf16[192,768]{1,0:T(8,128)(2,1)S(1)}, bf16[192,768]{1,0:T(8,128)(2,1)S(1)}, u32[]{:S(2)}, u32[]{:S(2)}) %collective-permute-start.19) | collective-permute-done | bytes 294944 | tf_op jit(solution)/shard_map/ppermute | solution.py:592
  57.3 14.2 %ffn_a.1 = (bf16[1024,768]{1,0:T(8,128)(2,1)S(1)}, bf16[1024,768]{1,0:T(8,128)(2,1)S(1)}, bf16[2,1152,384]{2,1,0:T(8,128)(2,1)S(1)}, bf16[2,1152,384]{2,1,0:T(8,128)(2,1)S(1)}, f32[8,128]{1,0:T(8,128)S(1)}) custom-call(s32[18]{0:T(128)S(1)} %pad_add_fusion.refs_3_.refs_0_.info_ref, bf16[1024,768]{1,0:T(8,128)(2,1)S(1)} %get-tuple-element.194.refs_1_, ...), custom_call_target="tpu_custom_call" | custom-call | flops 19800000512 | tf_op jit(solution)/shard_map/ffn_a/pallas_call | solution.py:59
  72.7 3.1 %collective-permute-done.28.refs_2_ = bf16[2,1152,384]{2,1,0:T(8,128)(2,1)S(1)} collective-permute-done((bf16[2,1152,384]{2,1,0:T(8,128)(2,1)S(1)}, bf16[2,1152,384]{2,1,0:T(8,128)(2,1)S(1)}, u32[]{:S(2)}, u32[]{:S(2)}) %collective-permute-start.28) | collective-permute-done | bytes 1769504 | tf_op jit(solution)/shard_map/ppermute | solution.py:588
  75.8 1.0 land.13
  76.8 2.5 %collective-permute-start.30 = (bf16[2,288,384]{2,1,0:T(8,128)(2,1)S(1)}, bf16[2,288,384]{2,1,0:T(8,128)(2,1)S(1)}, u32[]{:S(2)}, u32[]{:S(2)}) collective-permute-start(bf16[2,288,384]{2,1,0:T(8,128)(2,1)S(1)} %get-tuple-element.227), channel_id=1, source_target_pairs={{0,4},{4,0},{8,12},{12,8},{16,20},{20,16},{24,28},{28,24},{1,5},{5... | collective-permute-start | bytes 1327112 | tf_op jit(solution)/shard_map/ppermute | solution.py:640
  79.2 1.2 collective-permute-start.29
  80.4 13.2 %ffn_b.1 = (bf16[1024,768]{1,0:T(8,128)(2,1)}, bf16[1024,768]{1,0:T(8,128)(2,1)S(1)}, bf16[1024,768]{1,0:T(8,128)(2,1)S(1)}, bf16[2,960,384]{2,1,0:T(8,128)(2,1)...) custom-call(s32[18]{0:T(128)S(1)} %pad_add_fusion.refs_3_.refs_0_.info_ref, ...), custom_call_target="tpu_custom_call" | custom-call | flops 15399999488 | tf_op jit(solution)/shard_map/ffn_b/pallas_call | solution.py:59
  95.5 6.5 %attend_back.3 = (bf16[1152,768]{1,0:T(8,128)(2,1)S(1)}, bf16[1152,768]{1,0:T(8,128)(2,1)S(1)}, bf16[1152,768]{1,0:T(8,128)(2,1)S(1)}, bf16[2,576,512]{2,1,0:T(8...) custom-call(s32[18]{0:T(128)S(1)} %pad_add_fusion.refs_3_.refs_0_.info_ref, ...), custom_call_target="tpu_custom_call" | custom-call | flops 4400000000 | tf_op jit(solution)/shard_map/attend_back/pallas_call | solution.py:59
  103.0 1.5 land.15
  104.4 1.6 collective-permute-start.34
  106.1 1.1 collective-permute-start.36
  107.2 1.2 collective-permute-start.35
  108.4 6.5 %attend_back.4 = (bf16[1152,768]{1,0:T(8,128)(2,1)S(1)}, bf16[1152,768]{1,0:T(8,128)(2,1)S(1)}, bf16[1152,768]{1,0:T(8,128)(2,1)S(1)}, bf16[2,576,512]{2,1,0:T(8...) custom-call(s32[18]{0:T(128)S(1)} %pad_add_fusion.refs_3_.refs_0_.in, ...), custom_call_target="tpu_custom_call", output_to_operand_aliasing={{0}: (10, {}), {1}: (11, {}), {2}: (12, {}), {3}: (13, {}),... | custom-call | flops 4400000000 | tf_op jit(solution)/shard_map/attend_back/pallas_call | solution.py:59
  115.6 1.4 collective-permute-done.35.refs_5_
  117.8 1.3 collective-permute-start.39
  119.5 1.8 collective-permute-start.37
  121.3 6.7 %attend_back.5 = (bf16[1152,768]{1,0:T(8,128)(2,1)S(1)}, bf16[1152,768]{1,0:T(8,128)(2,1)S(1)}, bf16[1152,768]{1,0:T(8,128)(2,1)S(1)}, bf16[2,576,256]{2,1,0:T(8...) custom-call(s32[18]{0:T(128)S(1)} %pad_add_fusion.refs_3_.refs_0_.in, ...), custom_call_target="tpu_custom_call", output_to_operand_aliasing={{0}: (10, {}), {1}: (11, {}), {2}: (12, {})} | custom-call | flops 4400000000 | tf_op jit(solution)/shard_map/attend_back/pallas_call | solution.py:59
  128.1 1.0 land.17
  129.1 0.9 collective-permute-start.42
  130.0 1.2 collective-permute-start.43
  131.2 1.7 collective-permute-start.41
  133.0 4.8 %collective-permute-done.41.refs_4_ = bf16[240,384]{1,0:T(8,128)(2,1)S(1)} collective-permute-done((bf16[240,384]{1,0:T(8,128)(2,1)S(1)}, bf16[240,384]{1,0:T(8,128)(2,1)S(1)}, u32[]{:S(2)}, u32[]{:S(2)}) %collective-permute-start.41) | collective-permute-done | bytes 184352 | tf_op jit(solution)/shard_map/ppermute | solution.py:640
  140.1 1.2 collective-permute-start.47
  141.3 1.2 collective-permute-start.45
  142.5 3.6 %collective-permute-start.49 = (bf16[64,1536]{1,0:T(8,128)(2,1)S(1)}, bf16[64,1536]{1,0:T(8,128)(2,1)S(1)}, u32[]{:S(2)}, u32[]{:S(2)}) collective-permute-start(bf16[64,1536]{1,0:T(8,128)(2,1)S(1)} %get-tuple-element.283), channel_id=1, source_target_pairs={{0,4},{4,8},{8,12},{12,16},{16,20},{20,24},{24,28},{1,5},{5,9},{9,... | collective-permute-start | bytes 589832 | tf_op jit(solution)/shard_map/ppermute | solution.py:894
  146.1 1.3 collective-permute-start.50
  147.4 2.7 %collective-permute-start.48 = (bf16[2,144,256]{2,1,0:T(8,128)(2,1)S(1)}, bf16[2,144,256]{2,1,0:T(8,128)(2,1)S(1)}, u32[]{:S(2)}, u32[]{:S(2)}) collective-permute-start(bf16[2,144,256]{2,1,0:T(8,128)(2,1)S(1)} %get-tuple-element.282), channel_id=1, source_target_pairs={{0,4},{4,0},{8,12},{12,8},{16,20},{20,16},{24,28},{28,24},{1,5},{5... | collective-permute-start | bytes 442376 | tf_op jit(solution)/shard_map/ppermute | solution.py:640
  150.4 6.2 %collective-permute-done.48.refs_8_ = bf16[2,144,256]{2,1,0:T(8,128)(2,1)S(1)} collective-permute-done((bf16[2,144,256]{2,1,0:T(8,128)(2,1)S(1)}, bf16[2,144,256]{2,1,0:T(8,128)(2,1)S(1)}, u32[]{:S(2)}, u32[]{:S(2)}) %collective-permute-start.48) | collective-permute-done | bytes 147488 | tf_op jit(solution)/shard_map/ppermute | solution.py:640
  156.6 2.5 %collective-permute-start.53 = (bf16[144,512]{1,0:T(8,128)(2,1)S(1)}, bf16[144,512]{1,0:T(8,128)(2,1)S(1)}, u32[]{:S(2)}, u32[]{:S(2)}) collective-permute-start(bf16[144,512]{1,0:T(8,128)(2,1)S(1)} %get-tuple-element.296), channel_id=1, source_target_pairs={{0,4},{4,0},{8,12},{12,8},{16,20},{20,16},{24,28},{28,24},{1,5},{5... | collective-permute-start | bytes 442376 | tf_op jit(solution)/shard_map/ppermute | solution.py:640
  159.1 2.0 collective-permute-done.46.refs_4_
  162.7 1.3 collective-permute-start.56
  164.0 1.3 collective-permute-start.52
  166.0 7.5 %last.1 = (bf16[1024,768]{1,0:T(8,128)(2,1)}, f32[8,128]{1,0:T(8,128)S(1)}) custom-call(s32[18]{0:T(128)S(1)} %pad_add_fusion.refs_3_.refs_0_.info_ref, bf16[1024,768]{1,0:T(8,128)(2,1)S(1)} %bitcast.14, bf16[1152,768]{1,0:T(8,128)(2,1)S(1)} %get-tuple-element.259.refs_2_, bf16[1152,768]{1,0:T(8,128)(2,1)S(1)} %get-tuple-element.260.refs_3_, ...), custom_call_target="tpu_custom_call" | custom-call | flops 7699999744 | tf_op jit(solution)/shard_map/last/pallas_call | solution.py:59
  173.6 2.0 collective-permute-done.51.refs_2_
  177.3 1.7 collective-permute-start.58
  179.1 4.2 %collective-permute-done.58.refs_4_ = bf16[144,768]{1,0:T(8,128)(2,1)S(1)} collective-permute-done((bf16[144,768]{1,0:T(8,128)(2,1)S(1)}, bf16[144,768]{1,0:T(8,128)(2,1)S(1)}, u32[]{:S(2)}, u32[]{:S(2)}) %collective-permute-start.58) | collective-permute-done | bytes 221216 | tf_op jit(solution)/shard_map/ppermute | solution.py:640
  185.5 2.4 %collective-permute-start.59 = (bf16[144,768]{1,0:T(8,128)(2,1)S(1)}, bf16[144,768]{1,0:T(8,128)(2,1)S(1)}, u32[]{:S(2)}, u32[]{:S(2)}) collective-permute-start(bf16[144,768]{1,0:T(8,128)(2,1)S(1)} %get-tuple-element.306.refs_1_), channel_id=1, source_target_pairs={{0,16},{4,20},{8,24},{12,28},{16,0},{20,4},{24,8},{28,12},{1,17},{... | collective-permute-start | bytes 663560 | tf_op jit(solution)/shard_map/ppermute | solution.py:640
  188.0 2.9 %adam.5 = (f32[192,768]{1,0:T(8,128)}, f32[192,768]{1,0:T(8,128)}, f32[192,768]{1,0:T(8,128)}, f32[192,768]{1,0:T(8,128)}, f32[192,1]{1,0:T(8,128)}) custom-call(s32[18]{0:T(128)} %copy-done.7, bf16[960,384]{1,0:T(8,128)(2,1)} %copy-done.16, bf16[960,384]{1,0:T(8,128)(2,1)} %copy-done.16, bf16[192,768]{1,0:T(8,128)(2,1)} %refs_2_.1, f32[192,768]{1,0:T(8,128)} %refs_3_.1, ...), custom_call_target="tpu_custom_call" | custom-call | flops 3300000000 | tf_op jit(solution)/shard_map/adam/pallas_call | solution.py:570
  190.9 4.4 %collective-permute-done.59.refs_2_ = bf16[144,768]{1,0:T(8,128)(2,1)S(1)} collective-permute-done((bf16[144,768]{1,0:T(8,128)(2,1)S(1)}, bf16[144,768]{1,0:T(8,128)(2,1)S(1)}, u32[]{:S(2)}, u32[]{:S(2)}) %collective-permute-start.59) | collective-permute-done | bytes 221216 | tf_op jit(solution)/shard_map/ppermute | solution.py:640
  195.9 4.7 %adam.7 = (f32[288,768]{1,0:T(8,128)}, f32[288,768]{1,0:T(8,128)}, f32[288,768]{1,0:T(8,128)}, f32[288,768]{1,0:T(8,128)}, f32[288,1]{1,0:T(8,128)}) custom-call(s32[18]{0:T(128)} %copy-done.7, bf16[1152,384]{1,0:T(8,128)(2,1)} %copy-done.15, bf16[1152,384]{1,0:T(8,128)(2,1)} %copy-done.15, bf16[960,384]{1,0:T(8,128)(2,1)} %copy-done.16, ...), custom_call_target="tpu_custom_call" | custom-call | flops 3300000000 | tf_op jit(solution)/shard_map/adam/pallas_call | solution.py:570
  200.6 1.2 collective-permute-done.60.refs_2_
  203.0 1.1 collective-permute-start.61
  204.1 6.7 %adam.6 = (f32[192,2304]{1,0:T(8,128)}, f32[192,2304]{1,0:T(8,128)}, f32[192,2304]{1,0:T(8,128)}, f32[192,2304]{1,0:T(8,128)}, f32[192,1]{1,0:T(8,128)}) custom-call(s32[18]{0:T(128)} %copy-done.7, bf16[1152,384]{1,0:T(8,128)(2,1)} %copy-done.15, bf16[1152,384]{1,0:T(8,128)(2,1)} %copy-done.15, bf16[1152,384]{1,0:T(8,128)(2,1)} %copy-done.15, ...), custom_call_target="tpu_custom_call" | custom-call | flops 3300000000 | tf_op jit(solution)/shard_map/adam/pallas_call | solution.py:570
  210.9 1.0 reduce.1
  213.3 6.9 %adam.4 = (f32[192,2304]{1,0:T(8,128)}, f32[192,2304]{1,0:T(8,128)}, f32[192,2304]{1,0:T(8,128)}, f32[192,2304]{1,0:T(8,128)}, f32[192,1]{1,0:T(8,128)}) custom-call(s32[18]{0:T(128)} %copy-done.7, bf16[288,768]{1,0:T(8,128)(2,1)} %copy-done.12, bf16[288,768]{1,0:T(8,128)(2,1)} %copy-done.12, bf16[288,768]{1,0:T(8,128)(2,1)} %copy-done.12, ...), custom_call_target="tpu_custom_call" | custom-call | flops 3300000000 | tf_op jit(solution)/shard_map/adam/pallas_call | solution.py:570
  220.2 1.0 reduce
  (171 shorter events, 28.0 us)
Async XLA Ops:
  0.7 25.1 %collective-permute-start.6 = (bf16[192,2304]{1,0:T(8,128)(2,1)}, bf16[192,2304]{1,0:T(8,128)(2,1)S(1)}, u32[]{:S(2)}, u32[]{:S(2)}) collective-permute-start(bf16[192,2304]{1,0:T(8,128)(2,1)} %refs_6_.3), channel_id=1, source_target_pairs={{0,2},{2,0},{1,3},{3,1},{4,6},{6,4},{5,7},{7,5},{8,10},{10,8},{9,1... | collective-permute-start | bytes 2654216 | tf_op jit(solution)/shard_map/ppermute | solution.py:592
  3.7 19.6 %collective-permute-start.5 = (bf16[192,2304]{1,0:T(8,128)(2,1)}, bf16[192,2304]{1,0:T(8,128)(2,1)S(1)}, u32[]{:S(2)}, u32[]{:S(2)}) collective-permute-start(bf16[192,2304]{1,0:T(8,128)(2,1)} %refs_6_.3), channel_id=1, source_target_pairs={{0,1},{1,0},{2,3},{3,2},{4,5},{5,4},{6,7},{7,6},{8,9},{9,8},{10,11... | collective-permute-start | bytes 2654216 | tf_op jit(solution)/shard_map/ppermute | solution.py:588
  4.6 10.0 %collective-permute-start.1 = (bf16[64,768]{1,0:T(8,128)(2,1)S(1)}, bf16[64,768]{1,0:T(8,128)(2,1)S(1)}, u32[]{:S(2)}, u32[]{:S(2)}) collective-permute-start(bf16[64,768]{1,0:T(8,128)(2,1)S(1)} %get-tuple-element.344), channel_id=1, source_target_pairs={{4,0},{8,4},{12,8},{16,12},{20,16},{24,20},{28,24},{5,1},{9,5},{13... | collective-permute-start | bytes 294920 | tf_op jit(solution)/shard_map/ppermute | solution.py:825
  5.9 9.8 %collective-permute-start = (bf16[64,768]{1,0:T(8,128)(2,1)S(1)}, bf16[64,768]{1,0:T(8,128)(2,1)S(1)}, u32[]{:S(2)}, u32[]{:S(2)}) collective-permute-start(bf16[64,768]{1,0:T(8,128)(2,1)S(1)} %get-tuple-element.345), channel_id=1, source_target_pairs={{0,4},{4,8},{8,12},{12,16},{16,20},{20,24},{24,28},{1,5},{5,9},{9,... | collective-permute-start | bytes 294920 | tf_op jit(solution)/shard_map/ppermute | solution.py:825
  13.5 6.2 %collective-permute-start.11 = (bf16[96,768]{1,0:T(8,128)(2,1)S(1)}, bf16[96,768]{1,0:T(8,128)(2,1)S(1)}, u32[]{:S(2)}, u32[]{:S(2)}) collective-permute-start(bf16[96,768]{1,0:T(8,128)(2,1)S(1)} %get-tuple-element.181.refs_4_), channel_id=1, source_target_pairs={{0,1},{1,0},{2,3},{3,2},{4,5},{5,4},{6,7},{7,6},{8,9},{9,8},{10,11... | collective-permute-start | bytes 442376 | tf_op jit(solution)/shard_map/ppermute | solution.py:588
  15.3 5.0 %collective-permute-start.7 = (bf16[192,768]{1,0:T(8,128)(2,1)S(1)}, bf16[192,768]{1,0:T(8,128)(2,1)S(1)}, u32[]{:S(2)}, u32[]{:S(2)}) collective-permute-start(bf16[192,768]{1,0:T(8,128)(2,1)S(1)} %get-tuple-element.179.refs_3_), channel_id=1, source_target_pairs={{0,1},{1,0},{2,3},{3,2},{4,5},{5,4},{6,7},{7,6},{8,9},{9,8},{10,11... | collective-permute-start | bytes 884744 | tf_op jit(solution)/shard_map/ppermute | solution.py:588
  16.4 5.1 %collective-permute-start.10 = (bf16[192,768]{1,0:T(8,128)(2,1)S(1)}, bf16[192,768]{1,0:T(8,128)(2,1)S(1)}, u32[]{:S(2)}, u32[]{:S(2)}) collective-permute-start(bf16[192,768]{1,0:T(8,128)(2,1)S(1)} %get-tuple-element.180.refs_1_), channel_id=1, source_target_pairs={{0,1},{1,0},{2,3},{3,2},{4,5},{5,4},{6,7},{7,6},{8,9},{9,8},{10,11... | collective-permute-start | bytes 884744 | tf_op jit(solution)/shard_map/ppermute | solution.py:588
  19.7 2.4 %collective-permute-start.12 = (bf16[192,768]{1,0:T(8,128)(2,1)S(1)}, bf16[192,768]{1,0:T(8,128)(2,1)S(1)}, u32[]{:S(2)}, u32[]{:S(2)}) collective-permute-start(bf16[192,768]{1,0:T(8,128)(2,1)S(1)} %concatenate.21.refs_3_), channel_id=1, source_target_pairs={{0,1},{1,0},{2,3},{3,2},{4,5},{5,4},{6,7},{7,6},{8,9},{9,8},{10,11... | collective-permute-start | bytes 884744 | tf_op jit(solution)/shard_map/ppermute | solution.py:588
  20.3 2.1 collective-permute-start.8
  21.5 1.7 collective-permute-start.9
  22.1 3.6 %collective-permute-start.3 = (bf16[2,192]{1,0:T(2,128)(2,1)S(1)}, bf16[2,192]{1,0:T(2,128)(2,1)S(1)}, u32[]{:S(2)}, u32[]{:S(2)}) collective-permute-start(bf16[2,192]{1,0:T(2,128)(2,1)S(1)} %pad_maximum_fusion.4.refs_4_), channel_id=1, source_target_pairs={{0,2},{2,0},{1,3},{3,1},{4,6},{6,4},{5,7},{7,5},{8,10},{10,8},{9,1... | collective-permute-start | bytes 2312 | tf_op jit(solution)/shard_map/ppermute | solution.py:592
  22.3 3.4 %collective-permute-start.2 = (bf16[2,192]{1,0:T(2,128)(2,1)S(1)}, bf16[2,192]{1,0:T(2,128)(2,1)S(1)}, u32[]{:S(2)}, u32[]{:S(2)}) collective-permute-start(bf16[2,192]{1,0:T(2,128)(2,1)S(1)} %pad_maximum_fusion.4.refs_4_), channel_id=1, source_target_pairs={{0,1},{1,0},{2,3},{3,2},{4,5},{5,4},{6,7},{7,6},{8,9},{9,8},{10,11... | collective-permute-start | bytes 2312 | tf_op jit(solution)/shard_map/ppermute | solution.py:588
  22.4 161.5 %copy-start.7 = (s32[18]{0:T(128)}, s32[18]{0:T(128)S(1)}, u32[]{:S(2)}) copy-start(s32[18]{0:T(128)S(1)} %pad_add_fusion.refs_3_.refs_0_.info_ref) | copy-start | bytes 220
  25.7 2.6 %collective-permute-start.13 = (bf16[192,2304]{1,0:T(8,128)(2,1)S(1)}, bf16[192,2304]{1,0:T(8,128)(2,1)S(1)}, u32[]{:S(2)}, u32[]{:S(2)}) collective-permute-start(bf16[192,2304]{1,0:T(8,128)(2,1)S(1)} %get-tuple-element.182.refs_10_), channel_id=1, source_target_pairs={{0,1},{1,0},{2,3},{3,2},{4,5},{5,4},{6,7},{7,6},{8,9},{9,8},{10,11... | collective-permute-start | bytes 2654216 | tf_op jit(solution)/shard_map/ppermute | solution.py:588
  25.8 2.5 %collective-permute-start.4 = (bf16[2,192]{1,0:T(2,128)(2,1)S(1)}, bf16[2,192]{1,0:T(2,128)(2,1)S(1)}, u32[]{:S(2)}, u32[]{:S(2)}) collective-permute-start(bf16[2,192]{1,0:T(2,128)(2,1)S(1)} %collective-permute-done.3.refs_5_.refs_6_), channel_id=1, source_target_pairs={{0,1},{1,0},{2,3},{3,2},{4,5},{5,4},{6,7},{7,6},{8,9},{9,8},{10,11... | collective-permute-start | bytes 2312 | tf_op jit(solution)/shard_map/ppermute | solution.py:588
  26.3 9.6 %collective-permute-start.15 = (bf16[96,768]{1,0:T(8,128)(2,1)S(1)}, bf16[96,768]{1,0:T(8,128)(2,1)S(1)}, u32[]{:S(2)}, u32[]{:S(2)}) collective-permute-start(bf16[96,768]{1,0:T(8,128)(2,1)S(1)} %get-tuple-element.187), channel_id=1, source_target_pairs={{0,2},{2,0},{1,3},{3,1},{4,6},{6,4},{5,7},{7,5},{8,10},{10,8},{9,1... | collective-permute-start | bytes 442376 | tf_op jit(solution)/shard_map/ppermute | solution.py:592
  26.5 12.0 %collective-permute-start.14 = (bf16[192,768]{1,0:T(8,128)(2,1)S(1)}, bf16[192,768]{1,0:T(8,128)(2,1)S(1)}, u32[]{:S(2)}, u32[]{:S(2)}) collective-permute-start(bf16[192,768]{1,0:T(8,128)(2,1)S(1)} %get-tuple-element.186), channel_id=1, source_target_pairs={{0,2},{2,0},{1,3},{3,1},{4,6},{6,4},{5,7},{7,5},{8,10},{10,8},{9,1... | collective-permute-start | bytes 884744 | tf_op jit(solution)/shard_map/ppermute | solution.py:592
  28.4 14.5 %copy-start.1 = (bf16[192,768]{1,0:T(8,128)(2,1)S(1)}, bf16[192,768]{1,0:T(8,128)(2,1)}, u32[]{:S(2)}) copy-start(bf16[192,768]{1,0:T(8,128)(2,1)} %refs_2_.1) | copy-start | bytes 884740
  38.5 3.0 %collective-permute-start.16 = (bf16[192,768]{1,0:T(8,128)(2,1)S(1)}, bf16[192,768]{1,0:T(8,128)(2,1)S(1)}, u32[]{:S(2)}, u32[]{:S(2)}) collective-permute-start(bf16[192,768]{1,0:T(8,128)(2,1)S(1)} %get-tuple-element.189.refs_7_), channel_id=1, source_target_pairs={{0,1},{1,0},{2,3},{3,2},{4,5},{5,4},{6,7},{7,6},{8,9},{9,8},{10,11... | collective-permute-start | bytes 884744 | tf_op jit(solution)/shard_map/ppermute | solution.py:588
  38.5 13.4 %collective-permute-start.18 = (bf16[192,768]{1,0:T(8,128)(2,1)S(1)}, bf16[192,768]{1,0:T(8,128)(2,1)S(1)}, u32[]{:S(2)}, u32[]{:S(2)}) collective-permute-start(bf16[192,768]{1,0:T(8,128)(2,1)S(1)} %get-tuple-element.196.refs_9_), channel_id=1, source_target_pairs={{0,2},{2,0},{1,3},{3,1},{4,6},{6,4},{5,7},{7,5},{8,10},{10,8},{9,1... | collective-permute-start | bytes 884744 | tf_op jit(solution)/shard_map/ppermute | solution.py:592
  38.7 13.2 %collective-permute-start.17 = (bf16[96,768]{1,0:T(8,128)(2,1)S(1)}, bf16[96,768]{1,0:T(8,128)(2,1)S(1)}, u32[]{:S(2)}, u32[]{:S(2)}) collective-permute-start(bf16[96,768]{1,0:T(8,128)(2,1)S(1)} %get-tuple-element.195.refs_5_), channel_id=1, source_target_pairs={{0,4},{4,0},{8,12},{12,8},{16,20},{20,16},{24,28},{28,24},{1,5},{5... | collective-permute-start | bytes 442376 | tf_op jit(solution)/shard_map/ppermute | solution.py:854
  41.4 12.8 %collective-permute-start.19 = (bf16[192,768]{1,0:T(8,128)(2,1)S(1)}, bf16[192,768]{1,0:T(8,128)(2,1)S(1)}, u32[]{:S(2)}, u32[]{:S(2)}) collective-permute-start(bf16[192,768]{1,0:T(8,128)(2,1)S(1)} %get-tuple-element.197.refs_13_), channel_id=1, source_target_pairs={{0,2},{2,0},{1,3},{3,1},{4,6},{6,4},{5,7},{7,5},{8,10},{10,8},{9,1... | collective-permute-start | bytes 884744 | tf_op jit(solution)/shard_map/ppermute | solution.py:592
  54.2 3.1 %collective-permute-start.22 = (bf16[192,768]{1,0:T(8,128)(2,1)S(1)}, bf16[192,768]{1,0:T(8,128)(2,1)S(1)}, u32[]{:S(2)}, u32[]{:S(2)}) collective-permute-start(bf16[192,768]{1,0:T(8,128)(2,1)S(1)} %get-tuple-element.201.refs_11_), channel_id=1, source_target_pairs={{0,1},{1,0},{2,3},{3,2},{4,5},{5,4},{6,7},{7,6},{8,9},{9,8},{10,11... | collective-permute-start | bytes 884744 | tf_op jit(solution)/shard_map/ppermute | solution.py:588
  54.2 3.1 %collective-permute-start.23 = (bf16[192,768]{1,0:T(8,128)(2,1)S(1)}, bf16[192,768]{1,0:T(8,128)(2,1)S(1)}, u32[]{:S(2)}, u32[]{:S(2)}) collective-permute-start(bf16[192,768]{1,0:T(8,128)(2,1)S(1)} %get-tuple-element.202.refs_15_), channel_id=1, source_target_pairs={{0,1},{1,0},{2,3},{3,2},{4,5},{5,4},{6,7},{7,6},{8,9},{9,8},{10,11... | collective-permute-start | bytes 884744 | tf_op jit(solution)/shard_map/ppermute | solution.py:588
  54.7 1.7 collective-permute-start.20
  54.7 2.5 %collective-permute-start.21 = (bf16[96,768]{1,0:T(8,128)(2,1)S(1)}, bf16[96,768]{1,0:T(8,128)(2,1)S(1)}, u32[]{:S(2)}, u32[]{:S(2)}) collective-permute-start(bf16[96,768]{1,0:T(8,128)(2,1)S(1)} %get-tuple-element.200.refs_6_), channel_id=1, source_target_pairs={{0,1},{1,0},{2,3},{3,2},{4,5},{5,4},{6,7},{7,6},{8,9},{9,8},{10,11... | collective-permute-start | bytes 442376 | tf_op jit(solution)/shard_map/ppermute | solution.py:588
  55.2 16.2 %collective-permute-start.25 = (bf16[96,768]{1,0:T(8,128)(2,1)S(1)}, bf16[96,768]{1,0:T(8,128)(2,1)S(1)}, u32[]{:S(2)}, u32[]{:S(2)}) collective-permute-start(bf16[96,768]{1,0:T(8,128)(2,1)S(1)} %get-tuple-element.205.refs_7_), channel_id=1, source_target_pairs={{0,2},{2,0},{1,3},{3,1},{4,6},{6,4},{5,7},{7,5},{8,10},{10,8},{9,1... | collective-permute-start | bytes 442376 | tf_op jit(solution)/shard_map/ppermute | solution.py:592
  56.4 15.1 %collective-permute-start.24 = (bf16[192,768]{1,0:T(8,128)(2,1)S(1)}, bf16[192,768]{1,0:T(8,128)(2,1)S(1)}, u32[]{:S(2)}, u32[]{:S(2)}) collective-permute-start(bf16[192,768]{1,0:T(8,128)(2,1)S(1)} %get-tuple-element.199.refs_3_), channel_id=1, source_target_pairs={{0,2},{2,0},{1,3},{3,1},{4,6},{6,4},{5,7},{7,5},{8,10},{10,8},{9,1... | collective-permute-start | bytes 884744 | tf_op jit(solution)/shard_map/ppermute | solution.py:592
  72.0 3.8 %collective-permute-start.28 = (bf16[2,1152,384]{2,1,0:T(8,128)(2,1)S(1)}, bf16[2,1152,384]{2,1,0:T(8,128)(2,1)S(1)}, u32[]{:S(2)}, u32[]{:S(2)}) collective-permute-start(bf16[2,1152,384]{2,1,0:T(8,128)(2,1)S(1)} %get-tuple-element.215), channel_id=1, source_target_pairs={{0,1},{1,0},{2,3},{3,2},{4,5},{5,4},{6,7},{7,6},{8,9},{9,8},{10,11... | collective-permute-start | bytes 5308424 | tf_op jit(solution)/shard_map/ppermute | solution.py:588
  72.1 8.3 %collective-permute-start.26 = (bf16[192,768]{1,0:T(8,128)(2,1)S(1)}, bf16[192,768]{1,0:T(8,128)(2,1)S(1)}, u32[]{:S(2)}, u32[]{:S(2)}) collective-permute-start(bf16[192,768]{1,0:T(8,128)(2,1)S(1)} %get-tuple-element.207.refs_5_), channel_id=1, source_target_pairs={{0,1},{1,0},{2,3},{3,2},{4,5},{5,4},{6,7},{7,6},{8,9},{9,8},{10,11... | collective-permute-start | bytes 884744 | tf_op jit(solution)/shard_map/ppermute | solution.py:588
  72.6 7.8 %collective-permute-start.27 = (bf16[96,768]{1,0:T(8,128)(2,1)S(1)}, bf16[96,768]{1,0:T(8,128)(2,1)S(1)}, u32[]{:S(2)}, u32[]{:S(2)}) collective-permute-start(bf16[96,768]{1,0:T(8,128)(2,1)S(1)} %get-tuple-element.208.refs_9_), channel_id=1, source_target_pairs={{0,1},{1,0},{2,3},{3,2},{4,5},{5,4},{6,7},{7,6},{8,9},{9,8},{10,11... | collective-permute-start | bytes 442376 | tf_op jit(solution)/shard_map/ppermute | solution.py:588
  76.8 16.9 %collective-permute-start.30 = (bf16[2,288,384]{2,1,0:T(8,128)(2,1)S(1)}, bf16[2,288,384]{2,1,0:T(8,128)(2,1)S(1)}, u32[]{:S(2)}, u32[]{:S(2)}) collective-permute-start(bf16[2,288,384]{2,1,0:T(8,128)(2,1)S(1)} %get-tuple-element.227), channel_id=1, source_target_pairs={{0,4},{4,0},{8,12},{12,8},{16,20},{20,16},{24,28},{28,24},{1,5},{5... | collective-permute-start | bytes 1327112 | tf_op jit(solution)/shard_map/ppermute | solution.py:640
  79.2 14.4 %collective-permute-start.29 = (bf16[576,384]{1,0:T(8,128)(2,1)S(1)}, bf16[576,384]{1,0:T(8,128)(2,1)S(1)}, u32[]{:S(2)}, u32[]{:S(2)}) collective-permute-start(bf16[576,384]{1,0:T(8,128)(2,1)S(1)} %get-tuple-element.218.refs_18_), channel_id=1, source_target_pairs={{0,2},{2,0},{1,3},{3,1},{4,6},{6,4},{5,7},{7,5},{8,10},{10,8},{9,1... | collective-permute-start | bytes 1327112 | tf_op jit(solution)/shard_map/ppermute | solution.py:592
  94.5 8.5 %collective-permute-start.33 = (bf16[2,960,384]{2,1,0:T(8,128)(2,1)S(1)}, bf16[2,960,384]{2,1,0:T(8,128)(2,1)S(1)}, u32[]{:S(2)}, u32[]{:S(2)}) collective-permute-start(bf16[2,960,384]{2,1,0:T(8,128)(2,1)S(1)} %get-tuple-element.232.refs_12_), channel_id=1, source_target_pairs={{0,1},{1,0},{2,3},{3,2},{4,5},{5,4},{6,7},{7,6},{8,9},{9,8},{10,11... | collective-permute-start | bytes 4423688 | tf_op jit(solution)/shard_map/ppermute | solution.py:588
  94.5 7.8 %collective-permute-start.32 = (bf16[288,384]{1,0:T(8,128)(2,1)S(1)}, bf16[288,384]{1,0:T(8,128)(2,1)S(1)}, u32[]{:S(2)}, u32[]{:S(2)}) collective-permute-start(bf16[288,384]{1,0:T(8,128)(2,1)S(1)} %get-tuple-element.240), channel_id=1, source_target_pairs={{0,2},{2,0},{1,3},{3,1},{4,6},{6,4},{5,7},{7,5},{8,10},{10,8},{9,1... | collective-permute-start | bytes 663560 | tf_op jit(solution)/shard_map/ppermute | solution.py:592
  95.5 7.5 %collective-permute-start.31 = (bf16[288,384]{1,0:T(8,128)(2,1)S(1)}, bf16[288,384]{1,0:T(8,128)(2,1)S(1)}, u32[]{:S(2)}, u32[]{:S(2)}) collective-permute-start(bf16[288,384]{1,0:T(8,128)(2,1)S(1)} %get-tuple-element.231.refs_11_), channel_id=1, source_target_pairs={{0,4},{4,0},{8,12},{12,8},{16,20},{20,16},{24,28},{28,24},{1,5},{5... | collective-permute-start | bytes 663560 | tf_op jit(solution)/shard_map/ppermute | solution.py:640
  104.4 10.5 %collective-permute-start.34 = (bf16[288,384]{1,0:T(8,128)(2,1)S(1)}, bf16[288,384]{1,0:T(8,128)(2,1)S(1)}, u32[]{:S(2)}, u32[]{:S(2)}) collective-permute-start(bf16[288,384]{1,0:T(8,128)(2,1)S(1)} %get-tuple-element.244.refs_16_), channel_id=1, source_target_pairs={{0,8},{4,12},{8,0},{12,4},{16,24},{20,28},{24,16},{28,20},{1,9},{5... | collective-permute-start | bytes 663560 | tf_op jit(solution)/shard_map/ppermute | solution.py:640
  106.1 9.5 %collective-permute-start.36 = (bf16[2,240,384]{2,1,0:T(8,128)(2,1)S(1)}, bf16[2,240,384]{2,1,0:T(8,128)(2,1)S(1)}, u32[]{:S(2)}, u32[]{:S(2)}) collective-permute-start(bf16[2,240,384]{2,1,0:T(8,128)(2,1)S(1)} %get-tuple-element.252), channel_id=1, source_target_pairs={{0,4},{4,0},{8,12},{12,8},{16,20},{20,16},{24,28},{28,24},{1,5},{5... | collective-permute-start | bytes 1105928 | tf_op jit(solution)/shard_map/ppermute | solution.py:640
  107.2 9.8 %collective-permute-start.35 = (bf16[480,384]{1,0:T(8,128)(2,1)S(1)}, bf16[480,384]{1,0:T(8,128)(2,1)S(1)}, u32[]{:S(2)}, u32[]{:S(2)}) collective-permute-start(bf16[480,384]{1,0:T(8,128)(2,1)S(1)} %get-tuple-element.245.refs_17_), channel_id=1, source_target_pairs={{0,2},{2,0},{1,3},{3,1},{4,6},{6,4},{5,7},{7,5},{8,10},{10,8},{9,1... | collective-permute-start | bytes 1105928 | tf_op jit(solution)/shard_map/ppermute | solution.py:592
  117.8 10.3 %collective-permute-start.40 = (bf16[2,576,512]{2,1,0:T(8,128)(2,1)S(1)}, bf16[2,576,512]{2,1,0:T(8,128)(2,1)S(1)}, u32[]{:S(2)}, u32[]{:S(2)}) collective-permute-start(bf16[2,576,512]{2,1,0:T(8,128)(2,1)S(1)} %get-tuple-element.258.refs_16_), channel_id=1, source_target_pairs={{0,1},{1,0},{2,3},{3,2},{4,5},{5,4},{6,7},{7,6},{8,9},{9,8},{10,11... | collective-permute-start | bytes 3538952 | tf_op jit(solution)/shard_map/ppermute | solution.py:588
  117.8 10.2 %collective-permute-start.39 = (bf16[240,384]{1,0:T(8,128)(2,1)S(1)}, bf16[240,384]{1,0:T(8,128)(2,1)S(1)}, u32[]{:S(2)}, u32[]{:S(2)}) collective-permute-start(bf16[240,384]{1,0:T(8,128)(2,1)S(1)} %get-tuple-element.264), channel_id=1, source_target_pairs={{0,2},{2,0},{1,3},{3,1},{4,6},{6,4},{5,7},{7,5},{8,10},{10,8},{9,1... | collective-permute-start | bytes 552968 | tf_op jit(solution)/shard_map/ppermute | solution.py:592
  119.1 8.9 %collective-permute-start.38 = (bf16[240,384]{1,0:T(8,128)(2,1)S(1)}, bf16[240,384]{1,0:T(8,128)(2,1)S(1)}, u32[]{:S(2)}, u32[]{:S(2)}) collective-permute-start(bf16[240,384]{1,0:T(8,128)(2,1)S(1)} %get-tuple-element.257.refs_15_), channel_id=1, source_target_pairs={{0,4},{4,0},{8,12},{12,8},{16,20},{20,16},{24,28},{28,24},{1,5},{5... | collective-permute-start | bytes 552968 | tf_op jit(solution)/shard_map/ppermute | solution.py:640
  119.5 13.5 %collective-permute-start.37 = (bf16[288,384]{1,0:T(8,128)(2,1)S(1)}, bf16[288,384]{1,0:T(8,128)(2,1)S(1)}, u32[]{:S(2)}, u32[]{:S(2)}) collective-permute-start(bf16[288,384]{1,0:T(8,128)(2,1)S(1)} %get-tuple-element.256.refs_14_.refs_1_), channel_id=1, source_target_pairs={{0,16},{4,20},{8,24},{12,28},{16,0},{20,4},{24,8},{28,12},{1,17},{... | collective-permute-start | bytes 663560 | tf_op jit(solution)/shard_map/ppermute | solution.py:640
  129.0 10.2 %collective-permute-start.44 = (bf16[2,576,256]{2,1,0:T(8,128)(2,1)S(1)}, bf16[2,576,256]{2,1,0:T(8,128)(2,1)S(1)}, u32[]{:S(2)}, u32[]{:S(2)}) collective-permute-start(bf16[2,576,256]{2,1,0:T(8,128)(2,1)S(1)} %get-tuple-element.275), channel_id=1, source_target_pairs={{0,1},{1,0},{2,3},{3,2},{4,5},{5,4},{6,7},{7,6},{8,9},{9,8},{10,11... | collective-permute-start | bytes 1769480 | tf_op jit(solution)/shard_map/ppermute | solution.py:588
  129.1 9.5 %collective-permute-start.42 = (bf16[288,512]{1,0:T(8,128)(2,1)S(1)}, bf16[288,512]{1,0:T(8,128)(2,1)S(1)}, u32[]{:S(2)}, u32[]{:S(2)}) collective-permute-start(bf16[288,512]{1,0:T(8,128)(2,1)S(1)} %get-tuple-element.272), channel_id=1, source_target_pairs={{0,2},{2,0},{1,3},{3,1},{4,6},{6,4},{5,7},{7,5},{8,10},{10,8},{9,1... | collective-permute-start | bytes 884744 | tf_op jit(solution)/shard_map/ppermute | solution.py:592
  130.0 9.1 %collective-permute-start.43 = (bf16[2,144,512]{2,1,0:T(8,128)(2,1)S(1)}, bf16[2,144,512]{2,1,0:T(8,128)(2,1)S(1)}, u32[]{:S(2)}, u32[]{:S(2)}) collective-permute-start(bf16[2,144,512]{2,1,0:T(8,128)(2,1)S(1)} %get-tuple-element.273), channel_id=1, source_target_pairs={{0,4},{4,0},{8,12},{12,8},{16,20},{20,16},{24,28},{28,24},{1,5},{5... | collective-permute-start | bytes 884744 | tf_op jit(solution)/shard_map/ppermute | solution.py:640
  131.2 6.5 %collective-permute-start.41 = (bf16[240,384]{1,0:T(8,128)(2,1)S(1)}, bf16[240,384]{1,0:T(8,128)(2,1)S(1)}, u32[]{:S(2)}, u32[]{:S(2)}) collective-permute-start(bf16[240,384]{1,0:T(8,128)(2,1)S(1)} %get-tuple-element.269), channel_id=1, source_target_pairs={{0,8},{4,12},{8,0},{12,4},{16,24},{20,28},{24,16},{28,20},{1,9},{5... | collective-permute-start | bytes 552968 | tf_op jit(solution)/shard_map/ppermute | solution.py:640
  140.1 10.0 %collective-permute-start.47 = (bf16[288,256]{1,0:T(8,128)(2,1)S(1)}, bf16[288,256]{1,0:T(8,128)(2,1)S(1)}, u32[]{:S(2)}, u32[]{:S(2)}) collective-permute-start(bf16[288,256]{1,0:T(8,128)(2,1)S(1)} %get-tuple-element.281), channel_id=1, source_target_pairs={{0,2},{2,0},{1,3},{3,1},{4,6},{6,4},{5,7},{7,5},{8,10},{10,8},{9,1... | collective-permute-start | bytes 442376 | tf_op jit(solution)/shard_map/ppermute | solution.py:592
  141.3 20.7 %collective-permute-start.45 = (bf16[288,384]{1,0:T(8,128)(2,1)S(1)}, bf16[288,384]{1,0:T(8,128)(2,1)S(1)}, u32[]{:S(2)}, u32[]{:S(2)}) collective-permute-start(bf16[288,384]{1,0:T(8,128)(2,1)S(1)} %get-tuple-element.277.refs_1_), channel_id=1, source_target_pairs={{0,8},{4,12},{8,0},{12,4},{16,24},{20,28},{24,16},{28,20},{1,9},{5... | collective-permute-start | bytes 663560 | tf_op jit(solution)/shard_map/ppermute | solution.py:640
  142.5 19.5 %collective-permute-start.49 = (bf16[64,1536]{1,0:T(8,128)(2,1)S(1)}, bf16[64,1536]{1,0:T(8,128)(2,1)S(1)}, u32[]{:S(2)}, u32[]{:S(2)}) collective-permute-start(bf16[64,1536]{1,0:T(8,128)(2,1)S(1)} %get-tuple-element.283), channel_id=1, source_target_pairs={{0,4},{4,8},{8,12},{12,16},{16,20},{20,24},{24,28},{1,5},{5,9},{9,... | collective-permute-start | bytes 589832 | tf_op jit(solution)/shard_map/ppermute | solution.py:894
  146.1 15.9 %collective-permute-start.50 = (bf16[64,1536]{1,0:T(8,128)(2,1)S(1)}, bf16[64,1536]{1,0:T(8,128)(2,1)S(1)}, u32[]{:S(2)}, u32[]{:S(2)}) collective-permute-start(bf16[64,1536]{1,0:T(8,128)(2,1)S(1)} %get-tuple-element.284), channel_id=1, source_target_pairs={{4,0},{8,4},{12,8},{16,12},{20,16},{24,20},{28,24},{5,1},{9,5},{13... | collective-permute-start | bytes 589832 | tf_op jit(solution)/shard_map/ppermute | solution.py:894
  147.4 9.2 %collective-permute-start.48 = (bf16[2,144,256]{2,1,0:T(8,128)(2,1)S(1)}, bf16[2,144,256]{2,1,0:T(8,128)(2,1)S(1)}, u32[]{:S(2)}, u32[]{:S(2)}) collective-permute-start(bf16[2,144,256]{2,1,0:T(8,128)(2,1)S(1)} %get-tuple-element.282), channel_id=1, source_target_pairs={{0,4},{4,0},{8,12},{12,8},{16,20},{20,16},{24,28},{28,24},{1,5},{5... | collective-permute-start | bytes 442376 | tf_op jit(solution)/shard_map/ppermute | solution.py:640
  150.1 11.0 %collective-permute-start.46 = (bf16[240,384]{1,0:T(8,128)(2,1)S(1)}, bf16[240,384]{1,0:T(8,128)(2,1)S(1)}, u32[]{:S(2)}, u32[]{:S(2)}) collective-permute-start(bf16[240,384]{1,0:T(8,128)(2,1)S(1)} %get-tuple-element.278.refs_3_), channel_id=1, source_target_pairs={{0,16},{4,20},{8,24},{12,28},{16,0},{20,4},{24,8},{28,12},{1,17},{... | collective-permute-start | bytes 552968 | tf_op jit(solution)/shard_map/ppermute | solution.py:640
  156.6 8.6 %collective-permute-start.53 = (bf16[144,512]{1,0:T(8,128)(2,1)S(1)}, bf16[144,512]{1,0:T(8,128)(2,1)S(1)}, u32[]{:S(2)}, u32[]{:S(2)}) collective-permute-start(bf16[144,512]{1,0:T(8,128)(2,1)S(1)} %get-tuple-element.296), channel_id=1, source_target_pairs={{0,4},{4,0},{8,12},{12,8},{16,20},{20,16},{24,28},{28,24},{1,5},{5... | collective-permute-start | bytes 442376 | tf_op jit(solution)/shard_map/ppermute | solution.py:640
  161.2 12.4 %collective-permute-start.54 = (bf16[144,512]{1,0:T(8,128)(2,1)S(1)}, bf16[144,512]{1,0:T(8,128)(2,1)S(1)}, u32[]{:S(2)}, u32[]{:S(2)}) collective-permute-start(bf16[144,512]{1,0:T(8,128)(2,1)S(1)} %get-tuple-element.297), channel_id=1, source_target_pairs={{0,2},{2,0},{1,3},{3,1},{4,6},{6,4},{5,7},{7,5},{8,10},{10,8},{9,1... | collective-permute-start | bytes 442376 | tf_op jit(solution)/shard_map/ppermute | solution.py:592
  162.7 10.8 %collective-permute-start.56 = (bf16[144,256]{1,0:T(8,128)(2,1)S(1)}, bf16[144,256]{1,0:T(8,128)(2,1)S(1)}, u32[]{:S(2)}, u32[]{:S(2)}) collective-permute-start(bf16[144,256]{1,0:T(8,128)(2,1)S(1)} %get-tuple-element.300), channel_id=1, source_target_pairs={{0,2},{2,0},{1,3},{3,1},{4,6},{6,4},{5,7},{7,5},{8,10},{10,8},{9,1... | collective-permute-start | bytes 221192 | tf_op jit(solution)/shard_map/ppermute | solution.py:592
  164.0 9.6 %collective-permute-start.55 = (bf16[144,256]{1,0:T(8,128)(2,1)S(1)}, bf16[144,256]{1,0:T(8,128)(2,1)S(1)}, u32[]{:S(2)}, u32[]{:S(2)}) collective-permute-start(bf16[144,256]{1,0:T(8,128)(2,1)S(1)} %get-tuple-element.292.refs_16_), channel_id=1, source_target_pairs={{0,4},{4,0},{8,12},{12,8},{16,20},{20,16},{24,28},{28,24},{1,5},{5... | collective-permute-start | bytes 221192 | tf_op jit(solution)/shard_map/ppermute | solution.py:640
  164.0 9.6 %collective-permute-start.52 = (bf16[240,384]{1,0:T(8,128)(2,1)S(1)}, bf16[240,384]{1,0:T(8,128)(2,1)S(1)}, u32[]{:S(2)}, u32[]{:S(2)}) collective-permute-start(bf16[240,384]{1,0:T(8,128)(2,1)S(1)} %get-tuple-element.291.refs_15_.refs_3_), channel_id=1, source_target_pairs={{0,8},{4,12},{8,0},{12,4},{16,24},{20,28},{24,16},{28,20},{1,9},{5... | collective-permute-start | bytes 552968 | tf_op jit(solution)/shard_map/ppermute | solution.py:640
  165.3 10.3 %collective-permute-start.51 = (bf16[576,384]{1,0:T(8,128)(2,1)S(1)}, bf16[576,384]{1,0:T(8,128)(2,1)S(1)}, u32[]{:S(2)}, u32[]{:S(2)}) collective-permute-start(bf16[576,384]{1,0:T(8,128)(2,1)S(1)} %get-tuple-element.290.refs_14_.refs_1_), channel_id=1, source_target_pairs={{0,4},{4,0},{8,12},{12,8},{16,20},{20,16},{24,28},{28,24},{1,5},{5... | collective-permute-start | bytes 1327112 | tf_op jit(solution)/shard_map/ppermute | solution.py:640
  176.4 7.6 %collective-permute-start.57 = (bf16[480,384]{1,0:T(8,128)(2,1)S(1)}, bf16[480,384]{1,0:T(8,128)(2,1)S(1)}, u32[]{:S(2)}, u32[]{:S(2)}) collective-permute-start(bf16[480,384]{1,0:T(8,128)(2,1)S(1)} %get-tuple-element.302.refs_1_), channel_id=1, source_target_pairs={{0,4},{4,0},{8,12},{12,8},{16,20},{20,16},{24,28},{28,24},{1,5},{5... | collective-permute-start | bytes 1105928 | tf_op jit(solution)/shard_map/ppermute | solution.py:640
  177.3 5.9 %collective-permute-start.58 = (bf16[144,768]{1,0:T(8,128)(2,1)S(1)}, bf16[144,768]{1,0:T(8,128)(2,1)S(1)}, u32[]{:S(2)}, u32[]{:S(2)}) collective-permute-start(bf16[144,768]{1,0:T(8,128)(2,1)S(1)} %get-tuple-element.304), channel_id=1, source_target_pairs={{0,8},{4,12},{8,0},{12,4},{16,24},{20,28},{24,16},{28,20},{1,9},{5... | collective-permute-start | bytes 663560 | tf_op jit(solution)/shard_map/ppermute | solution.py:640
  185.5 9.7 %collective-permute-start.59 = (bf16[144,768]{1,0:T(8,128)(2,1)S(1)}, bf16[144,768]{1,0:T(8,128)(2,1)S(1)}, u32[]{:S(2)}, u32[]{:S(2)}) collective-permute-start(bf16[144,768]{1,0:T(8,128)(2,1)S(1)} %get-tuple-element.306.refs_1_), channel_id=1, source_target_pairs={{0,16},{4,20},{8,24},{12,28},{16,0},{20,4},{24,8},{28,12},{1,17},{... | collective-permute-start | bytes 663560 | tf_op jit(solution)/shard_map/ppermute | solution.py:640
  195.8 6.0 %collective-permute-start.60 = (bf16[144,768]{1,0:T(8,128)(2,1)S(1)}, bf16[144,768]{1,0:T(8,128)(2,1)S(1)}, u32[]{:S(2)}, u32[]{:S(2)}) collective-permute-start(bf16[144,768]{1,0:T(8,128)(2,1)S(1)} %get-tuple-element.308.refs_1_), channel_id=1, source_target_pairs={{0,8},{4,12},{8,0},{12,4},{16,24},{20,28},{24,16},{28,20},{1,9},{5... | collective-permute-start | bytes 663560 | tf_op jit(solution)/shard_map/ppermute | solution.py:640
  203.0 9.5 %collective-permute-start.61 = (bf16[288,768]{1,0:T(8,128)(2,1)S(1)}, bf16[288,768]{1,0:T(8,128)(2,1)S(1)}, u32[]{:S(2)}, u32[]{:S(2)}) collective-permute-start(bf16[288,768]{1,0:T(8,128)(2,1)S(1)} %get-tuple-element.310.refs_0_.refs_1_.refs_2_), channel_id=1, source_target_pairs={{0,4},{4,0},{8,12},{12,8},{16,20},{20,16},{24,28},{28,24},{1,5},{5... | collective-permute-start | bytes 1327112 | tf_op jit(solution)/shard_map/ppermute | solution.py:640
  (28 other events, 167.5 us)

commit v7 on v6

--- a/solution.py
+++ b/solution.py
@@ -847,10 +847,10 @@
     attn_parts = attn_in, mate, far, farmate
     gains = gain_own, gain_mate, gain_far, to_core(gain_far)
     nt, q, k, v, cos, sin, gain, token = qkv_call(info, x, x_low, x_high, gains, attn_parts)
-    out_far, g_mine, token = together_at([out_far, g_mine, token])
+    out_far, g_mine, down_a, token = together_at([out_far, g_mine, down_a, token])
+    da_far = to_chip(down_a)
     out_farmate = to_core(out_far)
-    out_farmate, down_a, token = together_at([out_farmate, down_a, token])
-    da_far = to_chip(down_a)
+    out_farmate, token = together_at([out_farmate, token])
     g_other = lax.ppermute(g_mine, "seq", [(i, i ^ 1) for i in range(count)])
     out_parts = attn_out, out_mate, out_far, out_farmate
     mixed, middle, n2, out_w, lse, token = attend_call(info, q, k, v, x, out_parts, gain, deps=(token,))

time: 225 us -> 225 us (level)
  no operation moved by 1% of the time
where the time goes in v7:
time: 225 us; the launch traced here: 222 us
  Pallas kernels  102 us (45%)
  starting transfers between devices  59.9 us (27%)
  waiting for transfers between devices  41.8 us (19%)
  local copies, waits for them, and re-layouts  10.6 us (5%)
  other arithmetic  5.68 us (3%)
    pallas_call x8, Pallas kernels, call(): pl.pallas_call(wrapped, in_specs=list(in_specs) + [pl.BlockSpec(memory_sp...  71.3 us
    ppermute x20, waiting for transfers between devices, along_seq(): return lax.ppermute(a, 'seq', [(i, i ^ 1 << shift) for i in range(count)])  27.3 us
    ppermute x20, starting transfers between devices, along_seq(): return lax.ppermute(a, 'seq', [(i, i ^ 1 << shift) for i in range(count)])  25.4 us
    pallas_call x4, Pallas kernels, adam_call(): pl.pallas_call(body, grid=(r // rows_at_once,), in_specs=[smem()] + [pl.B...  21.3 us
    ppermute x16, starting transfers between devices, to_chip(): return lax.ppermute(a, 'wshard', CHIPS)  17 us
    pallas_call x12, Pallas kernels, boundary(): pl.pallas_call(body, grid=(1,), in_specs=[smem()] + [full(a.shape) for a...  9.73 us
    ppermute x16, waiting for transfers between devices, to_chip(): return lax.ppermute(a, 'wshard', CHIPS)  9.7 us
    ppermute x21, waiting for transfers between devices, to_core(): return lax.ppermute(a, 'wshard', CORES)  4.85 us
  transfers between devices with their start and end apart: 62, of which 20 were waited for; matrix products, arithmetic and copies ran while one was open for 5% of the time, Pallas kernels for 40%

profile of v7, /device:TPU:0, one launch (start us, length us, event | category | flops | bytes accessed | tf_op | source)
XLA Modules:
  0.0 222.0 jit_solution(17361530354051773752)
XLA Ops:
  0.7 3.0 %collective-permute-start.6 = (bf16[192,2304]{1,0:T(8,128)(2,1)}, bf16[192,2304]{1,0:T(8,128)(2,1)S(1)}, u32[]{:S(2)}, u32[]{:S(2)}) collective-permute-start(bf16[192,2304]{1,0:T(8,128)(2,1)} %refs_6_.3), channel_id=1, source_target_pairs={{0,2},{2,0},{1,3},{3,1},{4,6},{6,4},{5,7},{7,5},{8,10},{10,8},{9,1... | collective-permute-start | bytes 2654216 | tf_op jit(solution)/shard_map/ppermute | solution.py:592
  3.7 1.0 slice_bitcast_fusion
  4.6 1.3 collective-permute-start.1
  5.9 4.6 %collective-permute-start = (bf16[64,768]{1,0:T(8,128)(2,1)S(1)}, bf16[64,768]{1,0:T(8,128)(2,1)S(1)}, u32[]{:S(2)}, u32[]{:S(2)}) collective-permute-start(bf16[64,768]{1,0:T(8,128)(2,1)S(1)} %get-tuple-element.345), channel_id=1, source_target_pairs={{0,4},{4,8},{8,12},{12,16},{16,20},{20,24},{24,28},{1,5},{5,9},{9,... | collective-permute-start | bytes 294920 | tf_op jit(solution)/shard_map/ppermute | solution.py:825
  10.5 0.9 slice.119.refs_2_
  11.5 1.0 slice.118.refs_1_
  12.5 1.0 copy-done
  13.6 1.1 fusion.9
  17.3 1.1 concatenate.21.refs_3_
  18.5 1.2 pad_maximum_fusion.refs_3_
  20.4 1.2 pad_maximum_fusion.1.refs_2_
  23.3 2.4 %collective-permute-done.3.refs_5_.refs_6_ = bf16[2,192]{1,0:T(2,128)(2,1)S(1)} collective-permute-done((bf16[2,192]{1,0:T(2,128)(2,1)S(1)}, bf16[2,192]{1,0:T(2,128)(2,1)S(1)}, u32[]{:S(2)}, u32[]{:S(2)}) %collective-permute-start.3) | collective-permute-done | bytes 800 | tf_op jit(solution)/shard_map/ppermute | solution.py:592
  26.5 1.8 collective-permute-start.14
  28.4 7.5 %qkv.1 = (bf16[768,1152]{1,0:T(8,128)(2,1)S(1)}, bf16[1152,768]{1,0:T(8,128)(2,1)S(1)}, bf16[1152,768]{1,0:T(8,128)(2,1)S(1)}, bf16[1152,768]{1,0:T(8,128)(2,1)S...) custom-call(s32[18]{0:T(128)S(1)} %pad_add_fusion.refs_3_.refs_0_.info_ref, ...), custom_call_target="tpu_custom_call" | custom-call | flops 9900000256 | tf_op jit(solution)/shard_map/qkv/pallas_call | solution.py:59
  35.9 2.5 %collective-permute-done.14.refs_0_ = bf16[192,768]{1,0:T(8,128)(2,1)S(1)} collective-permute-done((bf16[192,768]{1,0:T(8,128)(2,1)S(1)}, bf16[192,768]{1,0:T(8,128)(2,1)S(1)}, u32[]{:S(2)}, u32[]{:S(2)}) %collective-permute-start.14) | collective-permute-done | bytes 294944 | tf_op jit(solution)/shard_map/ppermute | solution.py:592
  38.7 2.7 %collective-permute-start.17 = (bf16[96,768]{1,0:T(8,128)(2,1)S(1)}, bf16[96,768]{1,0:T(8,128)(2,1)S(1)}, u32[]{:S(2)}, u32[]{:S(2)}) collective-permute-start(bf16[96,768]{1,0:T(8,128)(2,1)S(1)} %get-tuple-element.195.refs_5_), channel_id=1, source_target_pairs={{0,4},{4,0},{8,12},{12,8},{16,20},{20,16},{24,28},{28,24},{1,5},{5... | collective-permute-start | bytes 442376 | tf_op jit(solution)/shard_map/ppermute | solution.py:854
  41.4 1.5 collective-permute-start.19
  42.9 9.0 %attend.1 = (bf16[1024,768]{1,0:T(8,128)(2,1)S(1)}, bf16[1024,768]{1,0:T(8,128)(2,1)S(1)}, bf16[1024,768]{1,0:T(8,128)(2,1)S(1)}, bf16[768,768]{1,0:T(8,128)(2,1...) custom-call(s32[18]{0:T(128)S(1)} %pad_add_fusion.refs_3_.refs_0_.info_ref, ...), custom_call_target="tpu_custom_call" | custom-call | flops 12099999744 | tf_op jit(solution)/shard_map/attend/pallas_call | solution.py:59
  52.0 2.2 %collective-permute-done.19.refs_2_ = bf16[192,768]{1,0:T(8,128)(2,1)S(1)} collective-permute-done((bf16[192,768]{1,0:T(8,128)(2,1)S(1)}, bf16[192,768]{1,0:T(8,128)(2,1)S(1)}, u32[]{:S(2)}, u32[]{:S(2)}) %collective-permute-start.19) | collective-permute-done | bytes 294944 | tf_op jit(solution)/shard_map/ppermute | solution.py:592
  57.3 14.2 %ffn_a.1 = (bf16[1024,768]{1,0:T(8,128)(2,1)S(1)}, bf16[1024,768]{1,0:T(8,128)(2,1)S(1)}, bf16[2,1152,384]{2,1,0:T(8,128)(2,1)S(1)}, bf16[2,1152,384]{2,1,0:T(8,128)(2,1)S(1)}, f32[8,128]{1,0:T(8,128)S(1)}) custom-call(s32[18]{0:T(128)S(1)} %pad_add_fusion.refs_3_.refs_0_.info_ref, bf16[1024,768]{1,0:T(8,128)(2,1)S(1)} %get-tuple-element.194.refs_1_, ...), custom_call_target="tpu_custom_call" | custom-call | flops 19800000512 | tf_op jit(solution)/shard_map/ffn_a/pallas_call | solution.py:59
  72.7 3.1 %collective-permute-done.28.refs_2_ = bf16[2,1152,384]{2,1,0:T(8,128)(2,1)S(1)} collective-permute-done((bf16[2,1152,384]{2,1,0:T(8,128)(2,1)S(1)}, bf16[2,1152,384]{2,1,0:T(8,128)(2,1)S(1)}, u32[]{:S(2)}, u32[]{:S(2)}) %collective-permute-start.28) | collective-permute-done | bytes 1769504 | tf_op jit(solution)/shard_map/ppermute | solution.py:588
  75.8 1.0 land.13
  76.8 2.5 %collective-permute-start.30 = (bf16[2,288,384]{2,1,0:T(8,128)(2,1)S(1)}, bf16[2,288,384]{2,1,0:T(8,128)(2,1)S(1)}, u32[]{:S(2)}, u32[]{:S(2)}) collective-permute-start(bf16[2,288,384]{2,1,0:T(8,128)(2,1)S(1)} %get-tuple-element.227), channel_id=1, source_target_pairs={{0,4},{4,0},{8,12},{12,8},{16,20},{20,16},{24,28},{28,24},{1,5},{5... | collective-permute-start | bytes 1327112 | tf_op jit(solution)/shard_map/ppermute | solution.py:640
  79.2 1.2 collective-permute-start.29
  80.4 13.2 %ffn_b.1 = (bf16[1024,768]{1,0:T(8,128)(2,1)}, bf16[1024,768]{1,0:T(8,128)(2,1)S(1)}, bf16[1024,768]{1,0:T(8,128)(2,1)S(1)}, bf16[2,960,384]{2,1,0:T(8,128)(2,1)...) custom-call(s32[18]{0:T(128)S(1)} %pad_add_fusion.refs_3_.refs_0_.info_ref, ...), custom_call_target="tpu_custom_call" | custom-call | flops 15399999488 | tf_op jit(solution)/shard_map/ffn_b/pallas_call | solution.py:59
  95.5 6.5 %attend_back.3 = (bf16[1152,768]{1,0:T(8,128)(2,1)S(1)}, bf16[1152,768]{1,0:T(8,128)(2,1)S(1)}, bf16[1152,768]{1,0:T(8,128)(2,1)S(1)}, bf16[2,576,512]{2,1,0:T(8...) custom-call(s32[18]{0:T(128)S(1)} %pad_add_fusion.refs_3_.refs_0_.info_ref, ...), custom_call_target="tpu_custom_call" | custom-call | flops 4400000000 | tf_op jit(solution)/shard_map/attend_back/pallas_call | solution.py:59
  103.0 1.5 land.15
  104.4 1.6 collective-permute-start.34
  106.1 1.1 collective-permute-start.36
  107.2 1.2 collective-permute-start.35
  108.4 6.5 %attend_back.4 = (bf16[1152,768]{1,0:T(8,128)(2,1)S(1)}, bf16[1152,768]{1,0:T(8,128)(2,1)S(1)}, bf16[1152,768]{1,0:T(8,128)(2,1)S(1)}, bf16[2,576,512]{2,1,0:T(8...) custom-call(s32[18]{0:T(128)S(1)} %pad_add_fusion.refs_3_.refs_0_.in, ...), custom_call_target="tpu_custom_call", output_to_operand_aliasing={{0}: (10, {}), {1}: (11, {}), {2}: (12, {}), {3}: (13, {}),... | custom-call | flops 4400000000 | tf_op jit(solution)/shard_map/attend_back/pallas_call | solution.py:59
  115.6 1.4 collective-permute-done.35.refs_5_
  117.8 1.3 collective-permute-start.39
  119.5 1.8 collective-permute-start.37
  121.3 6.7 %attend_back.5 = (bf16[1152,768]{1,0:T(8,128)(2,1)S(1)}, bf16[1152,768]{1,0:T(8,128)(2,1)S(1)}, bf16[1152,768]{1,0:T(8,128)(2,1)S(1)}, bf16[2,576,256]{2,1,0:T(8...) custom-call(s32[18]{0:T(128)S(1)} %pad_add_fusion.refs_3_.refs_0_.in, ...), custom_call_target="tpu_custom_call", output_to_operand_aliasing={{0}: (10, {}), {1}: (11, {}), {2}: (12, {})} | custom-call | flops 4400000000 | tf_op jit(solution)/shard_map/attend_back/pallas_call | solution.py:59
  128.1 1.0 land.17
  129.1 0.9 collective-permute-start.42
  130.0 1.2 collective-permute-start.43
  131.2 1.7 collective-permute-start.41
  133.0 4.8 %collective-permute-done.41.refs_4_ = bf16[240,384]{1,0:T(8,128)(2,1)S(1)} collective-permute-done((bf16[240,384]{1,0:T(8,128)(2,1)S(1)}, bf16[240,384]{1,0:T(8,128)(2,1)S(1)}, u32[]{:S(2)}, u32[]{:S(2)}) %collective-permute-start.41) | collective-permute-done | bytes 184352 | tf_op jit(solution)/shard_map/ppermute | solution.py:640
  140.1 1.2 collective-permute-start.47
  141.3 1.2 collective-permute-start.45
  142.5 3.6 %collective-permute-start.49 = (bf16[64,1536]{1,0:T(8,128)(2,1)S(1)}, bf16[64,1536]{1,0:T(8,128)(2,1)S(1)}, u32[]{:S(2)}, u32[]{:S(2)}) collective-permute-start(bf16[64,1536]{1,0:T(8,128)(2,1)S(1)} %get-tuple-element.283), channel_id=1, source_target_pairs={{0,4},{4,8},{8,12},{12,16},{16,20},{20,24},{24,28},{1,5},{5,9},{9,... | collective-permute-start | bytes 589832 | tf_op jit(solution)/shard_map/ppermute | solution.py:894
  146.1 1.3 collective-permute-start.50
  147.4 2.7 %collective-permute-start.48 = (bf16[2,144,256]{2,1,0:T(8,128)(2,1)S(1)}, bf16[2,144,256]{2,1,0:T(8,128)(2,1)S(1)}, u32[]{:S(2)}, u32[]{:S(2)}) collective-permute-start(bf16[2,144,256]{2,1,0:T(8,128)(2,1)S(1)} %get-tuple-element.282), channel_id=1, source_target_pairs={{0,4},{4,0},{8,12},{12,8},{16,20},{20,16},{24,28},{28,24},{1,5},{5... | collective-permute-start | bytes 442376 | tf_op jit(solution)/shard_map/ppermute | solution.py:640
  150.4 6.2 %collective-permute-done.48.refs_8_ = bf16[2,144,256]{2,1,0:T(8,128)(2,1)S(1)} collective-permute-done((bf16[2,144,256]{2,1,0:T(8,128)(2,1)S(1)}, bf16[2,144,256]{2,1,0:T(8,128)(2,1)S(1)}, u32[]{:S(2)}, u32[]{:S(2)}) %collective-permute-start.48) | collective-permute-done | bytes 147488 | tf_op jit(solution)/shard_map/ppermute | solution.py:640
  156.6 2.5 %collective-permute-start.53 = (bf16[144,512]{1,0:T(8,128)(2,1)S(1)}, bf16[144,512]{1,0:T(8,128)(2,1)S(1)}, u32[]{:S(2)}, u32[]{:S(2)}) collective-permute-start(bf16[144,512]{1,0:T(8,128)(2,1)S(1)} %get-tuple-element.296), channel_id=1, source_target_pairs={{0,4},{4,0},{8,12},{12,8},{16,20},{20,16},{24,28},{28,24},{1,5},{5... | collective-permute-start | bytes 442376 | tf_op jit(solution)/shard_map/ppermute | solution.py:640
  159.1 2.0 collective-permute-done.46.refs_4_
  162.7 1.3 collective-permute-start.56
  164.0 1.3 collective-permute-start.52
  166.0 7.5 %last.1 = (bf16[1024,768]{1,0:T(8,128)(2,1)}, f32[8,128]{1,0:T(8,128)S(1)}) custom-call(s32[18]{0:T(128)S(1)} %pad_add_fusion.refs_3_.refs_0_.info_ref, bf16[1024,768]{1,0:T(8,128)(2,1)S(1)} %bitcast.14, bf16[1152,768]{1,0:T(8,128)(2,1)S(1)} %get-tuple-element.259.refs_2_, bf16[1152,768]{1,0:T(8,128)(2,1)S(1)} %get-tuple-element.260.refs_3_, ...), custom_call_target="tpu_custom_call" | custom-call | flops 7699999744 | tf_op jit(solution)/shard_map/last/pallas_call | solution.py:59
  173.6 2.0 collective-permute-done.51.refs_2_
  177.3 1.7 collective-permute-start.58
  179.1 4.2 %collective-permute-done.58.refs_4_ = bf16[144,768]{1,0:T(8,128)(2,1)S(1)} collective-permute-done((bf16[144,768]{1,0:T(8,128)(2,1)S(1)}, bf16[144,768]{1,0:T(8,128)(2,1)S(1)}, u32[]{:S(2)}, u32[]{:S(2)}) %collective-permute-start.58) | collective-permute-done | bytes 221216 | tf_op jit(solution)/shard_map/ppermute | solution.py:640
  185.5 2.4 %collective-permute-start.59 = (bf16[144,768]{1,0:T(8,128)(2,1)S(1)}, bf16[144,768]{1,0:T(8,128)(2,1)S(1)}, u32[]{:S(2)}, u32[]{:S(2)}) collective-permute-start(bf16[144,768]{1,0:T(8,128)(2,1)S(1)} %get-tuple-element.306.refs_1_), channel_id=1, source_target_pairs={{0,16},{4,20},{8,24},{12,28},{16,0},{20,4},{24,8},{28,12},{1,17},{... | collective-permute-start | bytes 663560 | tf_op jit(solution)/shard_map/ppermute | solution.py:640
  188.0 2.9 %adam.5 = (f32[192,768]{1,0:T(8,128)}, f32[192,768]{1,0:T(8,128)}, f32[192,768]{1,0:T(8,128)}, f32[192,768]{1,0:T(8,128)}, f32[192,1]{1,0:T(8,128)}) custom-call(s32[18]{0:T(128)} %copy-done.7, bf16[960,384]{1,0:T(8,128)(2,1)} %copy-done.16, bf16[960,384]{1,0:T(8,128)(2,1)} %copy-done.16, bf16[192,768]{1,0:T(8,128)(2,1)} %refs_2_.1, f32[192,768]{1,0:T(8,128)} %refs_3_.1, ...), custom_call_target="tpu_custom_call" | custom-call | flops 3300000000 | tf_op jit(solution)/shard_map/adam/pallas_call | solution.py:570
  190.9 4.4 %collective-permute-done.59.refs_2_ = bf16[144,768]{1,0:T(8,128)(2,1)S(1)} collective-permute-done((bf16[144,768]{1,0:T(8,128)(2,1)S(1)}, bf16[144,768]{1,0:T(8,128)(2,1)S(1)}, u32[]{:S(2)}, u32[]{:S(2)}) %collective-permute-start.59) | collective-permute-done | bytes 221216 | tf_op jit(solution)/shard_map/ppermute | solution.py:640
  195.9 4.7 %adam.7 = (f32[288,768]{1,0:T(8,128)}, f32[288,768]{1,0:T(8,128)}, f32[288,768]{1,0:T(8,128)}, f32[288,768]{1,0:T(8,128)}, f32[288,1]{1,0:T(8,128)}) custom-call(s32[18]{0:T(128)} %copy-done.7, bf16[1152,384]{1,0:T(8,128)(2,1)} %copy-done.15, bf16[1152,384]{1,0:T(8,128)(2,1)} %copy-done.15, bf16[960,384]{1,0:T(8,128)(2,1)} %copy-done.16, ...), custom_call_target="tpu_custom_call" | custom-call | flops 3300000000 | tf_op jit(solution)/shard_map/adam/pallas_call | solution.py:570
  200.6 1.2 collective-permute-done.60.refs_2_
  203.0 1.1 collective-permute-start.61
  204.1 6.7 %adam.6 = (f32[192,2304]{1,0:T(8,128)}, f32[192,2304]{1,0:T(8,128)}, f32[192,2304]{1,0:T(8,128)}, f32[192,2304]{1,0:T(8,128)}, f32[192,1]{1,0:T(8,128)}) custom-call(s32[18]{0:T(128)} %copy-done.7, bf16[1152,384]{1,0:T(8,128)(2,1)} %copy-done.15, bf16[1152,384]{1,0:T(8,128)(2,1)} %copy-done.15, bf16[1152,384]{1,0:T(8,128)(2,1)} %copy-done.15, ...), custom_call_target="tpu_custom_call" | custom-call | flops 3300000000 | tf_op jit(solution)/shard_map/adam/pallas_call | solution.py:570
  210.9 1.0 reduce.1
  213.3 6.9 %adam.4 = (f32[192,2304]{1,0:T(8,128)}, f32[192,2304]{1,0:T(8,128)}, f32[192,2304]{1,0:T(8,128)}, f32[192,2304]{1,0:T(8,128)}, f32[192,1]{1,0:T(8,128)}) custom-call(s32[18]{0:T(128)} %copy-done.7, bf16[288,768]{1,0:T(8,128)(2,1)} %copy-done.12, bf16[288,768]{1,0:T(8,128)(2,1)} %copy-done.12, bf16[288,768]{1,0:T(8,128)(2,1)} %copy-done.12, ...), custom_call_target="tpu_custom_call" | custom-call | flops 3300000000 | tf_op jit(solution)/shard_map/adam/pallas_call | solution.py:570
  220.2 1.0 reduce
  (171 shorter events, 28.0 us)
Async XLA Ops:
  0.7 25.1 %collective-permute-start.6 = (bf16[192,2304]{1,0:T(8,128)(2,1)}, bf16[192,2304]{1,0:T(8,128)(2,1)S(1)}, u32[]{:S(2)}, u32[]{:S(2)}) collective-permute-start(bf16[192,2304]{1,0:T(8,128)(2,1)} %refs_6_.3), channel_id=1, source_target_pairs={{0,2},{2,0},{1,3},{3,1},{4,6},{6,4},{5,7},{7,5},{8,10},{10,8},{9,1... | collective-permute-start | bytes 2654216 | tf_op jit(solution)/shard_map/ppermute | solution.py:592
  3.7 19.6 %collective-permute-start.5 = (bf16[192,2304]{1,0:T(8,128)(2,1)}, bf16[192,2304]{1,0:T(8,128)(2,1)S(1)}, u32[]{:S(2)}, u32[]{:S(2)}) collective-permute-start(bf16[192,2304]{1,0:T(8,128)(2,1)} %refs_6_.3), channel_id=1, source_target_pairs={{0,1},{1,0},{2,3},{3,2},{4,5},{5,4},{6,7},{7,6},{8,9},{9,8},{10,11... | collective-permute-start | bytes 2654216 | tf_op jit(solution)/shard_map/ppermute | solution.py:588
  4.6 10.0 %collective-permute-start.1 = (bf16[64,768]{1,0:T(8,128)(2,1)S(1)}, bf16[64,768]{1,0:T(8,128)(2,1)S(1)}, u32[]{:S(2)}, u32[]{:S(2)}) collective-permute-start(bf16[64,768]{1,0:T(8,128)(2,1)S(1)} %get-tuple-element.344), channel_id=1, source_target_pairs={{4,0},{8,4},{12,8},{16,12},{20,16},{24,20},{28,24},{5,1},{9,5},{13... | collective-permute-start | bytes 294920 | tf_op jit(solution)/shard_map/ppermute | solution.py:825
  5.9 9.8 %collective-permute-start = (bf16[64,768]{1,0:T(8,128)(2,1)S(1)}, bf16[64,768]{1,0:T(8,128)(2,1)S(1)}, u32[]{:S(2)}, u32[]{:S(2)}) collective-permute-start(bf16[64,768]{1,0:T(8,128)(2,1)S(1)} %get-tuple-element.345), channel_id=1, source_target_pairs={{0,4},{4,8},{8,12},{12,16},{16,20},{20,24},{24,28},{1,5},{5,9},{9,... | collective-permute-start | bytes 294920 | tf_op jit(solution)/shard_map/ppermute | solution.py:825
  13.5 6.2 %collective-permute-start.11 = (bf16[96,768]{1,0:T(8,128)(2,1)S(1)}, bf16[96,768]{1,0:T(8,128)(2,1)S(1)}, u32[]{:S(2)}, u32[]{:S(2)}) collective-permute-start(bf16[96,768]{1,0:T(8,128)(2,1)S(1)} %get-tuple-element.181.refs_4_), channel_id=1, source_target_pairs={{0,1},{1,0},{2,3},{3,2},{4,5},{5,4},{6,7},{7,6},{8,9},{9,8},{10,11... | collective-permute-start | bytes 442376 | tf_op jit(solution)/shard_map/ppermute | solution.py:588
  15.3 5.0 %collective-permute-start.7 = (bf16[192,768]{1,0:T(8,128)(2,1)S(1)}, bf16[192,768]{1,0:T(8,128)(2,1)S(1)}, u32[]{:S(2)}, u32[]{:S(2)}) collective-permute-start(bf16[192,768]{1,0:T(8,128)(2,1)S(1)} %get-tuple-element.179.refs_3_), channel_id=1, source_target_pairs={{0,1},{1,0},{2,3},{3,2},{4,5},{5,4},{6,7},{7,6},{8,9},{9,8},{10,11... | collective-permute-start | bytes 884744 | tf_op jit(solution)/shard_map/ppermute | solution.py:588
  16.4 5.1 %collective-permute-start.10 = (bf16[192,768]{1,0:T(8,128)(2,1)S(1)}, bf16[192,768]{1,0:T(8,128)(2,1)S(1)}, u32[]{:S(2)}, u32[]{:S(2)}) collective-permute-start(bf16[192,768]{1,0:T(8,128)(2,1)S(1)} %get-tuple-element.180.refs_2_), channel_id=1, source_target_pairs={{0,1},{1,0},{2,3},{3,2},{4,5},{5,4},{6,7},{7,6},{8,9},{9,8},{10,11... | collective-permute-start | bytes 884744 | tf_op jit(solution)/shard_map/ppermute | solution.py:588
  19.7 2.4 %collective-permute-start.12 = (bf16[192,768]{1,0:T(8,128)(2,1)S(1)}, bf16[192,768]{1,0:T(8,128)(2,1)S(1)}, u32[]{:S(2)}, u32[]{:S(2)}) collective-permute-start(bf16[192,768]{1,0:T(8,128)(2,1)S(1)} %concatenate.21.refs_3_), channel_id=1, source_target_pairs={{0,1},{1,0},{2,3},{3,2},{4,5},{5,4},{6,7},{7,6},{8,9},{9,8},{10,11... | collective-permute-start | bytes 884744 | tf_op jit(solution)/shard_map/ppermute | solution.py:588
  20.3 2.1 collective-permute-start.8
  21.5 1.7 collective-permute-start.9
  22.1 3.6 %collective-permute-start.3 = (bf16[2,192]{1,0:T(2,128)(2,1)S(1)}, bf16[2,192]{1,0:T(2,128)(2,1)S(1)}, u32[]{:S(2)}, u32[]{:S(2)}) collective-permute-start(bf16[2,192]{1,0:T(2,128)(2,1)S(1)} %pad_maximum_fusion.4.refs_4_), channel_id=1, source_target_pairs={{0,2},{2,0},{1,3},{3,1},{4,6},{6,4},{5,7},{7,5},{8,10},{10,8},{9,1... | collective-permute-start | bytes 2312 | tf_op jit(solution)/shard_map/ppermute | solution.py:592
  22.3 3.4 %collective-permute-start.2 = (bf16[2,192]{1,0:T(2,128)(2,1)S(1)}, bf16[2,192]{1,0:T(2,128)(2,1)S(1)}, u32[]{:S(2)}, u32[]{:S(2)}) collective-permute-start(bf16[2,192]{1,0:T(2,128)(2,1)S(1)} %pad_maximum_fusion.4.refs_4_), channel_id=1, source_target_pairs={{0,1},{1,0},{2,3},{3,2},{4,5},{5,4},{6,7},{7,6},{8,9},{9,8},{10,11... | collective-permute-start | bytes 2312 | tf_op jit(solution)/shard_map/ppermute | solution.py:588
  22.4 161.5 %copy-start.7 = (s32[18]{0:T(128)}, s32[18]{0:T(128)S(1)}, u32[]{:S(2)}) copy-start(s32[18]{0:T(128)S(1)} %pad_add_fusion.refs_3_.refs_0_.info_ref) | copy-start | bytes 220
  25.7 2.6 %collective-permute-start.13 = (bf16[192,2304]{1,0:T(8,128)(2,1)S(1)}, bf16[192,2304]{1,0:T(8,128)(2,1)S(1)}, u32[]{:S(2)}, u32[]{:S(2)}) collective-permute-start(bf16[192,2304]{1,0:T(8,128)(2,1)S(1)} %get-tuple-element.182.refs_10_), channel_id=1, source_target_pairs={{0,1},{1,0},{2,3},{3,2},{4,5},{5,4},{6,7},{7,6},{8,9},{9,8},{10,11... | collective-permute-start | bytes 2654216 | tf_op jit(solution)/shard_map/ppermute | solution.py:588
  25.8 2.5 %collective-permute-start.4 = (bf16[2,192]{1,0:T(2,128)(2,1)S(1)}, bf16[2,192]{1,0:T(2,128)(2,1)S(1)}, u32[]{:S(2)}, u32[]{:S(2)}) collective-permute-start(bf16[2,192]{1,0:T(2,128)(2,1)S(1)} %collective-permute-done.3.refs_5_.refs_6_), channel_id=1, source_target_pairs={{0,1},{1,0},{2,3},{3,2},{4,5},{5,4},{6,7},{7,6},{8,9},{9,8},{10,11... | collective-permute-start | bytes 2312 | tf_op jit(solution)/shard_map/ppermute | solution.py:588
  26.3 9.6 %collective-permute-start.15 = (bf16[96,768]{1,0:T(8,128)(2,1)S(1)}, bf16[96,768]{1,0:T(8,128)(2,1)S(1)}, u32[]{:S(2)}, u32[]{:S(2)}) collective-permute-start(bf16[96,768]{1,0:T(8,128)(2,1)S(1)} %get-tuple-element.187), channel_id=1, source_target_pairs={{0,2},{2,0},{1,3},{3,1},{4,6},{6,4},{5,7},{7,5},{8,10},{10,8},{9,1... | collective-permute-start | bytes 442376 | tf_op jit(solution)/shard_map/ppermute | solution.py:592
  26.5 12.0 %collective-permute-start.14 = (bf16[192,768]{1,0:T(8,128)(2,1)S(1)}, bf16[192,768]{1,0:T(8,128)(2,1)S(1)}, u32[]{:S(2)}, u32[]{:S(2)}) collective-permute-start(bf16[192,768]{1,0:T(8,128)(2,1)S(1)} %get-tuple-element.186), channel_id=1, source_target_pairs={{0,2},{2,0},{1,3},{3,1},{4,6},{6,4},{5,7},{7,5},{8,10},{10,8},{9,1... | collective-permute-start | bytes 884744 | tf_op jit(solution)/shard_map/ppermute | solution.py:592
  28.4 14.5 %copy-start.1 = (bf16[192,768]{1,0:T(8,128)(2,1)S(1)}, bf16[192,768]{1,0:T(8,128)(2,1)}, u32[]{:S(2)}) copy-start(bf16[192,768]{1,0:T(8,128)(2,1)} %refs_2_.1) | copy-start | bytes 884740
  38.5 4.5 %collective-permute-start.16 = (bf16[192,768]{1,0:T(8,128)(2,1)S(1)}, bf16[192,768]{1,0:T(8,128)(2,1)S(1)}, u32[]{:S(2)}, u32[]{:S(2)}) collective-permute-start(bf16[192,768]{1,0:T(8,128)(2,1)S(1)} %get-tuple-element.189.refs_7_), channel_id=1, source_target_pairs={{0,1},{1,0},{2,3},{3,2},{4,5},{5,4},{6,7},{7,6},{8,9},{9,8},{10,11... | collective-permute-start | bytes 884744 | tf_op jit(solution)/shard_map/ppermute | solution.py:588
  38.5 13.5 %collective-permute-start.18 = (bf16[192,768]{1,0:T(8,128)(2,1)S(1)}, bf16[192,768]{1,0:T(8,128)(2,1)S(1)}, u32[]{:S(2)}, u32[]{:S(2)}) collective-permute-start(bf16[192,768]{1,0:T(8,128)(2,1)S(1)} %get-tuple-element.196.refs_9_), channel_id=1, source_target_pairs={{0,2},{2,0},{1,3},{3,1},{4,6},{6,4},{5,7},{7,5},{8,10},{10,8},{9,1... | collective-permute-start | bytes 884744 | tf_op jit(solution)/shard_map/ppermute | solution.py:592
  38.7 13.2 %collective-permute-start.17 = (bf16[96,768]{1,0:T(8,128)(2,1)S(1)}, bf16[96,768]{1,0:T(8,128)(2,1)S(1)}, u32[]{:S(2)}, u32[]{:S(2)}) collective-permute-start(bf16[96,768]{1,0:T(8,128)(2,1)S(1)} %get-tuple-element.195.refs_5_), channel_id=1, source_target_pairs={{0,4},{4,0},{8,12},{12,8},{16,20},{20,16},{24,28},{28,24},{1,5},{5... | collective-permute-start | bytes 442376 | tf_op jit(solution)/shard_map/ppermute | solution.py:854
  41.4 12.8 %collective-permute-start.19 = (bf16[192,768]{1,0:T(8,128)(2,1)S(1)}, bf16[192,768]{1,0:T(8,128)(2,1)S(1)}, u32[]{:S(2)}, u32[]{:S(2)}) collective-permute-start(bf16[192,768]{1,0:T(8,128)(2,1)S(1)} %get-tuple-element.197.refs_13_), channel_id=1, source_target_pairs={{0,2},{2,0},{1,3},{3,1},{4,6},{6,4},{5,7},{7,5},{8,10},{10,8},{9,1... | collective-permute-start | bytes 884744 | tf_op jit(solution)/shard_map/ppermute | solution.py:592
  54.2 3.1 %collective-permute-start.22 = (bf16[192,768]{1,0:T(8,128)(2,1)S(1)}, bf16[192,768]{1,0:T(8,128)(2,1)S(1)}, u32[]{:S(2)}, u32[]{:S(2)}) collective-permute-start(bf16[192,768]{1,0:T(8,128)(2,1)S(1)} %get-tuple-element.201.refs_11_), channel_id=1, source_target_pairs={{0,1},{1,0},{2,3},{3,2},{4,5},{5,4},{6,7},{7,6},{8,9},{9,8},{10,11... | collective-permute-start | bytes 884744 | tf_op jit(solution)/shard_map/ppermute | solution.py:588
  54.2 3.1 %collective-permute-start.23 = (bf16[192,768]{1,0:T(8,128)(2,1)S(1)}, bf16[192,768]{1,0:T(8,128)(2,1)S(1)}, u32[]{:S(2)}, u32[]{:S(2)}) collective-permute-start(bf16[192,768]{1,0:T(8,128)(2,1)S(1)} %get-tuple-element.202.refs_15_), channel_id=1, source_target_pairs={{0,1},{1,0},{2,3},{3,2},{4,5},{5,4},{6,7},{7,6},{8,9},{9,8},{10,11... | collective-permute-start | bytes 884744 | tf_op jit(solution)/shard_map/ppermute | solution.py:588
  54.7 1.7 collective-permute-start.20
  54.7 2.5 %collective-permute-start.21 = (bf16[96,768]{1,0:T(8,128)(2,1)S(1)}, bf16[96,768]{1,0:T(8,128)(2,1)S(1)}, u32[]{:S(2)}, u32[]{:S(2)}) collective-permute-start(bf16[96,768]{1,0:T(8,128)(2,1)S(1)} %get-tuple-element.200.refs_6_), channel_id=1, source_target_pairs={{0,1},{1,0},{2,3},{3,2},{4,5},{5,4},{6,7},{7,6},{8,9},{9,8},{10,11... | collective-permute-start | bytes 442376 | tf_op jit(solution)/shard_map/ppermute | solution.py:588
  55.2 16.2 %collective-permute-start.25 = (bf16[96,768]{1,0:T(8,128)(2,1)S(1)}, bf16[96,768]{1,0:T(8,128)(2,1)S(1)}, u32[]{:S(2)}, u32[]{:S(2)}) collective-permute-start(bf16[96,768]{1,0:T(8,128)(2,1)S(1)} %get-tuple-element.205.refs_7_), channel_id=1, source_target_pairs={{0,2},{2,0},{1,3},{3,1},{4,6},{6,4},{5,7},{7,5},{8,10},{10,8},{9,1... | collective-permute-start | bytes 442376 | tf_op jit(solution)/shard_map/ppermute | solution.py:592
  56.4 15.1 %collective-permute-start.24 = (bf16[192,768]{1,0:T(8,128)(2,1)S(1)}, bf16[192,768]{1,0:T(8,128)(2,1)S(1)}, u32[]{:S(2)}, u32[]{:S(2)}) collective-permute-start(bf16[192,768]{1,0:T(8,128)(2,1)S(1)} %get-tuple-element.199.refs_3_), channel_id=1, source_target_pairs={{0,2},{2,0},{1,3},{3,1},{4,6},{6,4},{5,7},{7,5},{8,10},{10,8},{9,1... | collective-permute-start | bytes 884744 | tf_op jit(solution)/shard_map/ppermute | solution.py:592
  72.0 3.8 %collective-permute-start.28 = (bf16[2,1152,384]{2,1,0:T(8,128)(2,1)S(1)}, bf16[2,1152,384]{2,1,0:T(8,128)(2,1)S(1)}, u32[]{:S(2)}, u32[]{:S(2)}) collective-permute-start(bf16[2,1152,384]{2,1,0:T(8,128)(2,1)S(1)} %get-tuple-element.215), channel_id=1, source_target_pairs={{0,1},{1,0},{2,3},{3,2},{4,5},{5,4},{6,7},{7,6},{8,9},{9,8},{10,11... | collective-permute-start | bytes 5308424 | tf_op jit(solution)/shard_map/ppermute | solution.py:588
  72.1 8.3 %collective-permute-start.26 = (bf16[192,768]{1,0:T(8,128)(2,1)S(1)}, bf16[192,768]{1,0:T(8,128)(2,1)S(1)}, u32[]{:S(2)}, u32[]{:S(2)}) collective-permute-start(bf16[192,768]{1,0:T(8,128)(2,1)S(1)} %get-tuple-element.207.refs_5_), channel_id=1, source_target_pairs={{0,1},{1,0},{2,3},{3,2},{4,5},{5,4},{6,7},{7,6},{8,9},{9,8},{10,11... | collective-permute-start | bytes 884744 | tf_op jit(solution)/shard_map/ppermute | solution.py:588
  72.6 7.8 %collective-permute-start.27 = (bf16[96,768]{1,0:T(8,128)(2,1)S(1)}, bf16[96,768]{1,0:T(8,128)(2,1)S(1)}, u32[]{:S(2)}, u32[]{:S(2)}) collective-permute-start(bf16[96,768]{1,0:T(8,128)(2,1)S(1)} %get-tuple-element.208.refs_9_), channel_id=1, source_target_pairs={{0,1},{1,0},{2,3},{3,2},{4,5},{5,4},{6,7},{7,6},{8,9},{9,8},{10,11... | collective-permute-start | bytes 442376 | tf_op jit(solution)/shard_map/ppermute | solution.py:588
  76.8 16.9 %collective-permute-start.30 = (bf16[2,288,384]{2,1,0:T(8,128)(2,1)S(1)}, bf16[2,288,384]{2,1,0:T(8,128)(2,1)S(1)}, u32[]{:S(2)}, u32[]{:S(2)}) collective-permute-start(bf16[2,288,384]{2,1,0:T(8,128)(2,1)S(1)} %get-tuple-element.227), channel_id=1, source_target_pairs={{0,4},{4,0},{8,12},{12,8},{16,20},{20,16},{24,28},{28,24},{1,5},{5... | collective-permute-start | bytes 1327112 | tf_op jit(solution)/shard_map/ppermute | solution.py:640
  79.2 14.4 %collective-permute-start.29 = (bf16[576,384]{1,0:T(8,128)(2,1)S(1)}, bf16[576,384]{1,0:T(8,128)(2,1)S(1)}, u32[]{:S(2)}, u32[]{:S(2)}) collective-permute-start(bf16[576,384]{1,0:T(8,128)(2,1)S(1)} %get-tuple-element.218.refs_18_), channel_id=1, source_target_pairs={{0,2},{2,0},{1,3},{3,1},{4,6},{6,4},{5,7},{7,5},{8,10},{10,8},{9,1... | collective-permute-start | bytes 1327112 | tf_op jit(solution)/shard_map/ppermute | solution.py:592
  94.5 8.5 %collective-permute-start.33 = (bf16[2,960,384]{2,1,0:T(8,128)(2,1)S(1)}, bf16[2,960,384]{2,1,0:T(8,128)(2,1)S(1)}, u32[]{:S(2)}, u32[]{:S(2)}) collective-permute-start(bf16[2,960,384]{2,1,0:T(8,128)(2,1)S(1)} %get-tuple-element.232.refs_12_), channel_id=1, source_target_pairs={{0,1},{1,0},{2,3},{3,2},{4,5},{5,4},{6,7},{7,6},{8,9},{9,8},{10,11... | collective-permute-start | bytes 4423688 | tf_op jit(solution)/shard_map/ppermute | solution.py:588
  94.5 7.8 %collective-permute-start.32 = (bf16[288,384]{1,0:T(8,128)(2,1)S(1)}, bf16[288,384]{1,0:T(8,128)(2,1)S(1)}, u32[]{:S(2)}, u32[]{:S(2)}) collective-permute-start(bf16[288,384]{1,0:T(8,128)(2,1)S(1)} %get-tuple-element.240), channel_id=1, source_target_pairs={{0,2},{2,0},{1,3},{3,1},{4,6},{6,4},{5,7},{7,5},{8,10},{10,8},{9,1... | collective-permute-start | bytes 663560 | tf_op jit(solution)/shard_map/ppermute | solution.py:592
  95.5 7.5 %collective-permute-start.31 = (bf16[288,384]{1,0:T(8,128)(2,1)S(1)}, bf16[288,384]{1,0:T(8,128)(2,1)S(1)}, u32[]{:S(2)}, u32[]{:S(2)}) collective-permute-start(bf16[288,384]{1,0:T(8,128)(2,1)S(1)} %get-tuple-element.231.refs_11_), channel_id=1, source_target_pairs={{0,4},{4,0},{8,12},{12,8},{16,20},{20,16},{24,28},{28,24},{1,5},{5... | collective-permute-start | bytes 663560 | tf_op jit(solution)/shard_map/ppermute | solution.py:640
  104.4 10.5 %collective-permute-start.34 = (bf16[288,384]{1,0:T(8,128)(2,1)S(1)}, bf16[288,384]{1,0:T(8,128)(2,1)S(1)}, u32[]{:S(2)}, u32[]{:S(2)}) collective-permute-start(bf16[288,384]{1,0:T(8,128)(2,1)S(1)} %get-tuple-element.244.refs_16_), channel_id=1, source_target_pairs={{0,8},{4,12},{8,0},{12,4},{16,24},{20,28},{24,16},{28,20},{1,9},{5... | collective-permute-start | bytes 663560 | tf_op jit(solution)/shard_map/ppermute | solution.py:640
  106.1 9.5 %collective-permute-start.36 = (bf16[2,240,384]{2,1,0:T(8,128)(2,1)S(1)}, bf16[2,240,384]{2,1,0:T(8,128)(2,1)S(1)}, u32[]{:S(2)}, u32[]{:S(2)}) collective-permute-start(bf16[2,240,384]{2,1,0:T(8,128)(2,1)S(1)} %get-tuple-element.252), channel_id=1, source_target_pairs={{0,4},{4,0},{8,12},{12,8},{16,20},{20,16},{24,28},{28,24},{1,5},{5... | collective-permute-start | bytes 1105928 | tf_op jit(solution)/shard_map/ppermute | solution.py:640
  107.2 9.8 %collective-permute-start.35 = (bf16[480,384]{1,0:T(8,128)(2,1)S(1)}, bf16[480,384]{1,0:T(8,128)(2,1)S(1)}, u32[]{:S(2)}, u32[]{:S(2)}) collective-permute-start(bf16[480,384]{1,0:T(8,128)(2,1)S(1)} %get-tuple-element.245.refs_17_), channel_id=1, source_target_pairs={{0,2},{2,0},{1,3},{3,1},{4,6},{6,4},{5,7},{7,5},{8,10},{10,8},{9,1... | collective-permute-start | bytes 1105928 | tf_op jit(solution)/shard_map/ppermute | solution.py:592
  117.8 10.3 %collective-permute-start.40 = (bf16[2,576,512]{2,1,0:T(8,128)(2,1)S(1)}, bf16[2,576,512]{2,1,0:T(8,128)(2,1)S(1)}, u32[]{:S(2)}, u32[]{:S(2)}) collective-permute-start(bf16[2,576,512]{2,1,0:T(8,128)(2,1)S(1)} %get-tuple-element.258.refs_16_), channel_id=1, source_target_pairs={{0,1},{1,0},{2,3},{3,2},{4,5},{5,4},{6,7},{7,6},{8,9},{9,8},{10,11... | collective-permute-start | bytes 3538952 | tf_op jit(solution)/shard_map/ppermute | solution.py:588
  117.8 10.2 %collective-permute-start.39 = (bf16[240,384]{1,0:T(8,128)(2,1)S(1)}, bf16[240,384]{1,0:T(8,128)(2,1)S(1)}, u32[]{:S(2)}, u32[]{:S(2)}) collective-permute-start(bf16[240,384]{1,0:T(8,128)(2,1)S(1)} %get-tuple-element.264), channel_id=1, source_target_pairs={{0,2},{2,0},{1,3},{3,1},{4,6},{6,4},{5,7},{7,5},{8,10},{10,8},{9,1... | collective-permute-start | bytes 552968 | tf_op jit(solution)/shard_map/ppermute | solution.py:592
  119.1 8.9 %collective-permute-start.38 = (bf16[240,384]{1,0:T(8,128)(2,1)S(1)}, bf16[240,384]{1,0:T(8,128)(2,1)S(1)}, u32[]{:S(2)}, u32[]{:S(2)}) collective-permute-start(bf16[240,384]{1,0:T(8,128)(2,1)S(1)} %get-tuple-element.257.refs_15_), channel_id=1, source_target_pairs={{0,4},{4,0},{8,12},{12,8},{16,20},{20,16},{24,28},{28,24},{1,5},{5... | collective-permute-start | bytes 552968 | tf_op jit(solution)/shard_map/ppermute | solution.py:640
  119.5 13.5 %collective-permute-start.37 = (bf16[288,384]{1,0:T(8,128)(2,1)S(1)}, bf16[288,384]{1,0:T(8,128)(2,1)S(1)}, u32[]{:S(2)}, u32[]{:S(2)}) collective-permute-start(bf16[288,384]{1,0:T(8,128)(2,1)S(1)} %get-tuple-element.256.refs_14_.refs_1_), channel_id=1, source_target_pairs={{0,16},{4,20},{8,24},{12,28},{16,0},{20,4},{24,8},{28,12},{1,17},{... | collective-permute-start | bytes 663560 | tf_op jit(solution)/shard_map/ppermute | solution.py:640
  129.0 10.2 %collective-permute-start.44 = (bf16[2,576,256]{2,1,0:T(8,128)(2,1)S(1)}, bf16[2,576,256]{2,1,0:T(8,128)(2,1)S(1)}, u32[]{:S(2)}, u32[]{:S(2)}) collective-permute-start(bf16[2,576,256]{2,1,0:T(8,128)(2,1)S(1)} %get-tuple-element.275), channel_id=1, source_target_pairs={{0,1},{1,0},{2,3},{3,2},{4,5},{5,4},{6,7},{7,6},{8,9},{9,8},{10,11... | collective-permute-start | bytes 1769480 | tf_op jit(solution)/shard_map/ppermute | solution.py:588
  129.1 9.5 %collective-permute-start.42 = (bf16[288,512]{1,0:T(8,128)(2,1)S(1)}, bf16[288,512]{1,0:T(8,128)(2,1)S(1)}, u32[]{:S(2)}, u32[]{:S(2)}) collective-permute-start(bf16[288,512]{1,0:T(8,128)(2,1)S(1)} %get-tuple-element.272), channel_id=1, source_target_pairs={{0,2},{2,0},{1,3},{3,1},{4,6},{6,4},{5,7},{7,5},{8,10},{10,8},{9,1... | collective-permute-start | bytes 884744 | tf_op jit(solution)/shard_map/ppermute | solution.py:592
  130.0 9.1 %collective-permute-start.43 = (bf16[2,144,512]{2,1,0:T(8,128)(2,1)S(1)}, bf16[2,144,512]{2,1,0:T(8,128)(2,1)S(1)}, u32[]{:S(2)}, u32[]{:S(2)}) collective-permute-start(bf16[2,144,512]{2,1,0:T(8,128)(2,1)S(1)} %get-tuple-element.273), channel_id=1, source_target_pairs={{0,4},{4,0},{8,12},{12,8},{16,20},{20,16},{24,28},{28,24},{1,5},{5... | collective-permute-start | bytes 884744 | tf_op jit(solution)/shard_map/ppermute | solution.py:640
  131.2 6.5 %collective-permute-start.41 = (bf16[240,384]{1,0:T(8,128)(2,1)S(1)}, bf16[240,384]{1,0:T(8,128)(2,1)S(1)}, u32[]{:S(2)}, u32[]{:S(2)}) collective-permute-start(bf16[240,384]{1,0:T(8,128)(2,1)S(1)} %get-tuple-element.269), channel_id=1, source_target_pairs={{0,8},{4,12},{8,0},{12,4},{16,24},{20,28},{24,16},{28,20},{1,9},{5... | collective-permute-start | bytes 552968 | tf_op jit(solution)/shard_map/ppermute | solution.py:640
  140.1 10.0 %collective-permute-start.47 = (bf16[288,256]{1,0:T(8,128)(2,1)S(1)}, bf16[288,256]{1,0:T(8,128)(2,1)S(1)}, u32[]{:S(2)}, u32[]{:S(2)}) collective-permute-start(bf16[288,256]{1,0:T(8,128)(2,1)S(1)} %get-tuple-element.281), channel_id=1, source_target_pairs={{0,2},{2,0},{1,3},{3,1},{4,6},{6,4},{5,7},{7,5},{8,10},{10,8},{9,1... | collective-permute-start | bytes 442376 | tf_op jit(solution)/shard_map/ppermute | solution.py:592
  141.3 20.7 %collective-permute-start.45 = (bf16[288,384]{1,0:T(8,128)(2,1)S(1)}, bf16[288,384]{1,0:T(8,128)(2,1)S(1)}, u32[]{:S(2)}, u32[]{:S(2)}) collective-permute-start(bf16[288,384]{1,0:T(8,128)(2,1)S(1)} %get-tuple-element.277.refs_1_), channel_id=1, source_target_pairs={{0,8},{4,12},{8,0},{12,4},{16,24},{20,28},{24,16},{28,20},{1,9},{5... | collective-permute-start | bytes 663560 | tf_op jit(solution)/shard_map/ppermute | solution.py:640
  142.5 19.5 %collective-permute-start.49 = (bf16[64,1536]{1,0:T(8,128)(2,1)S(1)}, bf16[64,1536]{1,0:T(8,128)(2,1)S(1)}, u32[]{:S(2)}, u32[]{:S(2)}) collective-permute-start(bf16[64,1536]{1,0:T(8,128)(2,1)S(1)} %get-tuple-element.283), channel_id=1, source_target_pairs={{0,4},{4,8},{8,12},{12,16},{16,20},{20,24},{24,28},{1,5},{5,9},{9,... | collective-permute-start | bytes 589832 | tf_op jit(solution)/shard_map/ppermute | solution.py:894
  146.1 15.9 %collective-permute-start.50 = (bf16[64,1536]{1,0:T(8,128)(2,1)S(1)}, bf16[64,1536]{1,0:T(8,128)(2,1)S(1)}, u32[]{:S(2)}, u32[]{:S(2)}) collective-permute-start(bf16[64,1536]{1,0:T(8,128)(2,1)S(1)} %get-tuple-element.284), channel_id=1, source_target_pairs={{4,0},{8,4},{12,8},{16,12},{20,16},{24,20},{28,24},{5,1},{9,5},{13... | collective-permute-start | bytes 589832 | tf_op jit(solution)/shard_map/ppermute | solution.py:894
  147.4 9.2 %collective-permute-start.48 = (bf16[2,144,256]{2,1,0:T(8,128)(2,1)S(1)}, bf16[2,144,256]{2,1,0:T(8,128)(2,1)S(1)}, u32[]{:S(2)}, u32[]{:S(2)}) collective-permute-start(bf16[2,144,256]{2,1,0:T(8,128)(2,1)S(1)} %get-tuple-element.282), channel_id=1, source_target_pairs={{0,4},{4,0},{8,12},{12,8},{16,20},{20,16},{24,28},{28,24},{1,5},{5... | collective-permute-start | bytes 442376 | tf_op jit(solution)/shard_map/ppermute | solution.py:640
  150.1 11.0 %collective-permute-start.46 = (bf16[240,384]{1,0:T(8,128)(2,1)S(1)}, bf16[240,384]{1,0:T(8,128)(2,1)S(1)}, u32[]{:S(2)}, u32[]{:S(2)}) collective-permute-start(bf16[240,384]{1,0:T(8,128)(2,1)S(1)} %get-tuple-element.278.refs_3_), channel_id=1, source_target_pairs={{0,16},{4,20},{8,24},{12,28},{16,0},{20,4},{24,8},{28,12},{1,17},{... | collective-permute-start | bytes 552968 | tf_op jit(solution)/shard_map/ppermute | solution.py:640
  156.6 8.6 %collective-permute-start.53 = (bf16[144,512]{1,0:T(8,128)(2,1)S(1)}, bf16[144,512]{1,0:T(8,128)(2,1)S(1)}, u32[]{:S(2)}, u32[]{:S(2)}) collective-permute-start(bf16[144,512]{1,0:T(8,128)(2,1)S(1)} %get-tuple-element.296), channel_id=1, source_target_pairs={{0,4},{4,0},{8,12},{12,8},{16,20},{20,16},{24,28},{28,24},{1,5},{5... | collective-permute-start | bytes 442376 | tf_op jit(solution)/shard_map/ppermute | solution.py:640
  161.2 12.4 %collective-permute-start.54 = (bf16[144,512]{1,0:T(8,128)(2,1)S(1)}, bf16[144,512]{1,0:T(8,128)(2,1)S(1)}, u32[]{:S(2)}, u32[]{:S(2)}) collective-permute-start(bf16[144,512]{1,0:T(8,128)(2,1)S(1)} %get-tuple-element.297), channel_id=1, source_target_pairs={{0,2},{2,0},{1,3},{3,1},{4,6},{6,4},{5,7},{7,5},{8,10},{10,8},{9,1... | collective-permute-start | bytes 442376 | tf_op jit(solution)/shard_map/ppermute | solution.py:592
  162.7 10.8 %collective-permute-start.56 = (bf16[144,256]{1,0:T(8,128)(2,1)S(1)}, bf16[144,256]{1,0:T(8,128)(2,1)S(1)}, u32[]{:S(2)}, u32[]{:S(2)}) collective-permute-start(bf16[144,256]{1,0:T(8,128)(2,1)S(1)} %get-tuple-element.300), channel_id=1, source_target_pairs={{0,2},{2,0},{1,3},{3,1},{4,6},{6,4},{5,7},{7,5},{8,10},{10,8},{9,1... | collective-permute-start | bytes 221192 | tf_op jit(solution)/shard_map/ppermute | solution.py:592
  164.0 9.6 %collective-permute-start.55 = (bf16[144,256]{1,0:T(8,128)(2,1)S(1)}, bf16[144,256]{1,0:T(8,128)(2,1)S(1)}, u32[]{:S(2)}, u32[]{:S(2)}) collective-permute-start(bf16[144,256]{1,0:T(8,128)(2,1)S(1)} %get-tuple-element.292.refs_16_), channel_id=1, source_target_pairs={{0,4},{4,0},{8,12},{12,8},{16,20},{20,16},{24,28},{28,24},{1,5},{5... | collective-permute-start | bytes 221192 | tf_op jit(solution)/shard_map/ppermute | solution.py:640
  164.0 9.6 %collective-permute-start.52 = (bf16[240,384]{1,0:T(8,128)(2,1)S(1)}, bf16[240,384]{1,0:T(8,128)(2,1)S(1)}, u32[]{:S(2)}, u32[]{:S(2)}) collective-permute-start(bf16[240,384]{1,0:T(8,128)(2,1)S(1)} %get-tuple-element.291.refs_15_.refs_3_), channel_id=1, source_target_pairs={{0,8},{4,12},{8,0},{12,4},{16,24},{20,28},{24,16},{28,20},{1,9},{5... | collective-permute-start | bytes 552968 | tf_op jit(solution)/shard_map/ppermute | solution.py:640
  165.3 10.3 %collective-permute-start.51 = (bf16[576,384]{1,0:T(8,128)(2,1)S(1)}, bf16[576,384]{1,0:T(8,128)(2,1)S(1)}, u32[]{:S(2)}, u32[]{:S(2)}) collective-permute-start(bf16[576,384]{1,0:T(8,128)(2,1)S(1)} %get-tuple-element.290.refs_14_.refs_1_), channel_id=1, source_target_pairs={{0,4},{4,0},{8,12},{12,8},{16,20},{20,16},{24,28},{28,24},{1,5},{5... | collective-permute-start | bytes 1327112 | tf_op jit(solution)/shard_map/ppermute | solution.py:640
  176.4 7.6 %collective-permute-start.57 = (bf16[480,384]{1,0:T(8,128)(2,1)S(1)}, bf16[480,384]{1,0:T(8,128)(2,1)S(1)}, u32[]{:S(2)}, u32[]{:S(2)}) collective-permute-start(bf16[480,384]{1,0:T(8,128)(2,1)S(1)} %get-tuple-element.302.refs_1_), channel_id=1, source_target_pairs={{0,4},{4,0},{8,12},{12,8},{16,20},{20,16},{24,28},{28,24},{1,5},{5... | collective-permute-start | bytes 1105928 | tf_op jit(solution)/shard_map/ppermute | solution.py:640
  177.3 5.9 %collective-permute-start.58 = (bf16[144,768]{1,0:T(8,128)(2,1)S(1)}, bf16[144,768]{1,0:T(8,128)(2,1)S(1)}, u32[]{:S(2)}, u32[]{:S(2)}) collective-permute-start(bf16[144,768]{1,0:T(8,128)(2,1)S(1)} %get-tuple-element.304), channel_id=1, source_target_pairs={{0,8},{4,12},{8,0},{12,4},{16,24},{20,28},{24,16},{28,20},{1,9},{5... | collective-permute-start | bytes 663560 | tf_op jit(solution)/shard_map/ppermute | solution.py:640
  185.5 9.7 %collective-permute-start.59 = (bf16[144,768]{1,0:T(8,128)(2,1)S(1)}, bf16[144,768]{1,0:T(8,128)(2,1)S(1)}, u32[]{:S(2)}, u32[]{:S(2)}) collective-permute-start(bf16[144,768]{1,0:T(8,128)(2,1)S(1)} %get-tuple-element.306.refs_1_), channel_id=1, source_target_pairs={{0,16},{4,20},{8,24},{12,28},{16,0},{20,4},{24,8},{28,12},{1,17},{... | collective-permute-start | bytes 663560 | tf_op jit(solution)/shard_map/ppermute | solution.py:640
  195.8 6.0 %collective-permute-start.60 = (bf16[144,768]{1,0:T(8,128)(2,1)S(1)}, bf16[144,768]{1,0:T(8,128)(2,1)S(1)}, u32[]{:S(2)}, u32[]{:S(2)}) collective-permute-start(bf16[144,768]{1,0:T(8,128)(2,1)S(1)} %get-tuple-element.308.refs_1_), channel_id=1, source_target_pairs={{0,8},{4,12},{8,0},{12,4},{16,24},{20,28},{24,16},{28,20},{1,9},{5... | collective-permute-start | bytes 663560 | tf_op jit(solution)/shard_map/ppermute | solution.py:640
  203.0 9.5 %collective-permute-start.61 = (bf16[288,768]{1,0:T(8,128)(2,1)S(1)}, bf16[288,768]{1,0:T(8,128)(2,1)S(1)}, u32[]{:S(2)}, u32[]{:S(2)}) collective-permute-start(bf16[288,768]{1,0:T(8,128)(2,1)S(1)} %get-tuple-element.310.refs_0_.refs_1_.refs_2_), channel_id=1, source_target_pairs={{0,4},{4,0},{8,12},{12,8},{16,20},{20,16},{24,28},{28,24},{1,5},{5... | collective-permute-start | bytes 1327112 | tf_op jit(solution)/shard_map/ppermute | solution.py:640
  (28 other events, 167.5 us)
